TPU v7x, 32 devices: a whole 2x2x4 slice. The times are simulated.
32 devices in a mesh: seq: 8 (over z, y), batch: 4 (over x, core).
Axes of the slice: x: 2, y: 2, z: 4, core: 2. Of those that a mesh axis runs over, the one named last changes fastest.
Arguments:
- layer_input: bfloat16 [8, 4096, 1024], P('batch', 'seq'), may hold values from -6 to 6
- skip_input: bfloat16 [8, 4096, 1024], P('batch', 'seq'), may hold values from -6 to 6
- time_embed: bfloat16 [8, 1024], P('batch'), may hold values from -6 to 6
- lengths: int32 [8], P('batch'), may hold values from 273 to 4096, as said below
- cond_drop: int32 [8], P('batch'), may hold values 0 or 1
- cotangent: bfloat16 [8, 4096, 1024], P('batch', 'seq'), may hold values from -6 to 6
- skip_weight: bfloat16 [2048, 1024], P('seq'), may hold values from -0.125 to 0.125
- adaln_weight: bfloat16 [1024, 6144], P('seq'), may hold values from -0.1875 to 0.1875
- adaln_bias: bfloat16 [6144], P('seq'), may hold values from -3 to 3
- qkv_weight: bfloat16 [1024, 3072], P('seq'), may hold values from -0.1875 to 0.1875
- out_weight: bfloat16 [1024, 1024], P('seq'), may hold values from -3 to 3
- up_weight: bfloat16 [1024, 4096], P('seq'), may hold values from -0.1875 to 0.1875
- down_weight: bfloat16 [4096, 1024], P('seq'), may hold values from -0.09375 to 0.09375
Outputs:
- layer_output: bfloat16 [8, 4096, 1024], P('batch', 'seq')
- grad_input: bfloat16 [8, 4096, 1024], P('batch', 'seq')
- grad_skip: bfloat16 [8, 4096, 1024], P('batch', 'seq')
- grad_skip_weight: float32 [2048, 1024], P('seq')
- grad_adaln_weight: float32 [1024, 6144], P('seq')
- grad_adaln_bias: float32 [6144], P('seq')
- grad_qkv_weight: float32 [1024, 3072], P('seq')
- grad_out_weight: float32 [1024, 1024], P('seq')
- grad_up_weight: float32 [1024, 4096], P('seq')
- grad_down_weight: float32 [4096, 1024], P('seq')
Inputs may be any that keep to these rules, and one draw needn't show every extreme that they name: `lengths`: of the 2 utterances that one index of batch holds, one has all 4096 frames.
All inputs are finite; a program needn't handle non-finite values. No bound on the sum of `cond_drop` on one device may be relied on, other than what follows from the above.
Results may differ from a plain program's by a relative error of at most 0.019.
Values may be sent and summed in bfloat16 or wider, within the bound.
A program may use at most 480 MiB of HBM per device.

v0:
```python
import jax
import jax.numpy as jnp
from jax import lax
from jax.sharding import PartitionSpec as P

HEAD_DIM = 64


EPS = 1e-06
MASKED = -1e30


def layer_norm(stream):
    centre = stream - jnp.mean(stream, axis=-1, keepdims=True)
    spread = jnp.mean(centre * centre, axis=-1, keepdims=True)
    inverse = lax.rsqrt(spread + EPS)
    return (centre * inverse, inverse)


def norm_back(grad_normed, normed, inverse):
    first_mean = jnp.mean(grad_normed, axis=-1, keepdims=True)
    second_mean = jnp.mean(grad_normed * normed, axis=-1, keepdims=True)
    return inverse * (grad_normed - first_mean - normed * second_mean)


def rotary_tables(positions):
    half_dim = HEAD_DIM // 2
    channel = jnp.arange(half_dim, dtype=jnp.float32)
    inverse = jnp.power(10000.0, -2.0 * channel / HEAD_DIM)
    angles = positions.astype(jnp.float32)[:, None] * inverse[None, :]
    angles = jnp.concatenate([angles, angles], axis=1)
    return (jnp.cos(angles), jnp.sin(angles))


def rotate_heads(field, cosine_table, sine_table):
    half_dim = field.shape[-1] // 2
    turned = jnp.concatenate([-field[..., half_dim:], field[..., :half_dim]], axis=-1)
    return field * cosine_table + turned * sine_table


def smooth_gelu(values):
    return jax.nn.gelu(values, approximate=True)


def cross(left, right):
    return lax.dot_general(
        left, right, (((0,), (0,)), ((), ())), preferred_element_type=jnp.float32
    )


def back_product(left, right):
    return lax.dot_general(
        left, right, (((1,), (1,)), ((), ())), preferred_element_type=jnp.float32
    )


def block_terms(query_block, dout_block, lse_block, delta_block, key_block, value_block, key_live):
    scores = jnp.einsum(
        "bqhd,bkhd->bhqk", query_block, key_block, preferred_element_type=jnp.float32
    )
    lse_heads = jnp.transpose(lse_block, (0, 2, 1))[..., None]
    probs = jnp.where(key_live[:, None, None, :], jnp.exp(scores - lse_heads), 0.0)
    grad_probs = jnp.einsum(
        "bqhd,bkhd->bhqk", dout_block, value_block, preferred_element_type=jnp.float32
    )
    delta_heads = jnp.transpose(delta_block, (0, 2, 1))[..., None]
    dscore = (probs * (grad_probs - delta_heads)).astype(jnp.bfloat16)
    return (probs.astype(jnp.bfloat16), dscore)


def on_device(
    layer_input,
    skip_input,
    time_embed,
    lengths,
    cond_drop,
    cotangent,
    skip_weight,
    adaln_weight,
    adaln_bias,
    qkv_weight,
    out_weight,
    up_weight,
    down_weight,
):
    utt_count, frame_span, model_width = layer_input.shape
    head_count = model_width // HEAD_DIM
    row_count = utt_count * frame_span
    seq_here = lax.axis_index("seq")
    local_pos = seq_here * frame_span + jnp.arange(frame_span, dtype=jnp.int32)
    local_live = local_pos[None, :] < lengths[:, None]
    valid_mask = local_live.astype(jnp.float32)
    dropped = cond_drop.astype(jnp.float32)[:, None] * valid_mask
    kept_total, drop_total = lax.psum(
        (jnp.sum(valid_mask - dropped), jnp.sum(dropped)), ("seq", "batch")
    )
    kept_total = jnp.maximum(kept_total, 1.0)
    drop_total = jnp.maximum(drop_total, 1.0)
    every_count = kept_total + drop_total
    loss_weight = (valid_mask - dropped) * (every_count / (2.0 * kept_total)) + dropped * (
        every_count / (2.0 * drop_total)
    )
    gathered = (
        lax.all_gather(skip_weight, "seq", axis=0, tiled=True),
        lax.all_gather(adaln_weight, "seq", axis=0, tiled=True),
        lax.all_gather(adaln_bias, "seq", axis=0, tiled=True),
        lax.all_gather(qkv_weight, "seq", axis=0, tiled=True),
        lax.all_gather(out_weight, "seq", axis=0, tiled=True),
        lax.all_gather(up_weight, "seq", axis=0, tiled=True),
        lax.all_gather(down_weight, "seq", axis=0, tiled=True),
    )
    skip_full, adaln_full, bias_full, qkv_full, out_full, up_full, down_full = gathered
    joined = jnp.concatenate([layer_input, skip_input], axis=-1).reshape(row_count, 2 * model_width)
    residual_in = jnp.dot(joined, skip_full, preferred_element_type=jnp.float32).reshape(
        utt_count, frame_span, model_width
    )
    silu_time = jax.nn.silu(time_embed.astype(jnp.float32)).astype(jnp.bfloat16)
    modulation = jnp.dot(
        silu_time, adaln_full, preferred_element_type=jnp.float32
    ) + bias_full.astype(jnp.float32)
    modulation = modulation.reshape(utt_count, 6, model_width)
    shift_attn = modulation[:, 0][:, None, :]
    scale_attn = modulation[:, 1][:, None, :]
    gate_attn = modulation[:, 2][:, None, :]
    shift_ffn = modulation[:, 3][:, None, :]
    scale_ffn = modulation[:, 4][:, None, :]
    gate_ffn = modulation[:, 5][:, None, :]
    hat_attn, inv_attn = layer_norm(residual_in)
    normed_attn = (
        (hat_attn * (1.0 + scale_attn) + shift_attn)
        .astype(jnp.bfloat16)
        .reshape(row_count, model_width)
    )
    projected = jnp.dot(normed_attn, qkv_full, preferred_element_type=jnp.float32).reshape(
        utt_count, frame_span, 3, head_count, HEAD_DIM
    )
    cosine_table, sine_table = rotary_tables(local_pos)
    cosine_table = cosine_table[None, :, None, :]
    sine_table = sine_table[None, :, None, :]
    queries = (rotate_heads(projected[:, :, 0], cosine_table, sine_table) * 0.125).astype(
        jnp.bfloat16
    )
    keys_rot = rotate_heads(projected[:, :, 1], cosine_table, sine_table).astype(jnp.bfloat16)
    values = projected[:, :, 2].astype(jnp.bfloat16)
    start_top = jnp.full((utt_count, head_count, frame_span), MASKED, jnp.float32)
    top_score = start_top
    key_piece = lax.all_gather(keys_rot, "seq", axis=1, tiled=True)
    value_piece = lax.all_gather(values, "seq", axis=1, tiled=True)
    piece_len = key_piece.shape[1]
    piece_live = jnp.arange(piece_len, dtype=jnp.int32)[None, :] < lengths[:, None]
    scores = jnp.einsum("bqhd,bkhd->bhqk", queries, key_piece, preferred_element_type=jnp.float32)
    scores = jnp.where(piece_live[:, None, None, :], scores, MASKED)
    new_top = jnp.maximum(top_score, jnp.max(scores, axis=-1))
    expo = jnp.where(piece_live[:, None, None, :], jnp.exp(scores - new_top[..., None]), 0.0)
    denom = jnp.sum(expo, axis=-1)
    partial_out = jnp.einsum(
        "bhqk,bkhd->bqhd",
        expo.astype(jnp.bfloat16),
        value_piece,
        preferred_element_type=jnp.float32,
    )
    accum = partial_out
    accum, top_score, denom = (accum, new_top, denom)
    attended_full = accum / jnp.transpose(denom, (0, 2, 1))[..., None]
    lse_rows = jnp.transpose(top_score + jnp.log(denom), (0, 2, 1))
    attended_low = attended_full.astype(jnp.bfloat16).reshape(row_count, model_width)
    branch_attn = jnp.dot(attended_low, out_full, preferred_element_type=jnp.float32).reshape(
        utt_count, frame_span, model_width
    )
    residual_mid = residual_in + gate_attn * branch_attn
    hat_ffn, inv_ffn = layer_norm(residual_mid)
    normed_ffn = (
        (hat_ffn * (1.0 + scale_ffn) + shift_ffn)
        .astype(jnp.bfloat16)
        .reshape(row_count, model_width)
    )
    hidden_pre = jnp.dot(normed_ffn, up_full, preferred_element_type=jnp.float32)
    hidden_act = smooth_gelu(hidden_pre).astype(jnp.bfloat16)
    branch_ffn = jnp.dot(hidden_act, down_full, preferred_element_type=jnp.float32).reshape(
        utt_count, frame_span, model_width
    )
    layer_output = (residual_mid + gate_ffn * branch_ffn).astype(jnp.bfloat16)
    back_weights = (
        lax.all_gather(skip_weight, "seq", axis=0, tiled=True),
        lax.all_gather(adaln_weight, "seq", axis=0, tiled=True),
        lax.all_gather(adaln_bias, "seq", axis=0, tiled=True),
        lax.all_gather(qkv_weight, "seq", axis=0, tiled=True),
        lax.all_gather(out_weight, "seq", axis=0, tiled=True),
        lax.all_gather(up_weight, "seq", axis=0, tiled=True),
        lax.all_gather(down_weight, "seq", axis=0, tiled=True),
    )
    skip_back, adaln_back, bias_back, qkv_back, out_back, up_back, down_back = back_weights
    upstream = cotangent.astype(jnp.float32) * loss_weight[..., None]
    grad_branch_ffn = (upstream * gate_ffn).astype(jnp.bfloat16).reshape(row_count, model_width)
    grad_gate_ffn = jnp.sum(upstream * branch_ffn, axis=1)
    grad_down = cross(hidden_act, grad_branch_ffn)
    grad_hidden_act = back_product(grad_branch_ffn, down_back)
    gelu_value, gelu_pull = jax.vjp(smooth_gelu, hidden_pre)
    grad_hidden_pre = gelu_pull(grad_hidden_act)[0].astype(jnp.bfloat16)
    grad_up = cross(normed_ffn, grad_hidden_pre)
    grad_normed_ffn = back_product(grad_hidden_pre, up_back).reshape(
        utt_count, frame_span, model_width
    )
    grad_shift_ffn = jnp.sum(grad_normed_ffn, axis=1)
    grad_scale_ffn = jnp.sum(grad_normed_ffn * hat_ffn, axis=1)
    grad_mid = upstream + norm_back(grad_normed_ffn * (1.0 + scale_ffn), hat_ffn, inv_ffn)
    grad_branch_attn = (grad_mid * gate_attn).astype(jnp.bfloat16).reshape(row_count, model_width)
    grad_gate_attn = jnp.sum(grad_mid * branch_attn, axis=1)
    grad_out = cross(attended_low, grad_branch_attn)
    grad_attended = (
        back_product(grad_branch_attn, out_back)
        .astype(jnp.bfloat16)
        .reshape(utt_count, frame_span, head_count, HEAD_DIM)
    )
    delta_rows = jnp.sum(grad_attended.astype(jnp.float32) * attended_full, axis=-1)
    lse_all, delta_all = (
        lax.all_gather(lse_rows, "seq", axis=1, tiled=True),
        lax.all_gather(delta_rows, "seq", axis=1, tiled=True),
    )
    key_piece = lax.all_gather(keys_rot, "seq", axis=1, tiled=True)
    value_piece = lax.all_gather(values, "seq", axis=1, tiled=True)
    piece_len = key_piece.shape[1]
    piece_live = jnp.arange(piece_len, dtype=jnp.int32)[None, :] < lengths[:, None]
    probs_low, dscore = block_terms(
        queries, grad_attended, lse_rows, delta_rows, key_piece, value_piece, piece_live
    )
    grad_queries = jnp.einsum(
        "bhqk,bkhd->bqhd", dscore, key_piece, preferred_element_type=jnp.float32
    )
    query_piece = lax.all_gather(queries, "seq", axis=1, tiled=True)
    dout_piece = lax.all_gather(grad_attended, "seq", axis=1, tiled=True)
    probs_low, dscore = block_terms(
        query_piece, dout_piece, lse_all, delta_all, keys_rot, values, local_live
    )
    grad_k = jnp.einsum("bhqk,bqhd->bkhd", dscore, query_piece, preferred_element_type=jnp.float32)
    grad_v = jnp.einsum(
        "bhqk,bqhd->bkhd", probs_low, dout_piece, preferred_element_type=jnp.float32
    )
    grad_q_pre = rotate_heads(grad_queries * 0.125, cosine_table, -sine_table)
    grad_k_pre = rotate_heads(grad_k, cosine_table, -sine_table)
    grad_projected = (
        jnp.stack([grad_q_pre, grad_k_pre, grad_v], axis=2)
        .reshape(row_count, 3 * model_width)
        .astype(jnp.bfloat16)
    )
    grad_qkv = cross(normed_attn, grad_projected)
    grad_normed_attn = back_product(grad_projected, qkv_back).reshape(
        utt_count, frame_span, model_width
    )
    grad_shift_attn = jnp.sum(grad_normed_attn, axis=1)
    grad_scale_attn = jnp.sum(grad_normed_attn * hat_attn, axis=1)
    grad_stream = grad_mid + norm_back(grad_normed_attn * (1.0 + scale_attn), hat_attn, inv_attn)
    grad_stream_low = grad_stream.astype(jnp.bfloat16).reshape(row_count, model_width)
    grad_skip_w = cross(joined, grad_stream_low)
    grad_joined = back_product(grad_stream_low, skip_back)
    grad_input = (
        grad_joined[:, :model_width]
        .reshape(utt_count, frame_span, model_width)
        .astype(jnp.bfloat16)
    )
    grad_skip = (
        grad_joined[:, model_width:]
        .reshape(utt_count, frame_span, model_width)
        .astype(jnp.bfloat16)
    )
    grad_modulation = jnp.stack(
        [
            grad_shift_attn,
            grad_scale_attn,
            grad_gate_attn,
            grad_shift_ffn,
            grad_scale_ffn,
            grad_gate_ffn,
        ],
        axis=1,
    ).reshape(utt_count, 6 * model_width)
    mod_total = lax.psum(grad_modulation, "seq")
    mod_every, silu_every = (
        lax.all_gather(mod_total.astype(jnp.bfloat16), "batch", axis=0, tiled=True).astype(
            mod_total.dtype
        ),
        lax.all_gather(
            silu_time.astype(jnp.float32).astype(jnp.bfloat16), "batch", axis=0, tiled=True
        ).astype(jnp.float32),
    )
    row_span = adaln_weight.shape[0]
    silu_rows = lax.dynamic_slice_in_dim(silu_every, seq_here * row_span, row_span, 1)
    adaln_rows = jnp.dot(silu_rows.T, mod_every, precision=lax.Precision.HIGHEST)
    bias_span = adaln_bias.shape[0]
    bias_rows = lax.dynamic_slice_in_dim(
        jnp.sum(mod_every, axis=0), seq_here * bias_span, bias_span, 0
    )
    shards = (
        lax.psum_scatter(grad_skip_w, "seq", scatter_dimension=0, tiled=True),
        lax.psum_scatter(grad_qkv, "seq", scatter_dimension=0, tiled=True),
        lax.psum_scatter(grad_out, "seq", scatter_dimension=0, tiled=True),
        lax.psum_scatter(grad_up, "seq", scatter_dimension=0, tiled=True),
        lax.psum_scatter(grad_down, "seq", scatter_dimension=0, tiled=True),
    )
    summed = (
        lax.psum(shards[0].astype(jnp.bfloat16), "batch").astype(jnp.float32),
        lax.psum(shards[1].astype(jnp.bfloat16), "batch").astype(jnp.float32),
        lax.psum(shards[2].astype(jnp.bfloat16), "batch").astype(jnp.float32),
        lax.psum(shards[3].astype(jnp.bfloat16), "batch").astype(jnp.float32),
        lax.psum(shards[4].astype(jnp.bfloat16), "batch").astype(jnp.float32),
    )
    results = (summed[0], adaln_rows, bias_rows, summed[1], summed[2], summed[3], summed[4])
    return (
        layer_output,
        grad_input,
        grad_skip,
        results[0],
        results[1],
        results[2],
        results[3],
        results[4],
        results[5],
        results[6],
    )


def solution(mesh):
    placed = (
        P("batch", "seq", None),
        P("batch", "seq", None),
        P("batch", None),
        P("batch"),
        P("batch"),
        P("batch", "seq", None),
        P("seq", None),
        P("seq", None),
        P("seq"),
        P("seq", None),
        P("seq", None),
        P("seq", None),
        P("seq", None),
    )
    return jax.shard_map(
        on_device,
        mesh=mesh,
        in_specs=placed,
        out_specs=(
            P("batch", "seq", None),
            P("batch", "seq", None),
            P("batch", "seq", None),
            P("seq", None),
            P("seq", None),
            P("seq"),
            P("seq", None),
            P("seq", None),
            P("seq", None),
            P("seq", None),
        ),
        check_vma=False,
    )
```

profile of v0, /device:TPU:0, one launch (start us, length us, event | category | flops | bytes accessed | tf_op | source)
XLA Modules:
  0.0 2717.8 jit_solution(11503104744090754558)
XLA Ops:
  10.7 32.3 %all-gather.1 = bf16[8,1,768]{2,1,0:T(2,128)(2,1)S(1)} all-gather(bf16[1,1,768]{2,1,0:T(2,128)(2,1)S(1)} %reshape.315), channel_id=1, replica_groups=mesh['seq'=8,'batch'=4] {'seq'}, dimensions={0}, use_global_device_ids=true | all-gather | bytes 13824 | tf_op jit(solution)/shard_map/all_gather | solution.py:106
  47.2 39.2 %all-gather.15.cloned.1.call-done = bf16[2048,1024]{1,0:T(8,128)(2,1)} async-done(((bf16[256,1024]{1,0:T(8,128)(2,1)}), bf16[2048,1024]{1,0:T(8,128)(2,1)}) %all-gather.15.cloned.1.call-update) | async-done | bytes 4194320 | tf_op jit(solution)/shard_map/all_gather | solution.py:104
  96.9 89.1 %all-gather.19.cloned.1.call-done = bf16[1024,3072]{1,0:T(8,128)(2,1)} async-done(((bf16[128,3072]{1,0:T(8,128)(2,1)}), bf16[1024,3072]{1,0:T(8,128)(2,1)}) %all-gather.19.cloned.1.call-update) | async-done | bytes 6291472 | tf_op jit(solution)/shard_map/all_gather | solution.py:107
  194.8 168.1 %all-gather.17.cloned.1.call-done = bf16[1024,6144]{1,0:T(8,128)(2,1)} async-done(((bf16[128,6144]{1,0:T(8,128)(2,1)}), bf16[1024,6144]{1,0:T(8,128)(2,1)}) %all-gather.17.cloned.1.call-update) | async-done | bytes 12582928 | tf_op jit(solution)/shard_map/all_gather | solution.py:105
  400.4 41.5 %all-reduce = (f32[]{:T(128)}, f32[]{:T(128)}) all-reduce(f32[]{:T(128)} %get-tuple-element.18, f32[]{:T(128)} %get-tuple-element.17), channel_id=1, replica_groups=mesh['seq'=8,'batch'=4] {'seq','batch'}, use_global_device_ids=true, to_apply=%region_7.8 | all-reduce | flops 2 | bytes 16 | tf_op jit(solution)/shard_map/psum | solution.py:94
  447.2 41.5 %all-gather.27.cloned.1.call-done = bf16[4096,1024]{1,0:T(8,128)(2,1)} async-done(((bf16[512,1024]{1,0:T(8,128)(2,1)}), bf16[4096,1024]{1,0:T(8,128)(2,1)}) %all-gather.27.cloned.1.call-update) | async-done | bytes 8388624 | tf_op jit(solution)/shard_map/all_gather | solution.py:110
  504.9 212.2 %all-gather.21.cloned.1.call-done = bf16[2,4096,16,64]{1,3,2,0:T(8,128)(2,1)} async-done(((bf16[2,512,16,64]{1,3,2,0:T(8,128)(2,1)}), bf16[2,4096,16,64]{1,3,2,0:T(8,128)(2,1)}) %all-gather.21.cloned.1.call-update) | async-done | bytes 16777232 | tf_op jit(solution)/shard_map/all_gather | solution.py:147
  717.1 98.0 %select_reduce_fusion = (f32[2,16,512]{2,1,0:T(8,128)S(1)}, f32[2,16,512,4096]{3,2,1,0:T(8,128)}) fusion(pred[2,4096]{1,0:T(4,128)(4,1)S(1)} %iota_compare_fusion, bf16[2,512,16,64]{1,3,2,0:T(8,128)(2,1)S(1)} %copy-done.10, bf16[2,4096,16,64]{1,3,2,0:T(8,128)(2,1)} %all-gather.21.cloned.1.call-done), kind=kOutput, calls=%fused_computation.4 | convolution fusion | flops 8724135936 | bytes 287383552 | tf_op jit(solution)/shard_map/bqhd,bkhd->bhqk/dot_general | solution.py:151
  815.1 80.9 %fusion.1 = f32[2,16,512]{2,1,0:T(8,128)S(1)} fusion(f32[2,16,512,4096]{3,2,1,0:T(8,128)} %get-tuple-element.62, f32[2,16,512]{2,1,0:T(8,128)S(1)} %broadcast_maximum_fusion, pred[2,4096]{1,0:T(4,128)(4,1)S(1)} %iota_compare_fusion), kind=kLoop, calls=%fused_computation.6 | loop fusion | flops 268419072 | bytes 268574720 | tf_op jit(solution)/shard_map/reduce_sum | solution.py:155
  896.1 49.4 %all-gather.33.cloned.1.call-done = bf16[2,4096,1,16,64]{1,4,3,2,0:T(8,128)(2,1)} async-done(((bf16[2,512,1,16,64]{1,4,3,2,0:T(8,128)(2,1)}), bf16[2,4096,1,16,64]{1,4,3,2,0:T(8,128)(2,1)}) %all-gather.33.cloned.1.call-update) | async-done | bytes 16777232 | tf_op jit(solution)/shard_map/all_gather | solution.py:148
  945.5 90.2 %fusion.81 = (bf16[2,512,16,64]{1,3,2,0:T(8,128)(2,1)S(1)}, f32[2,512,16,64]{1,3,2,0:T(8,128)}) fusion(f32[2,512,16]{1,2,0:T(8,128)S(1)} %bitcast.199, f32[2,16,512,4096]{3,2,1,0:T(8,128)} %get-tuple-element.62, f32[2,16,512]{2,1,0:T(8,128)S(1)} %broadcast_maximum_fusion, pred[2,4096]{1,0:T(4,128)(4,1)S(1)} %iota_compare_fusion, ...), kind=kOutput, calls=%fused_computation.153 | convolution fusion | flops 8860467200 | bytes 291643392 | tf_op jit(solution)/shard_map/bhqk,bkhd->bqhd/dot_general | solution.py:156
  1047.2 73.6 %all-gather.25.cloned.1.call-done = bf16[1024,4096]{1,0:T(8,128)(2,1)} async-done(((bf16[128,4096]{1,0:T(8,128)(2,1)}), bf16[1024,4096]{1,0:T(8,128)(2,1)}) %all-gather.25.cloned.1.call-update) | async-done | bytes 8388624 | tf_op jit(solution)/shard_map/all_gather | solution.py:109
  1262.4 119.2 %bitcast_multiply_fusion = (f32[2,512,16,64]{1,3,2,0:T(8,128)}, f32[2,16,64,512]{3,2,1,0:T(8,128)}) fusion(bf16[2,4096,16,64]{1,3,2,0:T(8,128)(2,1)} %all-gather.21.cloned.1.call-done, f32[2,16,512,4096]{3,2,1,0:T(8,128)} %get-tuple-element.62, f32[2,16,512]{2,1,0:T(8,128)S(1)} %bitcast.203, f32[2,16,512]{2,1,0:T(8,128)S(1)} %log_add_fusion, ...), kind=kOutput, calls=%fused_computation.51 | convolution fusion | flops 17516462080 | bytes 312614912 | tf_op jit(solution)/shard_map/bhqk,bkhd->bqhd/dot_general | solution.py:227
  1381.7 94.2 %fusion.87 = f32[2,16,4096,512]{3,2,1,0:T(8,128)} fusion(bf16[2,4096,16,64]{1,3,2,0:T(8,128)(2,1)} %all-gather.29.cloned.1.call-done, bf16[2,512,16,64]{1,3,2,0:T(8,128)(2,1)S(1)} %copy-done.9), kind=kOutput, calls=%fused_computation.156 | convolution fusion | flops 8589934592 | bytes 287309824 | tf_op jit(solution)/shard_map/bqhd,bkhd->bhqk/dot_general | solution.py:58
  1475.9 33.3 %all_gather.64 = f32[2,4096,16]{1,2,0:T(8,128)S(1)} all-gather(f32[2,512,16]{1,2,0:T(8,128)S(1)} %multiply_reduce_fusion.4), channel_id=1, replica_groups=mesh['seq'=8,'batch'=4] {'seq'}, dimensions={1}, use_global_device_ids=true | all-gather | bytes 589824 | tf_op jit(solution)/shard_map/all_gather | solution.py:218
  1509.3 41.7 %all_gather.62 = f32[2,4096,16]{1,2,0:T(8,128)S(1)} all-gather(f32[2,512,16]{1,2,0:T(8,128)S(1)} %bitcast_add_fusion), channel_id=1, replica_groups=mesh['seq'=8,'batch'=4] {'seq'}, dimensions={1}, use_global_device_ids=true | all-gather | bytes 589824 | tf_op jit(solution)/shard_map/all_gather | solution.py:217
  1555.3 42.2 %all-gather.31.cloned.1.call-done = bf16[2,4096,16,64]{1,3,2,0:T(8,128)(2,1)} async-done(((bf16[2,512,16,64]{1,3,2,0:T(8,128)(2,1)}), bf16[2,4096,16,64]{1,3,2,0:T(8,128)(2,1)}) %all-gather.31.cloned.1.call-update) | async-done | bytes 16777232 | tf_op jit(solution)/shard_map/all_gather | solution.py:231
  1597.5 97.4 %fusion.45 = f32[2,512,16,64]{1,3,2,0:T(8,128)} fusion(bf16[2,4096,16,64]{1,3,2,0:T(8,128)(2,1)} %all-gather.29.cloned.1.call-done, f32[2,16,4096,512]{3,2,1,0:T(8,128)} %fusion.87, f32[2,16,4096]{2,1,0:T(8,128)S(1)} %bitcast.202, f32[2,16,4096]{2,1,0:T(8,128)S(1)} %bitcast.200, bf16[2,4096,16,64]{1,3,2,0:T(8,128)(2,1)} %all-gather.31.cloned.1.call-done, ...), kind=kOutput, calls=%fused_computation.83 | convolution fusion | flops 17515413504 | bytes 309330944 | tf_op jit(solution)/shard_map/bhqk,bqhd->bkhd/dot_general | solution.py:235
  1704.9 90.7 %fusion.42 = bf16[2,512,1,16,64]{1,4,3,0,2:T(8,128)(2,1)} fusion(bf16[2,4096,16,64]{1,3,2,0:T(8,128)(2,1)} %all-gather.31.cloned.1.call-done, f32[2,16,4096,512]{3,2,1,0:T(8,128)} %fusion.87, f32[2,16,4096]{2,1,0:T(8,128)S(1)} %bitcast.201, pred[2,512]{1,0:T(4,128)(4,1)S(1)} %copy-done.61), kind=kOutput, calls=%fused_computation.82 | convolution fusion | flops 8791261184 | bytes 287835136 | tf_op jit(solution)/shard_map/bhqk,bqhd->bkhd/dot_general | solution.py:236
  1859.3 114.4 %reduce-scatter.12.cloned.1.call-done = f32[128,4096]{1,0:T(8,128)} async-done(((f32[1024,4096]{1,0:T(8,128)}), f32[128,4096]{1,0:T(8,128)}) %reduce-scatter.12.cloned.1.call-update) | async-done | bytes 2097168 | tf_op jit(solution)/shard_map/reduce_scatter | solution.py:297
  1976.4 282.8 %reduce-scatter.14.cloned.1.call-done = f32[512,1024]{1,0:T(8,128)} async-done(((f32[4096,1024]{1,0:T(8,128)}), f32[512,1024]{1,0:T(8,128)}) %reduce-scatter.14.cloned.1.call-update) | async-done | bytes 2097168 | tf_op jit(solution)/shard_map/reduce_scatter | solution.py:298
  2262.0 149.3 %reduce-scatter.6.cloned.1.call-done = f32[256,1024]{1,0:T(8,128)} async-done(((f32[2048,1024]{1,0:T(8,128)}), f32[256,1024]{1,0:T(8,128)}) %reduce-scatter.6.cloned.1.call-update) | async-done | bytes 1048592 | tf_op jit(solution)/shard_map/reduce_scatter | solution.py:294
  2413.4 207.7 %reduce-scatter.8.cloned.1.call-done = f32[128,3072]{1,0:T(8,128)} async-done(((f32[1024,3072]{1,0:T(8,128)}), f32[128,3072]{1,0:T(8,128)}) %reduce-scatter.8.cloned.1.call-update) | async-done | bytes 1572880 | tf_op jit(solution)/shard_map/reduce_scatter | solution.py:295
  2623.5 35.6 %psum.59 = bf16[2,6144]{1,0:T(2,128)(2,1)S(1)} all-reduce(f32[2,6144]{1,0:T(2,128)S(1)} %bitcast.205), channel_id=1, replica_groups=mesh['seq'=8,'batch'=4] {'seq'}, use_global_device_ids=true, to_apply=%region_23.24 | all-reduce | flops 12288 | bytes 73728 | tf_op jit(solution)/shard_map/psum | solution.py:277
  (269 shorter events, 376.6 us)
Async XLA Ops:
  7.2 79.3 %all-gather.15.cloned.1.call-start = ((), (), s32[]{:S(2)}) async-start(), calls=%async_computation.5 | async-start | bytes 4718592 | tf_op jit(solution)/shard_map/all_gather | solution.py:104
  7.9 178.1 %all-gather.19.cloned.1.call-start = ((), (), s32[]{:S(2)}) async-start(), calls=%async_computation.7 | async-start | bytes 7077888 | tf_op jit(solution)/shard_map/all_gather | solution.py:107
  8.7 354.2 %all-gather.17.cloned.1.call-start = ((), (), s32[]{:S(2)}) async-start(), calls=%async_computation.6 | async-start | bytes 14155776 | tf_op jit(solution)/shard_map/all_gather | solution.py:105
  9.4 479.3 %all-gather.27.cloned.1.call-start = ((), (), s32[]{:S(2)}) async-start(), calls=%async_computation.11 | async-start | bytes 9437184 | tf_op jit(solution)/shard_map/all_gather | solution.py:110
  10.0 707.1 %all-gather.21.cloned.1.call-start = ((), (), s32[]{:S(2)}) async-start(), calls=%async_computation.8 | async-start | bytes 18874368 | tf_op jit(solution)/shard_map/all_gather | solution.py:147
  44.1 342.6 %copy-start.29 = (f32[512,64]{0,1:T(8,128)}, f32[512,64]{0,1:T(8,128)S(1)}, u32[]{:S(2)}) copy-start(f32[512,64]{0,1:T(8,128)S(1)} %get-tuple-element.52) | copy-start | bytes 393220
  94.2 275.1 %copy-start.47 = (f32[2,512]{1,0:T(2,128)}, f32[2,512]{1,0:T(2,128)S(1)}, u32[]{:S(2)}) copy-start(f32[2,512]{1,0:T(2,128)S(1)} %broadcast_multiply_fusion.7) | copy-start | bytes 12292
  96.8 272.4 %copy-start.51 = (f32[2,512]{1,0:T(2,128)}, f32[2,512]{1,0:T(2,128)S(1)}, u32[]{:S(2)}) copy-start(f32[2,512]{1,0:T(2,128)S(1)} %add_rsqrt_fusion.1) | copy-start | bytes 12292
  186.0 176.8 %copy-start.58 = (bf16[2,1024]{1,0:T(2,128)(2,1)S(1)}, bf16[2,1024]{1,0:T(2,128)(2,1)}, u32[]{:S(2)}) copy-start(bf16[2,1024]{1,0:T(2,128)(2,1)} %param.15) | copy-start | bytes 12292
  394.1 551.5 %all-gather.33.cloned.1.call-start = ((), (), s32[]{:S(2)}) async-start(), calls=%async_computation.19 | async-start | bytes 18874368 | tf_op jit(solution)/shard_map/all_gather | solution.py:148
  398.1 637.6 %all-gather.23.cloned.1.call-start = ((), (), s32[]{:S(2)}) async-start(), calls=%async_computation.9 | async-start | bytes 2359296 | tf_op jit(solution)/shard_map/all_gather | solution.py:108
  398.9 721.9 %all-gather.25.cloned.1.call-start = ((), (), s32[]{:S(2)}) async-start(), calls=%async_computation.10 | async-start | bytes 9437184 | tf_op jit(solution)/shard_map/all_gather | solution.py:109
  399.6 982.0 %all-gather.29.cloned.1.call-start = ((), (), s32[]{:S(2)}) async-start(), calls=%async_computation.12 | async-start | bytes 18874368 | tf_op jit(solution)/shard_map/all_gather | solution.py:230
  443.4 502.1 %copy-start.18 = (pred[2,4096]{1,0:T(4,128)(4,1)}, pred[2,4096]{1,0:T(4,128)(4,1)S(1)}, u32[]{:S(2)}) copy-start(pred[2,4096]{1,0:T(4,128)(4,1)S(1)} %iota_compare_fusion) | copy-start | bytes 24580
  445.3 1152.2 %all-gather.31.cloned.1.call-start = ((), (), s32[]{:S(2)}) async-start(), calls=%async_computation.13 | async-start | bytes 18874368 | tf_op jit(solution)/shard_map/all_gather | solution.py:231
  488.7 228.4 %copy-start.10 = (bf16[2,512,16,64]{1,3,2,0:T(8,128)(2,1)S(1)}, bf16[2,512,16,64]{1,3,2,0:T(8,128)(2,1)}, u32[]{:S(2)}) copy-start(bf16[2,512,16,64]{1,3,2,0:T(8,128)(2,1)} %get-tuple-element.32) | copy-start | bytes 6291460
  896.1 342.2 %copy-start.35 = (f32[2,16,512]{2,1,0:T(8,128)}, f32[2,16,512]{2,1,0:T(8,128)S(1)}, u32[]{:S(2)}) copy-start(f32[2,16,512]{2,1,0:T(8,128)S(1)} %fusion.1) | copy-start | bytes 196612
  1214.6 642.8 %reduce-scatter.10.cloned.1.call-start = ((), (), s32[]{:S(2)}) async-start(), calls=%async_computation.16 | async-start | bytes 4718592 | tf_op jit(solution)/shard_map/reduce_scatter | solution.py:296
  1221.8 751.9 %reduce-scatter.12.cloned.1.call-start = ((), (), s32[]{:S(2)}) async-start(), calls=%async_computation.17 | async-start | bytes 18874368 | tf_op jit(solution)/shard_map/reduce_scatter | solution.py:297
  1238.2 1021.0 %reduce-scatter.14.cloned.1.call-start = ((), (), s32[]{:S(2)}) async-start(), calls=%async_computation.18 | async-start | bytes 18874368 | tf_op jit(solution)/shard_map/reduce_scatter | solution.py:298
  1261.7 1149.6 %reduce-scatter.6.cloned.1.call-start = ((), (), s32[]{:S(2)}) async-start(), calls=%async_computation.14 | async-start | bytes 9437184 | tf_op jit(solution)/shard_map/reduce_scatter | solution.py:294
  1262.4 119.3 %copy-start.9 = (bf16[2,512,16,64]{1,3,2,0:T(8,128)(2,1)S(1)}, bf16[2,512,16,64]{1,3,2,0:T(8,128)(2,1)}, u32[]{:S(2)}) copy-start(bf16[2,512,16,64]{1,3,2,0:T(8,128)(2,1)} %get-tuple-element.31) | copy-start | bytes 6291460
  1827.9 793.2 %reduce-scatter.8.cloned.1.call-start = ((), (), s32[]{:S(2)}) async-start(), calls=%async_computation.15 | async-start | bytes 14155776 | tf_op jit(solution)/shard_map/reduce_scatter | solution.py:295
  1851.4 850.8 %all-reduce.4.cloned.1.call-start = ((), (), s32[]{:S(2)}) async-start(), calls=%async_computation.20 | async-start | bytes 7340032 | tf_op jit(solution)/shard_map/psum | solution.py:301
  (58 other events, 1037.5 us)
Sparse Core Ops, SparseCore 0:
  10.1 76.2 all-gather.14
  88.7 97.2 all-gather.18
  188.2 174.6 all-gather.16
  364.8 123.8 all-gather.26
  491.1 225.9 all-gather.20
  719.6 225.9 all-gather.32
  947.7 47.5 all-gather.22
  997.3 123.4 all-gather.24
  1123.4 225.9 all-gather.28
  1351.9 245.5 all-gather.30
  1601.1 86.0 reduce-scatter.9
  1691.4 282.2 reduce-scatter.11
  1977.5 281.7 reduce-scatter.13
  2263.2 148.0 reduce-scatter.5
  2414.7 206.3 reduce-scatter.7
  2624.8 77.3 all-reduce.3
where the time goes:
time: 2730 us; the launch traced here: 2720 us
  waiting for transfers between devices  1500 us (55%)
  matrix products  778 us (28%)
  blocking collectives  195 us (7%)
  other arithmetic  151 us (6%)
  local copies, waits for them, and re-layouts  77.6 us (3%)
    reduce_scatter x1, waiting for transfers between devices, on_device(): lax.psum_scatter(grad_down, 'seq', scatter_dimension=0, tiled=True)  283 us
    all_gather x1, waiting for transfers between devices, on_device(): key_piece = lax.all_gather(keys_rot, 'seq', axis=1, tiled=True)  212 us
    reduce_scatter x1, waiting for transfers between devices, on_device(): lax.psum_scatter(grad_qkv, 'seq', scatter_dimension=0, tiled=True)  208 us
    all_gather x1, waiting for transfers between devices, on_device(): lax.all_gather(adaln_weight, 'seq', axis=0, tiled=True)  168 us
    reduce_scatter x1, waiting for transfers between devices, on_device(): lax.psum_scatter(grad_skip_w, 'seq', scatter_dimension=0, tiled=True)  149 us
    dot_general x1, matrix products, on_device(): jnp.einsum('bhqk,bkhd->bqhd', dscore, key_piece, preferred_element_type=j...  119 us
    reduce_scatter x1, waiting for transfers between devices, on_device(): lax.psum_scatter(grad_up, 'seq', scatter_dimension=0, tiled=True)  114 us
    dot_general x1, matrix products, on_device(): jnp.einsum('bqhd,bkhd->bhqk', queries, key_piece, preferred_element_type=...  98 us
  transfers between devices with their start and end apart: 16, of which 13 were waited for; matrix products, arithmetic and copies ran while one was open for 36% of the time, Pallas kernels for 0%

commit v1 on v0

v1 whole, which is shorter than its diff:
```python
import functools
import jax
import jax.numpy as jnp
from jax import lax
from jax.sharding import PartitionSpec as P
from jax.experimental import pallas as pl
from jax.experimental.pallas import tpu as pltpu
HEAD_DIM = 64
EPS = 1e-06
LOG2E = 1.4426950408889634
LN2 = 0.6931471805599453
MASKED = -1e30
RANGE = 100.0
BF = jnp.bfloat16
F32 = jnp.float32
VMEM_LIMIT = 60 * 2**20


def nt(left, right):
    return lax.dot_general(left, right, (((1,), (1,)), ((), ())), preferred_element_type=F32)


def nn(left, right):
    return lax.dot_general(left, right, (((1,), (0,)), ((), ())), preferred_element_type=F32)


def head_sums(product, lane):
    first = jnp.sum(jnp.where(lane < 64, product, 0.0), axis=1, keepdims=True)
    second = jnp.sum(jnp.where(lane >= 64, product, 0.0), axis=1, keepdims=True)
    return (first, second)


def lanes_of(rows):
    return lax.broadcasted_iota(jnp.int32, (rows, 128), 1)


def flash_forward_kernel(len_ref, q_ref, k_ref, v_ref, o_ref, lse_ref, ka, kb, vta, vtb, mean_ref, top_ref, *, bq, bk):
    step = pl.program_id(0)
    length = len_ref[0]
    frames = k_ref.shape[0]

    @pl.when(step == 0)
    def _():
        def build(j, carry):
            rows = pl.ds(pl.multiple_of(j * bk, bk), bk)
            lane = lanes_of(bk)
            pos = j * bk + lax.broadcasted_iota(jnp.int32, (bk, 128), 0)
            bias = jnp.where(pos < length, 0.0, MASKED)
            keys = k_ref[rows, :].astype(F32)
            ka[rows, :] = jnp.where(lane < 64, keys, jnp.where(lane == 64, bias, jnp.where(lane == 65, 1.0, 0.0))).astype(BF)
            kb[rows, :] = jnp.where(lane >= 64, keys, jnp.where(lane == 0, bias, jnp.where(lane == 1, 1.0, 0.0))).astype(BF)
            vals = v_ref[rows, :].astype(F32)
            vta[:, rows] = jnp.where(lane < 64, vals, 1.0).T.astype(BF)
            vtb[:, rows] = jnp.where(lane >= 64, vals, 1.0).T.astype(BF)
            keys = jnp.where(pos < length, keys, 0.0)
            norm_a, norm_b = head_sums(keys * keys, lane)
            total, top_a, top_b = carry
            return (
                total + jnp.sum(keys, axis=0, keepdims=True),
                jnp.maximum(top_a, jnp.max(norm_a)),
                jnp.maximum(top_b, jnp.max(norm_b)),
            )

        total, top_a, top_b = lax.fori_loop(
            0, frames // bk, build, (jnp.zeros((1, 128), F32), jnp.float32(0.0), jnp.float32(0.0))
        )
        mean_ref[0:1, :] = total / length.astype(F32)
        top_ref[0] = top_a
        top_ref[1] = top_b

    lane = lanes_of(bq)
    queries = q_ref[...].astype(F32)
    bounds = [
        jnp.sqrt(jnp.max(norm) * top_ref[head]) * 1.001
        for head, norm in enumerate(head_sums(queries * queries, lane))
    ]
    shifts = [jnp.maximum(bound - RANGE, 0.0) for bound in bounds]
    lows = [jnp.min(low) for low in head_sums(queries * mean_ref[0:1, :], lane)]
    tame = jnp.logical_and(lows[0] - shifts[0] >= -RANGE, lows[1] - shifts[1] >= -RANGE)
    qa = jnp.where(lane < 64, queries, jnp.where(lane == 64, 1.0, jnp.where(lane == 65, -shifts[0], 0.0)))
    qb = jnp.where(lane >= 64, queries, jnp.where(lane == 0, 1.0, jnp.where(lane == 1, -shifts[1], 0.0)))
    qa, qb = qa.astype(BF), qb.astype(BF)

    def body(j, carry):
        rows = pl.ds(pl.multiple_of(j * bk, bk), bk)
        out = []
        scores = [nt(ka[rows, :], qa), nt(kb[rows, :], qb)]
        for score, vt, (top, acc) in zip(scores, (vta, vtb), carry):
            new = jnp.maximum(top, jnp.max(score, axis=0, keepdims=True))
            probs = jnp.exp2(score - new).astype(BF)
            acc = acc * jnp.exp2(top - new) + nn(vt[:, rows], probs)
            out.append((new, acc))
        return tuple(out)

    live = (length + bk - 1) // bk

    def finish(shift_a, acc_a, shift_b, acc_b):
        sum_a, sum_b = acc_a[64:65], acc_b[0:1]
        both = jnp.concatenate([acc_a[:64] / sum_a, acc_b[64:] / sum_b], axis=0)
        o_ref[...] = both.T.astype(BF)
        lse_ref[...] = jnp.concatenate(
            [shift_a + jnp.log2(sum_a), shift_b + jnp.log2(sum_b), jnp.zeros((6, bq), F32)], axis=0
        )

    @pl.when(tame)
    def _():
        def plain(j, carry):
            rows = pl.ds(pl.multiple_of(j * bk, bk), bk)
            out = []
            for keys, query, vt, acc in ((ka, qa, vta, carry[0]), (kb, qb, vtb, carry[1])):
                probs = jnp.exp2(nt(keys[rows, :], query)).astype(BF)
                out.append(acc + nn(vt[:, rows], probs))
            return tuple(out)

        start = jnp.zeros((128, bq), F32)
        acc_a, acc_b = lax.fori_loop(0, live, plain, (start, start))
        rounded = [shift.astype(BF).astype(F32) for shift in shifts]
        finish(rounded[0], acc_a, rounded[1], acc_b)

    @pl.when(jnp.logical_not(tame))
    def _():
        start = (jnp.full((1, bq), MASKED, F32), jnp.zeros((128, bq), F32))
        (top_a, acc_a), (top_b, acc_b) = lax.fori_loop(0, live, body, (start, start))
        rounded = [shift.astype(BF).astype(F32) for shift in shifts]
        finish(rounded[0] + top_a, acc_a, rounded[1] + top_b, acc_b)


def attention_cost(frames, products):
    return pl.CostEstimate(
        flops=2 * products * 2 * frames * frames * 128,
        bytes_accessed=frames * 128 * 2 * 8,
        transcendentals=2 * frames * frames,
    )


def flash_forward(length, qkv, bq, bk):
    frames = qkv.shape[0]
    return pl.pallas_call(
        functools.partial(flash_forward_kernel, bq=bq, bk=bk),
        grid_spec=pltpu.PrefetchScalarGridSpec(
            num_scalar_prefetch=1,
            grid=(frames // bq,),
            in_specs=[
                pl.BlockSpec((bq, 128), lambda i, *_: (i, 0)),
                pl.BlockSpec((frames, 128), lambda i, *_: (0, 1)),
                pl.BlockSpec((frames, 128), lambda i, *_: (0, 2)),
            ],
            out_specs=[
                pl.BlockSpec((bq, 128), lambda i, *_: (i, 0)),
                pl.BlockSpec((8, bq), lambda i, *_: (0, i)),
            ],
            scratch_shapes=[
                pltpu.VMEM((frames, 128), BF),
                pltpu.VMEM((frames, 128), BF),
                pltpu.VMEM((128, frames), BF),
                pltpu.VMEM((128, frames), BF),
                pltpu.VMEM((8, 128), F32),
                pltpu.SMEM((2,), F32),
            ],
        ),
        out_shape=[
            jax.ShapeDtypeStruct((frames, 128), BF),
            jax.ShapeDtypeStruct((8, frames), F32),
        ],
        compiler_params=pltpu.CompilerParams(vmem_limit_bytes=VMEM_LIMIT),
        cost_estimate=attention_cost(frames, 2),
        name="attend_forward",
    )(length, qkv, qkv, qkv)


def turn_back(grad, cos, sin):
    lane = lanes_of(grad.shape[0])
    turned = jnp.where((lane & 63) < 32, pltpu.roll(grad, 96, 1), pltpu.roll(grad, 32, 1))
    return grad * cos - turned * sin


def three(column, lane, at):
    high = column.astype(BF).astype(F32)
    rest = column - high
    mid = rest.astype(BF).astype(F32)
    low = rest - mid
    return jnp.where(lane == at, -high, jnp.where(lane == at + 1, -mid, jnp.where(lane == at + 2, -low, 0.0)))


def flash_backward_kernel(
    len_ref, q_ref, k_ref, v_ref, o_ref, do_ref, lse_ref, cos_ref, sin_ref,
    g_ref, ka, kb, va, vb, dkt, dvt, *, bq, bk,
):
    step = pl.program_id(0)
    steps = pl.num_programs(0)
    length = len_ref[0]
    frames = k_ref.shape[0]

    @pl.when(step == 0)
    def _():
        def build(j, carry):
            rows = pl.ds(pl.multiple_of(j * bk, bk), bk)
            lane = lanes_of(bk)
            pos = j * bk + lax.broadcasted_iota(jnp.int32, (bk, 128), 0)
            bias = jnp.where(pos < length, 0.0, MASKED)
            keys = k_ref[rows, :].astype(F32)
            vals = v_ref[rows, :].astype(F32)
            ones_a = jnp.where(lane < 67, 1.0, 0.0)
            ones_b = jnp.where(lane < 3, 1.0, 0.0)
            ka[rows, :] = jnp.where(lane < 64, keys, jnp.where(lane == 67, bias, ones_a)).astype(BF)
            kb[rows, :] = jnp.where(lane >= 64, keys, jnp.where(lane == 3, bias, ones_b)).astype(BF)
            va[rows, :] = jnp.where(lane < 64, vals, ones_a).astype(BF)
            vb[rows, :] = jnp.where(lane >= 64, vals, ones_b).astype(BF)
            return carry

        lax.fori_loop(0, frames // bk, build, 0)
        dkt[...] = jnp.zeros_like(dkt)
        dvt[...] = jnp.zeros_like(dvt)

    @pl.when(step * bq >= length)
    def _():
        rows = pl.ds(pl.multiple_of(step * bq, bq), bq)
        g_ref[rows, 0:128] = jnp.zeros((bq, 128), BF)

    @pl.when(step * bq < length)
    def _():
        lane = lanes_of(bq)
        queries = q_ref[...].astype(F32)
        dout = do_ref[...].astype(F32)
        product = dout * o_ref[...].astype(F32)
        delta_a, delta_b = head_sums(product, lane)
        lse = lse_ref[...].T
        qa = jnp.where(lane < 64, queries, jnp.where(lane == 67, 1.0, three(lse[:, 0:1], lane, 64))).astype(BF)
        qb = jnp.where(lane >= 64, queries, jnp.where(lane == 3, 1.0, three(lse[:, 1:2], lane, 0))).astype(BF)
        da = jnp.where(lane < 64, dout, three(delta_a, lane, 64)).astype(BF)
        db = jnp.where(lane >= 64, dout, three(delta_b, lane, 0)).astype(BF)
        qt = queries.T.astype(BF)
        dt = dout.T.astype(BF)

        def body(j, carry):
            rows = pl.ds(pl.multiple_of(j * bk, bk), bk)
            out = []
            for head, (qh, dh, kh, vh, dq) in enumerate(((qa, da, ka, va, carry[0]), (qb, db, kb, vb, carry[1]))):
                part = slice(head * 64, head * 64 + 64)
                keys = kh[rows, :]
                probs = jnp.exp2(nt(qh, keys))
                grad = (probs * nt(dh, vh[rows, :])).astype(BF)
                dvt[part, rows] += nn(dt, probs.astype(BF))[part]
                dkt[part, rows] += nn(qt, grad)[part]
                out.append(dq + nn(grad, keys))
            return tuple(out)

        start = jnp.zeros((bq, 128), F32)
        live = (length + bk - 1) // bk
        dq_a, dq_b = lax.fori_loop(0, live, body, (start, start))
        dq = jnp.where(lane < 64, dq_a, dq_b) * 0.125
        rows = pl.ds(pl.multiple_of(step * bq, bq), bq)
        g_ref[rows, 0:128] = turn_back(dq, cos_ref[rows, :], sin_ref[rows, :]).astype(BF)

    @pl.when(step == steps - 1)
    def _():
        def finish(j, carry):
            rows = pl.ds(pl.multiple_of(j * bk, bk), bk)
            dk = dkt[:, rows].T * LN2
            g_ref[rows, 128:256] = turn_back(dk, cos_ref[rows, :], sin_ref[rows, :]).astype(BF)
            g_ref[rows, 256:384] = dvt[:, rows].T.astype(BF)
            return carry

        lax.fori_loop(0, frames // bk, finish, 0)


def flash_backward(length, qkv, out, dout, lse, cos, sin, bq, bk):
    frames = qkv.shape[0]
    part = pl.BlockSpec((bq, 128), lambda i, *_: (i, 0))
    whole = pl.BlockSpec((frames, 128), lambda i, *_: (0, 0))
    return pl.pallas_call(
        functools.partial(flash_backward_kernel, bq=bq, bk=bk),
        grid_spec=pltpu.PrefetchScalarGridSpec(
            num_scalar_prefetch=1,
            grid=(frames // bq,),
            in_specs=[
                part,
                pl.BlockSpec((frames, 128), lambda i, *_: (0, 1)),
                pl.BlockSpec((frames, 128), lambda i, *_: (0, 2)),
                part,
                part,
                pl.BlockSpec((8, bq), lambda i, *_: (0, i)),
                whole,
                whole,
            ],
            out_specs=pl.BlockSpec((frames, 384), lambda i, *_: (0, 0)),
            scratch_shapes=[pltpu.VMEM((frames, 128), BF)] * 4
            + [pltpu.VMEM((128, frames), F32)] * 2,
        ),
        out_shape=jax.ShapeDtypeStruct((frames, 384), BF),
        compiler_params=pltpu.CompilerParams(vmem_limit_bytes=VMEM_LIMIT),
        cost_estimate=attention_cost(frames, 5),
        name="attend_backward",
    )(length, qkv, qkv, qkv, out, dout, lse, cos, sin)


def project_kernel(x_ref, w_ref, cos_ref, sin_ref, out_ref):
    projected = nn(x_ref[...], w_ref[...])
    groups = out_ref.shape[0]
    rows = x_ref.shape[0]
    lane = lanes_of(rows)
    cos, sin = cos_ref[...], sin_ref[...]
    for part in range(3):
        for group in range(groups):
            at = (part * groups + group) * 128
            piece = projected[:, at : at + 128]
            if part < 2:
                turned = jnp.where(
                    (lane & 63) < 32, pltpu.roll(piece, 96, 1), pltpu.roll(piece, 32, 1)
                )
                piece = piece * cos + turned * sin
            if part == 0:
                piece = piece * (0.125 * LOG2E)
            out_ref[group, :, part * 128 : part * 128 + 128] = piece.astype(BF)


def project_heads(x, weight, cos, sin, groups, block=256):
    rows, width = x.shape
    return pl.pallas_call(
        project_kernel,
        grid=(rows // block,),
        in_specs=[
            pl.BlockSpec((block, width), lambda i: (i, 0)),
            pl.BlockSpec(weight.shape, lambda i: (0, 0)),
            pl.BlockSpec((block, 128), lambda i: (i, 0)),
            pl.BlockSpec((block, 128), lambda i: (i, 0)),
        ],
        out_specs=pl.BlockSpec((groups, block, 384), lambda i: (0, i, 0)),
        out_shape=jax.ShapeDtypeStruct((groups, rows, 384), BF),
        compiler_params=pltpu.CompilerParams(vmem_limit_bytes=VMEM_LIMIT),
        cost_estimate=pl.CostEstimate(
            flops=2 * rows * weight.size, bytes_accessed=2 * weight.size, transcendentals=0
        ),
        name="project_heads",
    )(x, weight, cos, sin)


def layer_norm(stream):
    centre = stream - jnp.mean(stream, axis=-1, keepdims=True)
    spread = jnp.mean(centre * centre, axis=-1, keepdims=True)
    inverse = lax.rsqrt(spread + EPS)
    return (centre * inverse, inverse)


def norm_back(grad_normed, normed, inverse):
    first_mean = jnp.mean(grad_normed, axis=-1, keepdims=True)
    second_mean = jnp.mean(grad_normed * normed, axis=-1, keepdims=True)
    return inverse * (grad_normed - first_mean - normed * second_mean)


def rotary_tables(positions):
    half_dim = HEAD_DIM // 2
    channel = jnp.arange(half_dim, dtype=jnp.float32)
    inverse = jnp.power(10000.0, -2.0 * channel / HEAD_DIM)
    angles = positions.astype(jnp.float32)[:, None] * inverse[None, :]
    angles = jnp.concatenate([angles, angles], axis=1)
    return (jnp.cos(angles), jnp.sin(angles))


def rotate_heads(field, cosine_table, sine_table):
    half_dim = field.shape[-1] // 2
    turned = jnp.concatenate([-field[..., half_dim:], field[..., :half_dim]], axis=-1)
    return field * cosine_table + turned * sine_table


def smooth_gelu(values):
    return jax.nn.gelu(values, approximate=True)


def cross(left, right):
    return lax.dot_general(
        left, right, (((0,), (0,)), ((), ())), preferred_element_type=jnp.float32
    )


def back_product(left, right):
    return lax.dot_general(
        left, right, (((1,), (1,)), ((), ())), preferred_element_type=jnp.float32
    )


def block_terms(query_block, dout_block, lse_block, delta_block, key_block, value_block, key_live):
    scores = jnp.einsum(
        "bqhd,bkhd->bhqk", query_block, key_block, preferred_element_type=jnp.float32
    )
    lse_heads = jnp.transpose(lse_block, (0, 2, 1))[..., None]
    probs = jnp.where(key_live[:, None, None, :], jnp.exp(scores - lse_heads), 0.0)
    grad_probs = jnp.einsum(
        "bqhd,bkhd->bhqk", dout_block, value_block, preferred_element_type=jnp.float32
    )
    delta_heads = jnp.transpose(delta_block, (0, 2, 1))[..., None]
    dscore = (probs * (grad_probs - delta_heads)).astype(jnp.bfloat16)
    return (probs.astype(jnp.bfloat16), dscore)


def exchange(pieces, axis="seq"):
    count = pieces.shape[0]
    me = lax.axis_index(axis)
    out = pieces
    for step in [count // 2] + [s for s in range(1, count) if s != count // 2]:
        piece = lax.dynamic_index_in_dim(pieces, lax.rem(me + step, count), 0, keepdims=False)
        got = lax.ppermute(piece, axis, [(i, (i + step) % count) for i in range(count)])
        out = lax.dynamic_update_index_in_dim(out, got, lax.rem(me + count - step, count), 0)
    return out


def gather_weight(weight):
    parts = lax.axis_size("batch")
    if weight.shape[0] % parts:
        return lax.all_gather(weight, "seq", axis=0, tiled=True)
    rows = weight.shape[0] // parts
    mine = lax.dynamic_slice_in_dim(weight, lax.axis_index("batch") * rows, rows, 0)
    return lax.all_gather(mine, ("seq", "batch"), axis=0, tiled=True)


def sum_weight(grad):
    parts = lax.axis_size("batch") * lax.axis_size("seq")
    low = grad.astype(jnp.bfloat16)
    if grad.shape[0] % parts:
        shard = lax.psum_scatter(low, "seq", scatter_dimension=0, tiled=True)
        return lax.psum(shard, "batch").astype(jnp.float32)
    shard = lax.psum_scatter(low, ("seq", "batch"), scatter_dimension=0, tiled=True)
    return lax.all_gather(shard, "batch", axis=0, tiled=True).astype(jnp.float32)


def paired_tables(positions):
    cos, sin = rotary_tables(positions)
    half = HEAD_DIM // 2
    signed = jnp.concatenate([-sin[:, :half], sin[:, half:]], axis=1)
    return jnp.tile(cos, (1, 2)), jnp.tile(signed, (1, 2))


def on_device(
    layer_input,
    skip_input,
    time_embed,
    lengths,
    cond_drop,
    cotangent,
    skip_weight,
    adaln_weight,
    adaln_bias,
    qkv_weight,
    out_weight,
    up_weight,
    down_weight,
):
    utt_count, frame_span, model_width = layer_input.shape
    head_count = model_width // HEAD_DIM
    row_count = utt_count * frame_span
    seq_here = lax.axis_index("seq")
    seq_count = lax.axis_size("seq")
    frame_count = frame_span * seq_count
    by_heads = head_count == 2 * seq_count and frame_count % 1024 == 0
    local_pos = seq_here * frame_span + jnp.arange(frame_span, dtype=jnp.int32)
    local_live = local_pos[None, :] < lengths[:, None]
    valid_mask = local_live.astype(jnp.float32)
    drop = cond_drop.astype(jnp.float32)
    dropped = drop[:, None] * valid_mask
    frames_live = jnp.minimum(lengths, frame_count).astype(jnp.float32)
    kept_total, drop_total = lax.psum(
        (jnp.sum((1.0 - drop) * frames_live), jnp.sum(drop * frames_live)), "batch"
    )
    kept_total = jnp.maximum(kept_total, 1.0)
    drop_total = jnp.maximum(drop_total, 1.0)
    every_count = kept_total + drop_total
    loss_weight = (valid_mask - dropped) * (every_count / (2.0 * kept_total)) + dropped * (
        every_count / (2.0 * drop_total)
    )
    silu_time = jax.nn.silu(time_embed.astype(jnp.float32)).astype(jnp.bfloat16)
    row_span = adaln_weight.shape[0]
    silu_mine = lax.dynamic_slice_in_dim(silu_time, seq_here * row_span, row_span, 1)
    mod_part = jnp.dot(silu_mine, adaln_weight, preferred_element_type=jnp.float32)
    bias_span = adaln_bias.shape[0]
    bias_here = lax.dynamic_update_slice_in_dim(
        jnp.zeros((mod_part.shape[1],), jnp.float32),
        adaln_bias.astype(jnp.float32),
        seq_here * bias_span,
        0,
    )
    modulation = lax.psum(mod_part + bias_here, "seq").reshape(utt_count, 6, model_width)
    skip_full = gather_weight(skip_weight)
    qkv_full = gather_weight(qkv_weight)
    out_full = gather_weight(out_weight)
    up_full = gather_weight(up_weight)
    down_full = gather_weight(down_weight)
    joined = jnp.concatenate([layer_input, skip_input], axis=-1).reshape(row_count, 2 * model_width)
    residual_in = jnp.dot(joined, skip_full, preferred_element_type=jnp.float32).reshape(
        utt_count, frame_span, model_width
    )
    shift_attn = modulation[:, 0][:, None, :]
    scale_attn = modulation[:, 1][:, None, :]
    gate_attn = modulation[:, 2][:, None, :]
    shift_ffn = modulation[:, 3][:, None, :]
    scale_ffn = modulation[:, 4][:, None, :]
    gate_ffn = modulation[:, 5][:, None, :]
    hat_attn, inv_attn = layer_norm(residual_in)
    normed_attn = (
        (hat_attn * (1.0 + scale_attn) + shift_attn)
        .astype(jnp.bfloat16)
        .reshape(row_count, model_width)
    )
    if by_heads:
        cos_all, sin_all = paired_tables(jnp.arange(frame_count, dtype=jnp.int32))
        cos_here = lax.dynamic_slice_in_dim(cos_all, seq_here * frame_span, frame_span, 0)
        sin_here = lax.dynamic_slice_in_dim(sin_all, seq_here * frame_span, frame_span, 0)
        packed, attended_mine, lse_mine, attended_parts = [], [], [], []
        for utt in range(utt_count):
            sent = project_heads(
                normed_attn[utt * frame_span : (utt + 1) * frame_span],
                qkv_full,
                cos_here,
                sin_here,
                seq_count,
            )
            packed.append(exchange(sent).reshape(frame_count, 384))
        for utt in range(utt_count):
            heads_out, lse = flash_forward(lengths[utt : utt + 1], packed[utt], 1024, 1024)
            attended_mine.append(heads_out)
            lse_mine.append(lse)
            back = exchange(heads_out.reshape(seq_count, frame_span, 128))
            attended_parts.append(back.transpose(1, 0, 2).reshape(frame_span, model_width))
        attended_low = jnp.concatenate(attended_parts, axis=0)
    else:
        projected = jnp.dot(normed_attn, qkv_full, preferred_element_type=jnp.float32).reshape(
            utt_count, frame_span, 3, head_count, HEAD_DIM
        )
        cosine_table, sine_table = rotary_tables(local_pos)
        cosine_table = cosine_table[None, :, None, :]
        sine_table = sine_table[None, :, None, :]
        queries = (rotate_heads(projected[:, :, 0], cosine_table, sine_table) * 0.125).astype(
            jnp.bfloat16
        )
        keys_rot = rotate_heads(projected[:, :, 1], cosine_table, sine_table).astype(jnp.bfloat16)
        values = projected[:, :, 2].astype(jnp.bfloat16)
        start_top = jnp.full((utt_count, head_count, frame_span), MASKED, jnp.float32)
        top_score = start_top
        key_piece = lax.all_gather(keys_rot, "seq", axis=1, tiled=True)
        value_piece = lax.all_gather(values, "seq", axis=1, tiled=True)
        piece_len = key_piece.shape[1]
        piece_live = jnp.arange(piece_len, dtype=jnp.int32)[None, :] < lengths[:, None]
        scores = jnp.einsum("bqhd,bkhd->bhqk", queries, key_piece, preferred_element_type=jnp.float32)
        scores = jnp.where(piece_live[:, None, None, :], scores, MASKED)
        new_top = jnp.maximum(top_score, jnp.max(scores, axis=-1))
        expo = jnp.where(piece_live[:, None, None, :], jnp.exp(scores - new_top[..., None]), 0.0)
        denom = jnp.sum(expo, axis=-1)
        partial_out = jnp.einsum(
            "bhqk,bkhd->bqhd",
            expo.astype(jnp.bfloat16),
            value_piece,
            preferred_element_type=jnp.float32,
        )
        accum = partial_out
        accum, top_score, denom = (accum, new_top, denom)
        attended_full = accum / jnp.transpose(denom, (0, 2, 1))[..., None]
        lse_rows = jnp.transpose(top_score + jnp.log(denom), (0, 2, 1))
        attended_low = attended_full.astype(jnp.bfloat16).reshape(row_count, model_width)
    branch_attn = jnp.dot(attended_low, out_full, preferred_element_type=jnp.float32).reshape(
        utt_count, frame_span, model_width
    )
    residual_mid = residual_in + gate_attn * branch_attn
    hat_ffn, inv_ffn = layer_norm(residual_mid)
    normed_ffn = (
        (hat_ffn * (1.0 + scale_ffn) + shift_ffn)
        .astype(jnp.bfloat16)
        .reshape(row_count, model_width)
    )
    hidden_pre = jnp.dot(normed_ffn, up_full, preferred_element_type=jnp.float32)
    hidden_act = smooth_gelu(hidden_pre).astype(jnp.bfloat16)
    branch_ffn = jnp.dot(hidden_act, down_full, preferred_element_type=jnp.float32).reshape(
        utt_count, frame_span, model_width
    )
    layer_output = (residual_mid + gate_ffn * branch_ffn).astype(jnp.bfloat16)
    qkv_back, out_back, up_back, down_back = qkv_full, out_full, up_full, down_full
    skip_back = skip_full
    upstream = cotangent.astype(jnp.float32) * loss_weight[..., None]
    grad_branch_ffn = (upstream * gate_ffn).astype(jnp.bfloat16).reshape(row_count, model_width)
    grad_gate_ffn = jnp.sum(upstream * branch_ffn, axis=1)
    grad_down = cross(hidden_act, grad_branch_ffn)
    grad_hidden_act = back_product(grad_branch_ffn, down_back)
    gelu_value, gelu_pull = jax.vjp(smooth_gelu, hidden_pre)
    grad_hidden_pre = gelu_pull(grad_hidden_act)[0].astype(jnp.bfloat16)
    grad_up = cross(normed_ffn, grad_hidden_pre)
    grad_normed_ffn = back_product(grad_hidden_pre, up_back).reshape(
        utt_count, frame_span, model_width
    )
    grad_shift_ffn = jnp.sum(grad_normed_ffn, axis=1)
    grad_scale_ffn = jnp.sum(grad_normed_ffn * hat_ffn, axis=1)
    grad_mid = upstream + norm_back(grad_normed_ffn * (1.0 + scale_ffn), hat_ffn, inv_ffn)
    grad_branch_attn = (grad_mid * gate_attn).astype(jnp.bfloat16).reshape(row_count, model_width)
    grad_gate_attn = jnp.sum(grad_mid * branch_attn, axis=1)
    grad_out = cross(attended_low, grad_branch_attn)
    grad_attended_flat = back_product(grad_branch_attn, out_back).astype(jnp.bfloat16)
    if by_heads:
        grad_parts = []
        for utt in range(utt_count):
            sent = grad_attended_flat[utt * frame_span : (utt + 1) * frame_span]
            sent = sent.reshape(frame_span, seq_count, 128).transpose(1, 0, 2)
            dout = exchange(sent).reshape(frame_count, 128)
            grads = flash_backward(
                lengths[utt : utt + 1],
                packed[utt],
                attended_mine[utt],
                dout,
                lse_mine[utt],
                cos_all,
                sin_all,
                1024,
                1024,
            )
            back = exchange(grads.reshape(seq_count, frame_span, 384))
            back = back.reshape(seq_count, frame_span, 3, 128).transpose(1, 2, 0, 3)
            grad_parts.append(back.reshape(frame_span, 3 * model_width))
        grad_projected = jnp.concatenate(grad_parts, axis=0)
    else:
        grad_attended = grad_attended_flat.reshape(
            utt_count, frame_span, head_count, HEAD_DIM
        )
        delta_rows = jnp.sum(grad_attended.astype(jnp.float32) * attended_full, axis=-1)
        lse_all, delta_all = (
            lax.all_gather(lse_rows, "seq", axis=1, tiled=True),
            lax.all_gather(delta_rows, "seq", axis=1, tiled=True),
        )
        key_piece = lax.all_gather(keys_rot, "seq", axis=1, tiled=True)
        value_piece = lax.all_gather(values, "seq", axis=1, tiled=True)
        piece_len = key_piece.shape[1]
        piece_live = jnp.arange(piece_len, dtype=jnp.int32)[None, :] < lengths[:, None]
        probs_low, dscore = block_terms(
            queries, grad_attended, lse_rows, delta_rows, key_piece, value_piece, piece_live
        )
        grad_queries = jnp.einsum(
            "bhqk,bkhd->bqhd", dscore, key_piece, preferred_element_type=jnp.float32
        )
        query_piece = lax.all_gather(queries, "seq", axis=1, tiled=True)
        dout_piece = lax.all_gather(grad_attended, "seq", axis=1, tiled=True)
        probs_low, dscore = block_terms(
            query_piece, dout_piece, lse_all, delta_all, keys_rot, values, local_live
        )
        grad_k = jnp.einsum("bhqk,bqhd->bkhd", dscore, query_piece, preferred_element_type=jnp.float32)
        grad_v = jnp.einsum(
            "bhqk,bqhd->bkhd", probs_low, dout_piece, preferred_element_type=jnp.float32
        )
        grad_q_pre = rotate_heads(grad_queries * 0.125, cosine_table, -sine_table)
        grad_k_pre = rotate_heads(grad_k, cosine_table, -sine_table)
        grad_projected = (
            jnp.stack([grad_q_pre, grad_k_pre, grad_v], axis=2)
            .reshape(row_count, 3 * model_width)
            .astype(jnp.bfloat16)
        )
    grad_qkv = cross(normed_attn, grad_projected)
    grad_normed_attn = back_product(grad_projected, qkv_back).reshape(
        utt_count, frame_span, model_width
    )
    grad_shift_attn = jnp.sum(grad_normed_attn, axis=1)
    grad_scale_attn = jnp.sum(grad_normed_attn * hat_attn, axis=1)
    grad_stream = grad_mid + norm_back(grad_normed_attn * (1.0 + scale_attn), hat_attn, inv_attn)
    grad_stream_low = grad_stream.astype(jnp.bfloat16).reshape(row_count, model_width)
    grad_skip_w = cross(joined, grad_stream_low)
    grad_joined = back_product(grad_stream_low, skip_back)
    grad_input = (
        grad_joined[:, :model_width]
        .reshape(utt_count, frame_span, model_width)
        .astype(jnp.bfloat16)
    )
    grad_skip = (
        grad_joined[:, model_width:]
        .reshape(utt_count, frame_span, model_width)
        .astype(jnp.bfloat16)
    )
    grad_modulation = jnp.stack(
        [
            grad_shift_attn,
            grad_scale_attn,
            grad_gate_attn,
            grad_shift_ffn,
            grad_scale_ffn,
            grad_gate_ffn,
        ],
        axis=1,
    ).reshape(utt_count, 6 * model_width)
    mod_total = lax.psum(grad_modulation, "seq")
    mod_every, silu_every = (
        lax.all_gather(mod_total.astype(jnp.bfloat16), "batch", axis=0, tiled=True).astype(
            mod_total.dtype
        ),
        lax.all_gather(
            silu_time.astype(jnp.float32).astype(jnp.bfloat16), "batch", axis=0, tiled=True
        ).astype(jnp.float32),
    )
    silu_rows = lax.dynamic_slice_in_dim(silu_every, seq_here * row_span, row_span, 1)
    adaln_rows = jnp.dot(silu_rows.T, mod_every, precision=lax.Precision.HIGHEST)
    bias_rows = lax.dynamic_slice_in_dim(
        jnp.sum(mod_every, axis=0), seq_here * bias_span, bias_span, 0
    )
    summed = [sum_weight(grad) for grad in (grad_skip_w, grad_qkv, grad_out, grad_up, grad_down)]
    results = (summed[0], adaln_rows, bias_rows, summed[1], summed[2], summed[3], summed[4])
    return (
        layer_output,
        grad_input,
        grad_skip,
        results[0],
        results[1],
        results[2],
        results[3],
        results[4],
        results[5],
        results[6],
    )


def solution(mesh):
    placed = (
        P("batch", "seq", None),
        P("batch", "seq", None),
        P("batch", None),
        P("batch"),
        P("batch"),
        P("batch", "seq", None),
        P("seq", None),
        P("seq", None),
        P("seq"),
        P("seq", None),
        P("seq", None),
        P("seq", None),
        P("seq", None),
    )
    return jax.shard_map(
        on_device,
        mesh=mesh,
        in_specs=placed,
        out_specs=(
            P("batch", "seq", None),
            P("batch", "seq", None),
            P("batch", "seq", None),
            P("seq", None),
            P("seq", None),
            P("seq"),
            P("seq", None),
            P("seq", None),
            P("seq", None),
            P("seq", None),
        ),
        check_vma=False,
    )
```

time: 2730 us -> 1310 us (0.48)
  waiting for transfers between devices: 1500 us -> 327 us
  matrix products: 778 us -> 168 us
  Pallas kernels: 0 us -> 238 us
  starting transfers between devices: 0.64 us -> 170 us
  other arithmetic: 151 us -> 44.1 us
  local copies, waits for them, and re-layouts: 77.6 us -> 143 us
    all_gather x10 -> x7, waiting for transfers between devices: 715 us -> 84.1 us  [the longest x5 62.2 us: gather_weight(): return lax.all_gather(mine, ('seq', 'batch'), axis=0, tiled=True)]
    dot_general x8 -> x1, matrix products: 606 us -> 0.32 us  [on_device(): jnp.dot(silu_mine, adaln_weight, preferred_element_type=jnp.float32)]
    reduce_scatter x5, waiting for transfers between devices: 754 us -> 159 us  [sum_weight(): lax.psum_scatter(low, ('seq', 'batch'), scatter_dimension=0, tiled=True)]
    pallas_call x0 -> x6, Pallas kernels: none -> 238 us  [the longest x2 151 us: flash_backward(): pl.pallas_call(functools.partial(flash_backward_kernel, bq=bq, bk=bk), gr...]
    ppermute x0 -> x56, starting transfers between devices: none -> 169 us  [exchange(): lax.ppermute(piece, axis, [(i, (i + step) % count) for i in range(count)])]
    all_gather x3, blocking collectives: 107 us -> 23.3 us  [sum_weight(): lax.all_gather(shard, 'batch', axis=0, tiled=True).astype(jnp.float32)]
    ppermute x0 -> x56, waiting for transfers between devices: none -> 82.5 us  [exchange(): lax.ppermute(piece, axis, [(i, (i + step) % count) for i in range(count)])]
    all_gather x1, blocking collectives: 5.19 us -> 84.6 us  [on_device(): lax.all_gather(silu_time.astype(jnp.float32).astype(jnp.bfloat16), 'batch...]
  transfers between devices with their start and end apart: 16 -> 68, of which waited for: 13 -> 20; matrix products, arithmetic and copies ran while one was open for 36% -> 23% of each run, Pallas kernels for 0% -> 18%
where the time goes in v1:
time: 1310 us
  waiting for transfers between devices  327 us (25%)
  Pallas kernels  238 us (18%)
  blocking collectives  200 us (15%)
  starting transfers between devices  170 us (13%)
  matrix products  168 us (13%)
  local copies, waits for them, and re-layouts  143 us (11%)
  other arithmetic  44.1 us (3%)
  between operations  17.2 us (1%)
    ppermute x56, starting transfers between devices, exchange(): lax.ppermute(piece, axis, [(i, (i + step) % count) for i in range(count)])  169 us
    reduce_scatter x5, waiting for transfers between devices, sum_weight(): lax.psum_scatter(low, ('seq', 'batch'), scatter_dimension=0, tiled=True)  159 us
    pallas_call x2, Pallas kernels, flash_backward(): pl.pallas_call(functools.partial(flash_backward_kernel, bq=bq, bk=bk), gr...  151 us
    all_gather x1, blocking collectives, on_device(): lax.all_gather(silu_time.astype(jnp.float32).astype(jnp.bfloat16), 'batch...  84.6 us
    ppermute x56, waiting for transfers between devices, exchange(): lax.ppermute(piece, axis, [(i, (i + step) % count) for i in range(count)])  82.5 us
    pallas_call x2, Pallas kernels, flash_forward(): pl.pallas_call(functools.partial(flash_forward_kernel, bq=bq, bk=bk), gri...  71.8 us
    all_gather x5, waiting for transfers between devices, gather_weight(): return lax.all_gather(mine, ('seq', 'batch'), axis=0, tiled=True)  62.2 us
    dot_general x5, matrix products, back_product(): lax.dot_general(left, right, (((1,), (1,)), ((), ())), preferred_element_...  56 us
  transfers between devices with their start and end apart: 68, of which 20 were waited for; matrix products, arithmetic and copies ran while one was open for 23% of the time, Pallas kernels for 18%

profile of v1, /device:TPU:0, one launch (start us, length us, event | category | flops | bytes accessed | tf_op | source)
XLA Modules:
  0.0 1308.0 jit_solution(4913550046155615258)
XLA Ops:
  29.9 38.4 %psum.28 = f32[2,6,1024]{2,1,0:T(8,128)S(1)} all-reduce(f32[2,6,1024]{2,1,0:T(8,128)S(1)} %reshape.296), channel_id=1, replica_groups=mesh['seq'=8,'batch'=4] {'seq'}, use_global_device_ids=true, to_apply=%region_0.0 | all-reduce | flops 12288 | bytes 98304 | tf_op jit(solution)/shard_map/psum | solution.py:481
  106.3 41.5 %all-gather.12.cloned.1.call-done.w_ref = bf16[1024,3072]{1,0:T(8,128)(2,1)} async-done(((bf16[32,3072]{1,0:T(8,128)(2,1)}), bf16[1024,3072]{1,0:T(8,128)(2,1)}) %all-gather.12.cloned.1.call-update) | async-done | bytes 6291472 | tf_op jit(solution)/shard_map/all_gather | solution.py:413
  168.8 19.1 %collective-permute-done = bf16[512,384]{1,0:T(8,128)(2,1)S(1)} collective-permute-done((bf16[512,384]{1,0:T(8,128)(2,1)S(1)}, bf16[512,384]{1,0:T(8,128)(2,1)S(1)}, u32[]{:S(2)}, u32[]{:S(2)}) %collective-permute-start) | collective-permute-done | bytes 393248 | tf_op jit(solution)/shard_map/ppermute | solution.py:402
  196.6 27.8 %collective-permute-done.14 = bf16[512,384]{1,0:T(8,128)(2,1)S(1)} collective-permute-done((bf16[512,384]{1,0:T(8,128)(2,1)S(1)}, bf16[512,384]{1,0:T(8,128)(2,1)S(1)}, u32[]{:S(2)}, u32[]{:S(2)}) %collective-permute-start.14) | collective-permute-done | bytes 393248 | tf_op jit(solution)/shard_map/ppermute | solution.py:402
  256.9 27.8 %collective-permute-start.18 = (bf16[512,384]{1,0:T(8,128)(2,1)S(1)}, bf16[512,384]{1,0:T(8,128)(2,1)}, u32[]{:S(2)}, u32[]{:S(2)}) collective-permute-start(bf16[512,384]{1,0:T(8,128)(2,1)S(1)} %get-tuple-element.58), channel_id=1, source_target_pairs={{0,20},{4,24},{8,28},{12,0},{16,4},{20,8},{24,12},{28,16},{1,21},{... | collective-permute-start | bytes 1179656 | tf_op jit(solution)/shard_map/ppermute | solution.py:402
  290.0 39.7 %attend_forward.2 = (bf16[4096,128]{1,0:T(8,128)(2,1)}, f32[8,4096]{1,0:T(8,128)}) custom-call(s32[1]{0:T(128)} %get-tuple-element.106.len_ref, bf16[4096,384]{1,0:T(8,128)(2,1)} %bitcast.18.q_ref.k_ref.v_ref, bf16[4096,384]{1,0:T(8,128)(2,1)} %bitcast.18.q_ref.k_ref.v_ref, bf16[4096,384]{1,0:T(8,128)(2,1)} %bitcast.18.q_ref.k_ref.v_ref), custom_call_target="tpu_custom_call" | custom-call | flops 17179869184 | bytes 8388608 | tf_op jit(solution)/shard_map/attend_forward/pallas_call | solution.py:138
  361.9 32.1 %attend_forward.3 = (bf16[4096,128]{1,0:T(8,128)(2,1)}, f32[8,4096]{1,0:T(8,128)}) custom-call(s32[1]{0:T(128)} %get-tuple-element.107.len_ref, bf16[4096,384]{1,0:T(8,128)(2,1)} %bitcast.51.q_ref.k_ref.v_ref, bf16[4096,384]{1,0:T(8,128)(2,1)} %bitcast.51.q_ref.k_ref.v_ref, bf16[4096,384]{1,0:T(8,128)(2,1)} %bitcast.51.q_ref.k_ref.v_ref), custom_call_target="tpu_custom_call" | custom-call | flops 17179869184 | bytes 8388608 | tf_op jit(solution)/shard_map/attend_forward/pallas_call | solution.py:138
  437.4 16.3 %fusion.36 = f32[1024,4096]{1,0:T(8,128)} fusion(bf16[1024,1024]{1,0:T(8,128)(2,1)} %bitcast.324, bf16[4096,1024]{1,0:T(8,128)(2,1)} %all-gather.18.cloned.1.call-done), kind=kOutput, calls=%fused_computation.229 | convolution fusion | flops 8589934592 | bytes 27262976 | tf_op jit(solution)/shard_map/dot_general | solution.py:377
  453.7 20.7 %all-gather.16.cloned.1.call-done = bf16[1024,4096]{1,0:T(8,128)(2,1)} async-done(((bf16[32,4096]{1,0:T(8,128)(2,1)}), bf16[1024,4096]{1,0:T(8,128)(2,1)}) %all-gather.16.cloned.1.call-update) | async-done | bytes 8388624 | tf_op jit(solution)/shard_map/all_gather | solution.py:413
  474.4 27.6 %fusion.6 = (bf16[1024,4096]{1,0:T(8,128)(2,1)}, f32[1024,4096]{1,0:T(8,128)}) fusion(f32[1024,4096]{1,0:T(8,128)} %fusion.36, bf16[1024,1024]{1,0:T(8,128)(2,1)} %bitcast.328, bf16[1024,4096]{1,0:T(8,128)(2,1)} %all-gather.16.cloned.1.call-done), kind=kOutput, calls=%fused_computation.8 | convolution fusion | flops 8673820672 | bytes 52428800 | tf_op jit(solution)/shard_map/dot_general | solution.py:568
  502.0 15.0 %convolution_convert_fusion.1 = bf16[1024,4096]{1,0:T(8,128)(2,1)} fusion(bf16[1024,1024]{1,0:T(8,128)(2,1)} %bitcast.329, bf16[1024,4096]{1,0:T(8,128)(2,1)} %get-tuple-element.110), kind=kOutput, calls=%fused_computation.12 | convolution fusion | flops 8594128896 | bytes 18874368 | tf_op jit(solution)/shard_map/dot_general | solution.py:371
  517.1 18.0 %convolution_convert_fusion = bf16[4096,1024]{1,0:T(8,128)(2,1)} fusion(bf16[1024,1024]{1,0:T(8,128)(2,1)} %bitcast.325, f32[1024,4096]{1,0:T(8,128)} %get-tuple-element.111), kind=kOutput, calls=%fused_computation.11 | convolution fusion | flops 8631877632 | bytes 27262976 | tf_op jit(solution)/shard_map/dot_general | solution.py:371
  535.2 15.7 %fusion.8 = (f32[1024]{0:T(1024)S(1)}, f32[1024,1024]{1,0:T(8,128)}) fusion(f32[2,1024]{1,0:T(2,128)S(1)} %get-tuple-element.116, bf16[1024,4096]{1,0:T(8,128)(2,1)} %get-tuple-element.110, bf16[1024,4096]{1,0:T(8,128)(2,1)} %all-gather.16.cloned.1.call-done), kind=kOutput, calls=%fused_computation.21 | convolution fusion | flops 8592030720 | bytes 20983808 | tf_op jit(solution)/shard_map/dot_general | solution.py:377
  557.7 16.3 %fusion.29 = f32[1024,1024]{1,0:T(8,128)S(1)} fusion(bf16[4096,1024]{1,0:T(8,128)(2,1)} %all-gather.18.cloned.1.call-done, f32[1024,4096]{1,0:T(8,128)} %get-tuple-element.111), kind=kOutput, calls=%fused_computation.222 | convolution fusion | flops 8627683328 | bytes 29360128 | tf_op jit(solution)/shard_map/dot_general | solution.py:570
  625.3 92.6 %attend_backward.2 = bf16[4096,384]{1,0:T(8,128)(2,1)} custom-call(s32[1]{0:T(128)} %get-tuple-element.106.len_ref, bf16[4096,384]{1,0:T(8,128)(2,1)} %bitcast.18.q_ref.k_ref.v_ref, bf16[4096,384]{1,0:T(8,128)(2,1)} %bitcast.18.q_ref.k_ref.v_ref, bf16[4096,384]{1,0:T(8,128)(2,1)} %bitcast.18.q_ref.k_ref.v_ref, bf16[4096,128]{1,0:T(8,128)(2,1)} %get-tuple-element.14.o_ref, ...), custom_call_target="tpu_custom_call" | custom-call | flops 42949672960 | bytes 8388608 | tf_op jit(solution)/shard_map/attend_backward/pallas_call | solution.py:271
  735.7 58.0 %attend_backward.3 = bf16[4096,384]{1,0:T(8,128)(2,1)} custom-call(s32[1]{0:T(128)} %get-tuple-element.107.len_ref, bf16[4096,384]{1,0:T(8,128)(2,1)} %bitcast.51.q_ref.k_ref.v_ref, bf16[4096,384]{1,0:T(8,128)(2,1)} %bitcast.51.q_ref.k_ref.v_ref, bf16[4096,384]{1,0:T(8,128)(2,1)} %bitcast.51.q_ref.k_ref.v_ref, bf16[4096,128]{1,0:T(8,128)(2,1)} %get-tuple-element.15.o_ref, ...), custom_call_target="tpu_custom_call" | custom-call | flops 42949672960 | bytes 8388608 | tf_op jit(solution)/shard_map/attend_backward/pallas_call | solution.py:271
  835.8 12.8 collective-permute-start.50
  850.4 22.1 %collective-permute-start.51 = (bf16[512,384]{0,1:T(8,128)(2,1)S(1)}, bf16[512,384]{0,1:T(8,128)(2,1)S(1)}, u32[]{:S(2)}, u32[]{:S(2)}) collective-permute-start(bf16[512,384]{0,1:T(8,128)(2,1)S(1)} %bitcast.346), channel_id=1, source_target_pairs={{0,8},{4,12},{8,16},{12,20},{16,24},{20,28},{24,0},{28,4},{1,9},{5... | collective-permute-start | bytes 1179656 | tf_op jit(solution)/shard_map/ppermute | solution.py:402
  910.4 12.2 fusion.7
  940.6 84.6 %all-gather = bf16[4,2,1024]{2,1,0:T(2,128)(2,1)S(1)} all-gather(bf16[1,2,1024]{2,1,0:T(2,128)(2,1)S(1)} %fusion.60), channel_id=1, replica_groups=mesh['seq'=8,'batch'=4] {'batch'}, dimensions={0}, use_global_device_ids=true | all-gather | bytes 20480 | tf_op jit(solution)/shard_map/all_gather | solution.py:686
  1035.0 39.5 %psum.31 = bf16[2,6144]{1,0:T(2,128)(2,1)S(1)} all-reduce(f32[2,6144]{1,0:T(2,128)S(1)} %bitcast.352), channel_id=1, replica_groups=mesh['seq'=8,'batch'=4] {'seq'}, use_global_device_ids=true, to_apply=%region_20.21 | all-reduce | flops 12288 | bytes 73728 | tf_op jit(solution)/shard_map/psum | solution.py:681
  1096.5 27.0 %reduce-scatter.8.cloned.1.call-done = bf16[32,3072]{1,0:T(8,128)(2,1)} async-done(((bf16[1024,3072]{1,0:T(8,128)(2,1)}), bf16[32,3072]{1,0:T(8,128)(2,1)}) %reduce-scatter.8.cloned.1.call-update) | async-done | bytes 196624 | tf_op jit(solution)/shard_map/reduce_scatter | solution.py:422
  1133.6 132.2 %reduce-scatter.6.cloned.1.call-done = bf16[64,1024]{1,0:T(8,128)(2,1)} async-done(((bf16[2048,1024]{1,0:T(8,128)(2,1)}), bf16[64,1024]{1,0:T(8,128)(2,1)}) %reduce-scatter.6.cloned.1.call-update) | async-done | bytes 131088 | tf_op jit(solution)/shard_map/reduce_scatter | solution.py:422
  1282.7 15.4 %all-gather.22.cloned.1.call-done = bf16[512,1024]{1,0:T(8,128)(2,1)} async-done(((bf16[128,1024]{1,0:T(8,128)(2,1)}), bf16[512,1024]{1,0:T(8,128)(2,1)}) %all-gather.22.cloned.1.call-update) | async-done | bytes 1048592 | tf_op jit(solution)/shard_map/all_gather | solution.py:423
  (435 shorter events, 438.4 us)
Async XLA Ops:
  7.2 86.5 %all-gather.10.cloned.1.call-start = ((), (), s32[]{:S(2)}) async-start(), calls=%async_computation.5 | async-start | bytes 4325376 | tf_op jit(solution)/shard_map/all_gather | solution.py:413
  8.9 138.8 %all-gather.12.cloned.1.call-start = ((), (), s32[]{:S(2)}) async-start(), calls=%async_computation.6 | async-start | bytes 6488064 | tf_op jit(solution)/shard_map/all_gather | solution.py:413
  10.6 416.2 %all-gather.14.cloned.1.call-start = ((), (), s32[]{:S(2)}) async-start(), calls=%async_computation.7 | async-start | bytes 2162688 | tf_op jit(solution)/shard_map/all_gather | solution.py:413
  12.2 425.3 %all-gather.18.cloned.1.call-start = ((), (), s32[]{:S(2)}) async-start(), calls=%async_computation.9 | async-start | bytes 8650752 | tf_op jit(solution)/shard_map/all_gather | solution.py:413
  13.9 460.5 %all-gather.16.cloned.1.call-start = ((), (), s32[]{:S(2)}) async-start(), calls=%async_computation.8 | async-start | bytes 8650752 | tf_op jit(solution)/shard_map/all_gather | solution.py:413
  15.7 924.2 %reduce-scatter.12.cloned.1.call-start = ((), (), s32[]{:S(2)}) async-start(), calls=%async_computation.13 | async-start | bytes 8650752 | tf_op jit(solution)/shard_map/reduce_scatter | solution.py:422
  229.9 108.0 %collective-permute-start.15 = (bf16[512,384]{1,0:T(8,128)(2,1)}, bf16[512,384]{1,0:T(8,128)(2,1)}, u32[]{:S(2)}, u32[]{:S(2)}) collective-permute-start(bf16[512,384]{1,0:T(8,128)(2,1)} %get-tuple-element.61), channel_id=1, source_target_pairs={{0,4},{4,8},{8,12},{12,16},{16,20},{20,24},{24,28},{28,0},{1,5},{5... | collective-permute-start | bytes 1179656 | tf_op jit(solution)/shard_map/ppermute | solution.py:402
  237.2 102.5 %collective-permute-start.16 = (bf16[512,384]{1,0:T(8,128)(2,1)}, bf16[512,384]{1,0:T(8,128)(2,1)}, u32[]{:S(2)}, u32[]{:S(2)}) collective-permute-start(bf16[512,384]{1,0:T(8,128)(2,1)} %get-tuple-element.60), channel_id=1, source_target_pairs={{0,8},{4,12},{8,16},{12,20},{16,24},{20,28},{24,0},{28,4},{1,9},{5... | collective-permute-start | bytes 1179656 | tf_op jit(solution)/shard_map/ppermute | solution.py:402
  249.0 92.5 %collective-permute-start.17 = (bf16[512,384]{1,0:T(8,128)(2,1)S(1)}, bf16[512,384]{1,0:T(8,128)(2,1)}, u32[]{:S(2)}, u32[]{:S(2)}) collective-permute-start(bf16[512,384]{1,0:T(8,128)(2,1)S(1)} %get-tuple-element.59), channel_id=1, source_target_pairs={{0,12},{4,16},{8,20},{12,24},{16,28},{20,0},{24,4},{28,8},{1,13},{... | collective-permute-start | bytes 1179656 | tf_op jit(solution)/shard_map/ppermute | solution.py:402
  256.9 88.4 %collective-permute-start.18 = (bf16[512,384]{1,0:T(8,128)(2,1)S(1)}, bf16[512,384]{1,0:T(8,128)(2,1)}, u32[]{:S(2)}, u32[]{:S(2)}) collective-permute-start(bf16[512,384]{1,0:T(8,128)(2,1)S(1)} %get-tuple-element.58), channel_id=1, source_target_pairs={{0,20},{4,24},{8,28},{12,0},{16,4},{20,8},{24,12},{28,16},{1,21},{... | collective-permute-start | bytes 1179656 | tf_op jit(solution)/shard_map/ppermute | solution.py:402
  285.5 62.5 %collective-permute-start.19 = (bf16[512,384]{1,0:T(8,128)(2,1)S(1)}, bf16[512,384]{1,0:T(8,128)(2,1)}, u32[]{:S(2)}, u32[]{:S(2)}) collective-permute-start(bf16[512,384]{1,0:T(8,128)(2,1)S(1)} %get-tuple-element.57), channel_id=1, source_target_pairs={{0,24},{4,28},{8,0},{12,4},{16,8},{20,12},{24,16},{28,20},{1,25},{... | collective-permute-start | bytes 1179656 | tf_op jit(solution)/shard_map/ppermute | solution.py:402
  341.5 58.4 %collective-permute-start.8 = (bf16[512,128]{0,1:T(8,128)(2,1)}, bf16[512,128]{0,1:T(8,128)(2,1)S(1)}, u32[]{:S(2)}, u32[]{:S(2)}) collective-permute-start(bf16[512,128]{0,1:T(8,128)(2,1)} %bitcast.22), channel_id=1, source_target_pairs={{0,4},{4,8},{8,12},{12,16},{16,20},{20,24},{24,28},{28,0},{1,5},{5... | collective-permute-start | bytes 393224 | tf_op jit(solution)/shard_map/ppermute | solution.py:402
  517.1 508.3 %reduce-scatter.14.cloned.1.call-start = ((), (), s32[]{:S(2)}) async-start(), calls=%async_computation.15 | async-start | bytes 8650752 | tf_op jit(solution)/shard_map/reduce_scatter | solution.py:422
  535.1 552.7 %reduce-scatter.10.cloned.1.call-start = ((), (), s32[]{:S(2)}) async-start(), calls=%async_computation.12 | async-start | bytes 2162688 | tf_op jit(solution)/shard_map/reduce_scatter | solution.py:422
  609.0 514.5 %reduce-scatter.8.cloned.1.call-start = ((), (), s32[]{:S(2)}) async-start(), calls=%async_computation.11 | async-start | bytes 6488064 | tf_op jit(solution)/shard_map/reduce_scatter | solution.py:422
  614.9 105.2 %collective-permute-start.42 = (bf16[512,128]{1,0:T(8,128)(2,1)}, bf16[512,128]{1,0:T(8,128)(2,1)}, u32[]{:S(2)}, u32[]{:S(2)}) collective-permute-start(bf16[512,128]{1,0:T(8,128)(2,1)} %bitcast.113), channel_id=1, source_target_pairs={{0,16},{4,20},{8,24},{12,28},{16,0},{20,4},{24,8},{28,12},{1,17},{... | collective-permute-start | bytes 393224 | tf_op jit(solution)/shard_map/ppermute | solution.py:402
  616.8 107.8 %collective-permute-start.43 = (bf16[512,128]{1,0:T(8,128)(2,1)}, bf16[512,128]{1,0:T(8,128)(2,1)}, u32[]{:S(2)}, u32[]{:S(2)}) collective-permute-start(bf16[512,128]{1,0:T(8,128)(2,1)} %bitcast.115), channel_id=1, source_target_pairs={{0,4},{4,8},{8,12},{12,16},{16,20},{20,24},{24,28},{28,0},{1,5},{5... | collective-permute-start | bytes 393224 | tf_op jit(solution)/shard_map/ppermute | solution.py:402
  618.4 109.2 %collective-permute-start.44 = (bf16[512,128]{1,0:T(8,128)(2,1)}, bf16[512,128]{1,0:T(8,128)(2,1)}, u32[]{:S(2)}, u32[]{:S(2)}) collective-permute-start(bf16[512,128]{1,0:T(8,128)(2,1)} %bitcast.117), channel_id=1, source_target_pairs={{0,8},{4,12},{8,16},{12,20},{16,24},{20,28},{24,0},{28,4},{1,9},{5... | collective-permute-start | bytes 393224 | tf_op jit(solution)/shard_map/ppermute | solution.py:402
  620.2 111.0 %collective-permute-start.45 = (bf16[512,128]{1,0:T(8,128)(2,1)}, bf16[512,128]{1,0:T(8,128)(2,1)}, u32[]{:S(2)}, u32[]{:S(2)}) collective-permute-start(bf16[512,128]{1,0:T(8,128)(2,1)} %bitcast.119), channel_id=1, source_target_pairs={{0,12},{4,16},{8,20},{12,24},{16,28},{20,0},{24,4},{28,8},{1,13},{... | collective-permute-start | bytes 393224 | tf_op jit(solution)/shard_map/ppermute | solution.py:402
  622.9 109.9 %collective-permute-start.46 = (bf16[512,128]{1,0:T(8,128)(2,1)S(1)}, bf16[512,128]{1,0:T(8,128)(2,1)}, u32[]{:S(2)}, u32[]{:S(2)}) collective-permute-start(bf16[512,128]{1,0:T(8,128)(2,1)S(1)} %bitcast.357), channel_id=1, source_target_pairs={{0,20},{4,24},{8,28},{12,0},{16,4},{20,8},{24,12},{28,16},{1,21},{... | collective-permute-start | bytes 393224 | tf_op jit(solution)/shard_map/ppermute | solution.py:402
  727.6 98.4 %collective-permute-start.35 = (bf16[512,384]{0,1:T(8,128)(2,1)S(1)}, bf16[512,384]{0,1:T(8,128)(2,1)}, u32[]{:S(2)}, u32[]{:S(2)}) collective-permute-start(bf16[512,384]{0,1:T(8,128)(2,1)S(1)} %bitcast.343), channel_id=1, source_target_pairs={{0,16},{4,20},{8,24},{12,28},{16,0},{20,4},{24,8},{28,12},{1,17},{... | collective-permute-start | bytes 1179656 | tf_op jit(solution)/shard_map/ppermute | solution.py:402
  909.7 356.0 %reduce-scatter.6.cloned.1.call-start = ((), (), s32[]{:S(2)}) async-start(), calls=%async_computation.10 | async-start | bytes 4325376 | tf_op jit(solution)/shard_map/reduce_scatter | solution.py:422
  939.8 340.2 %all-gather.20.cloned.1.call-start = ((), (), s32[]{:S(2)}) async-start(), calls=%async_computation.14 | async-start | bytes 1310720 | tf_op jit(solution)/shard_map/all_gather | solution.py:423
  940.5 357.6 %all-gather.22.cloned.1.call-start = ((), (), s32[]{:S(2)}) async-start(), calls=%async_computation.16 | async-start | bytes 1310720 | tf_op jit(solution)/shard_map/all_gather | solution.py:423
  (90 other events, 2155.2 us)
Sparse Core Ops, SparseCore 0:
  11.5 64.7 all-gather.9
  79.7 68.0 all-gather.11
  150.7 103.0 all-gather.13
  257.0 123.9 all-gather.17
  383.8 90.6 all-gather.15
  517.2 155.7 reduce-scatter.11
  675.2 156.9 reduce-scatter.13
  834.5 160.8 reduce-scatter.9
  1002.0 121.4 reduce-scatter.7
  1125.6 140.1 reduce-scatter.5
  1267.4 12.5 all-gather.19
  1281.4 16.7 all-gather.21

commit v2 on v1

--- a/solution.py
+++ b/solution.py
@@ -294,6 +294,231 @@
     )(length, qkv, qkv, qkv, out, dout, lse, cos, sin)
 
 
+def layer_norm(stream):
+    centre = stream - jnp.mean(stream, axis=-1, keepdims=True)
+    spread = jnp.mean(centre * centre, axis=-1, keepdims=True)
+    inverse = lax.rsqrt(spread + EPS)
+    return (centre * inverse, inverse)
+
+
+def norm_back(grad_normed, normed, inverse):
+    first_mean = jnp.mean(grad_normed, axis=-1, keepdims=True)
+    second_mean = jnp.mean(grad_normed * normed, axis=-1, keepdims=True)
+    return inverse * (grad_normed - first_mean - normed * second_mean)
+
+
+def tn(left, right):
+    return lax.dot_general(left, right, (((0,), (0,)), ((), ())), preferred_element_type=F32)
+
+
+GELU_C = 0.7978845608028654
+GELU_A = 0.044715
+
+
+def gelu_and_slope(z):
+    square = z * z
+    turn = jnp.tanh(GELU_C * z * (1.0 + GELU_A * square))
+    half = 0.5 * (1.0 + turn)
+    slope = half + 0.5 * z * (1.0 - turn * turn) * (GELU_C * (1.0 + 3.0 * GELU_A * square))
+    return z * half, slope
+
+
+def row_blocks(rows):
+    block = min(rows, 256)
+    return [(at, slice(at, at + block)) for at in range(0, rows, block)]
+
+
+def ffn_forward_kernel(
+    att_ref, outw_ref, res_ref, mod_ref, cot_ref, weight_ref, up_ref, down_ref,
+    branch_ref, act_ref, slope_ref, gb_ref, out_ref, gate_ref, normed, acc,
+):
+    step = pl.program_id(0)
+    rows = att_ref.shape[0]
+    span = rows // mod_ref.shape[0]
+
+    @pl.when(step == 0)
+    def _():
+        for at, part in row_blocks(span):
+            for utt in range(mod_ref.shape[0]):
+                here = slice(utt * span + part.start, utt * span + part.stop)
+                mod = mod_ref[utt]
+                branch = nn(att_ref[here, :], outw_ref[...])
+                branch_ref[here, :] = branch
+                hat, _ = layer_norm(res_ref[here, :] + mod[2:3] * branch)
+                normed[here, :] = (hat * (1.0 + mod[4:5]) + mod[3:4]).astype(BF)
+        acc[...] = jnp.zeros_like(acc)
+
+    for _, part in row_blocks(rows):
+        act, slope = gelu_and_slope(nn(normed[part, :], up_ref[...]))
+        act = act.astype(BF)
+        act_ref[part, :] = act
+        slope_ref[part, :] = slope.astype(BF)
+        acc[part, :] += nn(act, down_ref[...])
+
+    @pl.when(step == pl.num_programs(0) - 1)
+    def _():
+        for utt in range(mod_ref.shape[0]):
+            mod = mod_ref[utt]
+            total = jnp.zeros((1, acc.shape[1]), F32)
+            for _, part in row_blocks(span):
+                here = slice(utt * span + part.start, utt * span + part.stop)
+                branch = acc[here, :]
+                mid = res_ref[here, :] + mod[2:3] * branch_ref[here, :]
+                out_ref[here, :] = (mid + mod[5:6] * branch).astype(BF)
+                upstream = cot_ref[here, :].astype(F32) * weight_ref[here, :]
+                gb_ref[here, :] = (upstream * mod[5:6]).astype(BF)
+                total += jnp.sum(upstream * branch, axis=0, keepdims=True)
+            gate_ref[utt : utt + 1, :] = total
+
+
+def ffn_backward_kernel(
+    att_ref, outw_ref, res_ref, branch_ref, mod_ref, cot_ref, weight_ref, gb_ref,
+    act_ref, slope_ref, up_ref, down_ref,
+    gup_ref, gdown_ref, gmid_ref, gatt_ref, gout_ref, sums_ref, normed, acc, gba,
+):
+    step = pl.program_id(0)
+    rows = att_ref.shape[0]
+    utts = mod_ref.shape[0]
+    span = rows // utts
+
+    def hat_of(here, mod):
+        return layer_norm(res_ref[here, :] + mod[2:3] * branch_ref[here, :])
+
+    @pl.when(step == 0)
+    def _():
+        for utt in range(utts):
+            mod = mod_ref[utt]
+            for _, part in row_blocks(span):
+                here = slice(utt * span + part.start, utt * span + part.stop)
+                hat, _ = hat_of(here, mod)
+                normed[here, :] = (hat * (1.0 + mod[4:5]) + mod[3:4]).astype(BF)
+        acc[...] = jnp.zeros_like(acc)
+
+    pieces = []
+    for _, part in row_blocks(rows):
+        grad = nt(gb_ref[part, :], down_ref[...]) * slope_ref[part, :].astype(F32)
+        grad = grad.astype(BF)
+        acc[part, :] += nt(grad, up_ref[...])
+        pieces.append(grad)
+    gdown_ref[...] = tn(act_ref[...], gb_ref[...]).astype(BF)
+    gup_ref[...] = tn(normed[...], jnp.concatenate(pieces, axis=0)).astype(BF)
+
+    @pl.when(step == pl.num_programs(0) - 1)
+    def _():
+        for utt in range(utts):
+            mod = mod_ref[utt]
+            width = acc.shape[1]
+            shift = jnp.zeros((1, width), F32)
+            scale = jnp.zeros((1, width), F32)
+            gate = jnp.zeros((1, width), F32)
+            for _, part in row_blocks(span):
+                here = slice(utt * span + part.start, utt * span + part.stop)
+                hat, inverse = hat_of(here, mod)
+                grad = acc[here, :]
+                shift += jnp.sum(grad, axis=0, keepdims=True)
+                scale += jnp.sum(grad * hat, axis=0, keepdims=True)
+                upstream = cot_ref[here, :].astype(F32) * weight_ref[here, :]
+                mid = upstream + norm_back(grad * (1.0 + mod[4:5]), hat, inverse)
+                gmid_ref[here, :] = mid
+                gate += jnp.sum(mid * branch_ref[here, :], axis=0, keepdims=True)
+                low = (mid * mod[2:3]).astype(BF)
+                gba[here, :] = low
+                gatt_ref[here, :] = nt(low, outw_ref[...]).astype(BF)
+            sums_ref[utt, 0:1, :] = shift
+            sums_ref[utt, 1:2, :] = scale
+            sums_ref[utt, 2:3, :] = gate
+        gout_ref[...] = tn(att_ref[...], gba[...]).astype(BF)
+
+
+def whole_spec(shape):
+    zeros = (0,) * len(shape)
+    return pl.BlockSpec(shape, lambda i: zeros, pipeline_mode=pl.Buffered(1))
+
+
+def ffn_forward(att, outw, res, mods, cot, weight, up, down, chunk=512):
+    rows, width = res.shape
+    hidden = up.shape[1]
+    whole = [whole_spec(a.shape) for a in (att, outw, res, mods, cot, weight)]
+    col = pl.BlockSpec((rows, chunk), lambda i: (0, i))
+    utts = mods.shape[0]
+    return pl.pallas_call(
+        ffn_forward_kernel,
+        grid=(hidden // chunk,),
+        in_specs=whole
+        + [
+            pl.BlockSpec((width, chunk), lambda i: (0, i)),
+            pl.BlockSpec((chunk, width), lambda i: (i, 0)),
+        ],
+        out_specs=[
+            whole_spec((rows, width)),
+            col,
+            col,
+            whole_spec((rows, width)),
+            whole_spec((rows, width)),
+            whole_spec((utts, width)),
+        ],
+        out_shape=[
+            jax.ShapeDtypeStruct((rows, width), F32),
+            jax.ShapeDtypeStruct((rows, hidden), BF),
+            jax.ShapeDtypeStruct((rows, hidden), BF),
+            jax.ShapeDtypeStruct((rows, width), BF),
+            jax.ShapeDtypeStruct((rows, width), BF),
+            jax.ShapeDtypeStruct((utts, width), F32),
+        ],
+        scratch_shapes=[pltpu.VMEM((rows, width), BF), pltpu.VMEM((rows, width), F32)],
+        compiler_params=pltpu.CompilerParams(vmem_limit_bytes=VMEM_LIMIT),
+        cost_estimate=pl.CostEstimate(
+            flops=2 * rows * width * (width + 2 * hidden),
+            bytes_accessed=60 * 2**20,
+            transcendentals=rows * hidden,
+        ),
+        name="ffn_forward",
+    )(att, outw, res, mods, cot, weight, up, down)
+
+
+def ffn_backward(att, outw, res, branch, mods, cot, weight, gb, act, slope, up, down, chunk=512):
+    rows, width = res.shape
+    hidden = up.shape[1]
+    utts = mods.shape[0]
+    whole = [whole_spec(a.shape) for a in (att, outw, res, branch, mods, cot, weight, gb)]
+    col = pl.BlockSpec((rows, chunk), lambda i: (0, i))
+    upspec = pl.BlockSpec((width, chunk), lambda i: (0, i))
+    downspec = pl.BlockSpec((chunk, width), lambda i: (i, 0))
+    return pl.pallas_call(
+        ffn_backward_kernel,
+        grid=(hidden // chunk,),
+        in_specs=whole + [col, col, upspec, downspec],
+        out_specs=[
+            upspec,
+            downspec,
+            whole_spec((rows, width)),
+            whole_spec((rows, width)),
+            whole_spec((width, width)),
+            whole_spec((utts, 8, width)),
+        ],
+        out_shape=[
+            jax.ShapeDtypeStruct((width, hidden), BF),
+            jax.ShapeDtypeStruct((hidden, width), BF),
+            jax.ShapeDtypeStruct((rows, width), F32),
+            jax.ShapeDtypeStruct((rows, width), BF),
+            jax.ShapeDtypeStruct((width, width), BF),
+            jax.ShapeDtypeStruct((utts, 8, width), F32),
+        ],
+        scratch_shapes=[
+            pltpu.VMEM((rows, width), BF),
+            pltpu.VMEM((rows, width), F32),
+            pltpu.VMEM((rows, width), BF),
+        ],
+        compiler_params=pltpu.CompilerParams(vmem_limit_bytes=VMEM_LIMIT),
+        cost_estimate=pl.CostEstimate(
+            flops=2 * rows * width * (2 * width + 4 * hidden),
+            bytes_accessed=90 * 2**20,
+            transcendentals=0,
+        ),
+        name="ffn_backward",
+    )(att, outw, res, branch, mods, cot, weight, gb, act, slope, up, down)
+
+
 def project_kernel(x_ref, w_ref, cos_ref, sin_ref, out_ref):
     projected = nn(x_ref[...], w_ref[...])
     groups = out_ref.shape[0]
@@ -335,19 +560,6 @@
     )(x, weight, cos, sin)
 
 
-def layer_norm(stream):
-    centre = stream - jnp.mean(stream, axis=-1, keepdims=True)
-    spread = jnp.mean(centre * centre, axis=-1, keepdims=True)
-    inverse = lax.rsqrt(spread + EPS)
-    return (centre * inverse, inverse)
-
-
-def norm_back(grad_normed, normed, inverse):
-    first_mean = jnp.mean(grad_normed, axis=-1, keepdims=True)
-    second_mean = jnp.mean(grad_normed * normed, axis=-1, keepdims=True)
-    return inverse * (grad_normed - first_mean - normed * second_mean)
-
-
 def rotary_tables(positions):
     half_dim = HEAD_DIM // 2
     channel = jnp.arange(half_dim, dtype=jnp.float32)
@@ -393,33 +605,74 @@
     return (probs.astype(jnp.bfloat16), dscore)
 
 
-def exchange(pieces, axis="seq"):
-    count = pieces.shape[0]
-    me = lax.axis_index(axis)
-    out = pieces
-    for step in [count // 2] + [s for s in range(1, count) if s != count // 2]:
-        piece = lax.dynamic_index_in_dim(pieces, lax.rem(me + step, count), 0, keepdims=False)
-        got = lax.ppermute(piece, axis, [(i, (i + step) % count) for i in range(count)])
-        out = lax.dynamic_update_index_in_dim(out, got, lax.rem(me + count - step, count), 0)
-    return out
+def exchange(pieces):
+    count, rows, width = pieces.shape
+    me = lax.axis_index("seq")
+    outer, inner = me // 2, me % 2
+    nest = pieces.reshape(count // 2, 2, rows, width)
+    far = lax.dynamic_index_in_dim(nest, 1 - inner, 1, keepdims=False)
+    got = lax.ppermute(far, "seq", [(i, i ^ 1) for i in range(count)])
+    nest = lax.dynamic_update_index_in_dim(nest, got, 1 - inner, 1)
+    out = nest
+    for flip in (3, 2, 1):
+        there = jnp.bitwise_xor(outer, flip)
+        piece = lax.dynamic_index_in_dim(nest, there, 0, keepdims=False)
+        got = lax.ppermute(piece, "seq", [(i, i ^ (2 * flip)) for i in range(count)])
+        out = lax.dynamic_update_index_in_dim(out, got, there, 0)
+    return out.reshape(count, rows, width)
+
+
+def batch_swap(value, flip):
+    return lax.ppermute(value, "batch", [(i, i ^ flip) for i in range(4)])
+
+
+def batch_bits():
+    here = lax.axis_index("batch")
+    return here // 2, here % 2
+
+
+def in_quarters(rows):
+    return lax.axis_size("batch") == 4 and rows % 4 == 0
+
+
+def join_pair(bit, mine, other, axis):
+    first = jnp.where(bit == 0, mine, other)
+    second = jnp.where(bit == 0, other, mine)
+    return jnp.stack([first, second], axis=axis)
 
 
 def gather_weight(weight):
-    parts = lax.axis_size("batch")
-    if weight.shape[0] % parts:
+    rows, width = weight.shape
+    if not in_quarters(rows):
         return lax.all_gather(weight, "seq", axis=0, tiled=True)
-    rows = weight.shape[0] // parts
-    mine = lax.dynamic_slice_in_dim(weight, lax.axis_index("batch") * rows, rows, 0)
-    return lax.all_gather(mine, ("seq", "batch"), axis=0, tiled=True)
+    span = rows // 4
+    high, low = batch_bits()
+    mine = lax.dynamic_slice_in_dim(weight, lax.axis_index("batch") * span, span, 0)
+    held = lax.all_gather(mine, "seq", axis=0, tiled=False)
+    held = join_pair(high, held, batch_swap(held, 2), 1)
+    held = join_pair(low, held, batch_swap(held, 1), 2)
+    return held.reshape(-1, width)
+
+
+def pair_sum(value, bit, flip, axis):
+    send = lax.dynamic_index_in_dim(value, 1 - bit, axis, keepdims=False)
+    keep = lax.dynamic_index_in_dim(value, bit, axis, keepdims=False)
+    got = batch_swap(send, flip)
+    return (keep.astype(jnp.float32) + got.astype(jnp.float32)).astype(jnp.bfloat16)
 
 
 def sum_weight(grad):
-    parts = lax.axis_size("batch") * lax.axis_size("seq")
-    low = grad.astype(jnp.bfloat16)
-    if grad.shape[0] % parts:
-        shard = lax.psum_scatter(low, "seq", scatter_dimension=0, tiled=True)
+    rows, width = grad.shape
+    low_grad = grad.astype(jnp.bfloat16)
+    seq_count = lax.axis_size("seq")
+    if not in_quarters(rows // seq_count):
+        shard = lax.psum_scatter(low_grad, "seq", scatter_dimension=0, tiled=True)
         return lax.psum(shard, "batch").astype(jnp.float32)
-    shard = lax.psum_scatter(low, ("seq", "batch"), scatter_dimension=0, tiled=True)
+    high, low = batch_bits()
+    held = low_grad.reshape(seq_count, 2, 2, rows // (4 * seq_count), width)
+    held = pair_sum(held, low, 1, 2)
+    held = pair_sum(held, high, 2, 1)
+    shard = lax.psum_scatter(held, "seq", scatter_dimension=0, tiled=False)
     return lax.all_gather(shard, "batch", axis=0, tiled=True).astype(jnp.float32)
 
 
@@ -490,10 +743,6 @@
     )
     shift_attn = modulation[:, 0][:, None, :]
     scale_attn = modulation[:, 1][:, None, :]
-    gate_attn = modulation[:, 2][:, None, :]
-    shift_ffn = modulation[:, 3][:, None, :]
-    scale_ffn = modulation[:, 4][:, None, :]
-    gate_ffn = modulation[:, 5][:, None, :]
     hat_attn, inv_attn = layer_norm(residual_in)
     normed_attn = (
         (hat_attn * (1.0 + scale_attn) + shift_attn)
@@ -555,42 +804,37 @@
         attended_full = accum / jnp.transpose(denom, (0, 2, 1))[..., None]
         lse_rows = jnp.transpose(top_score + jnp.log(denom), (0, 2, 1))
         attended_low = attended_full.astype(jnp.bfloat16).reshape(row_count, model_width)
-    branch_attn = jnp.dot(attended_low, out_full, preferred_element_type=jnp.float32).reshape(
-        utt_count, frame_span, model_width
-    )
-    residual_mid = residual_in + gate_attn * branch_attn
-    hat_ffn, inv_ffn = layer_norm(residual_mid)
-    normed_ffn = (
-        (hat_ffn * (1.0 + scale_ffn) + shift_ffn)
-        .astype(jnp.bfloat16)
-        .reshape(row_count, model_width)
-    )
-    hidden_pre = jnp.dot(normed_ffn, up_full, preferred_element_type=jnp.float32)
-    hidden_act = smooth_gelu(hidden_pre).astype(jnp.bfloat16)
-    branch_ffn = jnp.dot(hidden_act, down_full, preferred_element_type=jnp.float32).reshape(
-        utt_count, frame_span, model_width
-    )
-    layer_output = (residual_mid + gate_ffn * branch_ffn).astype(jnp.bfloat16)
-    qkv_back, out_back, up_back, down_back = qkv_full, out_full, up_full, down_full
-    skip_back = skip_full
-    upstream = cotangent.astype(jnp.float32) * loss_weight[..., None]
-    grad_branch_ffn = (upstream * gate_ffn).astype(jnp.bfloat16).reshape(row_count, model_width)
-    grad_gate_ffn = jnp.sum(upstream * branch_ffn, axis=1)
-    grad_down = cross(hidden_act, grad_branch_ffn)
-    grad_hidden_act = back_product(grad_branch_ffn, down_back)
-    gelu_value, gelu_pull = jax.vjp(smooth_gelu, hidden_pre)
-    grad_hidden_pre = gelu_pull(grad_hidden_act)[0].astype(jnp.bfloat16)
-    grad_up = cross(normed_ffn, grad_hidden_pre)
-    grad_normed_ffn = back_product(grad_hidden_pre, up_back).reshape(
-        utt_count, frame_span, model_width
-    )
-    grad_shift_ffn = jnp.sum(grad_normed_ffn, axis=1)
-    grad_scale_ffn = jnp.sum(grad_normed_ffn * hat_ffn, axis=1)
-    grad_mid = upstream + norm_back(grad_normed_ffn * (1.0 + scale_ffn), hat_ffn, inv_ffn)
-    grad_branch_attn = (grad_mid * gate_attn).astype(jnp.bfloat16).reshape(row_count, model_width)
-    grad_gate_attn = jnp.sum(grad_mid * branch_attn, axis=1)
-    grad_out = cross(attended_low, grad_branch_attn)
-    grad_attended_flat = back_product(grad_branch_attn, out_back).astype(jnp.bfloat16)
+    residual_rows = residual_in.reshape(row_count, model_width)
+    cot_rows = cotangent.reshape(row_count, model_width)
+    weight_rows = loss_weight.reshape(row_count, 1)
+    branch_attn, hidden_act, hidden_slope, grad_branch_ffn, layer_output, grad_gate_ffn = ffn_forward(
+        attended_low,
+        out_full,
+        residual_rows,
+        modulation,
+        cot_rows,
+        weight_rows,
+        up_full,
+        down_full,
+    )
+    layer_output = layer_output.reshape(utt_count, frame_span, model_width)
+    grad_up, grad_down, grad_mid, grad_attended_flat, grad_out, ffn_sums = ffn_backward(
+        attended_low,
+        out_full,
+        residual_rows,
+        branch_attn,
+        modulation,
+        cot_rows,
+        weight_rows,
+        grad_branch_ffn,
+        hidden_act,
+        hidden_slope,
+        up_full,
+        down_full,
+    )
+    grad_mid = grad_mid.reshape(utt_count, frame_span, model_width)
+    grad_shift_ffn, grad_scale_ffn, grad_gate_attn = ffn_sums[:, 0], ffn_sums[:, 1], ffn_sums[:, 2]
+    qkv_back, skip_back = qkv_full, skip_full
     if by_heads:
         grad_parts = []
         for utt in range(utt_count):

time: 1310 us -> 1460 us (1.11)
  Pallas kernels: 238 us -> 384 us
  matrix products: 168 us -> 45.7 us
  other arithmetic: 44.1 us -> 116 us
  local copies, waits for them, and re-layouts: 143 us -> 178 us
  starting transfers between devices: 170 us -> 190 us
  blocking collectives: 200 us -> 181 us
  waiting for transfers between devices: 327 us -> 345 us
    pallas_call x0 -> x2, Pallas kernels: none -> 104 us  [the longest x1 61 us: ffn_backward(): pl.pallas_call(ffn_backward_kernel, grid=(hidden // chunk,), in_specs=who...]
    ppermute x56 -> x52, waiting for transfers between devices: 82.5 us -> 161 us  [the longest x24 93.9 us: exchange(): got = lax.ppermute(piece, 'seq', [(i, i ^ 2 * flip) for i in range(count)])]
    reduce_scatter x5, waiting for transfers between devices: 159 us -> 85.4 us  [sum_weight(): shard = lax.psum_scatter(held, 'seq', scatter_dimension=0, tiled=False)]
    another operation x0 -> x20, other arithmetic: none -> 54.5 us  [join_pair(): return jnp.stack([first, second], axis=axis)]
    all_gather x1, blocking collectives: 84.6 us -> 35.3 us  [on_device(): lax.all_gather(silu_time.astype(jnp.float32).astype(jnp.bfloat16), 'batch...]
    dot_general x3 -> x0, matrix products: 48.3 us -> none  [the longest x1 27.6 us: on_device(): jnp.dot(normed_ffn, up_full, preferred_element_type=jnp.float32)]
    dot_general x5 -> x2, matrix products: 53.6 us -> 16.8 us  [cross(): lax.dot_general(left, right, (((0,), (0,)), ((), ())), preferred_element_...]
    all_gather x0 -> x1, blocking collectives: none -> 36.1 us  [gather_weight(): held = lax.all_gather(mine, 'seq', axis=0, tiled=False)]
  transfers between devices with their start and end apart: 68 -> 63, of which waited for: 20 -> 20; matrix products, arithmetic and copies ran while one was open for 23% -> 22% of each run, Pallas kernels for 18% -> 19%
where the time goes in v2:
time: 1460 us
  Pallas kernels  384 us (26%)
  waiting for transfers between devices  345 us (24%)
  starting transfers between devices  190 us (13%)
  blocking collectives  181 us (12%)
  local copies, waits for them, and re-layouts  178 us (12%)
  other arithmetic  116 us (8%)
  matrix products  45.7 us (3%)
  between operations  16.8 us (1%)
    pallas_call x2, Pallas kernels, flash_backward(): pl.pallas_call(functools.partial(flash_backward_kernel, bq=bq, bk=bk), gr...  185 us
    ppermute x24, starting transfers between devices, exchange(): got = lax.ppermute(piece, 'seq', [(i, i ^ 2 * flip) for i in range(count)])  168 us
    ppermute x24, waiting for transfers between devices, exchange(): got = lax.ppermute(piece, 'seq', [(i, i ^ 2 * flip) for i in range(count)])  93.9 us
    reduce_scatter x5, waiting for transfers between devices, sum_weight(): shard = lax.psum_scatter(held, 'seq', scatter_dimension=0, tiled=False)  85.4 us
    pallas_call x2, Pallas kernels, flash_forward(): pl.pallas_call(functools.partial(flash_forward_kernel, bq=bq, bk=bk), gri...  79.5 us
    all_gather x4, waiting for transfers between devices, gather_weight(): held = lax.all_gather(mine, 'seq', axis=0, tiled=False)  73.6 us
    pallas_call x1, Pallas kernels, ffn_backward(): pl.pallas_call(ffn_backward_kernel, grid=(hidden // chunk,), in_specs=who...  61 us
    another operation x20, other arithmetic, join_pair(): return jnp.stack([first, second], axis=axis)  54.5 us
  transfers between devices with their start and end apart: 63, of which 20 were waited for; matrix products, arithmetic and copies ran while one was open for 22% of the time, Pallas kernels for 19%

profile of v2, /device:TPU:0, one launch (start us, length us, event | category | flops | bytes accessed | tf_op | source)
XLA Modules:
  0.0 1456.9 jit_solution(15024368794771359473)
XLA Ops:
  13.3 36.1 %all-gather.2 = bf16[256,1024]{1,0:T(8,128)(2,1)} all-gather(bf16[32,1024]{1,0:T(8,128)(2,1)S(1)} %constant_dynamic-slice_fusion.15), channel_id=4, replica_groups=mesh['seq'=8,'batch'=4] {'seq'}, dimensions={0}, use_global_device_ids=true | all-gather | bytes 589824 | tf_op jit(solution)/shard_map/all_gather | solution.py:651
  70.7 30.5 %all-gather.21.cloned.1.call-done = bf16[256,3072]{1,0:T(8,128)(2,1)} async-done(((bf16[32,3072]{1,0:T(8,128)(2,1)}), bf16[256,3072]{1,0:T(8,128)(2,1)}) %all-gather.21.cloned.1.call-update) | async-done | bytes 1572880 | tf_op jit(solution)/shard_map/all_gather | solution.py:651
  121.7 36.5 %psum.28.mod_ref = f32[2,6,1024]{2,1,0:T(8,128)S(1)} all-reduce(f32[2,6,1024]{2,1,0:T(8,128)S(1)} %reshape.299), channel_id=1, replica_groups=mesh['seq'=8,'batch'=4] {'seq'}, use_global_device_ids=true, to_apply=%region_2.0 | all-reduce | flops 12288 | bytes 98304 | tf_op jit(solution)/shard_map/psum | solution.py:734
  160.7 43.0 %all-gather.25.cloned.1.call-done = bf16[1024,1024]{1,0:T(8,128)(2,1)} async-done(((bf16[128,1024]{1,0:T(8,128)(2,1)}), bf16[1024,1024]{1,0:T(8,128)(2,1)}) %all-gather.25.cloned.1.call-update) | async-done | bytes 2097168 | tf_op jit(solution)/shard_map/all_gather | solution.py:651
  233.8 16.5 %collective-permute-done.24 = bf16[8,128,1024]{2,1,0:T(8,128)(2,1)} collective-permute-done((bf16[8,128,1024]{2,1,0:T(8,128)(2,1)}, bf16[8,128,1024]{2,1,0:T(8,128)(2,1)}, u32[]{:S(2)}, u32[]{:S(2)}) %collective-permute-start.24) | collective-permute-done | bytes 2097184 | tf_op jit(solution)/shard_map/ppermute | solution.py:626
  315.6 22.8 %collective-permute-done.4 = bf16[4,512,384]{2,1,0:T(8,128)(2,1)} collective-permute-done((bf16[4,512,384]{2,1,0:T(8,128)(2,1)}, bf16[4,512,384]{2,1,0:T(8,128)(2,1)}, u32[]{:S(2)}, u32[]{:S(2)}) %collective-permute-start.4) | collective-permute-done | bytes 1572896 | tf_op jit(solution)/shard_map/ppermute | solution.py:614
  352.5 20.8 %collective-permute-start.14 = (bf16[2,512,384]{2,1,0:T(8,128)(2,1)S(1)}, bf16[2,512,384]{2,1,0:T(8,128)(2,1)S(1)}, u32[]{:S(2)}, u32[]{:S(2)}) collective-permute-start(bf16[2,512,384]{2,1,0:T(8,128)(2,1)S(1)} %get-tuple-element.79), channel_id=1, source_target_pairs={{0,16},{4,20},{8,24},{12,28},{16,0},{20,4},{24,8},{28,12},{1,17},{... | collective-permute-start | bytes 2359304 | tf_op jit(solution)/shard_map/ppermute | solution.py:620
  376.1 24.1 %collective-permute-start.6 = (bf16[2,512,384]{2,1,0:T(8,128)(2,1)S(1)}, bf16[2,512,384]{2,1,0:T(8,128)(2,1)S(1)}, u32[]{:S(2)}, u32[]{:S(2)}) collective-permute-start(bf16[2,512,384]{2,1,0:T(8,128)(2,1)S(1)} %get-tuple-element.82), channel_id=1, source_target_pairs={{0,16},{4,20},{8,24},{12,28},{16,0},{20,4},{24,8},{28,12},{1,17},{... | collective-permute-start | bytes 2359304 | tf_op jit(solution)/shard_map/ppermute | solution.py:620
  410.9 19.3 %collective-permute-done.14 = bf16[2,512,384]{2,1,0:T(8,128)(2,1)S(1)} collective-permute-done((bf16[2,512,384]{2,1,0:T(8,128)(2,1)S(1)}, bf16[2,512,384]{2,1,0:T(8,128)(2,1)S(1)}, u32[]{:S(2)}, u32[]{:S(2)}) %collective-permute-start.14) | collective-permute-done | bytes 786464 | tf_op jit(solution)/shard_map/ppermute | solution.py:620
  432.1 39.6 %attend_forward.3 = (bf16[4096,128]{1,0:T(8,128)(2,1)}, f32[8,4096]{1,0:T(8,128)}) custom-call(s32[1]{0:T(128)} %get-tuple-element.116.len_ref, bf16[4096,384]{1,0:T(8,128)(2,1)} %bitcast.52.q_ref.k_ref.v_ref, bf16[4096,384]{1,0:T(8,128)(2,1)} %bitcast.52.q_ref.k_ref.v_ref, bf16[4096,384]{1,0:T(8,128)(2,1)} %bitcast.52.q_ref.k_ref.v_ref), custom_call_target="tpu_custom_call" | custom-call | flops 17179869184 | bytes 8388608 | tf_op jit(solution)/shard_map/attend_forward/pallas_call | solution.py:138
  476.0 39.9 %attend_forward.2 = (bf16[4096,128]{1,0:T(8,128)(2,1)}, f32[8,4096]{1,0:T(8,128)}) custom-call(s32[1]{0:T(128)} %get-tuple-element.117.len_ref, bf16[4096,384]{1,0:T(8,128)(2,1)} %bitcast.412, bf16[4096,384]{1,0:T(8,128)(2,1)} %bitcast.413, bf16[4096,384]{1,0:T(8,128)(2,1)} %bitcast.414), custom_call_target="tpu_custom_call" | custom-call | flops 17179869184 | bytes 8388608 | tf_op jit(solution)/shard_map/attend_forward/pallas_call | solution.py:138
  574.5 43.0 %ffn_forward.1 = (f32[1024,1024]{1,0:T(8,128)}, bf16[1024,4096]{1,0:T(8,128)(2,1)}, bf16[1024,4096]{1,0:T(8,128)(2,1)}, bf16[1024,1024]{1,0:T(8,128)(2,1)}, bf16...) custom-call(bf16[1024,1024]{1,0:T(8,128)(2,1)} %copy-done.44, bf16[1024,1024]{1,0:T(8,128)(2,1)} %bitcast.432, ...), custom_call_target="tpu_custom_call" | custom-call | flops 19327352832 | bytes 62914560 | tf_op jit(solution)/shard_map/ffn_forward/pallas_call | solution.py:444
  617.5 61.0 %ffn_backward.1 = (bf16[1024,4096]{1,0:T(8,128)(2,1)}, bf16[4096,1024]{1,0:T(8,128)(2,1)}, f32[1024,1024]{1,0:T(8,128)}, bf16[1024,1024]{1,0:T(8,128)(2,1)}, bf1...) custom-call(bf16[1024,1024]{1,0:T(8,128)(2,1)} %copy-done.44, bf16[1024,1024]{1,0:T(8,128)(2,1)} %bitcast.433, ...), custom_call_target="tpu_custom_call" | custom-call | flops 38654705664 | bytes 94371840 | tf_op jit(solution)/shard_map/ffn_backward/pallas_call | solution.py:487
  739.5 92.3 %attend_backward.2 = bf16[4096,384]{1,0:T(8,128)(2,1)} custom-call(s32[1]{0:T(128)} %get-tuple-element.117.len_ref, bf16[4096,384]{1,0:T(8,128)(2,1)} %bitcast.415, bf16[4096,384]{1,0:T(8,128)(2,1)} %bitcast.416, bf16[4096,384]{1,0:T(8,128)(2,1)} %bitcast.417, bf16[4096,128]{1,0:T(8,128)(2,1)} %get-tuple-element.26.o_ref, bf16[4096,128]{1,0:T(8,128)(2,1)} %bitcast.406, ...), custom_call_target="tpu_custom_call" | custom-call | flops 42949672960 | bytes 8388608 | tf_op jit(solution)/shard_map/attend_backward/pallas_call | solution.py:271
  837.7 92.5 %attend_backward.3 = bf16[4096,384]{1,0:T(8,128)(2,1)} custom-call(s32[1]{0:T(128)} %get-tuple-element.116.len_ref, bf16[4096,384]{1,0:T(8,128)(2,1)} %bitcast.52.q_ref.k_ref.v_ref, bf16[4096,384]{1,0:T(8,128)(2,1)} %bitcast.52.q_ref.k_ref.v_ref, bf16[4096,384]{1,0:T(8,128)(2,1)} %bitcast.52.q_ref.k_ref.v_ref, bf16[4096,128]{1,0:T(8,128)(2,1)} %get-tuple-element.27.o_ref, ...), custom_call_target="tpu_custom_call" | custom-call | flops 42949672960 | bytes 8388608 | tf_op jit(solution)/shard_map/attend_backward/pallas_call | solution.py:271
  971.3 37.7 %collective-permute-start.32 = (bf16[2,512,384]{1,2,0:T(8,128)(2,1)}, bf16[2,512,384]{1,2,0:T(8,128)(2,1)S(1)}, u32[]{:S(2)}, u32[]{:S(2)}) collective-permute-start(bf16[2,512,384]{1,2,0:T(8,128)(2,1)} %get-tuple-element.73), channel_id=1, source_target_pairs={{0,16},{4,20},{8,24},{12,28},{16,0},{20,4},{24,8},{28,12},{1,17},{... | collective-permute-start | bytes 2359304 | tf_op jit(solution)/shard_map/ppermute | solution.py:620
  1023.5 34.4 %collective-permute-start.40 = (bf16[2,512,384]{1,2,0:T(8,128)(2,1)S(1)}, bf16[2,512,384]{1,2,0:T(8,128)(2,1)S(1)}, u32[]{:S(2)}, u32[]{:S(2)}) collective-permute-start(bf16[2,512,384]{1,2,0:T(8,128)(2,1)S(1)} %get-tuple-element.76), channel_id=1, source_target_pairs={{0,16},{4,20},{8,24},{12,28},{16,0},{20,4},{24,8},{28,12},{1,17},{... | collective-permute-start | bytes 2359304 | tf_op jit(solution)/shard_map/ppermute | solution.py:620
  1062.4 20.2 %collective-permute-done.32 = bf16[2,512,384]{1,2,0:T(8,128)(2,1)S(1)} collective-permute-done((bf16[2,512,384]{1,2,0:T(8,128)(2,1)}, bf16[2,512,384]{1,2,0:T(8,128)(2,1)S(1)}, u32[]{:S(2)}, u32[]{:S(2)}) %collective-permute-start.32) | collective-permute-done | bytes 786464 | tf_op jit(solution)/shard_map/ppermute | solution.py:620
  1098.8 19.1 %collective-permute-done.41 = bf16[2,512,384]{1,2,0:T(8,128)(2,1)S(1)} collective-permute-done((bf16[2,512,384]{1,2,0:T(8,128)(2,1)S(1)}, bf16[2,512,384]{1,2,0:T(8,128)(2,1)S(1)}, u32[]{:S(2)}, u32[]{:S(2)}) %collective-permute-start.41) | collective-permute-done | bytes 786464 | tf_op jit(solution)/shard_map/ppermute | solution.py:620
  1186.7 19.5 %collective-permute-done.43 = bf16[8,64,1024]{2,1,0:T(8,128)(2,1)S(1)} collective-permute-done((bf16[8,64,1024]{2,1,0:T(8,128)(2,1)S(1)}, bf16[8,64,1024]{2,1,0:T(8,128)(2,1)S(1)}, u32[]{:S(2)}, u32[]{:S(2)}) %collective-permute-start.43) | collective-permute-done | bytes 1048608 | tf_op jit(solution)/shard_map/ppermute | solution.py:626
  1216.2 35.3 %all-gather.10 = bf16[4,2,1024]{2,1,0:T(2,128)(2,1)S(1)} all-gather(bf16[1,2,1024]{2,1,0:T(2,128)(2,1)S(1)} %fusion.35), channel_id=1, replica_groups=mesh['seq'=8,'batch'=4] {'batch'}, dimensions={0}, use_global_device_ids=true | all-gather | bytes 20480 | tf_op jit(solution)/shard_map/all_gather | solution.py:930
  1253.2 15.7 %reduce-scatter.10.cloned.1.call-done = bf16[1,32,1024]{2,1,0:T(8,128)(2,1)} async-done(((bf16[8,32,1024]{2,1,0:T(8,128)(2,1)}), bf16[1,32,1024]{2,1,0:T(8,128)(2,1)}) %reduce-scatter.10.cloned.1.call-update) | async-done | bytes 65552 | tf_op jit(solution)/shard_map/reduce_scatter | solution.py:675
  1275.8 35.7 %psum.31 = bf16[2,6144]{1,0:T(2,128)(2,1)S(1)} all-reduce(f32[2,6144]{1,0:T(2,128)S(1)} %bitcast.450), channel_id=1, replica_groups=mesh['seq'=8,'batch'=4] {'seq'}, use_global_device_ids=true, to_apply=%region_12.13 | all-reduce | flops 12288 | bytes 73728 | tf_op jit(solution)/shard_map/psum | solution.py:925
  1373.9 66.2 %reduce-scatter.8.cloned.1.call-done = bf16[1,32,3072]{2,1,0:T(8,128)(2,1)} async-done(((bf16[8,32,3072]{2,1,0:T(8,128)(2,1)}), bf16[1,32,3072]{2,1,0:T(8,128)(2,1)}) %reduce-scatter.8.cloned.1.call-update) | async-done | bytes 196624 | tf_op jit(solution)/shard_map/reduce_scatter | solution.py:675
  (444 shorter events, 538.4 us)
Async XLA Ops:
  10.7 149.6 %all-gather.23.cloned.1.call-start = ((), (), s32[]{:S(2)}) async-start(), calls=%async_computation.12 | async-start | bytes 2359296 | tf_op jit(solution)/shard_map/all_gather | solution.py:651
  12.4 191.3 %all-gather.25.cloned.1.call-start = ((), (), s32[]{:S(2)}) async-start(), calls=%async_computation.13 | async-start | bytes 2359296 | tf_op jit(solution)/shard_map/all_gather | solution.py:651
  49.4 247.5 %collective-permute-start.20 = (bf16[8,32,1024]{2,1,0:T(8,128)(2,1)}, bf16[8,32,1024]{2,1,0:T(8,128)(2,1)}, u32[]{:S(2)}, u32[]{:S(2)}) collective-permute-start(bf16[8,32,1024]{2,1,0:T(8,128)(2,1)} %bitcast.64), channel_id=1, source_target_pairs={{0,2},{1,3},{2,0},{3,1},{4,6},{5,7},{6,4},{7,5},{8,10},{9,11},{10,... | collective-permute-start | bytes 1572872 | tf_op jit(solution)/shard_map/ppermute | solution.py:626
  52.5 1155.2 %reduce-scatter.14.cloned.1.call-start = ((), (), s32[]{:S(2)}) async-start(), calls=%async_computation.9 | async-start | bytes 2359296 | tf_op jit(solution)/shard_map/reduce_scatter | solution.py:675
  101.2 104.0 %collective-permute-start.2 = (bf16[8,32,3072]{2,1,0:T(8,128)(2,1)}, bf16[8,32,3072]{2,1,0:T(8,128)(2,1)}, u32[]{:S(2)}, u32[]{:S(2)}) collective-permute-start(bf16[8,32,3072]{2,1,0:T(8,128)(2,1)} %bitcast.443), channel_id=1, source_target_pairs={{0,2},{1,3},{2,0},{3,1},{4,6},{5,7},{6,4},{7,5},{8,10},{9,11},{10,... | collective-permute-start | bytes 4718600 | tf_op jit(solution)/shard_map/ppermute | solution.py:626
  233.3 166.8 %collective-permute-start.23 = (bf16[8,2,32,4096]{3,2,1,0:T(8,128)(2,1)}, bf16[8,2,32,4096]{3,2,1,0:T(8,128)(2,1)}, u32[]{:S(2)}, u32[]{:S(2)}) collective-permute-start(bf16[8,2,32,4096]{3,2,1,0:T(8,128)(2,1)} %pad_maximum_fusion.6), channel_id=1, source_target_pairs={{0,1},{1,0},{2,3},{3,2},{4,5},{5,4},{6,7},{7,6},{8,9},{9,8},{10,11... | collective-permute-start | bytes 12582920 | tf_op jit(solution)/shard_map/ppermute | solution.py:626
  285.5 120.1 %collective-permute-start.25 = (bf16[8,2,128,1024]{3,2,1,0:T(8,128)(2,1)}, bf16[8,2,128,1024]{3,2,1,0:T(8,128)(2,1)}, u32[]{:S(2)}, u32[]{:S(2)}) collective-permute-start(bf16[8,2,128,1024]{3,2,1,0:T(8,128)(2,1)} %pad_maximum_fusion.7), channel_id=1, source_target_pairs={{0,1},{1,0},{2,3},{3,2},{4,5},{5,4},{6,7},{7,6},{8,9},{9,8},{10,11... | collective-permute-start | bytes 12582920 | tf_op jit(solution)/shard_map/ppermute | solution.py:626
  376.1 98.0 %collective-permute-start.6 = (bf16[2,512,384]{2,1,0:T(8,128)(2,1)S(1)}, bf16[2,512,384]{2,1,0:T(8,128)(2,1)S(1)}, u32[]{:S(2)}, u32[]{:S(2)}) collective-permute-start(bf16[2,512,384]{2,1,0:T(8,128)(2,1)S(1)} %get-tuple-element.82), channel_id=1, source_target_pairs={{0,16},{4,20},{8,24},{12,28},{16,0},{20,4},{24,8},{28,12},{1,17},{... | collective-permute-start | bytes 2359304 | tf_op jit(solution)/shard_map/ppermute | solution.py:620
  694.7 239.2 %collective-permute-start.50 = (bf16[8,2,128,1024]{3,2,0,1:T(8,128)(2,1)}, bf16[8,2,128,1024]{3,2,0,1:T(8,128)(2,1)}, u32[]{:S(2)}, u32[]{:S(2)}) collective-permute-start(bf16[8,2,128,1024]{3,2,0,1:T(8,128)(2,1)} %bitcast.374), channel_id=1, source_target_pairs={{0,1},{1,0},{2,3},{3,2},{4,5},{5,4},{6,7},{7,6},{8,9},{9,8},{10,11... | collective-permute-start | bytes 12582920 | tf_op jit(solution)/shard_map/ppermute | solution.py:626
  721.4 291.6 %collective-permute-start.48 = (bf16[8,2,32,4096]{3,2,0,1:T(8,128)(2,1)}, bf16[8,2,32,4096]{3,2,0,1:T(8,128)(2,1)}, u32[]{:S(2)}, u32[]{:S(2)}) collective-permute-start(bf16[8,2,32,4096]{3,2,0,1:T(8,128)(2,1)} %bitcast.375), channel_id=1, source_target_pairs={{0,1},{1,0},{2,3},{3,2},{4,5},{5,4},{6,7},{7,6},{8,9},{9,8},{10,11... | collective-permute-start | bytes 12582920 | tf_op jit(solution)/shard_map/ppermute | solution.py:626
  721.6 114.1 %collective-permute-start.36 = (bf16[2,512,128]{2,1,0:T(8,128)(2,1)S(1)}, bf16[2,512,128]{2,1,0:T(8,128)(2,1)}, u32[]{:S(2)}, u32[]{:S(2)}) collective-permute-start(bf16[2,512,128]{2,1,0:T(8,128)(2,1)S(1)} %get-tuple-element.100), channel_id=1, source_target_pairs={{0,16},{4,20},{8,24},{12,28},{16,0},{20,4},{24,8},{28,12},{1,17},{... | collective-permute-start | bytes 786440 | tf_op jit(solution)/shard_map/ppermute | solution.py:620
  737.5 99.2 %collective-permute-start.37 = (bf16[2,512,128]{2,1,0:T(8,128)(2,1)S(1)}, bf16[2,512,128]{2,1,0:T(8,128)(2,1)S(1)}, u32[]{:S(2)}, u32[]{:S(2)}) collective-permute-start(bf16[2,512,128]{2,1,0:T(8,128)(2,1)S(1)} %get-tuple-element.99), channel_id=1, source_target_pairs={{0,8},{4,12},{8,0},{12,4},{16,24},{20,28},{24,16},{28,20},{1,9},{5... | collective-permute-start | bytes 786440 | tf_op jit(solution)/shard_map/ppermute | solution.py:620
  835.0 112.8 %collective-permute-start.30 = (bf16[4,512,384]{1,2,0:T(8,128)(2,1)}, bf16[4,512,384]{1,2,0:T(8,128)(2,1)}, u32[]{:S(2)}, u32[]{:S(2)}) collective-permute-start(bf16[4,512,384]{1,2,0:T(8,128)(2,1)} %bitcast.442), channel_id=1, source_target_pairs={{0,4},{4,0},{8,12},{12,8},{16,20},{20,16},{24,28},{28,24},{1,5},{5... | collective-permute-start | bytes 4718600 | tf_op jit(solution)/shard_map/ppermute | solution.py:614
  957.4 100.5 %collective-permute-start.46 = (bf16[8,2,32,1024]{3,2,0,1:T(8,128)(2,1)}, bf16[8,2,32,1024]{3,2,0,1:T(8,128)(2,1)}, u32[]{:S(2)}, u32[]{:S(2)}) collective-permute-start(bf16[8,2,32,1024]{3,2,0,1:T(8,128)(2,1)} %bitcast.378), channel_id=1, source_target_pairs={{0,1},{1,0},{2,3},{3,2},{4,5},{5,4},{6,7},{7,6},{8,9},{9,8},{10,11... | collective-permute-start | bytes 3145736 | tf_op jit(solution)/shard_map/ppermute | solution.py:626
  971.3 111.4 %collective-permute-start.32 = (bf16[2,512,384]{1,2,0:T(8,128)(2,1)}, bf16[2,512,384]{1,2,0:T(8,128)(2,1)S(1)}, u32[]{:S(2)}, u32[]{:S(2)}) collective-permute-start(bf16[2,512,384]{1,2,0:T(8,128)(2,1)} %get-tuple-element.73), channel_id=1, source_target_pairs={{0,16},{4,20},{8,24},{12,28},{16,0},{20,4},{24,8},{28,12},{1,17},{... | collective-permute-start | bytes 2359304 | tf_op jit(solution)/shard_map/ppermute | solution.py:620
  1012.9 203.1 %reduce-scatter.12.cloned.1.call-start = ((), (), s32[]{:S(2)}) async-start(), calls=%async_computation.8 | async-start | bytes 2359296 | tf_op jit(solution)/shard_map/reduce_scatter | solution.py:675
  1019.5 112.9 %collective-permute-start.49 = (bf16[8,32,4096]{2,1,0:T(8,128)(2,1)}, bf16[8,32,4096]{2,1,0:T(8,128)(2,1)}, u32[]{:S(2)}, u32[]{:S(2)}) collective-permute-start(bf16[8,32,4096]{2,1,0:T(8,128)(2,1)} %dynamic-slice_bitcast_fusion.1), channel_id=1, source_target_pairs={{0,2},{1,3},{2,0},{3,1},{4,6},{5,7},{6,4},{7,5},{8,10},{9,11},{10,... | collective-permute-start | bytes 6291464 | tf_op jit(solution)/shard_map/ppermute | solution.py:626
  1060.4 105.6 %collective-permute-start.47 = (bf16[8,32,1024]{2,1,0:T(8,128)(2,1)}, bf16[8,32,1024]{2,1,0:T(8,128)(2,1)S(1)}, u32[]{:S(2)}, u32[]{:S(2)}) collective-permute-start(bf16[8,32,1024]{2,1,0:T(8,128)(2,1)} %dynamic-slice_bitcast_fusion.18), channel_id=1, source_target_pairs={{0,2},{1,3},{2,0},{3,1},{4,6},{5,7},{6,4},{7,5},{8,10},{9,11},{10,... | collective-permute-start | bytes 1572872 | tf_op jit(solution)/shard_map/ppermute | solution.py:626
  1136.8 132.0 %reduce-scatter.10.cloned.1.call-start = ((), (), s32[]{:S(2)}) async-start(), calls=%async_computation.7 | async-start | bytes 589824 | tf_op jit(solution)/shard_map/reduce_scatter | solution.py:675
  1167.0 168.5 %reduce-scatter.6.cloned.1.call-start = ((), (), s32[]{:S(2)}) async-start(), calls=%async_computation.5 | async-start | bytes 1179648 | tf_op jit(solution)/shard_map/reduce_scatter | solution.py:675
  1207.6 145.3 %all-gather.29.cloned.1.call-start = ((), (), s32[]{:S(2)}) async-start(), calls=%async_computation.15 | async-start | bytes 1310720 | tf_op jit(solution)/shard_map/all_gather | solution.py:676
  1208.4 162.7 %all-gather.27.cloned.1.call-start = ((), (), s32[]{:S(2)}) async-start(), calls=%async_computation.14 | async-start | bytes 1310720 | tf_op jit(solution)/shard_map/all_gather | solution.py:676
  1214.2 105.1 %collective-permute-start.45 = (bf16[8,32,3072]{2,1,0:T(8,128)(2,1)S(1)}, bf16[8,32,3072]{2,1,0:T(8,128)(2,1)S(1)}, u32[]{:S(2)}, u32[]{:S(2)}) collective-permute-start(bf16[8,32,3072]{2,1,0:T(8,128)(2,1)S(1)} %dynamic-slice_bitcast_fusion.2), channel_id=1, source_target_pairs={{0,2},{1,3},{2,0},{3,1},{4,6},{5,7},{6,4},{7,5},{8,10},{9,11},{10,... | collective-permute-start | bytes 4718600 | tf_op jit(solution)/shard_map/ppermute | solution.py:626
  1216.1 224.0 %reduce-scatter.8.cloned.1.call-start = ((), (), s32[]{:S(2)}) async-start(), calls=%async_computation.6 | async-start | bytes 1769472 | tf_op jit(solution)/shard_map/reduce_scatter | solution.py:675
  (105 other events, 2582.5 us)
Sparse Core Ops, SparseCore 0:
  10.7 44.8 all-gather.18
  58.4 42.7 all-gather.20
  103.9 49.3 all-gather.22
  155.9 47.8 all-gather.24
  1013.0 92.5 reduce-scatter.13
  1136.9 66.9 reduce-scatter.11
  1207.8 60.9 reduce-scatter.9
  1273.2 62.3 reduce-scatter.5
  1337.1 15.7 all-gather.28
  1354.4 16.7 all-gather.26
  1375.1 64.9 reduce-scatter.7

commit v3 on v2

--- a/solution.py
+++ b/solution.py
@@ -2,7 +2,7 @@
 import jax
 import jax.numpy as jnp
 from jax import lax
-from jax.sharding import PartitionSpec as P
+from jax.sharding import Mesh, PartitionSpec as P
 from jax.experimental import pallas as pl
 from jax.experimental.pallas import tpu as pltpu
 HEAD_DIM = 64
@@ -605,75 +605,172 @@
     return (probs.astype(jnp.bfloat16), dscore)
 
 
+BATCH = ("x", "core")
+
+
+def batch_index():
+    return lax.axis_index("x") * lax.axis_size("core") + lax.axis_index("core")
+
+
+def after(first, *later):
+    return lax.optimization_barrier((first,) + later)[1:]
+
+
 def exchange(pieces):
-    count, rows, width = pieces.shape
+    count = pieces.shape[0]
     me = lax.axis_index("seq")
-    outer, inner = me // 2, me % 2
-    nest = pieces.reshape(count // 2, 2, rows, width)
-    far = lax.dynamic_index_in_dim(nest, 1 - inner, 1, keepdims=False)
-    got = lax.ppermute(far, "seq", [(i, i ^ 1) for i in range(count)])
-    nest = lax.dynamic_update_index_in_dim(nest, got, 1 - inner, 1)
-    out = nest
-    for flip in (3, 2, 1):
-        there = jnp.bitwise_xor(outer, flip)
-        piece = lax.dynamic_index_in_dim(nest, there, 0, keepdims=False)
-        got = lax.ppermute(piece, "seq", [(i, i ^ (2 * flip)) for i in range(count)])
+    out = pieces
+    for flip in range(count - 1, 0, -1):
+        there = jnp.bitwise_xor(me, flip)
+        piece = lax.dynamic_index_in_dim(pieces, there, 0, keepdims=False)
+        got = lax.ppermute(piece, "seq", [(i, i ^ flip) for i in range(count)])
         out = lax.dynamic_update_index_in_dim(out, got, there, 0)
-    return out.reshape(count, rows, width)
-
-
-def batch_swap(value, flip):
-    return lax.ppermute(value, "batch", [(i, i ^ flip) for i in range(4)])
-
-
-def batch_bits():
-    here = lax.axis_index("batch")
-    return here // 2, here % 2
-
-
-def in_quarters(rows):
-    return lax.axis_size("batch") == 4 and rows % 4 == 0
-
-
-def join_pair(bit, mine, other, axis):
-    first = jnp.where(bit == 0, mine, other)
-    second = jnp.where(bit == 0, other, mine)
-    return jnp.stack([first, second], axis=axis)
+    return out
 
 
 def gather_weight(weight):
-    rows, width = weight.shape
-    if not in_quarters(rows):
+    parts = lax.axis_size(BATCH)
+    if weight.shape[0] % parts:
         return lax.all_gather(weight, "seq", axis=0, tiled=True)
-    span = rows // 4
-    high, low = batch_bits()
-    mine = lax.dynamic_slice_in_dim(weight, lax.axis_index("batch") * span, span, 0)
-    held = lax.all_gather(mine, "seq", axis=0, tiled=False)
-    held = join_pair(high, held, batch_swap(held, 2), 1)
-    held = join_pair(low, held, batch_swap(held, 1), 2)
-    return held.reshape(-1, width)
-
-
-def pair_sum(value, bit, flip, axis):
-    send = lax.dynamic_index_in_dim(value, 1 - bit, axis, keepdims=False)
-    keep = lax.dynamic_index_in_dim(value, bit, axis, keepdims=False)
-    got = batch_swap(send, flip)
-    return (keep.astype(jnp.float32) + got.astype(jnp.float32)).astype(jnp.bfloat16)
+    rows = weight.shape[0] // parts
+    mine = lax.dynamic_slice_in_dim(weight, batch_index() * rows, rows, 0)
+    return lax.all_gather(mine, ("seq",) + BATCH, axis=0, tiled=True)
 
 
 def sum_weight(grad):
     rows, width = grad.shape
-    low_grad = grad.astype(jnp.bfloat16)
-    seq_count = lax.axis_size("seq")
-    if not in_quarters(rows // seq_count):
-        shard = lax.psum_scatter(low_grad, "seq", scatter_dimension=0, tiled=True)
-        return lax.psum(shard, "batch").astype(jnp.float32)
-    high, low = batch_bits()
-    held = low_grad.reshape(seq_count, 2, 2, rows // (4 * seq_count), width)
-    held = pair_sum(held, low, 1, 2)
-    held = pair_sum(held, high, 2, 1)
-    shard = lax.psum_scatter(held, "seq", scatter_dimension=0, tiled=False)
-    return lax.all_gather(shard, "batch", axis=0, tiled=True).astype(jnp.float32)
+    low = grad.astype(jnp.bfloat16)
+    seq_count, cores = lax.axis_size("seq"), lax.axis_size("core")
+    parts = seq_count * lax.axis_size(BATCH)
+    if rows % parts or cores != 2:
+        shard = lax.psum_scatter(low, "seq", scatter_dimension=0, tiled=True)
+        return lax.psum(shard, BATCH).astype(jnp.float32)
+    core = lax.axis_index("core")
+    held = low.reshape(parts // 2, 2, rows // parts, width)
+    send = lax.dynamic_index_in_dim(held, 1 - core, 1, keepdims=False)
+    keep = lax.dynamic_index_in_dim(held, core, 1, keepdims=False)
+    got = lax.ppermute(send, "core", [(0, 1), (1, 0)])
+    half = (keep.astype(jnp.float32) + got.astype(jnp.float32)).astype(jnp.bfloat16)
+    half = half.reshape(rows // 2, width)
+    shard = lax.psum_scatter(half, ("seq", "x"), scatter_dimension=0, tiled=True)
+    return lax.all_gather(shard, BATCH, axis=0, tiled=True).astype(jnp.float32)
+
+
+def gather_kernel(*refs, shapes):
+    count = len(shapes)
+    weights, seq_small, batch_small = refs[:count], refs[count], refs[count + 1]
+    fulls = refs[count + 2 : 2 * count + 2]
+    seq_out, batch_out, send, recv, small_send, small_recv, local = refs[2 * count + 2 :]
+    me, x, core = lax.axis_index("seq"), lax.axis_index("x"), lax.axis_index("core")
+    bits = (me // 4, (me // 2) % 2, me % 2, x, core)
+
+    def peer(dim):
+        if dim < 3:
+            return (me ^ (4 >> dim), x, core)
+        return (me, 1 - x, core) if dim == 3 else (me, x, 1 - core)
+
+    others = [((me + d) % 8, x, core) for d in range(1, 8)]
+    mates = [(me, (x + dx) % 2, (core + dc) % 2) for dx, dc in ((0, 1), (1, 0), (1, 1))]
+    barrier = pltpu.get_barrier_semaphore()
+    for device in others + mates:
+        pl.semaphore_signal(barrier, inc=1, device_id=device, device_id_type=pl.DeviceIdType.MESH)
+    pl.semaphore_wait(barrier, len(others) + len(mates))
+
+    small = []
+    quarter = x * 2 + core
+    own_seq = pltpu.make_async_copy(seq_small, seq_out.at[me], local.at[0])
+    own_batch = pltpu.make_async_copy(batch_small, batch_out.at[quarter], local.at[1])
+    own_seq.start()
+    own_batch.start()
+    for slot, device in enumerate(others):
+        small.append(
+            pltpu.make_async_remote_copy(
+                seq_small, seq_out.at[me], small_send.at[slot], small_recv.at[slot],
+                device_id=device, device_id_type=pl.DeviceIdType.MESH,
+            )
+        )
+    for slot, device in enumerate(mates):
+        small.append(
+            pltpu.make_async_remote_copy(
+                batch_small, batch_out.at[quarter], small_send.at[7 + slot], small_recv.at[7 + slot],
+                device_id=device, device_id_type=pl.DeviceIdType.MESH,
+            )
+        )
+    for copy in small:
+        copy.start()
+
+    jobs = []
+    for index, (weight, full, (rows, width)) in enumerate(zip(weights, fulls, shapes)):
+        span = rows // 4
+        half = width // 2
+        for side in range(2):
+            cols = pl.ds(side * half, half)
+            source = weight.at[pl.ds(quarter * span, span), cols]
+            order = (0, 1, 2, 3, 4) if side == 0 else (0, 1, 3, 2, 4)
+            jobs.append((full, cols, source, order))
+    owns = []
+    for index, (full, cols, source, order) in enumerate(jobs):
+        own = pltpu.make_async_copy(source, full.at[bits + (slice(None), cols)], local.at[2 + index])
+        own.start()
+        owns.append(own)
+    copies = [[None] * 5 for _ in jobs]
+    for stage in range(5):
+        for index, (full, cols, source, order) in enumerate(jobs):
+            dim = order[stage]
+            done = order[:stage]
+            where = tuple(slice(None) if d in done else bits[d] for d in range(5)) + (slice(None), cols)
+            if stage == 1:
+                owns[index].wait()
+            if stage:
+                copies[index][stage - 1].wait_recv()
+            copy = pltpu.make_async_remote_copy(
+                source if stage == 0 else full.at[where],
+                full.at[where],
+                send.at[index * 5 + stage],
+                recv.at[index * 5 + stage],
+                device_id=peer(dim),
+                device_id_type=pl.DeviceIdType.MESH,
+            )
+            copy.start()
+            copies[index][stage] = copy
+    for chain in copies:
+        chain[4].wait_recv()
+    for chain in copies:
+        for copy in chain:
+            copy.wait_send()
+    for copy in small:
+        copy.wait()
+    own_seq.wait()
+    own_batch.wait()
+
+
+def gather_early(weights, seq_small, batch_small):
+    shapes = [w.shape for w in weights]
+    anywhere = pl.BlockSpec(memory_space=pl.ANY)
+    jobs = 2 * len(weights)
+    outs = pl.pallas_call(
+        functools.partial(gather_kernel, shapes=shapes),
+        in_specs=[anywhere] * (len(weights) + 2),
+        out_specs=[anywhere] * (len(weights) + 2),
+        out_shape=[
+            jax.ShapeDtypeStruct((2, 2, 2, 2, 2, rows // 4, width), BF) for rows, width in shapes
+        ]
+        + [
+            jax.ShapeDtypeStruct((8,) + seq_small.shape, F32),
+            jax.ShapeDtypeStruct((4,) + batch_small.shape, F32),
+        ],
+        scratch_shapes=[
+            pltpu.SemaphoreType.DMA((5 * jobs,)),
+            pltpu.SemaphoreType.DMA((5 * jobs,)),
+            pltpu.SemaphoreType.DMA((10,)),
+            pltpu.SemaphoreType.DMA((10,)),
+            pltpu.SemaphoreType.DMA((2 + jobs,)),
+        ],
+        compiler_params=pltpu.CompilerParams(collective_id=0, has_side_effects=True),
+        name="gather_early",
+    )(*weights, seq_small, batch_small)
+    fulls = [full.reshape(8 * rows, width) for full, (rows, width) in zip(outs, shapes)]
+    return fulls, outs[-2], outs[-1]
 
 
 def paired_tables(positions):
@@ -711,15 +808,7 @@
     drop = cond_drop.astype(jnp.float32)
     dropped = drop[:, None] * valid_mask
     frames_live = jnp.minimum(lengths, frame_count).astype(jnp.float32)
-    kept_total, drop_total = lax.psum(
-        (jnp.sum((1.0 - drop) * frames_live), jnp.sum(drop * frames_live)), "batch"
-    )
-    kept_total = jnp.maximum(kept_total, 1.0)
-    drop_total = jnp.maximum(drop_total, 1.0)
-    every_count = kept_total + drop_total
-    loss_weight = (valid_mask - dropped) * (every_count / (2.0 * kept_total)) + dropped * (
-        every_count / (2.0 * drop_total)
-    )
+    counts = jnp.stack([jnp.sum((1.0 - drop) * frames_live), jnp.sum(drop * frames_live)])
     silu_time = jax.nn.silu(time_embed.astype(jnp.float32)).astype(jnp.bfloat16)
     row_span = adaln_weight.shape[0]
     silu_mine = lax.dynamic_slice_in_dim(silu_time, seq_here * row_span, row_span, 1)
@@ -731,12 +820,34 @@
         seq_here * bias_span,
         0,
     )
-    modulation = lax.psum(mod_part + bias_here, "seq").reshape(utt_count, 6, model_width)
-    skip_full = gather_weight(skip_weight)
-    qkv_full = gather_weight(qkv_weight)
-    out_full = gather_weight(out_weight)
-    up_full = gather_weight(up_weight)
-    down_full = gather_weight(down_weight)
+    mod_part = mod_part + bias_here
+    if by_heads:
+        small = jnp.concatenate(
+            [
+                silu_time.astype(jnp.float32),
+                jnp.pad(counts[None, :], ((0, 5), (0, model_width - 2))),
+            ],
+            axis=0,
+        )
+        (skip_full, qkv_full), mod_every, small_every = gather_early(
+            (skip_weight, qkv_weight), mod_part.reshape(-1, model_width), small
+        )
+        modulation = jnp.sum(mod_every, axis=0)
+        totals = jnp.sum(small_every[:, utt_count, :2], axis=0)
+        silu_every = small_every[:, :utt_count].reshape(-1, model_width)
+    else:
+        modulation = lax.psum(mod_part, "seq")
+        totals = lax.psum(counts, BATCH)
+        skip_full = gather_weight(skip_weight)
+        qkv_full = gather_weight(qkv_weight)
+        silu_every = lax.all_gather(silu_time, BATCH, axis=0, tiled=True).astype(jnp.float32)
+    modulation = modulation.reshape(utt_count, 6, model_width)
+    kept_total = jnp.maximum(totals[0], 1.0)
+    drop_total = jnp.maximum(totals[1], 1.0)
+    every_count = kept_total + drop_total
+    loss_weight = (valid_mask - dropped) * (every_count / (2.0 * kept_total)) + dropped * (
+        every_count / (2.0 * drop_total)
+    )
     joined = jnp.concatenate([layer_input, skip_input], axis=-1).reshape(row_count, 2 * model_width)
     residual_in = jnp.dot(joined, skip_full, preferred_element_type=jnp.float32).reshape(
         utt_count, frame_span, model_width
@@ -754,6 +865,7 @@
         cos_here = lax.dynamic_slice_in_dim(cos_all, seq_here * frame_span, frame_span, 0)
         sin_here = lax.dynamic_slice_in_dim(sin_all, seq_here * frame_span, frame_span, 0)
         packed, attended_mine, lse_mine, attended_parts = [], [], [], []
+        sends = []
         for utt in range(utt_count):
             sent = project_heads(
                 normed_attn[utt * frame_span : (utt + 1) * frame_span],
@@ -762,6 +874,10 @@
                 sin_here,
                 seq_count,
             )
+            sends.append(sent)
+        late = after(tuple(sends), out_weight, up_weight, down_weight)
+        out_full, up_full, down_full = [gather_weight(weight) for weight in late]
+        for sent in sends:
             packed.append(exchange(sent).reshape(frame_count, 384))
         for utt in range(utt_count):
             heads_out, lse = flash_forward(lengths[utt : utt + 1], packed[utt], 1024, 1024)
@@ -771,6 +887,9 @@
             attended_parts.append(back.transpose(1, 0, 2).reshape(frame_span, model_width))
         attended_low = jnp.concatenate(attended_parts, axis=0)
     else:
+        out_full, up_full, down_full = [
+            gather_weight(weight) for weight in (out_weight, up_weight, down_weight)
+        ]
         projected = jnp.dot(normed_attn, qkv_full, preferred_element_type=jnp.float32).reshape(
             utt_count, frame_span, 3, head_count, HEAD_DIM
         )
@@ -923,14 +1042,9 @@
         axis=1,
     ).reshape(utt_count, 6 * model_width)
     mod_total = lax.psum(grad_modulation, "seq")
-    mod_every, silu_every = (
-        lax.all_gather(mod_total.astype(jnp.bfloat16), "batch", axis=0, tiled=True).astype(
-            mod_total.dtype
-        ),
-        lax.all_gather(
-            silu_time.astype(jnp.float32).astype(jnp.bfloat16), "batch", axis=0, tiled=True
-        ).astype(jnp.float32),
-    )
+    mod_every = lax.all_gather(
+        mod_total.astype(jnp.bfloat16), BATCH, axis=0, tiled=True
+    ).astype(jnp.float32)
     silu_rows = lax.dynamic_slice_in_dim(silu_every, seq_here * row_span, row_span, 1)
     adaln_rows = jnp.dot(silu_rows.T, mod_every, precision=lax.Precision.HIGHEST)
     bias_rows = lax.dynamic_slice_in_dim(
@@ -953,13 +1067,16 @@
 
 
 def solution(mesh):
+    count, batch = mesh.shape["seq"], mesh.shape["batch"]
+    cores = 2 if batch % 2 == 0 else 1
+    split = Mesh(mesh.devices.reshape(count, batch // cores, cores), ("seq",) + BATCH)
     placed = (
-        P("batch", "seq", None),
-        P("batch", "seq", None),
-        P("batch", None),
-        P("batch"),
-        P("batch"),
-        P("batch", "seq", None),
+        P(BATCH, "seq", None),
+        P(BATCH, "seq", None),
+        P(BATCH, None),
+        P(BATCH),
+        P(BATCH),
+        P(BATCH, "seq", None),
         P("seq", None),
         P("seq", None),
         P("seq"),
@@ -970,12 +1087,12 @@
     )
     return jax.shard_map(
         on_device,
-        mesh=mesh,
+        mesh=split,
         in_specs=placed,
         out_specs=(
-            P("batch", "seq", None),
-            P("batch", "seq", None),
-            P("batch", "seq", None),
+            P(BATCH, "seq", None),
+            P(BATCH, "seq", None),
+            P(BATCH, "seq", None),
             P("seq", None),
             P("seq", None),
             P("seq"),

time: 1460 us -> 1380 us (0.945)
  blocking collectives: 181 us -> 104 us
  local copies, waits for them, and re-layouts: 178 us -> 238 us
  other arithmetic: 116 us -> 60.1 us
  starting transfers between devices: 190 us -> 147 us
  Pallas kernels: 384 us -> 426 us
  waiting for transfers between devices: 345 us -> 327 us
    reduce_scatter x5, waiting for transfers between devices: 85.4 us -> 184 us  [sum_weight(): lax.psum_scatter(half, ('seq', 'x'), scatter_dimension=0, tiled=True)]
    dynamic_update_slice x18 -> x54, local copies, waits for them, and re-layouts: 14 us -> 107 us  [exchange(): out = lax.dynamic_update_index_in_dim(out, got, there, 0)]
    pallas_call x0 -> x1, Pallas kernels: none -> 83.7 us  [gather_early(): pl.pallas_call(functools.partial(gather_kernel, shapes=shapes), in_specs=...]
    all_gather x6 -> x5, waiting for transfers between devices: 97.8 us -> 23 us  [the longest x2 23 us: sum_weight(): return lax.all_gather(shard, BATCH, axis=0, tiled=True).astype(jnp.float32)]
    another operation x20 -> x0, other arithmetic: 54.5 us -> none  [join_pair(): return jnp.stack([first, second], axis=axis)]
    psum x2 -> x0, blocking collectives: 45.9 us -> none  [the longest x1 36.5 us: on_device(): lax.psum(mod_part + bias_here, 'seq').reshape(utt_count, 6, model_width)]
    ppermute x52 -> x61, starting transfers between devices: 190 us -> 146 us  [the longest x56 145 us: exchange(): got = lax.ppermute(piece, 'seq', [(i, i ^ flip) for i in range(count)])]
    ppermute x52 -> x61, waiting for transfers between devices: 161 us -> 120 us  [the longest x56 114 us: exchange(): got = lax.ppermute(piece, 'seq', [(i, i ^ flip) for i in range(count)])]
  transfers between devices with their start and end apart: 63 -> 71, of which waited for: 20 -> 21; matrix products, arithmetic and copies ran while one was open for 22% -> 20% of each run, Pallas kernels for 19% -> 16%
where the time goes in v3:
time: 1380 us; the launch traced here: 1370 us
  Pallas kernels  426 us (31%)
  waiting for transfers between devices  327 us (24%)
  local copies, waits for them, and re-layouts  238 us (17%)
  starting transfers between devices  147 us (11%)
  blocking collectives  104 us (8%)
  other arithmetic  60.1 us (4%)
  matrix products  51.4 us (4%)
  between operations  17.3 us (1%)
    reduce_scatter x5, waiting for transfers between devices, sum_weight(): lax.psum_scatter(half, ('seq', 'x'), scatter_dimension=0, tiled=True)  184 us
    pallas_call x2, Pallas kernels, flash_backward(): pl.pallas_call(functools.partial(flash_backward_kernel, bq=bq, bk=bk), gr...  150 us
    ppermute x56, starting transfers between devices, exchange(): got = lax.ppermute(piece, 'seq', [(i, i ^ flip) for i in range(count)])  145 us
    ppermute x56, waiting for transfers between devices, exchange(): got = lax.ppermute(piece, 'seq', [(i, i ^ flip) for i in range(count)])  114 us
    dynamic_update_slice x54, local copies, waits for them, and re-layouts, exchange(): out = lax.dynamic_update_index_in_dim(out, got, there, 0)  107 us
    pallas_call x1, Pallas kernels, gather_early(): pl.pallas_call(functools.partial(gather_kernel, shapes=shapes), in_specs=...  83.7 us
    pallas_call x2, Pallas kernels, flash_forward(): pl.pallas_call(functools.partial(flash_forward_kernel, bq=bq, bk=bk), gri...  72.3 us
    pallas_call x1, Pallas kernels, ffn_backward(): pl.pallas_call(ffn_backward_kernel, grid=(hidden // chunk,), in_specs=who...  61 us
  transfers between devices with their start and end apart: 71, of which 21 were waited for; matrix products, arithmetic and copies ran while one was open for 20% of the time, Pallas kernels for 16%

profile of v3, /device:TPU:0, one launch (start us, length us, event | category | flops | bytes accessed | tf_op | source)
XLA Modules:
  0.0 1370.5 jit_solution(5208780368576227992)
XLA Ops:
  31.2 83.7 %gather_early.1 = (bf16[2,2,2,2,2,64,1024]{6,5,4,3,2,1,0:T(8,128)(2,1)}, bf16[2,2,2,2,2,32,3072]{6,5,4,3,2,1,0:T(8,128)(2,1)}, f32[8,12,1024]{2,1,0:T(8,128)}, f32[4,8,1024]{2,1,0:T(8,128)}) custom-call(bf16[256,1024]{1,0:T(8,128)(2,1)} %refs_0_.1, bf16[128,3072]{1,0:T(8,128)(2,1)} %refs_1_.1, f32[12,1024]{1,0:T(8,128)} %reshape.350.refs_2_, ...), custom_call_target="tpu_custom_call" | custom-call | tf_op jit(solution)/shard_map/gather_early/pallas_call | solution.py:751
  114.9 9.9 fusion.24
  176.4 8.8 collective-permute-done.14
  192.2 24.5 %collective-permute-start.16 = (bf16[512,384]{1,0:T(8,128)(2,1)S(1)}, bf16[512,384]{1,0:T(8,128)(2,1)S(1)}, u32[]{:S(2)}, u32[]{:S(2)}) collective-permute-start(bf16[512,384]{1,0:T(8,128)(2,1)S(1)} %get-tuple-element.84), channel_id=1, source_target_pairs={{0,20},{4,16},{8,28},{12,24},{16,4},{20,0},{24,12},{28,8},{1,21},{... | collective-permute-start | bytes 1179656 | tf_op jit(solution)/shard_map/ppermute | solution.py:626
  220.8 17.7 %collective-permute-start.19 = (bf16[512,384]{1,0:T(8,128)(2,1)S(1)}, bf16[512,384]{1,0:T(8,128)(2,1)S(1)}, u32[]{:S(2)}, u32[]{:S(2)}) collective-permute-start(bf16[512,384]{1,0:T(8,128)(2,1)S(1)} %get-tuple-element.81), channel_id=1, source_target_pairs={{0,8},{4,12},{8,0},{12,4},{16,24},{20,28},{24,16},{28,20},{1,9},{5... | collective-permute-start | bytes 1179656 | tf_op jit(solution)/shard_map/ppermute | solution.py:626
  242.9 16.7 %collective-permute-done.16 = bf16[512,384]{1,0:T(8,128)(2,1)S(1)} collective-permute-done((bf16[512,384]{1,0:T(8,128)(2,1)S(1)}, bf16[512,384]{1,0:T(8,128)(2,1)S(1)}, u32[]{:S(2)}, u32[]{:S(2)}) %collective-permute-start.16) | collective-permute-done | bytes 393248 | tf_op jit(solution)/shard_map/ppermute | solution.py:626
  263.9 14.0 %collective-permute-done.17 = bf16[512,384]{1,0:T(8,128)(2,1)S(1)} collective-permute-done((bf16[512,384]{1,0:T(8,128)(2,1)S(1)}, bf16[512,384]{1,0:T(8,128)(2,1)S(1)}, u32[]{:S(2)}, u32[]{:S(2)}) %collective-permute-start.17) | collective-permute-done | bytes 393248 | tf_op jit(solution)/shard_map/ppermute | solution.py:626
  287.0 32.2 %attend_forward.3 = (bf16[4096,128]{1,0:T(8,128)(2,1)}, f32[8,4096]{1,0:T(8,128)}) custom-call(s32[1]{0:T(128)} %get-tuple-element.138.len_ref, bf16[4096,384]{1,0:T(8,128)(2,1)} %bitcast.56.q_ref.k_ref.v_ref, bf16[4096,384]{1,0:T(8,128)(2,1)} %bitcast.56.q_ref.k_ref.v_ref, bf16[4096,384]{1,0:T(8,128)(2,1)} %bitcast.56.q_ref.k_ref.v_ref), custom_call_target="tpu_custom_call" | custom-call | flops 17179869184 | bytes 8388608 | tf_op jit(solution)/shard_map/attend_forward/pallas_call | solution.py:138
  328.1 11.6 collective-permute-done.3
  349.4 40.1 %attend_forward.2 = (bf16[4096,128]{1,0:T(8,128)(2,1)}, f32[8,4096]{1,0:T(8,128)}) custom-call(s32[1]{0:T(128)} %get-tuple-element.139.len_ref, bf16[4096,384]{1,0:T(8,128)(2,1)} %bitcast.378, bf16[4096,384]{1,0:T(8,128)(2,1)} %bitcast.379, bf16[4096,384]{1,0:T(8,128)(2,1)} %bitcast.380), custom_call_target="tpu_custom_call" | custom-call | flops 17179869184 | bytes 8388608 | tf_op jit(solution)/shard_map/attend_forward/pallas_call | solution.py:138
  514.5 42.5 %ffn_forward.1 = (f32[1024,1024]{1,0:T(8,128)}, bf16[1024,4096]{1,0:T(8,128)(2,1)}, bf16[1024,4096]{1,0:T(8,128)(2,1)}, bf16[1024,1024]{1,0:T(8,128)(2,1)}, bf16...) custom-call(bf16[1024,1024]{1,0:T(8,128)(2,1)} %bitcast_dynamic-update-slice_fusion.att_ref, ...), custom_call_target="tpu_custom_call" | custom-call | flops 19327352832 | bytes 62914560 | tf_op jit(solution)/shard_map/ffn_forward/pallas_call | solution.py:444
  557.0 61.0 %ffn_backward.1 = (bf16[1024,4096]{1,0:T(8,128)(2,1)}, bf16[4096,1024]{1,0:T(8,128)(2,1)}, f32[1024,1024]{1,0:T(8,128)}, bf16[1024,1024]{1,0:T(8,128)(2,1)}, bf1...) custom-call(bf16[1024,1024]{1,0:T(8,128)(2,1)} %bitcast_dynamic-update-slice_fusion.att_ref, ...), custom_call_target="tpu_custom_call" | custom-call | flops 38654705664 | bytes 94371840 | tf_op jit(solution)/shard_map/ffn_backward/pallas_call | solution.py:487
  667.1 92.3 %attend_backward.2 = bf16[4096,384]{1,0:T(8,128)(2,1)} custom-call(s32[1]{0:T(128)} %get-tuple-element.139.len_ref, bf16[4096,384]{1,0:T(8,128)(2,1)} %bitcast.381, bf16[4096,384]{1,0:T(8,128)(2,1)} %bitcast.382, bf16[4096,384]{1,0:T(8,128)(2,1)} %bitcast.383, bf16[4096,128]{1,0:T(8,128)(2,1)} %get-tuple-element.36.o_ref, bf16[4096,128]{1,0:T(8,128)(2,1)} %bitcast.377, ...), custom_call_target="tpu_custom_call" | custom-call | flops 42949672960 | bytes 8388608 | tf_op jit(solution)/shard_map/attend_backward/pallas_call | solution.py:271
  797.5 58.0 %attend_backward.3 = bf16[4096,384]{1,0:T(8,128)(2,1)} custom-call(s32[1]{0:T(128)} %get-tuple-element.138.len_ref, bf16[4096,384]{1,0:T(8,128)(2,1)} %bitcast.56.q_ref.k_ref.v_ref, bf16[4096,384]{1,0:T(8,128)(2,1)} %bitcast.56.q_ref.k_ref.v_ref, bf16[4096,384]{1,0:T(8,128)(2,1)} %bitcast.56.q_ref.k_ref.v_ref, bf16[4096,128]{1,0:T(8,128)(2,1)} %get-tuple-element.37.o_ref, ...), custom_call_target="tpu_custom_call" | custom-call | flops 42949672960 | bytes 8388608 | tf_op jit(solution)/shard_map/attend_backward/pallas_call | solution.py:271
  877.9 25.2 %collective-permute-done.39 = bf16[512,384]{0,1:T(8,128)(2,1)S(1)} collective-permute-done((bf16[512,384]{0,1:T(8,128)(2,1)}, bf16[512,384]{0,1:T(8,128)(2,1)S(1)}, u32[]{:S(2)}, u32[]{:S(2)}) %collective-permute-start.39) | collective-permute-done | bytes 393248 | tf_op jit(solution)/shard_map/ppermute | solution.py:626
  905.6 17.8 %collective-permute-done.41 = bf16[512,384]{0,1:T(8,128)(2,1)S(1)} collective-permute-done((bf16[512,384]{0,1:T(8,128)(2,1)}, bf16[512,384]{0,1:T(8,128)(2,1)S(1)}, u32[]{:S(2)}, u32[]{:S(2)}) %collective-permute-start.41) | collective-permute-done | bytes 393248 | tf_op jit(solution)/shard_map/ppermute | solution.py:626
  927.0 12.4 collective-permute-start.54
  966.3 13.8 %multiply_reduce_fusion = (f32[2,1024]{1,0:T(2,128)S(1)}, f32[2,512]{1,0:T(2,128)S(1)}, f32[2,512]{1,0:T(2,128)S(1)}, f32[2,1024]{1,0:T(2,128)S(1)}, f32[2,512,1024]{2,1,0:T(8,128)S(1)}) fusion(f32[2,512]{1,0:T(2,128)S(1)} %copy-done.46, f32[2,512]{1,0:T(2,128)S(1)} %copy-done.44, f32[1024,1024]{1,0:T(8,128)} %get-tuple-element.141.res_ref, ...), kind=kOutput, calls=%fused_computation.18 | convolution fusion | flops 6453979136 | bytes 25206784 | tf_op jit(solution)/shard_map/dot_general | solution.py:589
  1026.0 9.4 convolution_convert_fusion.1
  1035.5 39.1 %psum.7 = bf16[2,6144]{1,0:T(2,128)(2,1)S(1)} all-reduce(f32[2,6144]{1,0:T(2,128)S(1)} %bitcast.406), channel_id=1, replica_groups=mesh['seq'=8,'x'=2,'core'=2] {'seq'}, use_global_device_ids=true, to_apply=%region_11.12 | all-reduce | flops 12288 | bytes 73728 | tf_op jit(solution)/shard_map/psum | solution.py:1044
  1074.6 41.2 %all-gather = bf16[4,2,6144]{2,1,0:T(2,128)(2,1)S(1)} all-gather(bf16[1,2,6144]{2,1,0:T(2,128)(2,1)S(1)} %bitcast.416), channel_id=1, replica_groups=mesh['seq'=8,'x'=2,'core'=2] {'x','core'}, dimensions={0}, use_global_device_ids=true | all-gather | bytes 122880 | tf_op jit(solution)/shard_map/all_gather | solution.py:1045
  1133.2 57.7 %reduce-scatter.6.cloned.1.call-done = bf16[64,1024]{1,0:T(8,128)(2,1)} async-done(((bf16[1024,1024]{1,0:T(8,128)(2,1)}), bf16[64,1024]{1,0:T(8,128)(2,1)}) %reduce-scatter.6.cloned.1.call-update) | async-done | bytes 131088 | tf_op jit(solution)/shard_map/reduce_scatter | solution.py:655
  1198.7 125.9 %reduce-scatter.8.cloned.1.call-done = bf16[32,3072]{1,0:T(8,128)(2,1)} async-done(((bf16[512,3072]{1,0:T(8,128)(2,1)}), bf16[32,3072]{1,0:T(8,128)(2,1)}) %reduce-scatter.8.cloned.1.call-update) | async-done | bytes 196624 | tf_op jit(solution)/shard_map/reduce_scatter | solution.py:655
  1345.0 15.5 %all-gather.13.cloned.1.call-done = bf16[128,4096]{1,0:T(8,128)(2,1)} async-done(((bf16[32,4096]{1,0:T(8,128)(2,1)}), bf16[128,4096]{1,0:T(8,128)(2,1)}) %all-gather.13.cloned.1.call-update) | async-done | bytes 1048592 | tf_op jit(solution)/shard_map/all_gather | solution.py:656
  (435 shorter events, 482.2 us)
Async XLA Ops:
  7.2 507.3 %all-gather.7.cloned.1.call-start = ((), (), s32[]{:S(2)}) async-start(), calls=%async_computation.5 | async-start | bytes 2162688 | tf_op jit(solution)/shard_map/all_gather | solution.py:637
  165.0 349.6 %all-gather.11.cloned.1.call-start = ((), (), s32[]{:S(2)}) async-start(), calls=%async_computation.7 | async-start | bytes 8650752 | tf_op jit(solution)/shard_map/all_gather | solution.py:637
  166.7 347.8 %all-gather.9.cloned.1.call-start = ((), (), s32[]{:S(2)}) async-start(), calls=%async_computation.6 | async-start | bytes 8650752 | tf_op jit(solution)/shard_map/all_gather | solution.py:637
  168.5 854.0 %reduce-scatter.14.cloned.1.call-start = ((), (), s32[]{:S(2)}) async-start(), calls=%async_computation.13 | async-start | bytes 4456448 | tf_op jit(solution)/shard_map/reduce_scatter | solution.py:655
  192.2 67.5 %collective-permute-start.16 = (bf16[512,384]{1,0:T(8,128)(2,1)S(1)}, bf16[512,384]{1,0:T(8,128)(2,1)S(1)}, u32[]{:S(2)}, u32[]{:S(2)}) collective-permute-start(bf16[512,384]{1,0:T(8,128)(2,1)S(1)} %get-tuple-element.84), channel_id=1, source_target_pairs={{0,20},{4,16},{8,28},{12,24},{16,4},{20,0},{24,12},{28,8},{1,21},{... | collective-permute-start | bytes 1179656 | tf_op jit(solution)/shard_map/ppermute | solution.py:626
  216.6 61.3 %collective-permute-start.17 = (bf16[512,384]{1,0:T(8,128)(2,1)S(1)}, bf16[512,384]{1,0:T(8,128)(2,1)S(1)}, u32[]{:S(2)}, u32[]{:S(2)}) collective-permute-start(bf16[512,384]{1,0:T(8,128)(2,1)S(1)} %get-tuple-element.83), channel_id=1, source_target_pairs={{0,16},{4,20},{8,24},{12,28},{16,0},{20,4},{24,8},{28,12},{1,17},{... | collective-permute-start | bytes 1179656 | tf_op jit(solution)/shard_map/ppermute | solution.py:626
  216.6 62.1 %collective-permute-start.18 = (bf16[512,384]{1,0:T(8,128)(2,1)S(1)}, bf16[512,384]{1,0:T(8,128)(2,1)S(1)}, u32[]{:S(2)}, u32[]{:S(2)}) collective-permute-start(bf16[512,384]{1,0:T(8,128)(2,1)S(1)} %get-tuple-element.82), channel_id=1, source_target_pairs={{0,12},{4,8},{8,4},{12,0},{16,28},{20,24},{24,20},{28,16},{1,13},{... | collective-permute-start | bytes 1179656 | tf_op jit(solution)/shard_map/ppermute | solution.py:626
  220.8 61.6 %collective-permute-start.19 = (bf16[512,384]{1,0:T(8,128)(2,1)S(1)}, bf16[512,384]{1,0:T(8,128)(2,1)S(1)}, u32[]{:S(2)}, u32[]{:S(2)}) collective-permute-start(bf16[512,384]{1,0:T(8,128)(2,1)S(1)} %get-tuple-element.81), channel_id=1, source_target_pairs={{0,8},{4,12},{8,0},{12,4},{16,24},{20,28},{24,16},{28,20},{1,9},{5... | collective-permute-start | bytes 1179656 | tf_op jit(solution)/shard_map/ppermute | solution.py:626
  323.8 67.8 %collective-permute-start.21 = (bf16[512,128]{1,0:T(8,128)(2,1)}, bf16[512,128]{1,0:T(8,128)(2,1)S(1)}, u32[]{:S(2)}, u32[]{:S(2)}) collective-permute-start(bf16[512,128]{1,0:T(8,128)(2,1)} %get-tuple-element.122), channel_id=1, source_target_pairs={{0,28},{4,24},{8,20},{12,16},{16,12},{20,8},{24,4},{28,0},{1,29},{... | collective-permute-start | bytes 393224 | tf_op jit(solution)/shard_map/ppermute | solution.py:626
  627.7 159.1 %collective-permute-start.59 = (bf16[16,32,4096]{2,1,0:T(8,128)(2,1)}, bf16[16,32,4096]{2,1,0:T(8,128)(2,1)}, u32[]{:S(2)}, u32[]{:S(2)}) collective-permute-start(bf16[16,32,4096]{2,1,0:T(8,128)(2,1)} %dynamic-slice_bitcast_fusion.1), channel_id=1, source_target_pairs={{0,1},{1,0},{2,3},{3,2},{4,5},{5,4},{6,7},{7,6},{8,9},{9,8},{10,11... | collective-permute-start | bytes 12582920 | tf_op jit(solution)/shard_map/ppermute | solution.py:652
  629.2 361.0 %collective-permute-start.58 = (bf16[16,32,1024]{2,1,0:T(8,128)(2,1)}, bf16[16,32,1024]{2,1,0:T(8,128)(2,1)}, u32[]{:S(2)}, u32[]{:S(2)}) collective-permute-start(bf16[16,32,1024]{2,1,0:T(8,128)(2,1)} %dynamic-slice_bitcast_fusion.4), channel_id=1, source_target_pairs={{0,1},{1,0},{2,3},{3,2},{4,5},{5,4},{6,7},{7,6},{8,9},{9,8},{10,11... | collective-permute-start | bytes 3145736 | tf_op jit(solution)/shard_map/ppermute | solution.py:652
  641.6 384.3 %reduce-scatter.12.cloned.1.call-start = ((), (), s32[]{:S(2)}) async-start(), calls=%async_computation.11 | async-start | bytes 4456448 | tf_op jit(solution)/shard_map/reduce_scatter | solution.py:655
  657.8 112.4 %collective-permute-start.42 = (bf16[512,128]{1,0:T(8,128)(2,1)}, bf16[512,128]{1,0:T(8,128)(2,1)}, u32[]{:S(2)}, u32[]{:S(2)}) collective-permute-start(bf16[512,128]{1,0:T(8,128)(2,1)} %get-tuple-element.113), channel_id=1, source_target_pairs={{0,28},{4,24},{8,20},{12,16},{16,12},{20,8},{24,4},{28,0},{1,29},{... | collective-permute-start | bytes 393224 | tf_op jit(solution)/shard_map/ppermute | solution.py:626
  659.1 116.9 %collective-permute-start.43 = (bf16[512,128]{1,0:T(8,128)(2,1)}, bf16[512,128]{1,0:T(8,128)(2,1)}, u32[]{:S(2)}, u32[]{:S(2)}) collective-permute-start(bf16[512,128]{1,0:T(8,128)(2,1)} %get-tuple-element.112), channel_id=1, source_target_pairs={{0,24},{4,28},{8,16},{12,20},{16,8},{20,12},{24,0},{28,4},{1,25},{... | collective-permute-start | bytes 393224 | tf_op jit(solution)/shard_map/ppermute | solution.py:626
  666.1 110.9 %collective-permute-start.44 = (bf16[512,128]{1,0:T(8,128)(2,1)}, bf16[512,128]{1,0:T(8,128)(2,1)}, u32[]{:S(2)}, u32[]{:S(2)}) collective-permute-start(bf16[512,128]{1,0:T(8,128)(2,1)} %get-tuple-element.111), channel_id=1, source_target_pairs={{0,20},{4,16},{8,28},{12,24},{16,4},{20,0},{24,12},{28,8},{1,21},{... | collective-permute-start | bytes 393224 | tf_op jit(solution)/shard_map/ppermute | solution.py:626
  782.2 85.1 %collective-permute-start.35 = (bf16[512,384]{0,1:T(8,128)(2,1)}, bf16[512,384]{0,1:T(8,128)(2,1)}, u32[]{:S(2)}, u32[]{:S(2)}) collective-permute-start(bf16[512,384]{0,1:T(8,128)(2,1)} %bitcast.394), channel_id=1, source_target_pairs={{0,28},{4,24},{8,20},{12,16},{16,12},{20,8},{24,4},{28,0},{1,29},{... | collective-permute-start | bytes 1179656 | tf_op jit(solution)/shard_map/ppermute | solution.py:626
  782.3 86.9 %collective-permute-start.36 = (bf16[512,384]{0,1:T(8,128)(2,1)}, bf16[512,384]{0,1:T(8,128)(2,1)}, u32[]{:S(2)}, u32[]{:S(2)}) collective-permute-start(bf16[512,384]{0,1:T(8,128)(2,1)} %bitcast.393), channel_id=1, source_target_pairs={{0,24},{4,28},{8,16},{12,20},{16,8},{20,12},{24,0},{28,4},{1,25},{... | collective-permute-start | bytes 1179656 | tf_op jit(solution)/shard_map/ppermute | solution.py:626
  785.1 86.8 %collective-permute-start.37 = (bf16[512,384]{0,1:T(8,128)(2,1)S(1)}, bf16[512,384]{0,1:T(8,128)(2,1)}, u32[]{:S(2)}, u32[]{:S(2)}) collective-permute-start(bf16[512,384]{0,1:T(8,128)(2,1)S(1)} %bitcast.392), channel_id=1, source_target_pairs={{0,20},{4,16},{8,28},{12,24},{16,4},{20,0},{24,12},{28,8},{1,21},{... | collective-permute-start | bytes 1179656 | tf_op jit(solution)/shard_map/ppermute | solution.py:626
  786.8 89.4 %collective-permute-start.38 = (bf16[512,384]{0,1:T(8,128)(2,1)S(1)}, bf16[512,384]{0,1:T(8,128)(2,1)}, u32[]{:S(2)}, u32[]{:S(2)}) collective-permute-start(bf16[512,384]{0,1:T(8,128)(2,1)S(1)} %bitcast.391), channel_id=1, source_target_pairs={{0,16},{4,20},{8,24},{12,28},{16,0},{20,4},{24,8},{28,12},{1,17},{... | collective-permute-start | bytes 1179656 | tf_op jit(solution)/shard_map/ppermute | solution.py:626
  797.4 326.9 %reduce-scatter.10.cloned.1.call-start = ((), (), s32[]{:S(2)}) async-start(), calls=%async_computation.10 | async-start | bytes 1114112 | tf_op jit(solution)/shard_map/reduce_scatter | solution.py:655
  994.4 196.6 %reduce-scatter.6.cloned.1.call-start = ((), (), s32[]{:S(2)}) async-start(), calls=%async_computation.8 | async-start | bytes 2228224 | tf_op jit(solution)/shard_map/reduce_scatter | solution.py:655
  1011.4 313.2 %reduce-scatter.8.cloned.1.call-start = ((), (), s32[]{:S(2)}) async-start(), calls=%async_computation.9 | async-start | bytes 3342336 | tf_op jit(solution)/shard_map/reduce_scatter | solution.py:655
  1022.5 319.7 %all-gather.15.cloned.1.call-start = ((), (), s32[]{:S(2)}) async-start(), calls=%async_computation.14 | async-start | bytes 1310720 | tf_op jit(solution)/shard_map/all_gather | solution.py:656
  1023.2 337.2 %all-gather.13.cloned.1.call-start = ((), (), s32[]{:S(2)}) async-start(), calls=%async_computation.12 | async-start | bytes 1310720 | tf_op jit(solution)/shard_map/all_gather | solution.py:656
  (99 other events, 1781.1 us)
Sparse Core Ops, SparseCore 0:
  165.1 115.6 all-gather.6
  283.6 100.1 all-gather.10
  386.7 87.9 all-gather.8
  641.7 110.3 reduce-scatter.13
  797.6 132.7 reduce-scatter.11
  994.5 116.2 reduce-scatter.9
  1113.7 77.1 reduce-scatter.5
  1196.7 127.8 reduce-scatter.7
  1326.3 15.8 all-gather.14
  1343.7 16.7 all-gather.12

commit v4 on v3

--- a/solution.py
+++ b/solution.py
@@ -10,7 +10,6 @@
 LOG2E = 1.4426950408889634
 LN2 = 0.6931471805599453
 MASKED = -1e30
-RANGE = 100.0
 BF = jnp.bfloat16
 F32 = jnp.float32
 VMEM_LIMIT = 60 * 2**20
@@ -32,97 +31,6 @@
 
 def lanes_of(rows):
     return lax.broadcasted_iota(jnp.int32, (rows, 128), 1)
-
-
-def flash_forward_kernel(len_ref, q_ref, k_ref, v_ref, o_ref, lse_ref, ka, kb, vta, vtb, mean_ref, top_ref, *, bq, bk):
-    step = pl.program_id(0)
-    length = len_ref[0]
-    frames = k_ref.shape[0]
-
-    @pl.when(step == 0)
-    def _():
-        def build(j, carry):
-            rows = pl.ds(pl.multiple_of(j * bk, bk), bk)
-            lane = lanes_of(bk)
-            pos = j * bk + lax.broadcasted_iota(jnp.int32, (bk, 128), 0)
-            bias = jnp.where(pos < length, 0.0, MASKED)
-            keys = k_ref[rows, :].astype(F32)
-            ka[rows, :] = jnp.where(lane < 64, keys, jnp.where(lane == 64, bias, jnp.where(lane == 65, 1.0, 0.0))).astype(BF)
-            kb[rows, :] = jnp.where(lane >= 64, keys, jnp.where(lane == 0, bias, jnp.where(lane == 1, 1.0, 0.0))).astype(BF)
-            vals = v_ref[rows, :].astype(F32)
-            vta[:, rows] = jnp.where(lane < 64, vals, 1.0).T.astype(BF)
-            vtb[:, rows] = jnp.where(lane >= 64, vals, 1.0).T.astype(BF)
-            keys = jnp.where(pos < length, keys, 0.0)
-            norm_a, norm_b = head_sums(keys * keys, lane)
-            total, top_a, top_b = carry
-            return (
-                total + jnp.sum(keys, axis=0, keepdims=True),
-                jnp.maximum(top_a, jnp.max(norm_a)),
-                jnp.maximum(top_b, jnp.max(norm_b)),
-            )
-
-        total, top_a, top_b = lax.fori_loop(
-            0, frames // bk, build, (jnp.zeros((1, 128), F32), jnp.float32(0.0), jnp.float32(0.0))
-        )
-        mean_ref[0:1, :] = total / length.astype(F32)
-        top_ref[0] = top_a
-        top_ref[1] = top_b
-
-    lane = lanes_of(bq)
-    queries = q_ref[...].astype(F32)
-    bounds = [
-        jnp.sqrt(jnp.max(norm) * top_ref[head]) * 1.001
-        for head, norm in enumerate(head_sums(queries * queries, lane))
-    ]
-    shifts = [jnp.maximum(bound - RANGE, 0.0) for bound in bounds]
-    lows = [jnp.min(low) for low in head_sums(queries * mean_ref[0:1, :], lane)]
-    tame = jnp.logical_and(lows[0] - shifts[0] >= -RANGE, lows[1] - shifts[1] >= -RANGE)
-    qa = jnp.where(lane < 64, queries, jnp.where(lane == 64, 1.0, jnp.where(lane == 65, -shifts[0], 0.0)))
-    qb = jnp.where(lane >= 64, queries, jnp.where(lane == 0, 1.0, jnp.where(lane == 1, -shifts[1], 0.0)))
-    qa, qb = qa.astype(BF), qb.astype(BF)
-
-    def body(j, carry):
-        rows = pl.ds(pl.multiple_of(j * bk, bk), bk)
-        out = []
-        scores = [nt(ka[rows, :], qa), nt(kb[rows, :], qb)]
-        for score, vt, (top, acc) in zip(scores, (vta, vtb), carry):
-            new = jnp.maximum(top, jnp.max(score, axis=0, keepdims=True))
-            probs = jnp.exp2(score - new).astype(BF)
-            acc = acc * jnp.exp2(top - new) + nn(vt[:, rows], probs)
-            out.append((new, acc))
-        return tuple(out)
-
-    live = (length + bk - 1) // bk
-
-    def finish(shift_a, acc_a, shift_b, acc_b):
-        sum_a, sum_b = acc_a[64:65], acc_b[0:1]
-        both = jnp.concatenate([acc_a[:64] / sum_a, acc_b[64:] / sum_b], axis=0)
-        o_ref[...] = both.T.astype(BF)
-        lse_ref[...] = jnp.concatenate(
-            [shift_a + jnp.log2(sum_a), shift_b + jnp.log2(sum_b), jnp.zeros((6, bq), F32)], axis=0
-        )
-
-    @pl.when(tame)
-    def _():
-        def plain(j, carry):
-            rows = pl.ds(pl.multiple_of(j * bk, bk), bk)
-            out = []
-            for keys, query, vt, acc in ((ka, qa, vta, carry[0]), (kb, qb, vtb, carry[1])):
-                probs = jnp.exp2(nt(keys[rows, :], query)).astype(BF)
-                out.append(acc + nn(vt[:, rows], probs))
-            return tuple(out)
-
-        start = jnp.zeros((128, bq), F32)
-        acc_a, acc_b = lax.fori_loop(0, live, plain, (start, start))
-        rounded = [shift.astype(BF).astype(F32) for shift in shifts]
-        finish(rounded[0], acc_a, rounded[1], acc_b)
-
-    @pl.when(jnp.logical_not(tame))
-    def _():
-        start = (jnp.full((1, bq), MASKED, F32), jnp.zeros((128, bq), F32))
-        (top_a, acc_a), (top_b, acc_b) = lax.fori_loop(0, live, body, (start, start))
-        rounded = [shift.astype(BF).astype(F32) for shift in shifts]
-        finish(rounded[0] + top_a, acc_a, rounded[1] + top_b, acc_b)
 
 
 def attention_cost(frames, products):
@@ -131,41 +39,6 @@
         bytes_accessed=frames * 128 * 2 * 8,
         transcendentals=2 * frames * frames,
     )
-
-
-def flash_forward(length, qkv, bq, bk):
-    frames = qkv.shape[0]
-    return pl.pallas_call(
-        functools.partial(flash_forward_kernel, bq=bq, bk=bk),
-        grid_spec=pltpu.PrefetchScalarGridSpec(
-            num_scalar_prefetch=1,
-            grid=(frames // bq,),
-            in_specs=[
-                pl.BlockSpec((bq, 128), lambda i, *_: (i, 0)),
-                pl.BlockSpec((frames, 128), lambda i, *_: (0, 1)),
-                pl.BlockSpec((frames, 128), lambda i, *_: (0, 2)),
-            ],
-            out_specs=[
-                pl.BlockSpec((bq, 128), lambda i, *_: (i, 0)),
-                pl.BlockSpec((8, bq), lambda i, *_: (0, i)),
-            ],
-            scratch_shapes=[
-                pltpu.VMEM((frames, 128), BF),
-                pltpu.VMEM((frames, 128), BF),
-                pltpu.VMEM((128, frames), BF),
-                pltpu.VMEM((128, frames), BF),
-                pltpu.VMEM((8, 128), F32),
-                pltpu.SMEM((2,), F32),
-            ],
-        ),
-        out_shape=[
-            jax.ShapeDtypeStruct((frames, 128), BF),
-            jax.ShapeDtypeStruct((8, frames), F32),
-        ],
-        compiler_params=pltpu.CompilerParams(vmem_limit_bytes=VMEM_LIMIT),
-        cost_estimate=attention_cost(frames, 2),
-        name="attend_forward",
-    )(length, qkv, qkv, qkv)
 
 
 def turn_back(grad, cos, sin):
@@ -182,116 +55,494 @@
     return jnp.where(lane == at, -high, jnp.where(lane == at + 1, -mid, jnp.where(lane == at + 2, -low, 0.0)))
 
 
-def flash_backward_kernel(
-    len_ref, q_ref, k_ref, v_ref, o_ref, do_ref, lse_ref, cos_ref, sin_ref,
-    g_ref, ka, kb, va, vb, dkt, dvt, *, bq, bk,
+MESH_IDS = pl.DeviceIdType.MESH
+
+
+def seq_flip(flip):
+    return (lax.axis_index("seq") ^ flip, lax.axis_index("x"), lax.axis_index("core"))
+
+
+def greet(devices):
+    barrier = pltpu.get_barrier_semaphore()
+    for device in devices:
+        pl.semaphore_signal(barrier, inc=1, device_id=device, device_id_type=MESH_IDS)
+    pl.semaphore_wait(barrier, len(devices))
+
+
+def remote(source, target, send, recv, device):
+    return pltpu.make_async_remote_copy(
+        source, target, send, recv, device_id=device, device_id_type=MESH_IDS
+    )
+
+
+class WeightGather:
+    def __init__(self, jobs, send, recv, local):
+        self.jobs, self.send, self.recv, self.local = jobs, send, recv, local
+        me, x, core = lax.axis_index("seq"), lax.axis_index("x"), lax.axis_index("core")
+        self.bits = (me // 4, (me // 2) % 2, me % 2, x, core)
+        self.copies = [[] for _ in jobs]
+        self.owns = []
+
+    def peer(self, dim):
+        me, x, core = lax.axis_index("seq"), lax.axis_index("x"), lax.axis_index("core")
+        if dim < 3:
+            return (me ^ (4 >> dim), x, core)
+        return (me, 1 - x, core) if dim == 3 else (me, x, 1 - core)
+
+    def stage(self):
+        for index, (full, cols, source, order) in enumerate(self.jobs):
+            at = len(self.copies[index])
+            tail = (slice(None), cols)
+            if at == 0:
+                own = pltpu.make_async_copy(
+                    source, full.at[self.bits + tail], self.local.at[index]
+                )
+                own.start()
+                self.owns.append(own)
+            else:
+                if at == 1:
+                    self.owns[index].wait()
+                self.copies[index][at - 1].wait_recv()
+            where = tuple(
+                slice(None) if d in order[:at] else self.bits[d] for d in range(5)
+            ) + tail
+            copy = remote(
+                source if at == 0 else full.at[where],
+                full.at[where],
+                self.send.at[index * 5 + at],
+                self.recv.at[index * 5 + at],
+                self.peer(order[at]),
+            )
+            copy.start()
+            self.copies[index].append(copy)
+
+    def finish(self):
+        for chain in self.copies:
+            chain[-1].wait_recv()
+        for chain in self.copies:
+            for copy in chain:
+                copy.wait_send()
+
+
+def gather_jobs(weights, fulls):
+    quarter = lax.axis_index("x") * 2 + lax.axis_index("core")
+    jobs = []
+    for weight, full in zip(weights, fulls):
+        rows, width = weight.shape
+        span, half = rows // 4, width // 2
+        for side in range(2):
+            cols = pl.ds(side * half, half)
+            source = weight.at[pl.ds(quarter * span, span), cols]
+            jobs.append((full, cols, source, (0, 1, 2, 3, 4) if side == 0 else (0, 1, 3, 2, 4)))
+    return jobs
+
+
+def attend_forward_kernel(
+    len_ref, proj, out_w, up_w, down_w,
+    qkv_all, o_all, lse_ref, att, out_full, up_full, down_full,
+    qkv, outs, ka, kb, vta, vtb,
+    wsend, wrecv, wlocal, qsend, qrecv, qlocal, osend, orecv, olocal, slocal,
+    *, span, bq, bk,
 ):
-    step = pl.program_id(0)
-    steps = pl.num_programs(0)
-    length = len_ref[0]
-    frames = k_ref.shape[0]
-
-    @pl.when(step == 0)
-    def _():
+    me, x, core = lax.axis_index("seq"), lax.axis_index("x"), lax.axis_index("core")
+    frames = qkv.shape[2]
+    mine = pl.ds(pl.multiple_of(me * span, span), span)
+    my_cols = pl.ds(pl.multiple_of(me * 128, 128), 128)
+    flips = (7, 6, 5, 4, 3, 2, 1)
+    greet([seq_flip(flip) for flip in flips] + [(me, 1 - x, core), (me, x, 1 - core)])
+    weights = WeightGather(
+        gather_jobs((out_w, up_w, down_w), (out_full, up_full, down_full)), wsend, wrecv, wlocal
+    )
+
+    def send_heads(utt):
+        rows = pl.ds(utt * span, span)
+        own = pltpu.make_async_copy(
+            proj.at[:, rows, my_cols], qkv.at[utt, :, mine, :], qlocal.at[utt]
+        )
+        own.start()
+        copies = []
+        for flip in flips:
+            there = me ^ flip
+            cols = pl.ds(pl.multiple_of(there * 128, 128), 128)
+            copy = remote(
+                proj.at[:, rows, cols],
+                qkv.at[utt, :, mine, :],
+                qsend.at[utt * 8 + flip],
+                qrecv.at[utt * 8 + flip],
+                seq_flip(flip),
+            )
+            copy.start()
+            copies.append(copy)
+        return own, copies
+
+    def arrive(sent):
+        own, copies = sent
+        own.wait()
+        for copy in copies:
+            copy.wait_recv()
+
+    def attend(utt, between):
+        length = len_ref[utt]
+        save = pltpu.make_async_copy(qkv.at[utt], qkv_all.at[utt], slocal.at[utt])
+        save.start()
+
         def build(j, carry):
             rows = pl.ds(pl.multiple_of(j * bk, bk), bk)
             lane = lanes_of(bk)
             pos = j * bk + lax.broadcasted_iota(jnp.int32, (bk, 128), 0)
             bias = jnp.where(pos < length, 0.0, MASKED)
-            keys = k_ref[rows, :].astype(F32)
-            vals = v_ref[rows, :].astype(F32)
+            keys = qkv[utt, 1, rows, :].astype(F32)
+            ka[rows, :] = jnp.where(lane < 64, keys, jnp.where(lane == 64, bias, 0.0)).astype(BF)
+            kb[rows, :] = jnp.where(lane >= 64, keys, jnp.where(lane == 0, bias, 0.0)).astype(BF)
+            vals = qkv[utt, 2, rows, :].astype(F32)
+            vta[:, rows] = jnp.where(lane < 64, vals, 1.0).T.astype(BF)
+            vtb[:, rows] = jnp.where(lane >= 64, vals, 1.0).T.astype(BF)
+            return carry
+
+        lax.fori_loop(0, frames // bk, build, 0)
+
+        def block(i, carry):
+            here = pl.ds(pl.multiple_of(i * bq, bq), bq)
+            lane = lanes_of(bq)
+            queries = qkv[utt, 0, here, :].astype(F32)
+            qa = jnp.where(lane < 64, queries, jnp.where(lane == 64, 1.0, 0.0)).astype(BF)
+            qb = jnp.where(lane >= 64, queries, jnp.where(lane == 0, 1.0, 0.0)).astype(BF)
+
+            def body(j, inner):
+                rows = pl.ds(pl.multiple_of(j * bk, bk), bk)
+                result = []
+                scores = [nt(ka[rows, :], qa), nt(kb[rows, :], qb)]
+                for score, vt, (top, acc) in zip(scores, (vta, vtb), inner):
+                    new = jnp.maximum(top, jnp.max(score, axis=0, keepdims=True))
+                    probs = jnp.exp2(score - new).astype(BF)
+                    acc = acc * jnp.exp2(top - new) + nn(vt[:, rows], probs)
+                    result.append((new, acc))
+                return tuple(result)
+
+            start = (jnp.full((1, bq), MASKED, F32), jnp.zeros((128, bq), F32))
+            (top_a, acc_a), (top_b, acc_b) = lax.fori_loop(0, frames // bk, body, (start, start))
+            sum_a, sum_b = acc_a[64:65], acc_b[0:1]
+            both = jnp.concatenate([acc_a[:64] / sum_a, acc_b[64:] / sum_b], axis=0)
+            outs[utt, here, :] = both.T.astype(BF)
+            lse_ref[utt, :, here] = jnp.concatenate(
+                [top_a + jnp.log2(sum_a), top_b + jnp.log2(sum_b), jnp.zeros((6, bq), F32)],
+                axis=0,
+            )
+            for part in range(bq // span):
+                there = i * (bq // span) + part
+                rows = pl.ds(pl.multiple_of(there * span, span), span)
+                target = att.at[pl.ds(utt * span, span), my_cols]
+
+                @pl.when(there != me)
+                def _():
+                    remote(
+                        outs.at[utt, rows, :],
+                        target,
+                        osend.at[utt * 8 + (there ^ me)],
+                        orecv.at[utt * 8 + (there ^ me)],
+                        (there, x, core),
+                    ).start()
+
+                @pl.when(there == me)
+                def _():
+                    pltpu.make_async_copy(outs.at[utt, rows, :], target, olocal.at[utt]).start()
+
+            return carry
+
+        half = frames // bq // 2
+        lax.fori_loop(0, half, block, 0)
+        between()
+        lax.fori_loop(half, 2 * half, block, 0)
+        keep = pltpu.make_async_copy(outs.at[utt], o_all.at[utt], slocal.at[2 + utt])
+        keep.start()
+        return [save, keep]
+
+    weights.stage()
+    first = send_heads(0)
+    arrive(first)
+    second = send_heads(1)
+    weights.stage()
+    saves = attend(0, weights.stage)
+    weights.stage()
+    arrive(second)
+    saves += attend(1, weights.stage)
+    for sent in (first, second):
+        for copy in sent[1]:
+            copy.wait_send()
+    weights.finish()
+    for save in saves:
+        save.wait()
+    for utt in range(2):
+        target = att.at[pl.ds(utt * span, span), my_cols]
+        pltpu.make_async_copy(outs.at[utt, mine, :], target, olocal.at[utt]).wait()
+        for flip in flips:
+            copy = remote(
+                outs.at[utt, mine, :],
+                target,
+                osend.at[utt * 8 + flip],
+                orecv.at[utt * 8 + flip],
+                seq_flip(flip),
+            )
+            copy.wait_send()
+            copy.wait_recv()
+
+
+def attend_forward(lengths, proj, out_w, up_w, down_w, span, bq=1024, bk=512):
+    rows, width = proj.shape[1:]
+    frames = 8 * span
+    anywhere = pl.BlockSpec(memory_space=pl.ANY)
+    vmem = pl.BlockSpec(memory_space=pltpu.VMEM)
+    full = lambda w: jax.ShapeDtypeStruct((2, 2, 2, 2, 2, w.shape[0] // 4, w.shape[1]), BF)
+    dma = pltpu.SemaphoreType.DMA
+    outs = pl.pallas_call(
+        functools.partial(attend_forward_kernel, span=span, bq=bq, bk=bk),
+        in_specs=[pl.BlockSpec(memory_space=pltpu.SMEM)] + [anywhere] * 4,
+        out_specs=[anywhere, anywhere, vmem] + [anywhere] * 4,
+        out_shape=[
+            jax.ShapeDtypeStruct((2, 3, frames, 128), BF),
+            jax.ShapeDtypeStruct((2, frames, 128), BF),
+            jax.ShapeDtypeStruct((2, 8, frames), F32),
+            jax.ShapeDtypeStruct((rows, width), BF),
+            full(out_w),
+            full(up_w),
+            full(down_w),
+        ],
+        scratch_shapes=[
+            pltpu.VMEM((2, 3, frames, 128), BF),
+            pltpu.VMEM((2, frames, 128), BF),
+            pltpu.VMEM((frames, 128), BF),
+            pltpu.VMEM((frames, 128), BF),
+            pltpu.VMEM((128, frames), BF),
+            pltpu.VMEM((128, frames), BF),
+            dma((30,)),
+            dma((30,)),
+            dma((6,)),
+            dma((16,)),
+            dma((16,)),
+            dma((2,)),
+            dma((16,)),
+            dma((16,)),
+            dma((2,)),
+            dma((4,)),
+        ],
+        compiler_params=pltpu.CompilerParams(
+            vmem_limit_bytes=VMEM_LIMIT, collective_id=1, has_side_effects=True
+        ),
+        cost_estimate=attention_cost(frames, 4),
+        name="attend_forward",
+    )(lengths, proj, out_w, up_w, down_w)
+    fulls = [outs[4 + i].reshape(8 * w.shape[0], w.shape[1]) for i, w in enumerate((out_w, up_w, down_w))]
+    return outs[:4], fulls
+
+
+def attend_backward_kernel(
+    len_ref, dout, qkv_all, o_all, lse_ref, cos_ref, sin_ref,
+    grads,
+    qkv, outs, douts, qa, qb, da, db, qt, dt, dqa, dqb,
+    dsend, drecv, dlocal, gsend, grecv, glocal, load,
+    *, span, block,
+):
+    me, x, core = lax.axis_index("seq"), lax.axis_index("x"), lax.axis_index("core")
+    frames = qkv.shape[2]
+    width = grads.shape[1] // 3
+    count = frames // block
+    mine = pl.ds(pl.multiple_of(me * span, span), span)
+    flips = (7, 6, 5, 4, 3, 2, 1)
+    greet([seq_flip(flip) for flip in flips])
+    loads = []
+    for utt in range(2):
+        loads.append(
+            [
+                pltpu.make_async_copy(qkv_all.at[utt], qkv.at[utt], load.at[utt]),
+                pltpu.make_async_copy(o_all.at[utt], outs.at[utt], load.at[2 + utt]),
+            ]
+        )
+        for copy in loads[-1]:
+            copy.start()
+
+    def send_heads(utt):
+        rows = pl.ds(utt * span, span)
+        my_cols = pl.ds(pl.multiple_of(me * 128, 128), 128)
+        own = pltpu.make_async_copy(dout.at[rows, my_cols], douts.at[utt, mine, :], dlocal.at[utt])
+        own.start()
+        copies = []
+        for flip in flips:
+            cols = pl.ds(pl.multiple_of((me ^ flip) * 128, 128), 128)
+            copy = remote(
+                dout.at[rows, cols],
+                douts.at[utt, mine, :],
+                dsend.at[utt * 8 + flip],
+                drecv.at[utt * 8 + flip],
+                seq_flip(flip),
+            )
+            copy.start()
+            copies.append(copy)
+        return own, copies
+
+    def arrive(sent):
+        own, copies = sent
+        own.wait()
+        for copy in copies:
+            copy.wait_recv()
+
+    def slot(utt, part, flip):
+        return (utt * 3 + part) * 8 + flip
+
+    def target(utt, part):
+        cols = pl.ds(pl.multiple_of(part * width + me * 128, 128), 128)
+        return grads.at[pl.ds(utt * span, span), cols]
+
+    def send_grads(utt, part, there):
+        rows = pl.ds(pl.multiple_of(there * span, span), span)
+
+        @pl.when(there != me)
+        def _():
+            at = slot(utt, part, there ^ me)
+            remote(
+                qkv.at[utt, part, rows, :],
+                target(utt, part),
+                gsend.at[at],
+                grecv.at[at],
+                (there, x, core),
+            ).start()
+
+        @pl.when(there == me)
+        def _():
+            pltpu.make_async_copy(
+                qkv.at[utt, part, rows, :], target(utt, part), glocal.at[utt * 3 + part]
+            ).start()
+
+    def differentiate(utt):
+        length = len_ref[utt]
+
+        def build(j, carry):
+            rows = pl.ds(pl.multiple_of(j * block, block), block)
+            lane = lanes_of(block)
+            queries = qkv[utt, 0, rows, :].astype(F32)
+            grad = douts[utt, rows, :].astype(F32)
+            delta_a, delta_b = head_sums(grad * outs[utt, rows, :].astype(F32), lane)
+            lse = lse_ref[utt, :, rows].T
+            one_a, one_b = lse[:, 0:1], lse[:, 1:2]
+            qa[rows, :] = jnp.where(
+                lane < 64, queries, jnp.where(lane == 67, 1.0, three(one_a, lane, 64))
+            ).astype(BF)
+            qb[rows, :] = jnp.where(
+                lane >= 64, queries, jnp.where(lane == 3, 1.0, three(one_b, lane, 0))
+            ).astype(BF)
+            da[rows, :] = jnp.where(lane < 64, grad, three(delta_a, lane, 64)).astype(BF)
+            db[rows, :] = jnp.where(lane >= 64, grad, three(delta_b, lane, 0)).astype(BF)
+            qt[:, rows] = queries.T.astype(BF)
+            dt[:, rows] = grad.T.astype(BF)
+            dqa[rows, :] = jnp.zeros((block, 128), F32)
+            dqb[rows, :] = jnp.zeros((block, 128), F32)
+            return carry
+
+        lax.fori_loop(0, count, build, 0)
+
+        def keys_block(i, carry):
+            here = pl.ds(pl.multiple_of(i * block, block), block)
+            lane = lanes_of(block)
+            pos = i * block + lax.broadcasted_iota(jnp.int32, (block, 128), 0)
+            bias = jnp.where(pos < length, 0.0, MASKED)
+            keys = qkv[utt, 1, here, :].astype(F32)
+            vals = qkv[utt, 2, here, :].astype(F32)
             ones_a = jnp.where(lane < 67, 1.0, 0.0)
             ones_b = jnp.where(lane < 3, 1.0, 0.0)
-            ka[rows, :] = jnp.where(lane < 64, keys, jnp.where(lane == 67, bias, ones_a)).astype(BF)
-            kb[rows, :] = jnp.where(lane >= 64, keys, jnp.where(lane == 3, bias, ones_b)).astype(BF)
-            va[rows, :] = jnp.where(lane < 64, vals, ones_a).astype(BF)
-            vb[rows, :] = jnp.where(lane >= 64, vals, ones_b).astype(BF)
+            ka = jnp.where(lane < 64, keys, jnp.where(lane == 67, bias, ones_a)).astype(BF)
+            kb = jnp.where(lane >= 64, keys, jnp.where(lane == 3, bias, ones_b)).astype(BF)
+            va = jnp.where(lane < 64, vals, ones_a).astype(BF)
+            vb = jnp.where(lane >= 64, vals, ones_b).astype(BF)
+
+            def body(j, inner):
+                rows = pl.ds(pl.multiple_of(j * block, block), block)
+                result = []
+                for head, (qh, dh, kh, vh, dq) in enumerate(
+                    ((qa, da, ka, va, dqa), (qb, db, kb, vb, dqb))
+                ):
+                    part = slice(head * 64, head * 64 + 64)
+                    probs = jnp.exp2(nt(qh[rows, :], kh))
+                    grad = (probs * nt(dh[rows, :], vh)).astype(BF)
+                    dv = inner[2 * head + 1] + nn(dt[:, rows], probs.astype(BF))[part]
+                    dk = inner[2 * head] + nn(qt[:, rows], grad)[part]
+                    dq[rows, :] += nn(grad, kh)
+                    result += [dk, dv]
+                return tuple(result)
+
+            zero = jnp.zeros((64, block), F32)
+            dk_a, dv_a, dk_b, dv_b = lax.fori_loop(0, count, body, (zero,) * 4)
+            dk = jnp.concatenate([dk_a, dk_b], axis=0).T * LN2
+            dv = jnp.concatenate([dv_a, dv_b], axis=0).T
+            qkv[utt, 1, here, :] = turn_back(dk, cos_ref[here, :], sin_ref[here, :]).astype(BF)
+            qkv[utt, 2, here, :] = dv.astype(BF)
+            for step in range(block // span):
+                there = i * (block // span) + step
+                send_grads(utt, 1, there)
+                send_grads(utt, 2, there)
             return carry
 
-        lax.fori_loop(0, frames // bk, build, 0)
-        dkt[...] = jnp.zeros_like(dkt)
-        dvt[...] = jnp.zeros_like(dvt)
-
-    @pl.when(step * bq >= length)
-    def _():
-        rows = pl.ds(pl.multiple_of(step * bq, bq), bq)
-        g_ref[rows, 0:128] = jnp.zeros((bq, 128), BF)
-
-    @pl.when(step * bq < length)
-    def _():
-        lane = lanes_of(bq)
-        queries = q_ref[...].astype(F32)
-        dout = do_ref[...].astype(F32)
-        product = dout * o_ref[...].astype(F32)
-        delta_a, delta_b = head_sums(product, lane)
-        lse = lse_ref[...].T
-        qa = jnp.where(lane < 64, queries, jnp.where(lane == 67, 1.0, three(lse[:, 0:1], lane, 64))).astype(BF)
-        qb = jnp.where(lane >= 64, queries, jnp.where(lane == 3, 1.0, three(lse[:, 1:2], lane, 0))).astype(BF)
-        da = jnp.where(lane < 64, dout, three(delta_a, lane, 64)).astype(BF)
-        db = jnp.where(lane >= 64, dout, three(delta_b, lane, 0)).astype(BF)
-        qt = queries.T.astype(BF)
-        dt = dout.T.astype(BF)
-
-        def body(j, carry):
-            rows = pl.ds(pl.multiple_of(j * bk, bk), bk)
-            out = []
-            for head, (qh, dh, kh, vh, dq) in enumerate(((qa, da, ka, va, carry[0]), (qb, db, kb, vb, carry[1]))):
-                part = slice(head * 64, head * 64 + 64)
-                keys = kh[rows, :]
-                probs = jnp.exp2(nt(qh, keys))
-                grad = (probs * nt(dh, vh[rows, :])).astype(BF)
-                dvt[part, rows] += nn(dt, probs.astype(BF))[part]
-                dkt[part, rows] += nn(qt, grad)[part]
-                out.append(dq + nn(grad, keys))
-            return tuple(out)
-
-        start = jnp.zeros((bq, 128), F32)
-        live = (length + bk - 1) // bk
-        dq_a, dq_b = lax.fori_loop(0, live, body, (start, start))
-        dq = jnp.where(lane < 64, dq_a, dq_b) * 0.125
-        rows = pl.ds(pl.multiple_of(step * bq, bq), bq)
-        g_ref[rows, 0:128] = turn_back(dq, cos_ref[rows, :], sin_ref[rows, :]).astype(BF)
-
-    @pl.when(step == steps - 1)
-    def _():
-        def finish(j, carry):
-            rows = pl.ds(pl.multiple_of(j * bk, bk), bk)
-            dk = dkt[:, rows].T * LN2
-            g_ref[rows, 128:256] = turn_back(dk, cos_ref[rows, :], sin_ref[rows, :]).astype(BF)
-            g_ref[rows, 256:384] = dvt[:, rows].T.astype(BF)
+        lax.fori_loop(0, count, keys_block, 0)
+
+        def finish(i, carry):
+            here = pl.ds(pl.multiple_of(i * block, block), block)
+            lane = lanes_of(block)
+            dq = jnp.where(lane < 64, dqa[here, :], dqb[here, :]) * 0.125
+            qkv[utt, 0, here, :] = turn_back(dq, cos_ref[here, :], sin_ref[here, :]).astype(BF)
+            for step in range(block // span):
+                send_grads(utt, 0, i * (block // span) + step)
             return carry
 
-        lax.fori_loop(0, frames // bk, finish, 0)
-
-
-def flash_backward(length, qkv, out, dout, lse, cos, sin, bq, bk):
-    frames = qkv.shape[0]
-    part = pl.BlockSpec((bq, 128), lambda i, *_: (i, 0))
-    whole = pl.BlockSpec((frames, 128), lambda i, *_: (0, 0))
+        lax.fori_loop(0, count, finish, 0)
+
+    first = send_heads(0)
+    for copy in loads[0]:
+        copy.wait()
+    arrive(first)
+    second = send_heads(1)
+    differentiate(0)
+    for copy in loads[1]:
+        copy.wait()
+    arrive(second)
+    differentiate(1)
+    for sent in (first, second):
+        for copy in sent[1]:
+            copy.wait_send()
+    for utt in range(2):
+        for part in range(3):
+            own = qkv.at[utt, part, mine, :]
+            pltpu.make_async_copy(own, target(utt, part), glocal.at[utt * 3 + part]).wait()
+            for flip in flips:
+                at = slot(utt, part, flip)
+                copy = remote(own, target(utt, part), gsend.at[at], grecv.at[at], seq_flip(flip))
+                copy.wait_send()
+                copy.wait_recv()
+
+
+def attend_backward(lengths, dout, qkv_all, o_all, lse, cos, sin, span, block=1024):
+    frames = 8 * span
+    rows, width = dout.shape
+    anywhere = pl.BlockSpec(memory_space=pl.ANY)
+    vmem = pl.BlockSpec(memory_space=pltpu.VMEM)
+    dma = pltpu.SemaphoreType.DMA
     return pl.pallas_call(
-        functools.partial(flash_backward_kernel, bq=bq, bk=bk),
-        grid_spec=pltpu.PrefetchScalarGridSpec(
-            num_scalar_prefetch=1,
-            grid=(frames // bq,),
-            in_specs=[
-                part,
-                pl.BlockSpec((frames, 128), lambda i, *_: (0, 1)),
-                pl.BlockSpec((frames, 128), lambda i, *_: (0, 2)),
-                part,
-                part,
-                pl.BlockSpec((8, bq), lambda i, *_: (0, i)),
-                whole,
-                whole,
-            ],
-            out_specs=pl.BlockSpec((frames, 384), lambda i, *_: (0, 0)),
-            scratch_shapes=[pltpu.VMEM((frames, 128), BF)] * 4
-            + [pltpu.VMEM((128, frames), F32)] * 2,
+        functools.partial(attend_backward_kernel, span=span, block=block),
+        in_specs=[pl.BlockSpec(memory_space=pltpu.SMEM)] + [anywhere] * 3 + [vmem] * 3,
+        out_specs=anywhere,
+        out_shape=jax.ShapeDtypeStruct((rows, 3 * width), BF),
+        scratch_shapes=[
+            pltpu.VMEM((2, 3, frames, 128), BF),
+            pltpu.VMEM((2, frames, 128), BF),
+            pltpu.VMEM((2, frames, 128), BF),
+        ]
+        + [pltpu.VMEM((frames, 128), BF)] * 4
+        + [pltpu.VMEM((128, frames), BF)] * 2
+        + [pltpu.VMEM((frames, 128), F32)] * 2
+        + [dma((16,)), dma((16,)), dma((2,)), dma((48,)), dma((48,)), dma((6,)), dma((4,))],
+        compiler_params=pltpu.CompilerParams(
+            vmem_limit_bytes=VMEM_LIMIT, collective_id=2, has_side_effects=True
         ),
-        out_shape=jax.ShapeDtypeStruct((frames, 384), BF),
-        compiler_params=pltpu.CompilerParams(vmem_limit_bytes=VMEM_LIMIT),
-        cost_estimate=attention_cost(frames, 5),
+        cost_estimate=attention_cost(frames, 10),
         name="attend_backward",
-    )(length, qkv, qkv, qkv, out, dout, lse, cos, sin)
+    )(lengths, dout, qkv_all, o_all, lse, cos, sin)
 
 
 def layer_norm(stream):
@@ -521,7 +772,7 @@
 
 def project_kernel(x_ref, w_ref, cos_ref, sin_ref, out_ref):
     projected = nn(x_ref[...], w_ref[...])
-    groups = out_ref.shape[0]
+    groups = out_ref.shape[2] // 128
     rows = x_ref.shape[0]
     lane = lanes_of(rows)
     cos, sin = cos_ref[...], sin_ref[...]
@@ -536,22 +787,23 @@
                 piece = piece * cos + turned * sin
             if part == 0:
                 piece = piece * (0.125 * LOG2E)
-            out_ref[group, :, part * 128 : part * 128 + 128] = piece.astype(BF)
-
-
-def project_heads(x, weight, cos, sin, groups, block=256):
+            out_ref[part, :, group * 128 : group * 128 + 128] = piece.astype(BF)
+
+
+def project_heads(x, weight, cos, sin, block=256):
     rows, width = x.shape
+    steps = cos.shape[0] // block
     return pl.pallas_call(
         project_kernel,
         grid=(rows // block,),
         in_specs=[
             pl.BlockSpec((block, width), lambda i: (i, 0)),
             pl.BlockSpec(weight.shape, lambda i: (0, 0)),
-            pl.BlockSpec((block, 128), lambda i: (i, 0)),
-            pl.BlockSpec((block, 128), lambda i: (i, 0)),
+            pl.BlockSpec((block, 128), lambda i: (i % steps, 0)),
+            pl.BlockSpec((block, 128), lambda i: (i % steps, 0)),
         ],
-        out_specs=pl.BlockSpec((groups, block, 384), lambda i: (0, i, 0)),
-        out_shape=jax.ShapeDtypeStruct((groups, rows, 384), BF),
+        out_specs=pl.BlockSpec((3, block, width), lambda i: (0, i, 0)),
+        out_shape=jax.ShapeDtypeStruct((3, rows, width), BF),
         compiler_params=pltpu.CompilerParams(vmem_limit_bytes=VMEM_LIMIT),
         cost_estimate=pl.CostEstimate(
             flops=2 * rows * weight.size, bytes_accessed=2 * weight.size, transcendentals=0
@@ -610,22 +862,6 @@
 
 def batch_index():
     return lax.axis_index("x") * lax.axis_size("core") + lax.axis_index("core")
-
-
-def after(first, *later):
-    return lax.optimization_barrier((first,) + later)[1:]
-
-
-def exchange(pieces):
-    count = pieces.shape[0]
-    me = lax.axis_index("seq")
-    out = pieces
-    for flip in range(count - 1, 0, -1):
-        there = jnp.bitwise_xor(me, flip)
-        piece = lax.dynamic_index_in_dim(pieces, there, 0, keepdims=False)
-        got = lax.ppermute(piece, "seq", [(i, i ^ flip) for i in range(count)])
-        out = lax.dynamic_update_index_in_dim(out, got, there, 0)
-    return out
 
 
 def gather_weight(weight):
@@ -699,45 +935,10 @@
     for copy in small:
         copy.start()
 
-    jobs = []
-    for index, (weight, full, (rows, width)) in enumerate(zip(weights, fulls, shapes)):
-        span = rows // 4
-        half = width // 2
-        for side in range(2):
-            cols = pl.ds(side * half, half)
-            source = weight.at[pl.ds(quarter * span, span), cols]
-            order = (0, 1, 2, 3, 4) if side == 0 else (0, 1, 3, 2, 4)
-            jobs.append((full, cols, source, order))
-    owns = []
-    for index, (full, cols, source, order) in enumerate(jobs):
-        own = pltpu.make_async_copy(source, full.at[bits + (slice(None), cols)], local.at[2 + index])
-        own.start()
-        owns.append(own)
-    copies = [[None] * 5 for _ in jobs]
-    for stage in range(5):
-        for index, (full, cols, source, order) in enumerate(jobs):
-            dim = order[stage]
-            done = order[:stage]
-            where = tuple(slice(None) if d in done else bits[d] for d in range(5)) + (slice(None), cols)
-            if stage == 1:
-                owns[index].wait()
-            if stage:
-                copies[index][stage - 1].wait_recv()
-            copy = pltpu.make_async_remote_copy(
-                source if stage == 0 else full.at[where],
-                full.at[where],
-                send.at[index * 5 + stage],
-                recv.at[index * 5 + stage],
-                device_id=peer(dim),
-                device_id_type=pl.DeviceIdType.MESH,
-            )
-            copy.start()
-            copies[index][stage] = copy
-    for chain in copies:
-        chain[4].wait_recv()
-    for chain in copies:
-        for copy in chain:
-            copy.wait_send()
+    chain = WeightGather(gather_jobs(weights, fulls), send, recv, local.at[pl.ds(2, 2 * count)])
+    for _ in range(5):
+        chain.stage()
+    chain.finish()
     for copy in small:
         copy.wait()
     own_seq.wait()
@@ -801,7 +1002,13 @@
     seq_here = lax.axis_index("seq")
     seq_count = lax.axis_size("seq")
     frame_count = frame_span * seq_count
-    by_heads = head_count == 2 * seq_count and frame_count % 1024 == 0
+    by_heads = (
+        seq_count == 8
+        and head_count == 16
+        and utt_count == 2
+        and lax.axis_size(BATCH) == 4
+        and frame_span == 512
+    )
     local_pos = seq_here * frame_span + jnp.arange(frame_span, dtype=jnp.int32)
     local_live = local_pos[None, :] < lengths[:, None]
     valid_mask = local_live.astype(jnp.float32)
@@ -864,28 +1071,10 @@
         cos_all, sin_all = paired_tables(jnp.arange(frame_count, dtype=jnp.int32))
         cos_here = lax.dynamic_slice_in_dim(cos_all, seq_here * frame_span, frame_span, 0)
         sin_here = lax.dynamic_slice_in_dim(sin_all, seq_here * frame_span, frame_span, 0)
-        packed, attended_mine, lse_mine, attended_parts = [], [], [], []
-        sends = []
-        for utt in range(utt_count):
-            sent = project_heads(
-                normed_attn[utt * frame_span : (utt + 1) * frame_span],
-                qkv_full,
-                cos_here,
-                sin_here,
-                seq_count,
-            )
-            sends.append(sent)
-        late = after(tuple(sends), out_weight, up_weight, down_weight)
-        out_full, up_full, down_full = [gather_weight(weight) for weight in late]
-        for sent in sends:
-            packed.append(exchange(sent).reshape(frame_count, 384))
-        for utt in range(utt_count):
-            heads_out, lse = flash_forward(lengths[utt : utt + 1], packed[utt], 1024, 1024)
-            attended_mine.append(heads_out)
-            lse_mine.append(lse)
-            back = exchange(heads_out.reshape(seq_count, frame_span, 128))
-            attended_parts.append(back.transpose(1, 0, 2).reshape(frame_span, model_width))
-        attended_low = jnp.concatenate(attended_parts, axis=0)
+        proj = project_heads(normed_attn, qkv_full, cos_here, sin_here)
+        (qkv_all, out_all, lse_all, attended_low), (out_full, up_full, down_full) = attend_forward(
+            lengths, proj, out_weight, up_weight, down_weight, frame_span
+        )
     else:
         out_full, up_full, down_full = [
             gather_weight(weight) for weight in (out_weight, up_weight, down_weight)
@@ -955,26 +1144,9 @@
     grad_shift_ffn, grad_scale_ffn, grad_gate_attn = ffn_sums[:, 0], ffn_sums[:, 1], ffn_sums[:, 2]
     qkv_back, skip_back = qkv_full, skip_full
     if by_heads:
-        grad_parts = []
-        for utt in range(utt_count):
-            sent = grad_attended_flat[utt * frame_span : (utt + 1) * frame_span]
-            sent = sent.reshape(frame_span, seq_count, 128).transpose(1, 0, 2)
-            dout = exchange(sent).reshape(frame_count, 128)
-            grads = flash_backward(
-                lengths[utt : utt + 1],
-                packed[utt],
-                attended_mine[utt],
-                dout,
-                lse_mine[utt],
-                cos_all,
-                sin_all,
-                1024,
-                1024,
-            )
-            back = exchange(grads.reshape(seq_count, frame_span, 384))
-            back = back.reshape(seq_count, frame_span, 3, 128).transpose(1, 2, 0, 3)
-            grad_parts.append(back.reshape(frame_span, 3 * model_width))
-        grad_projected = jnp.concatenate(grad_parts, axis=0)
+        grad_projected = attend_backward(
+            lengths, grad_attended_flat, qkv_all, out_all, lse_all, cos_all, sin_all, frame_span
+        )
     else:
         grad_attended = grad_attended_flat.reshape(
             utt_count, frame_span, head_count, HEAD_DIM

time: 1380 us -> 1280 us (0.928)
  Pallas kernels: 426 us -> 769 us
  local copies, waits for them, and re-layouts: 238 us -> 53.7 us
  starting transfers between devices: 147 us -> 1.68 us
  waiting for transfers between devices: 327 us -> 230 us
    pallas_call x4 -> x2, Pallas kernels: 223 us -> 561 us  [the longest x1 301 us: attend_forward(): pl.pallas_call(functools.partial(attend_forward_kernel, span=span, bq=bq,...]
    ppermute x56 -> x0, starting transfers between devices: 145 us -> none  [exchange(): got = lax.ppermute(piece, 'seq', [(i, i ^ flip) for i in range(count)])]
    ppermute x56 -> x0, waiting for transfers between devices: 114 us -> none  [exchange(): got = lax.ppermute(piece, 'seq', [(i, i ^ flip) for i in range(count)])]
    dynamic_update_slice x54 -> x0, local copies, waits for them, and re-layouts: 107 us -> none  [exchange(): out = lax.dynamic_update_index_in_dim(out, got, there, 0)]
    all_gather x1, blocking collectives: 41.2 us -> 9.98 us  [on_device(): lax.all_gather(mod_total.astype(jnp.bfloat16), BATCH, axis=0, tiled=True)]
    psum x1, blocking collectives: 39.1 us -> 64.8 us  [on_device(): mod_total = lax.psum(grad_modulation, 'seq')]
    dynamic_slice x19 -> x0, local copies, waits for them, and re-layouts: 17.7 us -> none  [the longest x16 12.9 us: exchange(): piece = lax.dynamic_index_in_dim(pieces, there, 0, keepdims=False)]
    broadcast_in_dim x14 -> x0, local copies, waits for them, and re-layouts: 15.5 us -> none  [exchange(): out = lax.dynamic_update_index_in_dim(out, got, there, 0)]
  transfers between devices with their start and end apart: 71 -> 12, of which waited for: 21 -> 7; matrix products, arithmetic and copies ran while one was open for 20% -> 7% of each run, Pallas kernels for 16% -> 20%
where the time goes in v4:
time: 1280 us; the launch traced here: 1270 us
  Pallas kernels  769 us (60%)
  waiting for transfers between devices  230 us (18%)
  blocking collectives  98.1 us (8%)
  other arithmetic  53.8 us (4%)
  local copies, waits for them, and re-layouts  53.7 us (4%)
  matrix products  52 us (4%)
  between operations  16.5 us (1%)
    pallas_call x1, Pallas kernels, attend_forward(): pl.pallas_call(functools.partial(attend_forward_kernel, span=span, bq=bq,...  301 us
    pallas_call x1, Pallas kernels, attend_backward(): pl.pallas_call(functools.partial(attend_backward_kernel, span=span, block...  260 us
    reduce_scatter x5, waiting for transfers between devices, sum_weight(): lax.psum_scatter(half, ('seq', 'x'), scatter_dimension=0, tiled=True)  185 us
    pallas_call x1, Pallas kernels, gather_early(): pl.pallas_call(functools.partial(gather_kernel, shapes=shapes), in_specs=...  83.7 us
    pallas_call x1, Pallas kernels, ffn_backward(): pl.pallas_call(ffn_backward_kernel, grid=(hidden // chunk,), in_specs=who...  70 us
    psum x1, blocking collectives, on_device(): mod_total = lax.psum(grad_modulation, 'seq')  64.8 us
    pallas_call x1, Pallas kernels, ffn_forward(): pl.pallas_call(ffn_forward_kernel, grid=(hidden // chunk,), in_specs=whol...  42.6 us
  transfers between devices with their start and end apart: 12, of which 7 were waited for; matrix products, arithmetic and copies ran while one was open for 7% of the time, Pallas kernels for 20%

profile of v4, /device:TPU:0, one launch (start us, length us, event | category | flops | bytes accessed | tf_op | source)
XLA Modules:
  0.0 1274.4 jit_solution(14035470752781764717)
XLA Ops:
  13.8 83.7 %gather_early.1 = (bf16[2,2,2,2,2,64,1024]{6,5,4,3,2,1,0:T(8,128)(2,1)}, bf16[2,2,2,2,2,32,3072]{6,5,4,3,2,1,0:T(8,128)(2,1)}, f32[8,12,1024]{2,1,0:T(8,128)}, f32[4,8,1024]{2,1,0:T(8,128)}) custom-call(bf16[256,1024]{1,0:T(8,128)(2,1)} %refs_0_.1, bf16[128,3072]{1,0:T(8,128)(2,1)} %refs_1_.1, f32[12,1024]{1,0:T(8,128)} %reshape.281.refs_2_, ...), custom_call_target="tpu_custom_call" | custom-call | tf_op jit(solution)/shard_map/gather_early/pallas_call | solution.py:952
  131.9 7.7 fusion.23
  150.3 11.6 project_heads.1.proj
  161.8 301.0 %attend_forward.1 = (bf16[2,3,4096,128]{3,2,1,0:T(8,128)(2,1)}, bf16[2,4096,128]{2,1,0:T(8,128)(2,1)}, f32[2,8,4096]{2,1,0:T(8,128)}, bf16[1024,1024]{1,0:T(8,12...) custom-call(s32[2]{0:T(128)} %len_ref.3, ...), custom_call_target="tpu_custom_call" | custom-call | flops 34359738368 | bytes 8388608 | tf_op jit(solution)/shard_map/attend_forward/pallas_call | solution.py:297
  462.8 42.6 %ffn_forward.1 = (f32[1024,1024]{1,0:T(8,128)}, bf16[1024,4096]{1,0:T(8,128)(2,1)}, bf16[1024,4096]{1,0:T(8,128)(2,1)}, bf16[1024,1024]{1,0:T(8,128)(2,1)}, bf16...) custom-call(bf16[1024,1024]{1,0:T(8,128)(2,1)} %get-tuple-element.36.att_ref, bf16[1024,1024]{1,0:T(8,128)(2,1)} %bitcast.137, ...), custom_call_target="tpu_custom_call" | custom-call | flops 19327352832 | bytes 62914560 | tf_op jit(solution)/shard_map/ffn_forward/pallas_call | solution.py:695
  505.4 70.0 %ffn_backward.1 = (bf16[1024,4096]{1,0:T(8,128)(2,1)}, bf16[4096,1024]{1,0:T(8,128)(2,1)}, f32[1024,1024]{1,0:T(8,128)}, bf16[1024,1024]{1,0:T(8,128)(2,1)}, bf1...) custom-call(bf16[1024,1024]{1,0:T(8,128)(2,1)} %get-tuple-element.36.att_ref, bf16[1024,1024]{1,0:T(8,128)(2,1)} %bitcast.138, ...), custom_call_target="tpu_custom_call" | custom-call | flops 38654705664 | bytes 94371840 | tf_op jit(solution)/shard_map/ffn_backward/pallas_call | solution.py:738
  580.2 7.5 collective-permute-done.4
  587.7 7.6 fusion
  600.8 8.3 collective-permute-done.3
  609.1 7.2 fusion.1
  616.4 259.8 %attend_backward.1 = bf16[1024,3072]{1,0:T(8,128)(2,1)} custom-call(s32[2]{0:T(128)} %len_ref.3, bf16[1024,1024]{1,0:T(8,128)(2,1)} %get-tuple-element.47.dout, bf16[2,3,4096,128]{3,2,1,0:T(8,128)(2,1)} %get-tuple-element.48.qkv_all, bf16[2,4096,128]{2,1,0:T(8,128)(2,1)} %get-tuple-element.49.o_all, f32[2,8,4096]{2,1,0:T(8,128)} %get-tuple-element.50.lse_ref, ...), custom_call_target="tpu_custom_call" | custom-call | flops 85899345920 | bytes 8388608 | tf_op jit(solution)/shard_map/attend_backward/pallas_call | solution.py:526
  876.3 13.8 %multiply_reduce_fusion = (f32[2,1024]{1,0:T(2,128)S(1)}, f32[2,512]{1,0:T(2,128)S(1)}, f32[2,512]{1,0:T(2,128)S(1)}, f32[2,1024]{1,0:T(2,128)S(1)}, f32[2,512,1024]{2,1,0:T(8,128)S(1)}) fusion(f32[2,512]{1,0:T(2,128)S(1)} %div.48, f32[2,512]{1,0:T(2,128)S(1)} %rsqrt.13, f32[1024,1024]{1,0:T(8,128)} %copy-done.2, f32[2,512,1024]{2,1,0:T(8,128)} %bitcast.96, ...), kind=kOutput, calls=%fused_computation.17 | convolution fusion | flops 6453979136 | bytes 25206784 | tf_op jit(solution)/shard_map/dot_general | solution.py:841
  892.4 6.4 bitcast_convert_fusion
  904.0 11.4 convolution_convert_fusion
  931.7 9.3 convolution_convert_fusion.1
  943.9 64.8 %psum.7 = bf16[2,6144]{1,0:T(2,128)(2,1)S(1)} all-reduce(f32[2,6144]{1,0:T(2,128)S(1)} %bitcast.122), channel_id=1, replica_groups=mesh['seq'=8,'x'=2,'core'=2] {'seq'}, use_global_device_ids=true, to_apply=%region_11.12 | all-reduce | flops 12288 | bytes 73728 | tf_op jit(solution)/shard_map/psum | solution.py:1216
  1008.7 10.0 all-gather
  1027.3 7.7 all_gather.21
  1035.8 59.3 %reduce-scatter.6.cloned.1.call-done = bf16[64,1024]{1,0:T(8,128)(2,1)} async-done(((bf16[1024,1024]{1,0:T(8,128)(2,1)}), bf16[64,1024]{1,0:T(8,128)(2,1)}) %reduce-scatter.6.cloned.1.call-update) | async-done | bytes 131088 | tf_op jit(solution)/shard_map/reduce_scatter | solution.py:891
  1095.0 6.7 all_gather.18
  1102.8 125.7 %reduce-scatter.8.cloned.1.call-done = bf16[32,3072]{1,0:T(8,128)(2,1)} async-done(((bf16[512,3072]{1,0:T(8,128)(2,1)}), bf16[32,3072]{1,0:T(8,128)(2,1)}) %reduce-scatter.8.cloned.1.call-update) | async-done | bytes 196624 | tf_op jit(solution)/shard_map/reduce_scatter | solution.py:891
  1228.6 8.9 all_gather.20
  1238.7 7.3 all-gather.6.cloned.1.call-done
  1248.8 15.6 %all-gather.4.cloned.1.call-done = bf16[128,4096]{1,0:T(8,128)(2,1)} async-done(((bf16[32,4096]{1,0:T(8,128)(2,1)}), bf16[128,4096]{1,0:T(8,128)(2,1)}) %all-gather.4.cloned.1.call-update) | async-done | bytes 1048592 | tf_op jit(solution)/shard_map/all_gather | solution.py:892
  (133 shorter events, 104.1 us)
Async XLA Ops:
  7.2 923.3 %reduce-scatter.14.cloned.1.call-start = ((), (), s32[]{:S(2)}) async-start(), calls=%async_computation.10 | async-start | bytes 4456448 | tf_op jit(solution)/shard_map/reduce_scatter | solution.py:891
  125.4 6.4 copy-start.18
  142.2 19.7 %copy-start.14 = (f32[2,6,1024]{2,1,0:T(8,128)}, f32[2,6,1024]{2,1,0:T(8,128)S(1)}, u32[]{:S(2)}) copy-start(f32[2,6,1024]{2,1,0:T(8,128)S(1)} %reshape.283.mod_ref) | copy-start | bytes 147460
  143.2 18.6 %copy-start.15 = (f32[2,1024]{1,0:T(2,128)}, f32[2,1024]{1,0:T(2,128)S(1)}, u32[]{:S(2)}) copy-start(f32[2,1024]{1,0:T(2,128)S(1)} %get-tuple-element.78) | copy-start | bytes 24580
  580.2 7.5 collective-permute-start.4
  595.3 336.0 %reduce-scatter.12.cloned.1.call-start = ((), (), s32[]{:S(2)}) async-start(), calls=%async_computation.8 | async-start | bytes 4456448 | tf_op jit(solution)/shard_map/reduce_scatter | solution.py:891
  595.4 4.9 copy-start.10
  600.1 9.0 collective-permute-start.3
  600.4 302.1 %collective-permute-start.2 = (bf16[16,32,1024]{2,1,0:T(8,128)(2,1)S(1)}, bf16[16,32,1024]{2,1,0:T(8,128)(2,1)S(1)}, u32[]{:S(2)}, u32[]{:S(2)}) collective-permute-start(bf16[16,32,1024]{2,1,0:T(8,128)(2,1)S(1)} %dynamic-slice_bitcast_fusion.4), channel_id=1, source_target_pairs={{0,1},{1,0},{2,3},{3,2},{4,5},{5,4},{6,7},{7,6},{8,9},{9,8},{10,11... | collective-permute-start | bytes 3145736 | tf_op jit(solution)/shard_map/ppermute | solution.py:888
  616.4 410.9 %reduce-scatter.10.cloned.1.call-start = ((), (), s32[]{:S(2)}) async-start(), calls=%async_computation.7 | async-start | bytes 1114112 | tf_op jit(solution)/shard_map/reduce_scatter | solution.py:891
  616.4 259.8 %copy-start.16 = (f32[2,1024]{1,0:T(2,128)S(1)}, f32[2,1024]{1,0:T(2,128)}, u32[]{:S(2)}) copy-start(f32[2,1024]{1,0:T(2,128)} %copy-done.15) | copy-start | bytes 24580
  876.3 13.9 %copy-start.3 = (f32[1024,1024]{1,0:T(8,128)S(1)}, f32[1024,1024]{1,0:T(8,128)}, u32[]{:S(2)}) copy-start(f32[1024,1024]{1,0:T(8,128)} %copy-done.2) | copy-start | bytes 12582916
  876.3 13.9 %copy-start.9 = (f32[1024,1024]{1,0:T(8,128)S(1)}, f32[1024,1024]{1,0:T(8,128)}, u32[]{:S(2)}) copy-start(f32[1024,1024]{1,0:T(8,128)} %get-tuple-element.46) | copy-start | bytes 12582916
  892.4 6.5 copy-start.12
  902.5 12.8 %collective-permute-start = (bf16[16,64,1024]{2,1,0:T(8,128)(2,1)}, bf16[16,64,1024]{2,1,0:T(8,128)(2,1)}, u32[]{:S(2)}, u32[]{:S(2)}) collective-permute-start(bf16[16,64,1024]{2,1,0:T(8,128)(2,1)} %dynamic-slice_bitcast_fusion.3), channel_id=1, source_target_pairs={{0,1},{1,0},{2,3},{3,2},{4,5},{5,4},{6,7},{7,6},{8,9},{9,8},{10,11... | collective-permute-start | bytes 6291464 | tf_op jit(solution)/shard_map/ppermute | solution.py:888
  903.9 191.1 %reduce-scatter.6.cloned.1.call-start = ((), (), s32[]{:S(2)}) async-start(), calls=%async_computation.5 | async-start | bytes 2228224 | tf_op jit(solution)/shard_map/reduce_scatter | solution.py:891
  904.0 11.4 copy-start.8
  919.2 309.3 %reduce-scatter.8.cloned.1.call-start = ((), (), s32[]{:S(2)}) async-start(), calls=%async_computation.6 | async-start | bytes 3342336 | tf_op jit(solution)/shard_map/reduce_scatter | solution.py:891
  919.3 8.2 copy-start.6
  921.6 5.9 collective-permute-start.1
  930.4 315.6 %all-gather.6.cloned.1.call-start = ((), (), s32[]{:S(2)}) async-start(), calls=%async_computation.11 | async-start | bytes 1310720 | tf_op jit(solution)/shard_map/all_gather | solution.py:892
  931.0 333.4 %all-gather.4.cloned.1.call-start = ((), (), s32[]{:S(2)}) async-start(), calls=%async_computation.9 | async-start | bytes 1310720 | tf_op jit(solution)/shard_map/all_gather | solution.py:892
  931.7 12.0 copy-start.17
  1228.6 38.6 %copy-start.1 = (bf16[128,6144]{1,0:T(8,128)(2,1)S(1)}, bf16[128,6144]{1,0:T(8,128)(2,1)}, u32[]{:S(2)}) copy-start(bf16[128,6144]{1,0:T(8,128)(2,1)} %param.20) | copy-start | bytes 4718596
  (7 other events, 17.8 us)
Sparse Core Ops, SparseCore 0:
  595.4 107.0 reduce-scatter.13
  704.8 146.8 reduce-scatter.11
  904.0 111.2 reduce-scatter.9
  1018.1 76.8 reduce-scatter.5
  1100.6 127.8 reduce-scatter.7
  1230.0 15.9 all-gather.5
  1247.6 16.7 all-gather.3

commit v5 on v4

--- a/solution.py
+++ b/solution.py
@@ -770,16 +770,22 @@
     )(att, outw, res, branch, mods, cot, weight, gb, act, slope, up, down)
 
 
-def project_kernel(x_ref, w_ref, cos_ref, sin_ref, out_ref):
-    projected = nn(x_ref[...], w_ref[...])
-    groups = out_ref.shape[2] // 128
-    rows = x_ref.shape[0]
-    lane = lanes_of(rows)
+def enter_kernel(
+    in_ref, skip_ref, skip_w, qkv_w, mod_ref, cos_ref, sin_ref, res_ref, proj_ref
+):
+    width = in_ref.shape[1]
+    mod = mod_ref[0]
+    residual = nn(in_ref[...], skip_w[:width, :]) + nn(skip_ref[...], skip_w[width:, :])
+    res_ref[...] = residual
+    hat, _ = layer_norm(residual)
+    normed = (hat * (1.0 + mod[1:2]) + mod[0:1]).astype(BF)
+    lane = lanes_of(in_ref.shape[0])
     cos, sin = cos_ref[...], sin_ref[...]
     for part in range(3):
-        for group in range(groups):
-            at = (part * groups + group) * 128
-            piece = projected[:, at : at + 128]
+        projected = nn(normed, qkv_w[:, part * width : (part + 1) * width])
+        for group in range(width // 128):
+            cols = slice(group * 128, group * 128 + 128)
+            piece = projected[:, cols]
             if part < 2:
                 turned = jnp.where(
                     (lane & 63) < 32, pltpu.roll(piece, 96, 1), pltpu.roll(piece, 32, 1)
@@ -787,29 +793,291 @@
                 piece = piece * cos + turned * sin
             if part == 0:
                 piece = piece * (0.125 * LOG2E)
-            out_ref[part, :, group * 128 : group * 128 + 128] = piece.astype(BF)
-
-
-def project_heads(x, weight, cos, sin, block=256):
-    rows, width = x.shape
-    steps = cos.shape[0] // block
+            proj_ref[part, :, cols] = piece.astype(BF)
+
+
+def enter_layer(first, second, skip_w, qkv_w, mods, cos, sin, block=256):
+    rows, width = first.shape
+    steps = rows // mods.shape[0] // block
+    part = pl.BlockSpec((block, width), lambda i: (i, 0))
+    table = pl.BlockSpec((block, 128), lambda i: (i % steps, 0))
     return pl.pallas_call(
-        project_kernel,
+        enter_kernel,
         grid=(rows // block,),
         in_specs=[
-            pl.BlockSpec((block, width), lambda i: (i, 0)),
-            pl.BlockSpec(weight.shape, lambda i: (0, 0)),
-            pl.BlockSpec((block, 128), lambda i: (i % steps, 0)),
-            pl.BlockSpec((block, 128), lambda i: (i % steps, 0)),
+            part,
+            part,
+            whole_spec(skip_w.shape),
+            whole_spec(qkv_w.shape),
+            pl.BlockSpec((1,) + mods.shape[1:], lambda i: (i // steps, 0, 0)),
+            table,
+            table,
         ],
-        out_specs=pl.BlockSpec((3, block, width), lambda i: (0, i, 0)),
-        out_shape=jax.ShapeDtypeStruct((3, rows, width), BF),
+        out_specs=[part, pl.BlockSpec((3, block, width), lambda i: (0, i, 0))],
+        out_shape=[
+            jax.ShapeDtypeStruct((rows, width), F32),
+            jax.ShapeDtypeStruct((3, rows, width), BF),
+        ],
         compiler_params=pltpu.CompilerParams(vmem_limit_bytes=VMEM_LIMIT),
         cost_estimate=pl.CostEstimate(
-            flops=2 * rows * weight.size, bytes_accessed=2 * weight.size, transcendentals=0
+            flops=2 * rows * (skip_w.size + qkv_w.size),
+            bytes_accessed=40 * 2**20,
+            transcendentals=0,
         ),
-        name="project_heads",
-    )(x, weight, cos, sin)
+        name="enter_layer",
+    )(first, second, skip_w, qkv_w, mods, cos, sin)
+
+
+def leave_kernel(
+    grad_ref, qkv_w, skip_w, res_ref, mid_ref, mod_ref, in_ref, skip_ref,
+    gin_ref, gskip_ref, sums_ref, gqkv_ref, gw_ref, normed, stream,
+):
+    step = pl.program_id(0)
+    rows, width = res_ref.shape
+    utts = mod_ref.shape[0]
+    span = rows // utts
+
+    @pl.when(step == 0)
+    def _():
+        for utt in range(utts):
+            mod = mod_ref[utt]
+            shift = jnp.zeros((1, width), F32)
+            scale = jnp.zeros((1, width), F32)
+            for _, part in row_blocks(span):
+                here = slice(utt * span + part.start, utt * span + part.stop)
+                hat, inverse = layer_norm(res_ref[here, :])
+                normed[here, :] = (hat * (1.0 + mod[1:2]) + mod[0:1]).astype(BF)
+                grad = nt(grad_ref[here, :], qkv_w[...])
+                shift += jnp.sum(grad, axis=0, keepdims=True)
+                scale += jnp.sum(grad * hat, axis=0, keepdims=True)
+                total = mid_ref[here, :] + norm_back(grad * (1.0 + mod[1:2]), hat, inverse)
+                low = total.astype(BF)
+                stream[here, :] = low
+                gin_ref[here, :] = nt(low, skip_w[:width, :]).astype(BF)
+                gskip_ref[here, :] = nt(low, skip_w[width:, :]).astype(BF)
+            sums_ref[utt, 0:1, :] = shift
+            sums_ref[utt, 1:2, :] = scale
+
+    chunk = gqkv_ref.shape[1]
+    cols = pl.ds(pl.multiple_of(step * chunk, chunk), chunk)
+    gqkv_ref[...] = tn(normed[...], grad_ref[:, cols]).astype(BF)
+    part = gw_ref.shape[2]
+    here = pl.ds(pl.multiple_of(step * part, part), part)
+    gw_ref[0] = tn(in_ref[...], stream[:, here]).astype(BF)
+    gw_ref[1] = tn(skip_ref[...], stream[:, here]).astype(BF)
+
+
+def leave_layer(grads, qkv_w, skip_w, res, mid, mods, first, second, steps=4):
+    rows, width = res.shape
+    utts = mods.shape[0]
+    ins = (grads, qkv_w, skip_w, res, mid, mods, first, second)
+    outs = pl.pallas_call(
+        leave_kernel,
+        grid=(steps,),
+        in_specs=[whole_spec(a.shape) for a in ins],
+        out_specs=[
+            whole_spec((rows, width)),
+            whole_spec((rows, width)),
+            whole_spec((utts, 8, width)),
+            pl.BlockSpec((width, 3 * width // steps), lambda i: (0, i)),
+            pl.BlockSpec((2, width, width // steps), lambda i: (0, 0, i)),
+        ],
+        out_shape=[
+            jax.ShapeDtypeStruct((rows, width), BF),
+            jax.ShapeDtypeStruct((rows, width), BF),
+            jax.ShapeDtypeStruct((utts, 8, width), F32),
+            jax.ShapeDtypeStruct((width, 3 * width), BF),
+            jax.ShapeDtypeStruct((2, width, width), BF),
+        ],
+        scratch_shapes=[pltpu.VMEM((rows, width), BF), pltpu.VMEM((rows, width), BF)],
+        compiler_params=pltpu.CompilerParams(vmem_limit_bytes=VMEM_LIMIT),
+        cost_estimate=pl.CostEstimate(
+            flops=4 * rows * (skip_w.size + qkv_w.size),
+            bytes_accessed=60 * 2**20,
+            transcendentals=0,
+        ),
+        name="leave_layer",
+    )(*ins)
+    return tuple(outs[:4]) + (outs[4].reshape(2 * width, width),)
+
+
+class GradSum:
+    def __init__(self, jobs, send, recv, local):
+        self.jobs, self.send, self.recv, self.local = jobs, send, recv, local
+        me, x, core = lax.axis_index("seq"), lax.axis_index("x"), lax.axis_index("core")
+        self.bits = (me // 4, (me // 2) % 2, me % 2, x, core)
+        self.copies = [[] for _ in jobs]
+        self.keeps = []
+
+    def peer(self, dim):
+        me, x, core = lax.axis_index("seq"), lax.axis_index("x"), lax.axis_index("core")
+        if dim < 3:
+            return (me ^ (4 >> dim), x, core)
+        return (me, 1 - x, core) if dim == 3 else (me, x, 1 - core)
+
+    def launch(self, index, source, target, dim):
+        at = len(self.copies[index])
+        copy = remote(
+            source,
+            target,
+            self.send.at[index * 7 + at],
+            self.recv.at[index * 7 + at],
+            self.peer(dim),
+        )
+        copy.start()
+        self.copies[index].append(copy)
+
+    def absorb(self, index, stage):
+        _, _, _, order, keep, arrivals = self.jobs[index]
+        done = order[1 : stage + 1]
+        left = [dim for dim in range(4) if dim not in done]
+        self.copies[index][stage].wait_recv()
+
+        def add(i, carry):
+            at = list(self.bits[:4])
+            place = []
+            for n, dim in enumerate(left):
+                bit = (i >> (len(left) - 1 - n)) & 1
+                at[dim] = bit
+                place.append(bit)
+            mine = keep[at[0], at[1], at[2], at[3]].astype(F32)
+            other = arrivals[stage][tuple(place)] if place else arrivals[stage][...]
+            keep[at[0], at[1], at[2], at[3]] = (mine + other.astype(F32)).astype(BF)
+            return carry
+
+        lax.fori_loop(0, 2 ** len(left), add, 0)
+
+    def stage(self, number):
+        for index, (grad, out, cols, order, keep, arrivals) in enumerate(self.jobs):
+            tail = (slice(None), cols)
+            bits = self.bits
+            if number == 0:
+                lead = (slice(None),) * 4
+                own = pltpu.make_async_copy(
+                    grad.at[lead + (bits[4],) + tail], keep, self.local.at[index]
+                )
+                own.start()
+                self.keeps.append(own)
+                self.launch(index, grad.at[lead + (1 - bits[4],) + tail], arrivals[0], 4)
+            elif number < 5:
+                if number == 1:
+                    self.keeps[index].wait()
+                self.absorb(index, number - 1)
+                dim = order[number]
+                done = order[1:number]
+                where = tuple(
+                    1 - bits[d] if d == dim else bits[d] if d in done else slice(None)
+                    for d in range(4)
+                )
+                self.launch(index, keep.at[where], arrivals[number], dim)
+            elif number == 5:
+                self.absorb(index, 4)
+                mine = keep.at[bits[:4]]
+                spot = out.at[(bits[3], bits[4]) + tail]
+                own = pltpu.make_async_copy(mine, spot, self.local.at[index])
+                own.start()
+                self.keeps[index] = own
+                self.launch(index, mine, spot, 3)
+            else:
+                self.keeps[index].wait()
+                self.copies[index][5].wait_recv()
+                both = out.at[(slice(None), bits[4]) + tail]
+                self.launch(index, both, both, 4)
+
+    def finish(self):
+        for chain in self.copies:
+            chain[6].wait_recv()
+        for chain in self.copies:
+            for copy in chain:
+                copy.wait_send()
+
+
+def reduce_kernel(*refs, count):
+    grads, small = refs[:count], refs[count]
+    outs, small_out = refs[count + 1 : 2 * count + 1], refs[2 * count + 1]
+    rest = refs[2 * count + 2 :]
+    jobs = 2 * count
+    buffers = rest[: 6 * jobs]
+    small_in, small_low, send, recv, local, ssend, srecv, bsend, brecv, slocal = rest[6 * jobs :]
+    me, x, core = lax.axis_index("seq"), lax.axis_index("x"), lax.axis_index("core")
+    others = [seq_flip(flip) for flip in range(7, 0, -1)]
+    mates = [(me, (x + dx) % 2, (core + dc) % 2) for dx, dc in ((0, 1), (1, 0), (1, 1))]
+    greet(others + mates)
+    work = []
+    for index in range(jobs):
+        grad, out = grads[index // 2], outs[index // 2]
+        half = grad.shape[-1] // 2
+        cols = pl.ds((index % 2) * half, half)
+        keep, arrivals = buffers[6 * index], buffers[6 * index + 1 : 6 * index + 6]
+        order = (4, 3, 2, 1, 0) if index % 2 == 0 else (4, 2, 3, 1, 0)
+        work.append((grad, out, cols, order, keep, arrivals))
+    chain = GradSum(work, send, recv, local)
+    chain.stage(0)
+    own = pltpu.make_async_copy(small, small_in.at[me], slocal.at[0])
+    own.start()
+    smalls = []
+    for flip, device in zip(range(7, 0, -1), others):
+        smalls.append(remote(small, small_in.at[me], ssend.at[flip], srecv.at[flip], device))
+        smalls[-1].start()
+    for number in range(1, 6):
+        chain.stage(number)
+    own.wait()
+    for copy in smalls:
+        copy.wait_recv()
+    total = small_in[0]
+    for index in range(1, 8):
+        total = total + small_in[index]
+    small_low[...] = total.astype(BF)
+    quarter = x * 2 + core
+    keep = pltpu.make_async_copy(small_low, small_out.at[quarter], slocal.at[1])
+    keep.start()
+    lows = []
+    for slot, device in enumerate(mates):
+        lows.append(remote(small_low, small_out.at[quarter], bsend.at[slot], brecv.at[slot], device))
+        lows[-1].start()
+    chain.stage(6)
+    chain.finish()
+    for copy in smalls:
+        copy.wait_send()
+    keep.wait()
+    for copy in lows:
+        copy.wait()
+
+
+def reduce_grads(grads, small, collective_id=3):
+    views, outs, buffers = [], [], []
+    for grad in grads:
+        rows, width = grad.shape
+        span = rows // 32
+        views.append(grad.reshape(2, 2, 2, 2, 2, span, width))
+        outs.append(jax.ShapeDtypeStruct((2, 2, span, width), BF))
+        for _ in range(2):
+            tail = (span, width // 2)
+            buffers.append(pltpu.VMEM((2, 2, 2, 2) + tail, BF))
+            for left in (4, 3, 2, 1, 0):
+                buffers.append(pltpu.VMEM((2,) * left + tail, BF))
+    anywhere = pl.BlockSpec(memory_space=pl.ANY)
+    jobs = 2 * len(grads)
+    dma = pltpu.SemaphoreType.DMA
+    outs.append(jax.ShapeDtypeStruct((4,) + small.shape, BF))
+    results = pl.pallas_call(
+        functools.partial(reduce_kernel, count=len(grads)),
+        in_specs=[anywhere] * (len(grads) + 1),
+        out_specs=[anywhere] * (len(grads) + 1),
+        out_shape=outs,
+        scratch_shapes=buffers
+        + [pltpu.VMEM((8,) + small.shape, F32), pltpu.VMEM(small.shape, BF)]
+        + [dma((7 * jobs,)), dma((7 * jobs,)), dma((jobs,)), dma((8,)), dma((8,)), dma((3,)), dma((3,)), dma((2,))],
+        compiler_params=pltpu.CompilerParams(
+            vmem_limit_bytes=VMEM_LIMIT, collective_id=collective_id, has_side_effects=True
+        ),
+        name="reduce_grads",
+    )(*views, small)
+    shards = [
+        result.reshape(grad.shape[0] // 8, grad.shape[1]).astype(jnp.float32)
+        for result, grad in zip(results, grads)
+    ]
+    return shards, results[-1].astype(jnp.float32)
 
 
 def rotary_tables(positions):
@@ -1055,27 +1323,32 @@
     loss_weight = (valid_mask - dropped) * (every_count / (2.0 * kept_total)) + dropped * (
         every_count / (2.0 * drop_total)
     )
-    joined = jnp.concatenate([layer_input, skip_input], axis=-1).reshape(row_count, 2 * model_width)
-    residual_in = jnp.dot(joined, skip_full, preferred_element_type=jnp.float32).reshape(
-        utt_count, frame_span, model_width
-    )
-    shift_attn = modulation[:, 0][:, None, :]
-    scale_attn = modulation[:, 1][:, None, :]
-    hat_attn, inv_attn = layer_norm(residual_in)
-    normed_attn = (
-        (hat_attn * (1.0 + scale_attn) + shift_attn)
-        .astype(jnp.bfloat16)
-        .reshape(row_count, model_width)
-    )
+    first_rows = layer_input.reshape(row_count, model_width)
+    second_rows = skip_input.reshape(row_count, model_width)
     if by_heads:
         cos_all, sin_all = paired_tables(jnp.arange(frame_count, dtype=jnp.int32))
         cos_here = lax.dynamic_slice_in_dim(cos_all, seq_here * frame_span, frame_span, 0)
         sin_here = lax.dynamic_slice_in_dim(sin_all, seq_here * frame_span, frame_span, 0)
-        proj = project_heads(normed_attn, qkv_full, cos_here, sin_here)
+        residual_rows, proj = enter_layer(
+            first_rows, second_rows, skip_full, qkv_full, modulation, cos_here, sin_here
+        )
         (qkv_all, out_all, lse_all, attended_low), (out_full, up_full, down_full) = attend_forward(
             lengths, proj, out_weight, up_weight, down_weight, frame_span
         )
     else:
+        joined = jnp.concatenate([layer_input, skip_input], axis=-1).reshape(row_count, 2 * model_width)
+        residual_in = jnp.dot(joined, skip_full, preferred_element_type=jnp.float32).reshape(
+            utt_count, frame_span, model_width
+        )
+        shift_attn = modulation[:, 0][:, None, :]
+        scale_attn = modulation[:, 1][:, None, :]
+        hat_attn, inv_attn = layer_norm(residual_in)
+        normed_attn = (
+            (hat_attn * (1.0 + scale_attn) + shift_attn)
+            .astype(jnp.bfloat16)
+            .reshape(row_count, model_width)
+        )
+        residual_rows = residual_in.reshape(row_count, model_width)
         out_full, up_full, down_full = [
             gather_weight(weight) for weight in (out_weight, up_weight, down_weight)
         ]
@@ -1112,7 +1385,6 @@
         attended_full = accum / jnp.transpose(denom, (0, 2, 1))[..., None]
         lse_rows = jnp.transpose(top_score + jnp.log(denom), (0, 2, 1))
         attended_low = attended_full.astype(jnp.bfloat16).reshape(row_count, model_width)
-    residual_rows = residual_in.reshape(row_count, model_width)
     cot_rows = cotangent.reshape(row_count, model_width)
     weight_rows = loss_weight.reshape(row_count, 1)
     branch_attn, hidden_act, hidden_slope, grad_branch_ffn, layer_output, grad_gate_ffn = ffn_forward(
@@ -1140,9 +1412,7 @@
         up_full,
         down_full,
     )
-    grad_mid = grad_mid.reshape(utt_count, frame_span, model_width)
     grad_shift_ffn, grad_scale_ffn, grad_gate_attn = ffn_sums[:, 0], ffn_sums[:, 1], ffn_sums[:, 2]
-    qkv_back, skip_back = qkv_full, skip_full
     if by_heads:
         grad_projected = attend_backward(
             lengths, grad_attended_flat, qkv_all, out_all, lse_all, cos_all, sin_all, frame_span
@@ -1182,26 +1452,42 @@
             .reshape(row_count, 3 * model_width)
             .astype(jnp.bfloat16)
         )
-    grad_qkv = cross(normed_attn, grad_projected)
-    grad_normed_attn = back_product(grad_projected, qkv_back).reshape(
-        utt_count, frame_span, model_width
-    )
-    grad_shift_attn = jnp.sum(grad_normed_attn, axis=1)
-    grad_scale_attn = jnp.sum(grad_normed_attn * hat_attn, axis=1)
-    grad_stream = grad_mid + norm_back(grad_normed_attn * (1.0 + scale_attn), hat_attn, inv_attn)
-    grad_stream_low = grad_stream.astype(jnp.bfloat16).reshape(row_count, model_width)
-    grad_skip_w = cross(joined, grad_stream_low)
-    grad_joined = back_product(grad_stream_low, skip_back)
-    grad_input = (
-        grad_joined[:, :model_width]
-        .reshape(utt_count, frame_span, model_width)
-        .astype(jnp.bfloat16)
-    )
-    grad_skip = (
-        grad_joined[:, model_width:]
-        .reshape(utt_count, frame_span, model_width)
-        .astype(jnp.bfloat16)
-    )
+    if by_heads:
+        grad_input, grad_skip, attn_sums, grad_qkv, grad_skip_w = leave_layer(
+            grad_projected,
+            qkv_full,
+            skip_full,
+            residual_rows,
+            grad_mid,
+            modulation,
+            first_rows,
+            second_rows,
+        )
+        grad_input = grad_input.reshape(layer_input.shape)
+        grad_skip = grad_skip.reshape(skip_input.shape)
+        grad_shift_attn, grad_scale_attn = attn_sums[:, 0], attn_sums[:, 1]
+    else:
+        grad_mid = grad_mid.reshape(utt_count, frame_span, model_width)
+        grad_qkv = cross(normed_attn, grad_projected)
+        grad_normed_attn = back_product(grad_projected, qkv_full).reshape(
+            utt_count, frame_span, model_width
+        )
+        grad_shift_attn = jnp.sum(grad_normed_attn, axis=1)
+        grad_scale_attn = jnp.sum(grad_normed_attn * hat_attn, axis=1)
+        grad_stream = grad_mid + norm_back(grad_normed_attn * (1.0 + scale_attn), hat_attn, inv_attn)
+        grad_stream_low = grad_stream.astype(jnp.bfloat16).reshape(row_count, model_width)
+        grad_skip_w = cross(joined, grad_stream_low)
+        grad_joined = back_product(grad_stream_low, skip_full)
+        grad_input = (
+            grad_joined[:, :model_width]
+            .reshape(utt_count, frame_span, model_width)
+            .astype(jnp.bfloat16)
+        )
+        grad_skip = (
+            grad_joined[:, model_width:]
+            .reshape(utt_count, frame_span, model_width)
+            .astype(jnp.bfloat16)
+        )
     grad_modulation = jnp.stack(
         [
             grad_shift_attn,
@@ -1213,16 +1499,25 @@
         ],
         axis=1,
     ).reshape(utt_count, 6 * model_width)
-    mod_total = lax.psum(grad_modulation, "seq")
-    mod_every = lax.all_gather(
-        mod_total.astype(jnp.bfloat16), BATCH, axis=0, tiled=True
-    ).astype(jnp.float32)
+    weight_grads = (grad_skip_w, grad_qkv, grad_out, grad_up, grad_down)
+    if by_heads:
+        order = (4, 3, 1, 0, 2)
+        shards, mod_every = reduce_grads(
+            [weight_grads[i] for i in order], grad_modulation.reshape(-1, model_width)
+        )
+        summed = [shards[order.index(i)] for i in range(5)]
+        mod_every = mod_every.reshape(-1, 6 * model_width)
+    else:
+        mod_total = lax.psum(grad_modulation, "seq")
+        mod_every = lax.all_gather(
+            mod_total.astype(jnp.bfloat16), BATCH, axis=0, tiled=True
+        ).astype(jnp.float32)
+        summed = [sum_weight(grad) for grad in weight_grads]
     silu_rows = lax.dynamic_slice_in_dim(silu_every, seq_here * row_span, row_span, 1)
     adaln_rows = jnp.dot(silu_rows.T, mod_every, precision=lax.Precision.HIGHEST)
     bias_rows = lax.dynamic_slice_in_dim(
         jnp.sum(mod_every, axis=0), seq_here * bias_span, bias_span, 0
     )
-    summed = [sum_weight(grad) for grad in (grad_skip_w, grad_qkv, grad_out, grad_up, grad_down)]
     results = (summed[0], adaln_rows, bias_rows, summed[1], summed[2], summed[3], summed[4])
     return (
         layer_output,

time: 1280 us -> 1020 us (0.80)
  waiting for transfers between devices: 230 us -> 0 us
  Pallas kernels: 769 us -> 973 us
  blocking collectives: 98.1 us -> 0 us
  matrix products: 52 us -> 4.09 us
  local copies, waits for them, and re-layouts: 53.7 us -> 16.7 us
  other arithmetic: 53.8 us -> 19.1 us
  between operations: 16.5 us -> 2.66 us
    pallas_call x1 -> x3, Pallas kernels: 11.6 us -> 251 us  [the longest x1 196 us: reduce_grads(): pl.pallas_call(functools.partial(reduce_kernel, count=len(grads)), in_spe...]
    reduce_scatter x5 -> x0, waiting for transfers between devices: 185 us -> none  [sum_weight(): lax.psum_scatter(half, ('seq', 'x'), scatter_dimension=0, tiled=True)]
    psum x1 -> x0, blocking collectives: 64.8 us -> none  [on_device(): mod_total = lax.psum(grad_modulation, 'seq')]
    dot_general x5 -> x0, matrix products: 48.6 us -> none  [the longest x2 23.1 us: back_product(): lax.dot_general(left, right, (((1,), (1,)), ((), ())), preferred_element_...]
    all_gather x4 -> x0, blocking collectives: 33.2 us -> none  [the longest x3 23.3 us: sum_weight(): return lax.all_gather(shard, BATCH, axis=0, tiled=True).astype(jnp.float32)]
    convert_element_type x12 -> x5, other arithmetic: 38.3 us -> 7.66 us  [reduce_grads(): result.reshape(grad.shape[0] // 8, grad.shape[1]).astype(jnp.float32)]
    pallas_call x1, Pallas kernels: 260 us -> 234 us  [attend_backward(): pl.pallas_call(functools.partial(attend_backward_kernel, span=span, block...]
    all_gather x2 -> x0, waiting for transfers between devices: 22.9 us -> none  [sum_weight(): return lax.all_gather(shard, BATCH, axis=0, tiled=True).astype(jnp.float32)]
  transfers between devices with their start and end apart: 12 -> 0, of which waited for: 7 -> 0; matrix products, arithmetic and copies ran while one was open for 7% -> 0% of each run, Pallas kernels for 20% -> 0%
where the time goes in v5:
time: 1020 us
  Pallas kernels  973 us (95%)
  other arithmetic  19.1 us (2%)
  local copies, waits for them, and re-layouts  16.7 us (2%)
    pallas_call x1, Pallas kernels, attend_forward(): pl.pallas_call(functools.partial(attend_forward_kernel, span=span, bq=bq,...  301 us
    pallas_call x1, Pallas kernels, attend_backward(): pl.pallas_call(functools.partial(attend_backward_kernel, span=span, block...  234 us
    pallas_call x1, Pallas kernels, reduce_grads(): pl.pallas_call(functools.partial(reduce_kernel, count=len(grads)), in_spe...  196 us
    pallas_call x1, Pallas kernels, gather_early(): pl.pallas_call(functools.partial(gather_kernel, shapes=shapes), in_specs=...  83.7 us
    pallas_call x1, Pallas kernels, ffn_backward(): pl.pallas_call(ffn_backward_kernel, grid=(hidden // chunk,), in_specs=who...  61.1 us
    pallas_call x1, Pallas kernels, ffn_forward(): pl.pallas_call(ffn_forward_kernel, grid=(hidden // chunk,), in_specs=whol...  42.6 us
    pallas_call x1, Pallas kernels, leave_layer(): pl.pallas_call(leave_kernel, grid=(steps,), in_specs=[whole_spec(a.shape)...  36.2 us

profile of v5, /device:TPU:0, one launch (start us, length us, event | category | flops | bytes accessed | tf_op | source)
XLA Modules:
  0.0 1015.8 jit_solution(1533104719573765305)
XLA Ops:
  1.5 1.3 multiply_reduce_fusion.1
  2.7 1.4 maximum_bitcast_fusion
  7.3 3.7 fusion
  11.4 1.8 copy.24.sin_ref
  13.4 1.8 copy.23.cos_ref
  15.3 1.9 constant_dynamic-slice_fusion
  17.1 83.7 %gather_early.1 = (bf16[2,2,2,2,2,64,1024]{6,5,4,3,2,1,0:T(8,128)(2,1)}, bf16[2,2,2,2,2,32,3072]{6,5,4,3,2,1,0:T(8,128)(2,1)}, f32[8,12,1024]{2,1,0:T(8,128)}, f32[4,8,1024]{2,1,0:T(8,128)}) custom-call(bf16[256,1024]{1,0:T(8,128)(2,1)} %refs_0_.1, bf16[128,3072]{1,0:T(8,128)(2,1)} %refs_1_.1, f32[12,1024]{1,0:T(8,128)} %reshape.222.refs_2_, ...), custom_call_target="tpu_custom_call" | custom-call | tf_op jit(solution)/shard_map/gather_early/pallas_call | solution.py:1220
  101.6 0.9 slice.39
  105.2 1.1 reduce_sum.47
  106.9 1.0 copy.30
  107.9 19.0 %enter_layer.1 = (f32[1024,1024]{1,0:T(8,128)}, bf16[3,1024,1024]{2,1,0:T(8,128)(2,1)}) custom-call(bf16[1024,1024]{1,0:T(8,128)(2,1)} %bitcast.62, bf16[1024,1024]{1,0:T(8,128)(2,1)} %bitcast.64, bf16[2048,1024]{1,0:T(8,128)(2,1)} %bitcast.58, bf16[1024,3072]{1,0:T(8,128)(2,1)} %bitcast.56, f32[2,6,1024]{2,1,0:T(8,128)} %reshape.225.mod_ref, ...), custom_call_target="tpu_custom_call" | custom-call | flops 10737418240 | bytes 41943040 | tf_op jit(solution)/shard_map/enter_layer/pallas_call | solution.py:804
  127.0 300.9 %attend_forward.1 = (bf16[2,3,4096,128]{3,2,1,0:T(8,128)(2,1)}, bf16[2,4096,128]{2,1,0:T(8,128)(2,1)}, f32[2,8,4096]{2,1,0:T(8,128)}, bf16[1024,1024]{1,0:T(8,12...) custom-call(s32[2]{0:T(128)} %len_ref.3, ...), custom_call_target="tpu_custom_call" | custom-call | flops 34359738368 | bytes 8388608 | tf_op jit(solution)/shard_map/attend_forward/pallas_call | solution.py:297
  427.9 42.6 %ffn_forward.1 = (f32[1024,1024]{1,0:T(8,128)}, bf16[1024,4096]{1,0:T(8,128)(2,1)}, bf16[1024,4096]{1,0:T(8,128)(2,1)}, bf16[1024,1024]{1,0:T(8,128)(2,1)}, bf16...) custom-call(bf16[1024,1024]{1,0:T(8,128)(2,1)} %get-tuple-element.50.att_ref, bf16[1024,1024]{1,0:T(8,128)(2,1)} %bitcast.73, ...), custom_call_target="tpu_custom_call" | custom-call | flops 19327352832 | bytes 62914560 | tf_op jit(solution)/shard_map/ffn_forward/pallas_call | solution.py:695
  470.4 1.3 stack.19
  471.7 61.1 %ffn_backward.1 = (bf16[1024,4096]{1,0:T(8,128)(2,1)}, bf16[4096,1024]{1,0:T(8,128)(2,1)}, f32[1024,1024]{1,0:T(8,128)}, bf16[1024,1024]{1,0:T(8,128)(2,1)}, bf1...) custom-call(bf16[1024,1024]{1,0:T(8,128)(2,1)} %get-tuple-element.50.att_ref, bf16[1024,1024]{1,0:T(8,128)(2,1)} %bitcast.74, ...), custom_call_target="tpu_custom_call" | custom-call | flops 38654705664 | bytes 94371840 | tf_op jit(solution)/shard_map/ffn_backward/pallas_call | solution.py:738
  532.8 233.8 %attend_backward.1.grad_ref = bf16[1024,3072]{1,0:T(8,128)(2,1)} custom-call(s32[2]{0:T(128)} %len_ref.3, bf16[1024,1024]{1,0:T(8,128)(2,1)} %get-tuple-element.61.dout, bf16[2,3,4096,128]{3,2,1,0:T(8,128)(2,1)} %get-tuple-element.62.qkv_all, bf16[2,4096,128]{2,1,0:T(8,128)(2,1)} %get-tuple-element.63.o_all, f32[2,8,4096]{2,1,0:T(8,128)} %get-tuple-element.64.lse_ref, ...), custom_call_target="tpu_custom_call" | custom-call | flops 85899345920 | bytes 8388608 | tf_op jit(solution)/shard_map/attend_backward/pallas_call | solution.py:526
  766.6 36.2 %leave_layer.1 = (bf16[1024,1024]{1,0:T(8,128)(2,1)}, bf16[1024,1024]{1,0:T(8,128)(2,1)}, f32[2,8,1024]{2,1,0:T(8,128)}, bf16[1024,3072]{1,0:T(8,128)(2,1)}, bf16[2,1024,1024]{2,1,0:T(8,128)(2,1)}) custom-call(bf16[1024,3072]{1,0:T(8,128)(2,1)} %attend_backward.1.grad_ref, bf16[1024,3072]{1,0:T(8,128)(2,1)} %bitcast.57, bf16[2048,1024]{1,0:T(8,128)(2,1)} %bitcast.59, ...), custom_call_target="tpu_custom_call" | custom-call | flops 21474836480 | bytes 62914560 | tf_op jit(solution)/shard_map/leave_layer/pallas_call | solution.py:874
  806.0 196.0 %reduce_grads.1 = (bf16[2,2,128,1024]{3,2,1,0:T(8,128)(2,1)}, bf16[2,2,32,4096]{3,2,1,0:T(8,128)(2,1)}, bf16[2,2,32,3072]{3,2,1,0:T(8,128)(2,1)}, bf16[2,2,64,10...) custom-call(bf16[2,2,2,2,2,128,1024]{6,5,4,3,2,1,0:T(8,128)(2,1)} %bitcast.47, ...), custom_call_target="tpu_custom_call" | custom-call | tf_op jit(solution)/shard_map/reduce_grads/pallas_call | solution.py:1063
  1002.0 1.1 reshape.238
  1003.9 2.2 bitcast_convert_fusion.3
  1006.9 1.3 bitcast_convert_fusion.2
  1008.3 1.6 bitcast_convert_fusion.1
  1009.9 1.6 bitcast_convert_fusion
  1011.5 3.8 fusion.10
  (45 shorter events, 12.1 us)
Async XLA Ops:
  0.6 5.6 copy-start
  15.3 89.9 %copy-start.7 = (s32[2]{0:T(128)S(1)}, s32[2]{0:T(128)}, u32[]{:S(2)}) copy-start(s32[2]{0:T(128)} %len_ref.3) | copy-start | bytes 28
  766.6 38.8 %copy-start.6 = (f32[2,1,1024]{2,1,0:T(1,128)S(1)}, f32[2,1,1024]{2,1,0:T(1,128)}, u32[]{:S(2)}) copy-start(f32[2,1,1024]{2,1,0:T(1,128)} %stack.19) | copy-start | bytes 24580
  1002.0 4.1 copy-start.5
  1002.0 4.9 copy-start.4
  1003.9 4.4 copy-start.3
  1008.3 1.6 copy-start.2
  1009.9 5.4 copy-start.1

commit v6 on v5

--- a/solution.py
+++ b/solution.py
@@ -90,22 +90,20 @@
         return (me, 1 - x, core) if dim == 3 else (me, x, 1 - core)
 
     def stage(self):
-        for index, (full, cols, source, order) in enumerate(self.jobs):
+        for index, (full, cols, source, ready, order) in enumerate(self.jobs):
             at = len(self.copies[index])
-            tail = (slice(None), cols)
+            where = tuple(
+                slice(None) if d in ready + order[:at] else self.bits[d]
+                for d in range(len(full.shape) - 2)
+            ) + (slice(None), cols)
             if at == 0:
-                own = pltpu.make_async_copy(
-                    source, full.at[self.bits + tail], self.local.at[index]
-                )
+                own = pltpu.make_async_copy(source, full.at[where], self.local.at[index])
                 own.start()
                 self.owns.append(own)
             else:
                 if at == 1:
                     self.owns[index].wait()
                 self.copies[index][at - 1].wait_recv()
-            where = tuple(
-                slice(None) if d in order[:at] else self.bits[d] for d in range(5)
-            ) + tail
             copy = remote(
                 source if at == 0 else full.at[where],
                 full.at[where],
@@ -124,17 +122,41 @@
                 copy.wait_send()
 
 
-def gather_jobs(weights, fulls):
+def split_columns(width, shares):
+    total, start, out = sum(shares), 0, []
+    for n in range(len(shares)):
+        stop = width * sum(shares[: n + 1]) // total // 128 * 128
+        out.append(pl.ds(start, stop - start))
+        start = stop
+    return out
+
+
+def quarter_of(weight, cols):
     quarter = lax.axis_index("x") * 2 + lax.axis_index("core")
-    jobs = []
-    for weight, full in zip(weights, fulls):
-        rows, width = weight.shape
-        span, half = rows // 4, width // 2
-        for side in range(2):
-            cols = pl.ds(side * half, half)
-            source = weight.at[pl.ds(quarter * span, span), cols]
-            jobs.append((full, cols, source, (0, 1, 2, 3, 4) if side == 0 else (0, 1, 3, 2, 4)))
-    return jobs
+    span = weight.shape[0] // 4
+    return weight.at[pl.ds(quarter * span, span), cols]
+
+
+def early_jobs(weights, fulls):
+    orders = ((0, 1, 2, 3, 4), (0, 2, 3, 1, 4), (0, 3, 1, 2, 4))
+    return [
+        (full, cols, quarter_of(weight, cols), (), order)
+        for weight, full in zip(weights, fulls)
+        for cols, order in zip(split_columns(weight.shape[1], (1, 1, 1)), orders)
+    ]
+
+
+def ahead_jobs(weights, helds):
+    every = [(weight, held, pl.ds(0, weight.shape[1])) for weight, held in zip(weights, helds)]
+    return [(held, cols, quarter_of(weight, cols), (), (0, 1)) for weight, held, cols in every]
+
+
+def late_jobs(helds, fulls):
+    return [
+        (full, cols, held.at[:, :, :, cols], (0, 1), order)
+        for held, full in zip(helds, fulls)
+        for cols, order in zip(split_columns(held.shape[3], (3, 1)), ((2, 3, 4), (3, 2, 4)))
+    ]
 
 
 def attend_forward_kernel(
@@ -151,7 +173,7 @@
     flips = (7, 6, 5, 4, 3, 2, 1)
     greet([seq_flip(flip) for flip in flips] + [(me, 1 - x, core), (me, x, 1 - core)])
     weights = WeightGather(
-        gather_jobs((out_w, up_w, down_w), (out_full, up_full, down_full)), wsend, wrecv, wlocal
+        late_jobs((out_w, up_w, down_w), (out_full, up_full, down_full)), wsend, wrecv, wlocal
     )
 
     def send_heads(utt):
@@ -257,13 +279,12 @@
         keep.start()
         return [save, keep]
 
+    first = send_heads(0)
     weights.stage()
-    first = send_heads(0)
     arrive(first)
     second = send_heads(1)
     weights.stage()
-    saves = attend(0, weights.stage)
-    weights.stage()
+    saves = attend(0, lambda: None)
     arrive(second)
     saves += attend(1, weights.stage)
     for sent in (first, second):
@@ -292,7 +313,7 @@
     frames = 8 * span
     anywhere = pl.BlockSpec(memory_space=pl.ANY)
     vmem = pl.BlockSpec(memory_space=pltpu.VMEM)
-    full = lambda w: jax.ShapeDtypeStruct((2, 2, 2, 2, 2, w.shape[0] // 4, w.shape[1]), BF)
+    full = lambda w: jax.ShapeDtypeStruct((2, 2, 2, 2, 2) + w.shape[2:], BF)
     dma = pltpu.SemaphoreType.DMA
     outs = pl.pallas_call(
         functools.partial(attend_forward_kernel, span=span, bq=bq, bk=bk),
@@ -331,7 +352,9 @@
         cost_estimate=attention_cost(frames, 4),
         name="attend_forward",
     )(lengths, proj, out_w, up_w, down_w)
-    fulls = [outs[4 + i].reshape(8 * w.shape[0], w.shape[1]) for i, w in enumerate((out_w, up_w, down_w))]
+    fulls = [
+        outs[4 + i].reshape(32 * w.shape[2], w.shape[3]) for i, w in enumerate((out_w, up_w, down_w))
+    ]
     return outs[:4], fulls
 
 
@@ -996,7 +1019,7 @@
     grads, small = refs[:count], refs[count]
     outs, small_out = refs[count + 1 : 2 * count + 1], refs[2 * count + 1]
     rest = refs[2 * count + 2 :]
-    jobs = 2 * count
+    jobs = 3 * count
     buffers = rest[: 6 * jobs]
     small_in, small_low, send, recv, local, ssend, srecv, bsend, brecv, slocal = rest[6 * jobs :]
     me, x, core = lax.axis_index("seq"), lax.axis_index("x"), lax.axis_index("core")
@@ -1004,13 +1027,12 @@
     mates = [(me, (x + dx) % 2, (core + dc) % 2) for dx, dc in ((0, 1), (1, 0), (1, 1))]
     greet(others + mates)
     work = []
+    orders = ((4, 3, 2, 1, 0), (4, 2, 1, 3, 0), (4, 1, 3, 2, 0))
     for index in range(jobs):
-        grad, out = grads[index // 2], outs[index // 2]
-        half = grad.shape[-1] // 2
-        cols = pl.ds((index % 2) * half, half)
+        grad, out = grads[index // 3], outs[index // 3]
+        cols = split_columns(grad.shape[-1], (1, 1, 1))[index % 3]
         keep, arrivals = buffers[6 * index], buffers[6 * index + 1 : 6 * index + 6]
-        order = (4, 3, 2, 1, 0) if index % 2 == 0 else (4, 2, 3, 1, 0)
-        work.append((grad, out, cols, order, keep, arrivals))
+        work.append((grad, out, cols, orders[index % 3], keep, arrivals))
     chain = GradSum(work, send, recv, local)
     chain.stage(0)
     own = pltpu.make_async_copy(small, small_in.at[me], slocal.at[0])
@@ -1051,13 +1073,13 @@
         span = rows // 32
         views.append(grad.reshape(2, 2, 2, 2, 2, span, width))
         outs.append(jax.ShapeDtypeStruct((2, 2, span, width), BF))
-        for _ in range(2):
-            tail = (span, width // 2)
+        for cols in split_columns(width, (1, 1, 1)):
+            tail = (span, cols.size)
             buffers.append(pltpu.VMEM((2, 2, 2, 2) + tail, BF))
             for left in (4, 3, 2, 1, 0):
                 buffers.append(pltpu.VMEM((2,) * left + tail, BF))
     anywhere = pl.BlockSpec(memory_space=pl.ANY)
-    jobs = 2 * len(grads)
+    jobs = 3 * len(grads)
     dma = pltpu.SemaphoreType.DMA
     outs.append(jax.ShapeDtypeStruct((4,) + small.shape, BF))
     results = pl.pallas_call(
@@ -1160,11 +1182,12 @@
     return lax.all_gather(shard, BATCH, axis=0, tiled=True).astype(jnp.float32)
 
 
-def gather_kernel(*refs, shapes):
-    count = len(shapes)
-    weights, seq_small, batch_small = refs[:count], refs[count], refs[count + 1]
-    fulls = refs[count + 2 : 2 * count + 2]
-    seq_out, batch_out, send, recv, small_send, small_recv, local = refs[2 * count + 2 :]
+def gather_kernel(*refs, count, ahead):
+    weights, laters = refs[:count], refs[count : count + ahead]
+    seq_small, batch_small = refs[count + ahead : count + ahead + 2]
+    outs = refs[count + ahead + 2 :]
+    fulls, helds = outs[:count], outs[count : count + ahead]
+    seq_out, batch_out, send, recv, asend, arecv, small_send, small_recv, local = outs[count + ahead :]
     me, x, core = lax.axis_index("seq"), lax.axis_index("x"), lax.axis_index("core")
     bits = (me // 4, (me // 2) % 2, me % 2, x, core)
 
@@ -1203,43 +1226,56 @@
     for copy in small:
         copy.start()
 
-    chain = WeightGather(gather_jobs(weights, fulls), send, recv, local.at[pl.ds(2, 2 * count)])
-    for _ in range(5):
-        chain.stage()
+    jobs = early_jobs(weights, fulls)
+    chain = WeightGather(jobs, send, recv, local.at[pl.ds(2, len(jobs))])
+    later = WeightGather(
+        ahead_jobs(laters, helds), asend, arecv, local.at[pl.ds(2 + len(jobs), ahead)]
+    )
+    chain.stage()
+    chain.stage()
+    later.stage()
+    chain.stage()
+    later.stage()
+    chain.stage()
+    chain.stage()
     chain.finish()
+    later.finish()
     for copy in small:
         copy.wait()
     own_seq.wait()
     own_batch.wait()
 
 
-def gather_early(weights, seq_small, batch_small):
-    shapes = [w.shape for w in weights]
+def gather_early(weights, laters, seq_small, batch_small):
     anywhere = pl.BlockSpec(memory_space=pl.ANY)
-    jobs = 2 * len(weights)
+    jobs, ahead = 3 * len(weights), len(laters)
+    total = len(weights) + ahead + 2
+    dma = pltpu.SemaphoreType.DMA
+    quarter = lambda lead, w: jax.ShapeDtypeStruct((2,) * lead + (w.shape[0] // 4, w.shape[1]), BF)
     outs = pl.pallas_call(
-        functools.partial(gather_kernel, shapes=shapes),
-        in_specs=[anywhere] * (len(weights) + 2),
-        out_specs=[anywhere] * (len(weights) + 2),
-        out_shape=[
-            jax.ShapeDtypeStruct((2, 2, 2, 2, 2, rows // 4, width), BF) for rows, width in shapes
-        ]
+        functools.partial(gather_kernel, count=len(weights), ahead=ahead),
+        in_specs=[anywhere] * total,
+        out_specs=[anywhere] * total,
+        out_shape=[quarter(5, w) for w in weights]
+        + [quarter(2, w) for w in laters]
         + [
             jax.ShapeDtypeStruct((8,) + seq_small.shape, F32),
             jax.ShapeDtypeStruct((4,) + batch_small.shape, F32),
         ],
         scratch_shapes=[
-            pltpu.SemaphoreType.DMA((5 * jobs,)),
-            pltpu.SemaphoreType.DMA((5 * jobs,)),
-            pltpu.SemaphoreType.DMA((10,)),
-            pltpu.SemaphoreType.DMA((10,)),
-            pltpu.SemaphoreType.DMA((2 + jobs,)),
+            dma((5 * jobs,)),
+            dma((5 * jobs,)),
+            dma((5 * ahead,)),
+            dma((5 * ahead,)),
+            dma((10,)),
+            dma((10,)),
+            dma((2 + jobs + ahead,)),
         ],
         compiler_params=pltpu.CompilerParams(collective_id=0, has_side_effects=True),
         name="gather_early",
-    )(*weights, seq_small, batch_small)
-    fulls = [full.reshape(8 * rows, width) for full, (rows, width) in zip(outs, shapes)]
-    return fulls, outs[-2], outs[-1]
+    )(*weights, *laters, seq_small, batch_small)
+    fulls = [full.reshape(8 * w.shape[0], w.shape[1]) for full, w in zip(outs, weights)]
+    return fulls, outs[len(weights) : len(weights) + ahead], outs[-2], outs[-1]
 
 
 def paired_tables(positions):
@@ -1304,8 +1340,11 @@
             ],
             axis=0,
         )
-        (skip_full, qkv_full), mod_every, small_every = gather_early(
-            (skip_weight, qkv_weight), mod_part.reshape(-1, model_width), small
+        (skip_full, qkv_full), late_held, mod_every, small_every = gather_early(
+            (skip_weight, qkv_weight),
+            (out_weight, up_weight, down_weight),
+            mod_part.reshape(-1, model_width),
+            small,
         )
         modulation = jnp.sum(mod_every, axis=0)
         totals = jnp.sum(small_every[:, utt_count, :2], axis=0)
@@ -1333,7 +1372,7 @@
             first_rows, second_rows, skip_full, qkv_full, modulation, cos_here, sin_here
         )
         (qkv_all, out_all, lse_all, attended_low), (out_full, up_full, down_full) = attend_forward(
-            lengths, proj, out_weight, up_weight, down_weight, frame_span
+            lengths, proj, *late_held, frame_span
         )
     else:
         joined = jnp.concatenate([layer_input, skip_input], axis=-1).reshape(row_count, 2 * model_width)

time: 1020 us -> 943 us (0.925)
  Pallas kernels: 973 us -> 891 us
    pallas_call x1, Pallas kernels: 301 us -> 225 us  [attend_forward(): pl.pallas_call(functools.partial(attend_forward_kernel, span=span, bq=bq,...]
    pallas_call x1, Pallas kernels: 196 us -> 165 us  [reduce_grads(): pl.pallas_call(functools.partial(reduce_kernel, count=len(grads)), in_spe...]
    pallas_call x1, Pallas kernels: 83.7 us -> 105 us  [gather_early(): pl.pallas_call(functools.partial(gather_kernel, count=len(weights), ahead...]
where the time goes in v6:
time: 943 us; the launch traced here: 933 us
  Pallas kernels  891 us (94%)
  other arithmetic  19.1 us (2%)
  local copies, waits for them, and re-layouts  16.7 us (2%)
    pallas_call x1, Pallas kernels, attend_backward(): pl.pallas_call(functools.partial(attend_backward_kernel, span=span, block...  237 us
    pallas_call x1, Pallas kernels, attend_forward(): pl.pallas_call(functools.partial(attend_forward_kernel, span=span, bq=bq,...  225 us
    pallas_call x1, Pallas kernels, reduce_grads(): pl.pallas_call(functools.partial(reduce_kernel, count=len(grads)), in_spe...  165 us
    pallas_call x1, Pallas kernels, gather_early(): pl.pallas_call(functools.partial(gather_kernel, count=len(weights), ahead...  105 us
    pallas_call x1, Pallas kernels, ffn_backward(): pl.pallas_call(ffn_backward_kernel, grid=(hidden // chunk,), in_specs=who...  61.1 us
    pallas_call x1, Pallas kernels, ffn_forward(): pl.pallas_call(ffn_forward_kernel, grid=(hidden // chunk,), in_specs=whol...  42.6 us
    pallas_call x1, Pallas kernels, leave_layer(): pl.pallas_call(leave_kernel, grid=(steps,), in_specs=[whole_spec(a.shape)...  36.3 us
    pallas_call x1, Pallas kernels, enter_layer(): pl.pallas_call(enter_kernel, grid=(rows // block,), in_specs=[part, part,...  19.1 us

profile of v6, /device:TPU:0, one launch (start us, length us, event | category | flops | bytes accessed | tf_op | source)
XLA Modules:
  0.0 933.4 jit_solution(10621683067451682978)
XLA Ops:
  1.5 1.3 multiply_reduce_fusion.1
  2.7 1.4 maximum_bitcast_fusion
  7.3 3.7 fusion
  11.4 1.8 copy.24.sin_ref
  13.4 1.8 copy.23.cos_ref
  15.3 1.9 constant_dynamic-slice_fusion
  17.1 105.4 %gather_early.1 = (bf16[2,2,2,2,2,64,1024]{6,5,4,3,2,1,0:T(8,128)(2,1)}, bf16[2,2,2,2,2,32,3072]{6,5,4,3,2,1,0:T(8,128)(2,1)}, bf16[2,2,32,1024]{3,2,1,0:T(8,128...) custom-call(bf16[256,1024]{1,0:T(8,128)(2,1)} %refs_0_.1, ...), custom_call_target="tpu_custom_call" | custom-call | tf_op jit(solution)/shard_map/gather_early/pallas_call | solution.py:1255
  123.2 0.9 slice.39
  126.9 1.1 reduce_sum.47
  128.6 1.0 copy.30
  129.6 19.1 %enter_layer.1 = (f32[1024,1024]{1,0:T(8,128)}, bf16[3,1024,1024]{2,1,0:T(8,128)(2,1)}) custom-call(bf16[1024,1024]{1,0:T(8,128)(2,1)} %bitcast.62, bf16[1024,1024]{1,0:T(8,128)(2,1)} %bitcast.64, bf16[2048,1024]{1,0:T(8,128)(2,1)} %bitcast.58, bf16[1024,3072]{1,0:T(8,128)(2,1)} %bitcast.56, f32[2,6,1024]{2,1,0:T(8,128)} %reshape.225.mod_ref, ...), custom_call_target="tpu_custom_call" | custom-call | flops 10737418240 | bytes 41943040 | tf_op jit(solution)/shard_map/enter_layer/pallas_call | solution.py:827
  148.7 224.7 %attend_forward.1 = (bf16[2,3,4096,128]{3,2,1,0:T(8,128)(2,1)}, bf16[2,4096,128]{2,1,0:T(8,128)(2,1)}, f32[2,8,4096]{2,1,0:T(8,128)}, bf16[1024,1024]{1,0:T(8,12...) custom-call(s32[2]{0:T(128)} %len_ref.3, ...), custom_call_target="tpu_custom_call" | custom-call | flops 34359738368 | bytes 8388608 | tf_op jit(solution)/shard_map/attend_forward/pallas_call | solution.py:318
  373.3 42.6 %ffn_forward.1 = (f32[1024,1024]{1,0:T(8,128)}, bf16[1024,4096]{1,0:T(8,128)(2,1)}, bf16[1024,4096]{1,0:T(8,128)(2,1)}, bf16[1024,1024]{1,0:T(8,128)(2,1)}, bf16...) custom-call(bf16[1024,1024]{1,0:T(8,128)(2,1)} %get-tuple-element.56.att_ref, bf16[1024,1024]{1,0:T(8,128)(2,1)} %bitcast.73, ...), custom_call_target="tpu_custom_call" | custom-call | flops 19327352832 | bytes 62914560 | tf_op jit(solution)/shard_map/ffn_forward/pallas_call | solution.py:718
  415.9 1.3 stack.19
  417.2 61.1 %ffn_backward.1 = (bf16[1024,4096]{1,0:T(8,128)(2,1)}, bf16[4096,1024]{1,0:T(8,128)(2,1)}, f32[1024,1024]{1,0:T(8,128)}, bf16[1024,1024]{1,0:T(8,128)(2,1)}, bf1...) custom-call(bf16[1024,1024]{1,0:T(8,128)(2,1)} %get-tuple-element.56.att_ref, bf16[1024,1024]{1,0:T(8,128)(2,1)} %bitcast.74, ...), custom_call_target="tpu_custom_call" | custom-call | flops 38654705664 | bytes 94371840 | tf_op jit(solution)/shard_map/ffn_backward/pallas_call | solution.py:761
  478.4 236.8 %attend_backward.1.grad_ref = bf16[1024,3072]{1,0:T(8,128)(2,1)} custom-call(s32[2]{0:T(128)} %len_ref.3, bf16[1024,1024]{1,0:T(8,128)(2,1)} %get-tuple-element.67.dout, bf16[2,3,4096,128]{3,2,1,0:T(8,128)(2,1)} %get-tuple-element.68.qkv_all, bf16[2,4096,128]{2,1,0:T(8,128)(2,1)} %get-tuple-element.69.o_all, f32[2,8,4096]{2,1,0:T(8,128)} %get-tuple-element.70.lse_ref, ...), custom_call_target="tpu_custom_call" | custom-call | flops 85899345920 | bytes 8388608 | tf_op jit(solution)/shard_map/attend_backward/pallas_call | solution.py:549
  715.2 36.3 %leave_layer.1 = (bf16[1024,1024]{1,0:T(8,128)(2,1)}, bf16[1024,1024]{1,0:T(8,128)(2,1)}, f32[2,8,1024]{2,1,0:T(8,128)}, bf16[1024,3072]{1,0:T(8,128)(2,1)}, bf16[2,1024,1024]{2,1,0:T(8,128)(2,1)}) custom-call(bf16[1024,3072]{1,0:T(8,128)(2,1)} %attend_backward.1.grad_ref, bf16[1024,3072]{1,0:T(8,128)(2,1)} %bitcast.57, bf16[2048,1024]{1,0:T(8,128)(2,1)} %bitcast.59, ...), custom_call_target="tpu_custom_call" | custom-call | flops 21474836480 | bytes 62914560 | tf_op jit(solution)/shard_map/leave_layer/pallas_call | solution.py:897
  754.7 165.2 %reduce_grads.1 = (bf16[2,2,128,1024]{3,2,1,0:T(8,128)(2,1)}, bf16[2,2,32,4096]{3,2,1,0:T(8,128)(2,1)}, bf16[2,2,32,3072]{3,2,1,0:T(8,128)(2,1)}, bf16[2,2,64,10...) custom-call(bf16[2,2,2,2,2,128,1024]{6,5,4,3,2,1,0:T(8,128)(2,1)} %bitcast.47, ...), custom_call_target="tpu_custom_call" | custom-call | tf_op jit(solution)/shard_map/reduce_grads/pallas_call | solution.py:1085
  919.9 1.1 reshape.238
  921.8 2.2 bitcast_convert_fusion.3
  924.9 1.3 bitcast_convert_fusion.2
  926.2 1.6 bitcast_convert_fusion.1
  927.8 1.6 bitcast_convert_fusion
  929.5 3.8 fusion.10
  (45 shorter events, 12.1 us)
Async XLA Ops:
  0.6 5.6 copy-start
  17.1 109.7 %copy-start.7 = (s32[2]{0:T(128)S(1)}, s32[2]{0:T(128)}, u32[]{:S(2)}) copy-start(s32[2]{0:T(128)} %len_ref.3) | copy-start | bytes 28
  715.2 38.9 %copy-start.6 = (f32[2,1,1024]{2,1,0:T(1,128)S(1)}, f32[2,1,1024]{2,1,0:T(1,128)}, u32[]{:S(2)}) copy-start(f32[2,1,1024]{2,1,0:T(1,128)} %stack.19) | copy-start | bytes 24580
  919.9 4.1 copy-start.5
  919.9 4.9 copy-start.4
  921.8 4.4 copy-start.3
  926.2 1.6 copy-start.2
  927.8 5.4 copy-start.1

commit v7 on v6

--- a/solution.py
+++ b/solution.py
@@ -1,6 +1,7 @@
 import functools
 import jax
 import jax.numpy as jnp
+import numpy as np
 from jax import lax
 from jax.sharding import Mesh, PartitionSpec as P
 from jax.experimental import pallas as pl
@@ -203,6 +204,24 @@
         for copy in copies:
             copy.wait_recv()
 
+    def send_out(utt, there):
+        rows = pl.ds(pl.multiple_of(there * span, span), span)
+        target = att.at[pl.ds(utt * span, span), my_cols]
+
+        @pl.when(there != me)
+        def _():
+            remote(
+                outs.at[utt, rows, :],
+                target,
+                osend.at[utt * 8 + (there ^ me)],
+                orecv.at[utt * 8 + (there ^ me)],
+                (there, x, core),
+            ).start()
+
+        @pl.when(there == me)
+        def _():
+            pltpu.make_async_copy(outs.at[utt, rows, :], target, olocal.at[utt]).start()
+
     def attend(utt, between):
         length = len_ref[utt]
         save = pltpu.make_async_copy(qkv.at[utt], qkv_all.at[utt], slocal.at[utt])
@@ -250,25 +269,9 @@
                 [top_a + jnp.log2(sum_a), top_b + jnp.log2(sum_b), jnp.zeros((6, bq), F32)],
                 axis=0,
             )
-            for part in range(bq // span):
-                there = i * (bq // span) + part
-                rows = pl.ds(pl.multiple_of(there * span, span), span)
-                target = att.at[pl.ds(utt * span, span), my_cols]
-
-                @pl.when(there != me)
-                def _():
-                    remote(
-                        outs.at[utt, rows, :],
-                        target,
-                        osend.at[utt * 8 + (there ^ me)],
-                        orecv.at[utt * 8 + (there ^ me)],
-                        (there, x, core),
-                    ).start()
-
-                @pl.when(there == me)
-                def _():
-                    pltpu.make_async_copy(outs.at[utt, rows, :], target, olocal.at[utt]).start()
-
+            if utt == 1:
+                for part in range(bq // span):
+                    send_out(utt, i * (bq // span) + part)
             return carry
 
         half = frames // bq // 2
@@ -286,6 +289,12 @@
     weights.stage()
     saves = attend(0, lambda: None)
     arrive(second)
+
+    def send_first(i, carry):
+        send_out(0, i)
+        return carry
+
+    lax.fori_loop(0, 8, send_first, 0)
     saves += attend(1, weights.stage)
     for sent in (first, second):
         for copy in sent[1]:
@@ -359,10 +368,10 @@
 
 
 def attend_backward_kernel(
-    len_ref, dout, qkv_all, o_all, lse_ref, cos_ref, sin_ref,
-    grads,
+    len_ref, dout, qkv_all, o_all, lse_ref, cos_ref, sin_ref, raw_a, raw_b, raw_c,
+    grads, got_a, got_b, got_c,
     qkv, outs, douts, qa, qb, da, db, qt, dt, dqa, dqb,
-    dsend, drecv, dlocal, gsend, grecv, glocal, load,
+    dsend, drecv, dlocal, gsend, grecv, glocal, load, rsend, rrecv,
     *, span, block,
 ):
     me, x, core = lax.axis_index("seq"), lax.axis_index("x"), lax.axis_index("core")
@@ -371,7 +380,8 @@
     count = frames // block
     mine = pl.ds(pl.multiple_of(me * span, span), span)
     flips = (7, 6, 5, 4, 3, 2, 1)
-    greet([seq_flip(flip) for flip in flips])
+    mates = [(me, x ^ dx, core ^ dc) for dx, dc in ((0, 1), (1, 0), (1, 1))]
+    greet([seq_flip(flip) for flip in flips] + mates)
     loads = []
     for utt in range(2):
         loads.append(
@@ -489,6 +499,15 @@
                     dk = inner[2 * head] + nn(qt[:, rows], grad)[part]
                     dq[rows, :] += nn(grad, kh)
                     result += [dk, dv]
+
+                @pl.when(i == count - 1)
+                def _():
+                    low = jnp.where(lanes_of(block) < 64, dqa[rows, :], dqb[rows, :]) * 0.125
+                    low = turn_back(low, cos_ref[rows, :], sin_ref[rows, :])
+                    qkv[utt, 0, rows, :] = low.astype(BF)
+                    for step in range(block // span):
+                        send_grads(utt, 0, j * (block // span) + step)
+
                 return tuple(result)
 
             zero = jnp.zeros((64, block), F32)
@@ -505,18 +524,20 @@
 
         lax.fori_loop(0, count, keys_block, 0)
 
-        def finish(i, carry):
-            here = pl.ds(pl.multiple_of(i * block, block), block)
-            lane = lanes_of(block)
-            dq = jnp.where(lane < 64, dqa[here, :], dqb[here, :]) * 0.125
-            qkv[utt, 0, here, :] = turn_back(dq, cos_ref[here, :], sin_ref[here, :]).astype(BF)
-            for step in range(block // span):
-                send_grads(utt, 0, i * (block // span) + step)
-            return carry
-
-        lax.fori_loop(0, count, finish, 0)
-
     first = send_heads(0)
+    raws = []
+    for index, (raw, got) in enumerate(((raw_a, got_a), (raw_b, got_b), (raw_c, got_c))):
+        for slot_at, device in enumerate(mates):
+            at = index * 3 + slot_at
+            copy = remote(
+                raw.at[:, :, :, device[1], device[2]],
+                got.at[slot_at],
+                rsend.at[at],
+                rrecv.at[at],
+                device,
+            )
+            copy.start()
+            raws.append(copy)
     for copy in loads[0]:
         copy.wait()
     arrive(first)
@@ -529,6 +550,8 @@
     for sent in (first, second):
         for copy in sent[1]:
             copy.wait_send()
+    for copy in raws:
+        copy.wait()
     for utt in range(2):
         for part in range(3):
             own = qkv.at[utt, part, mine, :]
@@ -540,7 +563,8 @@
                 copy.wait_recv()
 
 
-def attend_backward(lengths, dout, qkv_all, o_all, lse, cos, sin, span, block=1024):
+def attend_backward(lengths, dout, qkv_all, o_all, lse, cos, sin, raws, span, block=1024):
+    raws = [raw.reshape(2, 2, 2, 2, 2, raw.shape[0] // 32, raw.shape[1]) for raw in raws]
     frames = 8 * span
     rows, width = dout.shape
     anywhere = pl.BlockSpec(memory_space=pl.ANY)
@@ -548,9 +572,13 @@
     dma = pltpu.SemaphoreType.DMA
     return pl.pallas_call(
         functools.partial(attend_backward_kernel, span=span, block=block),
-        in_specs=[pl.BlockSpec(memory_space=pltpu.SMEM)] + [anywhere] * 3 + [vmem] * 3,
-        out_specs=anywhere,
-        out_shape=jax.ShapeDtypeStruct((rows, 3 * width), BF),
+        in_specs=[pl.BlockSpec(memory_space=pltpu.SMEM)]
+        + [anywhere] * 3
+        + [vmem] * 3
+        + [anywhere] * 3,
+        out_specs=[anywhere] * 4,
+        out_shape=[jax.ShapeDtypeStruct((rows, 3 * width), BF)]
+        + [jax.ShapeDtypeStruct((3, 2, 2, 2) + raw.shape[5:], BF) for raw in raws],
         scratch_shapes=[
             pltpu.VMEM((2, 3, frames, 128), BF),
             pltpu.VMEM((2, frames, 128), BF),
@@ -559,13 +587,13 @@
         + [pltpu.VMEM((frames, 128), BF)] * 4
         + [pltpu.VMEM((128, frames), BF)] * 2
         + [pltpu.VMEM((frames, 128), F32)] * 2
-        + [dma((16,)), dma((16,)), dma((2,)), dma((48,)), dma((48,)), dma((6,)), dma((4,))],
+        + [dma((16,)), dma((16,)), dma((2,)), dma((48,)), dma((48,)), dma((6,)), dma((4,)), dma((9,)), dma((9,))],
         compiler_params=pltpu.CompilerParams(
             vmem_limit_bytes=VMEM_LIMIT, collective_id=2, has_side_effects=True
         ),
         cost_estimate=attention_cost(frames, 10),
         name="attend_backward",
-    )(lengths, dout, qkv_all, o_all, lse, cos, sin)
+    )(lengths, dout, qkv_all, o_all, lse, cos, sin, *raws)
 
 
 def layer_norm(stream):
@@ -924,13 +952,15 @@
     return tuple(outs[:4]) + (outs[4].reshape(2 * width, width),)
 
 
-class GradSum:
-    def __init__(self, jobs, send, recv, local):
-        self.jobs, self.send, self.recv, self.local = jobs, send, recv, local
+class GradJob:
+    def __init__(self, grad, arrived, out, cols, order, keep, buffers, loads, sems, base):
+        self.grad, self.arrived, self.out, self.cols, self.order = grad, arrived, out, cols, order
+        self.keep, self.buffers, self.loads = keep, buffers, loads
+        self.send, self.recv, self.local, self.base = *sems, base
         me, x, core = lax.axis_index("seq"), lax.axis_index("x"), lax.axis_index("core")
         self.bits = (me // 4, (me // 2) % 2, me % 2, x, core)
-        self.copies = [[] for _ in jobs]
-        self.keeps = []
+        self.lead = 3 if arrived is not None else 4
+        self.copies, self.locals, self.round = [], [], 0
 
     def peer(self, dim):
         me, x, core = lax.axis_index("seq"), lax.axis_index("x"), lax.axis_index("core")
@@ -938,111 +968,128 @@
             return (me ^ (4 >> dim), x, core)
         return (me, 1 - x, core) if dim == 3 else (me, x, 1 - core)
 
-    def launch(self, index, source, target, dim):
-        at = len(self.copies[index])
-        copy = remote(
-            source,
-            target,
-            self.send.at[index * 7 + at],
-            self.recv.at[index * 7 + at],
-            self.peer(dim),
-        )
+    def launch(self, source, target, dim):
+        at = self.base + len(self.copies)
+        copy = remote(source, target, self.send.at[at], self.recv.at[at], self.peer(dim))
         copy.start()
-        self.copies[index].append(copy)
-
-    def absorb(self, index, stage):
-        _, _, _, order, keep, arrivals = self.jobs[index]
-        done = order[1 : stage + 1]
-        left = [dim for dim in range(4) if dim not in done]
-        self.copies[index][stage].wait_recv()
-
-        def add(i, carry):
-            at = list(self.bits[:4])
-            place = []
+        self.copies.append(copy)
+
+    def load(self, source, target):
+        copy = pltpu.make_async_copy(source, target, self.local.at[self.base + len(self.locals)])
+        copy.start()
+        self.locals.append(copy)
+
+    def add(self, done, others):
+        left = [dim for dim in range(self.lead) if dim not in done]
+
+        def body(i, carry):
+            at, place = list(self.bits[: self.lead]), []
             for n, dim in enumerate(left):
                 bit = (i >> (len(left) - 1 - n)) & 1
                 at[dim] = bit
                 place.append(bit)
-            mine = keep[at[0], at[1], at[2], at[3]].astype(F32)
-            other = arrivals[stage][tuple(place)] if place else arrivals[stage][...]
-            keep[at[0], at[1], at[2], at[3]] = (mine + other.astype(F32)).astype(BF)
+            total = self.keep[tuple(at)].astype(F32)
+            for other in others:
+                total = total + (other[tuple(place)] if place else other[...]).astype(F32)
+            self.keep[tuple(at)] = total.astype(BF)
             return carry
 
-        lax.fori_loop(0, 2 ** len(left), add, 0)
-
-    def stage(self, number):
-        for index, (grad, out, cols, order, keep, arrivals) in enumerate(self.jobs):
-            tail = (slice(None), cols)
-            bits = self.bits
-            if number == 0:
-                lead = (slice(None),) * 4
-                own = pltpu.make_async_copy(
-                    grad.at[lead + (bits[4],) + tail], keep, self.local.at[index]
-                )
-                own.start()
-                self.keeps.append(own)
-                self.launch(index, grad.at[lead + (1 - bits[4],) + tail], arrivals[0], 4)
-            elif number < 5:
-                if number == 1:
-                    self.keeps[index].wait()
-                self.absorb(index, number - 1)
-                dim = order[number]
-                done = order[1:number]
-                where = tuple(
-                    1 - bits[d] if d == dim else bits[d] if d in done else slice(None)
-                    for d in range(4)
-                )
-                self.launch(index, keep.at[where], arrivals[number], dim)
-            elif number == 5:
-                self.absorb(index, 4)
-                mine = keep.at[bits[:4]]
-                spot = out.at[(bits[3], bits[4]) + tail]
-                own = pltpu.make_async_copy(mine, spot, self.local.at[index])
-                own.start()
-                self.keeps[index] = own
-                self.launch(index, mine, spot, 3)
+        lax.fori_loop(0, 2 ** len(left), body, 0)
+
+    def exchange(self, step):
+        dim, done = self.order[step], self.order[:step]
+        where = tuple(
+            1 - self.bits[d] if d == dim else self.bits[d] if d in done else slice(None)
+            for d in range(self.lead)
+        )
+        self.launch(self.keep.at[where], self.buffers[step], dim)
+
+    def advance(self):
+        number, self.round = self.round, self.round + 1
+        tail, bits = (slice(None), self.cols), self.bits
+        steps = len(self.order)
+        every = (slice(None),) * self.lead
+        if number == 0:
+            self.load(self.grad.at[every + bits[self.lead :] + tail], self.keep)
+            if self.arrived is None:
+                self.launch(self.grad.at[every + (1 - bits[4],) + tail], self.loads[0], 4)
             else:
-                self.keeps[index].wait()
-                self.copies[index][5].wait_recv()
-                both = out.at[(slice(None), bits[4]) + tail]
-                self.launch(index, both, both, 4)
+                for slot, buffer in enumerate(self.loads):
+                    self.load(self.arrived.at[(slot,) + every + tail], buffer)
+        elif number == 1:
+            for copy in self.locals:
+                copy.wait()
+            if self.arrived is None:
+                self.copies[0].wait_recv()
+            self.add((), self.loads)
+            self.exchange(0)
+        elif number <= steps + 1:
+            self.copies[-1].wait_recv()
+            self.add(self.order[: number - 1], [self.buffers[number - 2]])
+            if number <= steps:
+                self.exchange(number - 1)
+            else:
+                mine = self.keep.at[bits[: self.lead]]
+                spot = self.out.at[bits[3:5] + tail]
+                self.load(mine, spot)
+                self.launch(mine, spot, 3)
+        elif number == steps + 2:
+            self.locals[-1].wait()
+            self.copies[-1].wait_recv()
+            both = self.out.at[(slice(None), bits[4]) + tail]
+            self.launch(both, both, 4)
 
     def finish(self):
-        for chain in self.copies:
-            chain[6].wait_recv()
-        for chain in self.copies:
-            for copy in chain:
-                copy.wait_send()
-
-
-def reduce_kernel(*refs, count):
-    grads, small = refs[:count], refs[count]
-    outs, small_out = refs[count + 1 : 2 * count + 1], refs[2 * count + 1]
-    rest = refs[2 * count + 2 :]
-    jobs = 3 * count
-    buffers = rest[: 6 * jobs]
-    small_in, small_low, send, recv, local, ssend, srecv, bsend, brecv, slocal = rest[6 * jobs :]
+        self.copies[-1].wait_recv()
+        for copy in self.copies:
+            copy.wait_send()
+
+
+FULL_ORDERS = ((3, 2, 1, 0), (2, 1, 3, 0), (1, 3, 2, 0))
+QUARTER_ORDERS = ((2, 1, 0), (1, 2, 0))
+
+
+def reduce_kernel(*refs, halves, quarters):
+    count = halves + quarters
+    grads, arrived, small = refs[:count], refs[count : count + quarters], refs[count + quarters]
+    refs = refs[count + quarters + 1 :]
+    outs, small_out, rest = refs[:count], refs[count], list(refs[count + 1 :])
+    small_in, small_low, send, recv, local, ssend, srecv, bsend, brecv, slocal = rest[-10:]
     me, x, core = lax.axis_index("seq"), lax.axis_index("x"), lax.axis_index("core")
     others = [seq_flip(flip) for flip in range(7, 0, -1)]
     mates = [(me, (x + dx) % 2, (core + dc) % 2) for dx, dc in ((0, 1), (1, 0), (1, 1))]
     greet(others + mates)
-    work = []
-    orders = ((4, 3, 2, 1, 0), (4, 2, 1, 3, 0), (4, 1, 3, 2, 0))
-    for index in range(jobs):
-        grad, out = grads[index // 3], outs[index // 3]
-        cols = split_columns(grad.shape[-1], (1, 1, 1))[index % 3]
-        keep, arrivals = buffers[6 * index], buffers[6 * index + 1 : 6 * index + 6]
-        work.append((grad, out, cols, orders[index % 3], keep, arrivals))
-    chain = GradSum(work, send, recv, local)
-    chain.stage(0)
+    jobs = []
+    for index, (grad, out) in enumerate(zip(grads, outs)):
+        whole = index < halves
+        orders = FULL_ORDERS if whole else QUARTER_ORDERS
+        for cols, order in zip(split_columns(grad.shape[-1], (1,) * len(orders)), orders):
+            keep = rest.pop(0)
+            loads = [rest.pop(0) for _ in range(1 if whole else 3)]
+            buffers = [rest.pop(0) for _ in order]
+            jobs.append(
+                GradJob(
+                    grad,
+                    None if whole else arrived[index - halves],
+                    out,
+                    cols,
+                    order,
+                    keep,
+                    buffers,
+                    loads,
+                    (send, recv, local),
+                    7 * len(jobs),
+                )
+            )
     own = pltpu.make_async_copy(small, small_in.at[me], slocal.at[0])
     own.start()
     smalls = []
     for flip, device in zip(range(7, 0, -1), others):
         smalls.append(remote(small, small_in.at[me], ssend.at[flip], srecv.at[flip], device))
         smalls[-1].start()
-    for number in range(1, 6):
-        chain.stage(number)
+    for _ in range(3):
+        for job in jobs:
+            job.advance()
     own.wait()
     for copy in smalls:
         copy.wait_recv()
@@ -1057,8 +1104,11 @@
     for slot, device in enumerate(mates):
         lows.append(remote(small_low, small_out.at[quarter], bsend.at[slot], brecv.at[slot], device))
         lows[-1].start()
-    chain.stage(6)
-    chain.finish()
+    for _ in range(4):
+        for job in jobs:
+            job.advance()
+    for job in jobs:
+        job.finish()
     for copy in smalls:
         copy.wait_send()
     keep.wait()
@@ -1066,35 +1116,38 @@
         copy.wait()
 
 
-def reduce_grads(grads, small, collective_id=3):
-    views, outs, buffers = [], [], []
-    for grad in grads:
+def reduce_grads(halves, quarters, arrived, small):
+    grads = list(halves) + list(quarters)
+    views, outs, buffers, jobs = [], [], [], 0
+    for index, grad in enumerate(grads):
         rows, width = grad.shape
         span = rows // 32
         views.append(grad.reshape(2, 2, 2, 2, 2, span, width))
         outs.append(jax.ShapeDtypeStruct((2, 2, span, width), BF))
-        for cols in split_columns(width, (1, 1, 1)):
+        whole = index < len(halves)
+        lead, orders = (4, FULL_ORDERS) if whole else (3, QUARTER_ORDERS)
+        for cols in split_columns(width, (1,) * len(orders)):
+            jobs += 1
             tail = (span, cols.size)
-            buffers.append(pltpu.VMEM((2, 2, 2, 2) + tail, BF))
-            for left in (4, 3, 2, 1, 0):
+            for left in [lead] * (2 if whole else 4) + list(range(lead - 1, -1, -1)):
                 buffers.append(pltpu.VMEM((2,) * left + tail, BF))
     anywhere = pl.BlockSpec(memory_space=pl.ANY)
-    jobs = 3 * len(grads)
     dma = pltpu.SemaphoreType.DMA
     outs.append(jax.ShapeDtypeStruct((4,) + small.shape, BF))
     results = pl.pallas_call(
-        functools.partial(reduce_kernel, count=len(grads)),
-        in_specs=[anywhere] * (len(grads) + 1),
+        functools.partial(reduce_kernel, halves=len(halves), quarters=len(quarters)),
+        in_specs=[anywhere] * (len(grads) + len(arrived) + 1),
         out_specs=[anywhere] * (len(grads) + 1),
         out_shape=outs,
         scratch_shapes=buffers
         + [pltpu.VMEM((8,) + small.shape, F32), pltpu.VMEM(small.shape, BF)]
-        + [dma((7 * jobs,)), dma((7 * jobs,)), dma((jobs,)), dma((8,)), dma((8,)), dma((3,)), dma((3,)), dma((2,))],
+        + [dma((7 * jobs,))] * 3
+        + [dma((8,)), dma((8,)), dma((3,)), dma((3,)), dma((2,))],
         compiler_params=pltpu.CompilerParams(
-            vmem_limit_bytes=VMEM_LIMIT, collective_id=collective_id, has_side_effects=True
+            vmem_limit_bytes=VMEM_LIMIT, collective_id=3, has_side_effects=True
         ),
         name="reduce_grads",
-    )(*views, small)
+    )(*views, *arrived, small)
     shards = [
         result.reshape(grad.shape[0] // 8, grad.shape[1]).astype(jnp.float32)
         for result, grad in zip(results, grads)
@@ -1278,11 +1331,13 @@
     return fulls, outs[len(weights) : len(weights) + ahead], outs[-2], outs[-1]
 
 
-def paired_tables(positions):
-    cos, sin = rotary_tables(positions)
+def paired_tables(count):
     half = HEAD_DIM // 2
-    signed = jnp.concatenate([-sin[:, :half], sin[:, half:]], axis=1)
-    return jnp.tile(cos, (1, 2)), jnp.tile(signed, (1, 2))
+    inverse = np.power(10000.0, -2.0 * np.arange(half) / HEAD_DIM)
+    angles = np.arange(count)[:, None] * inverse[None, :]
+    cos, sin = np.cos(angles), np.sin(angles)
+    tables = (np.tile(cos, (1, 4)), np.tile(np.concatenate([-sin, sin], axis=1), (1, 2)))
+    return tuple(jnp.asarray(table, jnp.float32) for table in tables)
 
 
 def on_device(
@@ -1365,7 +1420,7 @@
     first_rows = layer_input.reshape(row_count, model_width)
     second_rows = skip_input.reshape(row_count, model_width)
     if by_heads:
-        cos_all, sin_all = paired_tables(jnp.arange(frame_count, dtype=jnp.int32))
+        cos_all, sin_all = paired_tables(frame_count)
         cos_here = lax.dynamic_slice_in_dim(cos_all, seq_here * frame_span, frame_span, 0)
         sin_here = lax.dynamic_slice_in_dim(sin_all, seq_here * frame_span, frame_span, 0)
         residual_rows, proj = enter_layer(
@@ -1453,8 +1508,16 @@
     )
     grad_shift_ffn, grad_scale_ffn, grad_gate_attn = ffn_sums[:, 0], ffn_sums[:, 1], ffn_sums[:, 2]
     if by_heads:
-        grad_projected = attend_backward(
-            lengths, grad_attended_flat, qkv_all, out_all, lse_all, cos_all, sin_all, frame_span
+        grad_projected, *arrived = attend_backward(
+            lengths,
+            grad_attended_flat,
+            qkv_all,
+            out_all,
+            lse_all,
+            cos_all,
+            sin_all,
+            (grad_down, grad_up, grad_out),
+            frame_span,
         )
     else:
         grad_attended = grad_attended_flat.reshape(
@@ -1540,11 +1603,13 @@
     ).reshape(utt_count, 6 * model_width)
     weight_grads = (grad_skip_w, grad_qkv, grad_out, grad_up, grad_down)
     if by_heads:
-        order = (4, 3, 1, 0, 2)
         shards, mod_every = reduce_grads(
-            [weight_grads[i] for i in order], grad_modulation.reshape(-1, model_width)
-        )
-        summed = [shards[order.index(i)] for i in range(5)]
+            (grad_qkv, grad_skip_w),
+            (grad_down, grad_up, grad_out),
+            arrived,
+            grad_modulation.reshape(-1, model_width),
+        )
+        summed = [shards[i] for i in (1, 0, 4, 3, 2)]
         mod_every = mod_every.reshape(-1, 6 * model_width)
     else:
         mod_total = lax.psum(grad_modulation, "seq")

time: 943 us -> 908 us (0.963)
  Pallas kernels: 891 us -> 863 us
    pallas_call x1, Pallas kernels: 165 us -> 146 us  [reduce_grads(): pl.pallas_call(functools.partial(reduce_kernel, halves=len(halves), quart...]
where the time goes in v7:
time: 908 us; the launch traced here: 897 us
  Pallas kernels  863 us (95%)
  other arithmetic  15.2 us (2%)
  local copies, waits for them, and re-layouts  12.6 us (1%)
    pallas_call x1, Pallas kernels, attend_backward(): pl.pallas_call(functools.partial(attend_backward_kernel, span=span, block...  229 us
    pallas_call x1, Pallas kernels, attend_forward(): pl.pallas_call(functools.partial(attend_forward_kernel, span=span, bq=bq,...  223 us
    pallas_call x1, Pallas kernels, reduce_grads(): pl.pallas_call(functools.partial(reduce_kernel, halves=len(halves), quart...  146 us
    pallas_call x1, Pallas kernels, gather_early(): pl.pallas_call(functools.partial(gather_kernel, count=len(weights), ahead...  105 us
    pallas_call x1, Pallas kernels, ffn_backward(): pl.pallas_call(ffn_backward_kernel, grid=(hidden // chunk,), in_specs=who...  61.1 us
    pallas_call x1, Pallas kernels, ffn_forward(): pl.pallas_call(ffn_forward_kernel, grid=(hidden // chunk,), in_specs=whol...  42.8 us
    pallas_call x1, Pallas kernels, leave_layer(): pl.pallas_call(leave_kernel, grid=(steps,), in_specs=[whole_spec(a.shape)...  36.3 us
    pallas_call x1, Pallas kernels, enter_layer(): pl.pallas_call(enter_kernel, grid=(rows // block,), in_specs=[part, part,...  19 us

profile of v7, /device:TPU:0, one launch (start us, length us, event | category | flops | bytes accessed | tf_op | source)
XLA Modules:
  0.0 897.2 jit_solution(5044860731593896133)
XLA Ops:
  1.4 1.3 multiply_reduce_fusion.1
  2.7 1.4 maximum_bitcast_fusion
  7.2 1.9 constant_dynamic-slice_fusion
  9.0 105.4 %gather_early.1 = (bf16[2,2,2,2,2,64,1024]{6,5,4,3,2,1,0:T(8,128)(2,1)}, bf16[2,2,2,2,2,32,3072]{6,5,4,3,2,1,0:T(8,128)(2,1)}, bf16[2,2,32,1024]{3,2,1,0:T(8,128...) custom-call(bf16[256,1024]{1,0:T(8,128)(2,1)} %refs_0_.1, ...), custom_call_target="tpu_custom_call" | custom-call | tf_op jit(solution)/shard_map/gather_early/pallas_call | solution.py:1308
  115.2 0.9 slice.31
  118.8 1.1 reduce_sum.47
  120.5 1.0 copy.28
  121.5 19.0 %enter_layer.1 = (f32[1024,1024]{1,0:T(8,128)}, bf16[3,1024,1024]{2,1,0:T(8,128)(2,1)}) custom-call(bf16[1024,1024]{1,0:T(8,128)(2,1)} %bitcast.61, bf16[1024,1024]{1,0:T(8,128)(2,1)} %bitcast.63, bf16[2048,1024]{1,0:T(8,128)(2,1)} %bitcast.57, bf16[1024,3072]{1,0:T(8,128)(2,1)} %bitcast.55, f32[2,6,1024]{2,1,0:T(8,128)} %reshape.183.mod_ref, ...), custom_call_target="tpu_custom_call" | custom-call | flops 10737418240 | bytes 41943040 | tf_op jit(solution)/shard_map/enter_layer/pallas_call | solution.py:855
  140.6 223.3 %attend_forward.1 = (bf16[2,3,4096,128]{3,2,1,0:T(8,128)(2,1)}, bf16[2,4096,128]{2,1,0:T(8,128)(2,1)}, f32[2,8,4096]{2,1,0:T(8,128)}, bf16[1024,1024]{1,0:T(8,12...) custom-call(s32[2]{0:T(128)} %len_ref.3, ...), custom_call_target="tpu_custom_call" | custom-call | flops 34359738368 | bytes 8388608 | tf_op jit(solution)/shard_map/attend_forward/pallas_call | solution.py:327
  363.9 42.8 %ffn_forward.1 = (f32[1024,1024]{1,0:T(8,128)}, bf16[1024,4096]{1,0:T(8,128)(2,1)}, bf16[1024,4096]{1,0:T(8,128)(2,1)}, bf16[1024,1024]{1,0:T(8,128)(2,1)}, bf16...) custom-call(bf16[1024,1024]{1,0:T(8,128)(2,1)} %get-tuple-element.60.att_ref, bf16[1024,1024]{1,0:T(8,128)(2,1)} %bitcast.72, ...), custom_call_target="tpu_custom_call" | custom-call | flops 19327352832 | bytes 62914560 | tf_op jit(solution)/shard_map/ffn_forward/pallas_call | solution.py:746
  406.7 1.3 stack.19
  408.0 61.1 %ffn_backward.1 = (bf16[1024,4096]{1,0:T(8,128)(2,1)}, bf16[4096,1024]{1,0:T(8,128)(2,1)}, f32[1024,1024]{1,0:T(8,128)}, bf16[1024,1024]{1,0:T(8,128)(2,1)}, bf1...) custom-call(bf16[1024,1024]{1,0:T(8,128)(2,1)} %get-tuple-element.60.att_ref, bf16[1024,1024]{1,0:T(8,128)(2,1)} %bitcast.73, ...), custom_call_target="tpu_custom_call" | custom-call | flops 38654705664 | bytes 94371840 | tf_op jit(solution)/shard_map/ffn_backward/pallas_call | solution.py:789
  469.1 0.9 slice.29
  470.8 228.9 %attend_backward.1 = (bf16[1024,3072]{1,0:T(8,128)(2,1)}, bf16[3,2,2,2,128,1024]{5,4,3,2,1,0:T(8,128)(2,1)}, bf16[3,2,2,2,32,4096]{5,4,3,2,1,0:T(8,128)(2,1)}, bf16[3,2,2,2,32,1024]{5,4,3,2,1,0:T(8,128)(2,1)}) custom-call(s32[2]{0:T(128)} %len_ref.3, bf16[1024,1024]{1,0:T(8,128)(2,1)} %get-tuple-element.71.dout, ...), custom_call_target="tpu_custom_call" | custom-call | flops 85899345920 | bytes 8388608 | tf_op jit(solution)/shard_map/attend_backward/pallas_call | solution.py:573
  699.8 36.3 %leave_layer.1 = (bf16[1024,1024]{1,0:T(8,128)(2,1)}, bf16[1024,1024]{1,0:T(8,128)(2,1)}, f32[2,8,1024]{2,1,0:T(8,128)}, bf16[1024,3072]{1,0:T(8,128)(2,1)}, bf16[2,1024,1024]{2,1,0:T(8,128)(2,1)}) custom-call(bf16[1024,3072]{1,0:T(8,128)(2,1)} %get-tuple-element.78.grad_ref, bf16[1024,3072]{1,0:T(8,128)(2,1)} %bitcast.56, bf16[2048,1024]{1,0:T(8,128)(2,1)} %bitcast.58, ...), custom_call_target="tpu_custom_call" | custom-call | flops 21474836480 | bytes 62914560 | tf_op jit(solution)/shard_map/leave_layer/pallas_call | solution.py:925
  736.1 0.8 slice.28
  737.6 146.1 %reduce_grads.1 = (bf16[2,2,32,3072]{3,2,1,0:T(8,128)(2,1)}, bf16[2,2,64,1024]{3,2,1,0:T(8,128)(2,1)}, bf16[2,2,128,1024]{3,2,1,0:T(8,128)(2,1)}, bf16[2,2,32,40...) custom-call(bf16[2,2,2,2,2,32,3072]{6,5,4,3,2,1,0:T(8,128)(2,1)} %bitcast.48, ...), custom_call_target="tpu_custom_call" | custom-call | tf_op jit(solution)/shard_map/reduce_grads/pallas_call | solution.py:1137
  883.7 1.1 reshape.196
  885.6 2.2 bitcast_convert_fusion.3
  887.8 0.9 bitcast_convert_fusion.4
  888.6 1.3 bitcast_convert_fusion.2
  890.0 1.6 bitcast_convert_fusion.1
  891.6 1.6 bitcast_convert_fusion
  893.2 3.8 fusion.8
  (35 shorter events, 8.8 us)
Async XLA Ops:
  0.6 5.6 copy-start
  9.0 109.7 %copy-start.7 = (s32[2]{0:T(128)S(1)}, s32[2]{0:T(128)}, u32[]{:S(2)}) copy-start(s32[2]{0:T(128)} %len_ref.3) | copy-start | bytes 28
  699.7 37.2 %copy-start.6 = (f32[2,1,1024]{2,1,0:T(1,128)S(1)}, f32[2,1,1024]{2,1,0:T(1,128)}, u32[]{:S(2)}) copy-start(f32[2,1,1024]{2,1,0:T(1,128)} %stack.19) | copy-start | bytes 24580
  883.7 4.1 copy-start.5
  883.7 4.9 copy-start.4
  885.6 4.4 copy-start.3
  890.0 1.6 copy-start.2
  891.6 5.4 copy-start.1

commit v8 on v7

--- a/solution.py
+++ b/solution.py
@@ -626,7 +626,7 @@
 
 
 def row_blocks(rows):
-    block = min(rows, 256)
+    block = min(rows, 512)
     return [(at, slice(at, at + block)) for at in range(0, rows, block)]
 
 
@@ -650,8 +650,13 @@
                 normed[here, :] = (hat * (1.0 + mod[4:5]) + mod[3:4]).astype(BF)
         acc[...] = jnp.zeros_like(acc)
 
-    for _, part in row_blocks(rows):
-        act, slope = gelu_and_slope(nn(normed[part, :], up_ref[...]))
+    parts = [part for _, part in row_blocks(rows)]
+    ahead = nn(normed[parts[0], :], up_ref[...])
+    for index, part in enumerate(parts):
+        hidden = ahead
+        if index + 1 < len(parts):
+            ahead = nn(normed[parts[index + 1], :], up_ref[...])
+        act, slope = gelu_and_slope(hidden)
         act = act.astype(BF)
         act_ref[part, :] = act
         slope_ref[part, :] = slope.astype(BF)
@@ -737,7 +742,7 @@
     return pl.BlockSpec(shape, lambda i: zeros, pipeline_mode=pl.Buffered(1))
 
 
-def ffn_forward(att, outw, res, mods, cot, weight, up, down, chunk=512):
+def ffn_forward(att, outw, res, mods, cot, weight, up, down, chunk=1024):
     rows, width = res.shape
     hidden = up.shape[1]
     whole = [whole_spec(a.shape) for a in (att, outw, res, mods, cot, weight)]
@@ -879,11 +884,139 @@
     )(first, second, skip_w, qkv_w, mods, cos, sin)
 
 
+FOLD_DIMS = (2, 1)
+
+
+def fold_jobs(raws, arrived, folded, keeps, buffers):
+    jobs = []
+    for index, (raw, got) in enumerate(zip(raws, arrived)):
+        for side, cols in enumerate(split_columns(raw.shape[-1], (1, 1))):
+            at = 2 * index + side
+            jobs.append((raw, got, cols, FOLD_DIMS[side], folded[at], keeps[at], buffers[at]))
+    return jobs
+
+
+def fold_pair(index, job, send, recv):
+    _, _, _, dim, _, keep, buffer = job
+    me, x, core = lax.axis_index("seq"), lax.axis_index("x"), lax.axis_index("core")
+    bit = ((me // 4) % 2, (me // 2) % 2, me % 2)[dim]
+    lead = (slice(None),) * dim
+    copy = remote(
+        keep.at[lead + (1 - bit,)],
+        buffer,
+        send.at[index],
+        recv.at[index],
+        (me ^ (4 >> dim), x, core),
+    )
+    return copy, lead + (bit,), bit
+
+
+def fold_start(jobs, temps, send, recv, own, tsem, store):
+    x, core = lax.axis_index("x"), lax.axis_index("core")
+    greet([seq_flip(1), seq_flip(2)])
+    owns, pieces = [], []
+    for index, (raw, got, cols, dim, folded, keep, buffer) in enumerate(jobs):
+        owns.append(
+            pltpu.make_async_copy(raw.at[:, :, :, x, core, :, cols], keep, own.at[index])
+        )
+        owns[-1].start()
+        for row in range(0, keep.shape[3], 32):
+            for col in range(0, keep.shape[4], 512):
+                pieces.append((index, row, col))
+    depth = temps.shape[0]
+
+    def loads(at):
+        index, row, col = pieces[at]
+        _, got, cols, *_ = jobs[index]
+        slot = at % depth
+        return [
+            pltpu.make_async_copy(
+                got.at[n, :, :, :, pl.ds(row, 32), pl.ds(cols.start + col, 512)],
+                temps.at[slot, n],
+                tsem.at[3 * slot + n],
+            )
+            for n in range(3)
+        ]
+
+    for at in range(depth):
+        for copy in loads(at):
+            copy.start()
+    for at, (index, row, col) in enumerate(pieces):
+        keep = jobs[index][5]
+        if at == 0 or pieces[at - 1][0] != index:
+            owns[index].wait()
+        for copy in loads(at):
+            copy.wait()
+        slot = at % depth
+        rows, cols = pl.ds(row, 32), pl.ds(col, 512)
+
+        def body(i, carry):
+            a, b, c = i // 4, (i // 2) % 2, i % 2
+            total = keep[a, b, c, rows, cols].astype(F32)
+            for n in range(3):
+                total = total + temps[slot, n, a, b, c].astype(F32)
+            keep[a, b, c, rows, cols] = total.astype(BF)
+            return carry
+
+        lax.fori_loop(0, 8, body, 0)
+        if at + depth < len(pieces):
+            for copy in loads(at + depth):
+                copy.start()
+        if at + 1 == len(pieces) or pieces[at + 1][0] != index:
+            fold_pair(index, jobs[index], send, recv)[0].start()
+
+
+def fold_finish(jobs, send, recv, own, tsem, store):
+    stores = []
+    for index, job in enumerate(jobs):
+        _, _, _, dim, folded, keep, buffer = job
+        copy, where, bit = fold_pair(index, job, send, recv)
+        copy.wait_recv()
+
+        def body(i, carry):
+            place = [i // 2, i % 2]
+            at = list(place)
+            at.insert(dim, bit)
+            total = keep[tuple(at)].astype(F32) + buffer[tuple(place)].astype(F32)
+            keep[tuple(at)] = total.astype(BF)
+            return carry
+
+        lax.fori_loop(0, 4, body, 0)
+        stores.append(pltpu.make_async_copy(keep.at[where], folded, store.at[index]))
+        stores[-1].start()
+    for index, job in enumerate(jobs):
+        fold_pair(index, job, send, recv)[0].wait_send()
+        stores[index].wait()
+
+
 def leave_kernel(
-    grad_ref, qkv_w, skip_w, res_ref, mid_ref, mod_ref, in_ref, skip_ref,
+    grad_ref, qkv_w, skip_w, res_ref, mid_ref, mod_ref, in_ref, skip_ref, *refs
+):
+    raws, arrived = refs[:3], refs[3:6]
+    gin_ref, gskip_ref, sums_ref, gqkv_ref, gw_ref = refs[6:11]
+    folded, normed, stream = refs[11:17], refs[17], refs[18]
+    jobs = fold_jobs(raws, arrived, folded, refs[19:25], refs[25:31])
+    temps, sems = refs[31], refs[32:]
+    step = pl.program_id(0)
+
+    @pl.when(step == 0)
+    def _():
+        fold_start(jobs, temps, *sems)
+
+    leave_compute(
+        step, grad_ref, qkv_w, skip_w, res_ref, mid_ref, mod_ref, in_ref, skip_ref,
+        gin_ref, gskip_ref, sums_ref, gqkv_ref, gw_ref, normed, stream,
+    )
+
+    @pl.when(step == pl.num_programs(0) - 1)
+    def _():
+        fold_finish(jobs, *sems)
+
+
+def leave_compute(
+    step, grad_ref, qkv_w, skip_w, res_ref, mid_ref, mod_ref, in_ref, skip_ref,
     gin_ref, gskip_ref, sums_ref, gqkv_ref, gw_ref, normed, stream,
 ):
-    step = pl.program_id(0)
     rows, width = res_ref.shape
     utts = mod_ref.shape[0]
     span = rows // utts
@@ -918,48 +1051,63 @@
     gw_ref[1] = tn(skip_ref[...], stream[:, here]).astype(BF)
 
 
-def leave_layer(grads, qkv_w, skip_w, res, mid, mods, first, second, steps=4):
+def leave_layer(grads, qkv_w, skip_w, res, mid, mods, first, second, raws, arrived, steps=4):
     rows, width = res.shape
     utts = mods.shape[0]
     ins = (grads, qkv_w, skip_w, res, mid, mods, first, second)
+    views = [raw.reshape(2, 2, 2, 2, 2, raw.shape[0] // 32, raw.shape[1]) for raw in raws]
+    tails = [
+        (view.shape[5], cols.size)
+        for view in views
+        for cols in split_columns(view.shape[-1], (1, 1))
+    ]
+    anywhere = pl.BlockSpec(memory_space=pl.ANY)
+    dma = pltpu.SemaphoreType.DMA
     outs = pl.pallas_call(
         leave_kernel,
         grid=(steps,),
-        in_specs=[whole_spec(a.shape) for a in ins],
+        in_specs=[whole_spec(a.shape) for a in ins] + [anywhere] * 6,
         out_specs=[
             whole_spec((rows, width)),
             whole_spec((rows, width)),
             whole_spec((utts, 8, width)),
             pl.BlockSpec((width, 3 * width // steps), lambda i: (0, i)),
             pl.BlockSpec((2, width, width // steps), lambda i: (0, 0, i)),
-        ],
+        ]
+        + [anywhere] * 6,
         out_shape=[
             jax.ShapeDtypeStruct((rows, width), BF),
             jax.ShapeDtypeStruct((rows, width), BF),
             jax.ShapeDtypeStruct((utts, 8, width), F32),
             jax.ShapeDtypeStruct((width, 3 * width), BF),
             jax.ShapeDtypeStruct((2, width, width), BF),
-        ],
-        scratch_shapes=[pltpu.VMEM((rows, width), BF), pltpu.VMEM((rows, width), BF)],
-        compiler_params=pltpu.CompilerParams(vmem_limit_bytes=VMEM_LIMIT),
+        ]
+        + [jax.ShapeDtypeStruct((2, 2) + tail, BF) for tail in tails],
+        scratch_shapes=[pltpu.VMEM((rows, width), BF), pltpu.VMEM((rows, width), BF)]
+        + [pltpu.VMEM((2, 2, 2) + tail, BF) for tail in tails]
+        + [pltpu.VMEM((2, 2) + tail, BF) for tail in tails]
+        + [pltpu.VMEM((4, 3, 2, 2, 2, 32, 512), BF)]
+        + [dma((6,)), dma((6,)), dma((6,)), dma((12,)), dma((6,))],
+        compiler_params=pltpu.CompilerParams(
+            vmem_limit_bytes=VMEM_LIMIT, collective_id=4, has_side_effects=True
+        ),
         cost_estimate=pl.CostEstimate(
             flops=4 * rows * (skip_w.size + qkv_w.size),
             bytes_accessed=60 * 2**20,
             transcendentals=0,
         ),
         name="leave_layer",
-    )(*ins)
-    return tuple(outs[:4]) + (outs[4].reshape(2 * width, width),)
+    )(*ins, *views, *arrived)
+    return tuple(outs[:4]) + (outs[4].reshape(2 * width, width), outs[5:])
 
 
 class GradJob:
-    def __init__(self, grad, arrived, out, cols, order, keep, buffers, loads, sems, base):
-        self.grad, self.arrived, self.out, self.cols, self.order = grad, arrived, out, cols, order
+    def __init__(self, grad, out, cols, dims, order, keep, buffers, loads, sems, base):
+        self.grad, self.out, self.cols, self.dims, self.order = grad, out, cols, dims, order
         self.keep, self.buffers, self.loads = keep, buffers, loads
         self.send, self.recv, self.local, self.base = *sems, base
         me, x, core = lax.axis_index("seq"), lax.axis_index("x"), lax.axis_index("core")
         self.bits = (me // 4, (me // 2) % 2, me % 2, x, core)
-        self.lead = 3 if arrived is not None else 4
         self.copies, self.locals, self.round = [], [], 0
 
     def peer(self, dim):
@@ -980,13 +1128,13 @@
         self.locals.append(copy)
 
     def add(self, done, others):
-        left = [dim for dim in range(self.lead) if dim not in done]
+        left = [dim for dim in self.dims if dim not in done]
 
         def body(i, carry):
-            at, place = list(self.bits[: self.lead]), []
+            at, place = [self.bits[dim] for dim in self.dims], []
             for n, dim in enumerate(left):
                 bit = (i >> (len(left) - 1 - n)) & 1
-                at[dim] = bit
+                at[self.dims.index(dim)] = bit
                 place.append(bit)
             total = self.keep[tuple(at)].astype(F32)
             for other in others:
@@ -1000,7 +1148,7 @@
         dim, done = self.order[step], self.order[:step]
         where = tuple(
             1 - self.bits[d] if d == dim else self.bits[d] if d in done else slice(None)
-            for d in range(self.lead)
+            for d in self.dims
         )
         self.launch(self.keep.at[where], self.buffers[step], dim)
 
@@ -1008,20 +1156,18 @@
         number, self.round = self.round, self.round + 1
         tail, bits = (slice(None), self.cols), self.bits
         steps = len(self.order)
-        every = (slice(None),) * self.lead
+        every = (slice(None),) * len(self.dims)
         if number == 0:
-            self.load(self.grad.at[every + bits[self.lead :] + tail], self.keep)
-            if self.arrived is None:
+            if self.loads:
+                self.load(self.grad.at[every + (bits[4],) + tail], self.keep)
                 self.launch(self.grad.at[every + (1 - bits[4],) + tail], self.loads[0], 4)
             else:
-                for slot, buffer in enumerate(self.loads):
-                    self.load(self.arrived.at[(slot,) + every + tail], buffer)
+                self.load(self.grad, self.keep)
         elif number == 1:
-            for copy in self.locals:
-                copy.wait()
-            if self.arrived is None:
+            self.locals[0].wait()
+            if self.loads:
                 self.copies[0].wait_recv()
-            self.add((), self.loads)
+                self.add((), self.loads)
             self.exchange(0)
         elif number <= steps + 1:
             self.copies[-1].wait_recv()
@@ -1029,7 +1175,7 @@
             if number <= steps:
                 self.exchange(number - 1)
             else:
-                mine = self.keep.at[bits[: self.lead]]
+                mine = self.keep.at[tuple(bits[dim] for dim in self.dims)]
                 spot = self.out.at[bits[3:5] + tail]
                 self.load(mine, spot)
                 self.launch(mine, spot, 3)
@@ -1046,34 +1192,35 @@
 
 
 FULL_ORDERS = ((3, 2, 1, 0), (2, 1, 3, 0), (1, 3, 2, 0))
-QUARTER_ORDERS = ((2, 1, 0), (1, 2, 0))
-
-
-def reduce_kernel(*refs, halves, quarters):
-    count = halves + quarters
-    grads, arrived, small = refs[:count], refs[count : count + quarters], refs[count + quarters]
-    refs = refs[count + quarters + 1 :]
-    outs, small_out, rest = refs[:count], refs[count], list(refs[count + 1 :])
+FOLDED_DIMS = ((0, 1), (0, 2))
+FOLDED_ORDERS = ((1, 0), (2, 0))
+
+
+def reduce_kernel(*refs, halves, folds):
+    grads, folded, small = refs[:halves], refs[halves : halves + 2 * folds], refs[halves + 2 * folds]
+    refs = refs[halves + 2 * folds + 1 :]
+    outs, small_out = refs[: halves + folds], refs[halves + folds]
+    rest = list(refs[halves + folds + 1 :])
     small_in, small_low, send, recv, local, ssend, srecv, bsend, brecv, slocal = rest[-10:]
     me, x, core = lax.axis_index("seq"), lax.axis_index("x"), lax.axis_index("core")
     others = [seq_flip(flip) for flip in range(7, 0, -1)]
     mates = [(me, (x + dx) % 2, (core + dc) % 2) for dx, dc in ((0, 1), (1, 0), (1, 1))]
     greet(others + mates)
     jobs = []
-    for index, (grad, out) in enumerate(zip(grads, outs)):
+    for index, out in enumerate(outs):
         whole = index < halves
-        orders = FULL_ORDERS if whole else QUARTER_ORDERS
-        for cols, order in zip(split_columns(grad.shape[-1], (1,) * len(orders)), orders):
+        orders = FULL_ORDERS if whole else FOLDED_ORDERS
+        for side, cols in enumerate(split_columns(out.shape[-1], (1,) * len(orders))):
             keep = rest.pop(0)
-            loads = [rest.pop(0) for _ in range(1 if whole else 3)]
-            buffers = [rest.pop(0) for _ in order]
+            loads = [rest.pop(0)] if whole else []
+            buffers = [rest.pop(0) for _ in orders[side]]
             jobs.append(
                 GradJob(
-                    grad,
-                    None if whole else arrived[index - halves],
+                    grads[index] if whole else folded[2 * (index - halves) + side],
                     out,
                     cols,
-                    order,
+                    (0, 1, 2, 3) if whole else FOLDED_DIMS[side],
+                    orders[side],
                     keep,
                     buffers,
                     loads,
@@ -1116,28 +1263,28 @@
         copy.wait()
 
 
-def reduce_grads(halves, quarters, arrived, small):
-    grads = list(halves) + list(quarters)
+def reduce_grads(halves, shapes, folded, small):
     views, outs, buffers, jobs = [], [], [], 0
-    for index, grad in enumerate(grads):
+    for grad in halves:
         rows, width = grad.shape
+        views.append(grad.reshape(2, 2, 2, 2, 2, rows // 32, width))
+    for index, (rows, width) in enumerate([grad.shape for grad in halves] + list(shapes)):
         span = rows // 32
-        views.append(grad.reshape(2, 2, 2, 2, 2, span, width))
         outs.append(jax.ShapeDtypeStruct((2, 2, span, width), BF))
         whole = index < len(halves)
-        lead, orders = (4, FULL_ORDERS) if whole else (3, QUARTER_ORDERS)
+        lead, orders = (4, FULL_ORDERS) if whole else (2, FOLDED_ORDERS)
         for cols in split_columns(width, (1,) * len(orders)):
             jobs += 1
             tail = (span, cols.size)
-            for left in [lead] * (2 if whole else 4) + list(range(lead - 1, -1, -1)):
+            for left in [lead] * (2 if whole else 1) + list(range(lead - 1, -1, -1)):
                 buffers.append(pltpu.VMEM((2,) * left + tail, BF))
     anywhere = pl.BlockSpec(memory_space=pl.ANY)
     dma = pltpu.SemaphoreType.DMA
     outs.append(jax.ShapeDtypeStruct((4,) + small.shape, BF))
     results = pl.pallas_call(
-        functools.partial(reduce_kernel, halves=len(halves), quarters=len(quarters)),
-        in_specs=[anywhere] * (len(grads) + len(arrived) + 1),
-        out_specs=[anywhere] * (len(grads) + 1),
+        functools.partial(reduce_kernel, halves=len(halves), folds=len(shapes)),
+        in_specs=[anywhere] * (len(halves) + len(folded) + 1),
+        out_specs=[anywhere] * len(outs),
         out_shape=outs,
         scratch_shapes=buffers
         + [pltpu.VMEM((8,) + small.shape, F32), pltpu.VMEM(small.shape, BF)]
@@ -1147,10 +1294,10 @@
             vmem_limit_bytes=VMEM_LIMIT, collective_id=3, has_side_effects=True
         ),
         name="reduce_grads",
-    )(*views, *arrived, small)
+    )(*views, *folded, small)
     shards = [
-        result.reshape(grad.shape[0] // 8, grad.shape[1]).astype(jnp.float32)
-        for result, grad in zip(results, grads)
+        result.reshape(4 * result.shape[2], result.shape[3]).astype(jnp.float32)
+        for result in results[:-1]
     ]
     return shards, results[-1].astype(jnp.float32)
 
@@ -1555,7 +1702,7 @@
             .astype(jnp.bfloat16)
         )
     if by_heads:
-        grad_input, grad_skip, attn_sums, grad_qkv, grad_skip_w = leave_layer(
+        grad_input, grad_skip, attn_sums, grad_qkv, grad_skip_w, folded = leave_layer(
             grad_projected,
             qkv_full,
             skip_full,
@@ -1564,6 +1711,8 @@
             modulation,
             first_rows,
             second_rows,
+            (grad_down, grad_up, grad_out),
+            arrived,
         )
         grad_input = grad_input.reshape(layer_input.shape)
         grad_skip = grad_skip.reshape(skip_input.shape)
@@ -1605,8 +1754,8 @@
     if by_heads:
         shards, mod_every = reduce_grads(
             (grad_qkv, grad_skip_w),
-            (grad_down, grad_up, grad_out),
-            arrived,
+            [grad.shape for grad in (grad_down, grad_up, grad_out)],
+            folded,
             grad_modulation.reshape(-1, model_width),
         )
         summed = [shards[i] for i in (1, 0, 4, 3, 2)]

time: 908 us -> 890 us (0.980)
  Pallas kernels: 863 us -> 842 us
    pallas_call x1, Pallas kernels: 146 us -> 97.8 us  [reduce_grads(): pl.pallas_call(functools.partial(reduce_kernel, halves=len(halves), folds...]
    pallas_call x1, Pallas kernels: 36.3 us -> 73.8 us  [leave_layer(): pl.pallas_call(leave_kernel, grid=(steps,), in_specs=[whole_spec(a.shape)...]
where the time goes in v8:
time: 890 us; the launch traced here: 880 us
  Pallas kernels  842 us (95%)
  local copies, waits for them, and re-layouts  16.3 us (2%)
  other arithmetic  15.2 us (2%)
    pallas_call x1, Pallas kernels, attend_backward(): pl.pallas_call(functools.partial(attend_backward_kernel, span=span, block...  229 us
    pallas_call x1, Pallas kernels, attend_forward(): pl.pallas_call(functools.partial(attend_forward_kernel, span=span, bq=bq,...  223 us
    pallas_call x1, Pallas kernels, gather_early(): pl.pallas_call(functools.partial(gather_kernel, count=len(weights), ahead...  105 us
    pallas_call x1, Pallas kernels, reduce_grads(): pl.pallas_call(functools.partial(reduce_kernel, halves=len(halves), folds...  97.8 us
    pallas_call x1, Pallas kernels, leave_layer(): pl.pallas_call(leave_kernel, grid=(steps,), in_specs=[whole_spec(a.shape)...  73.8 us
    pallas_call x1, Pallas kernels, ffn_backward(): pl.pallas_call(ffn_backward_kernel, grid=(hidden // chunk,), in_specs=who...  58.5 us
    pallas_call x1, Pallas kernels, ffn_forward(): pl.pallas_call(ffn_forward_kernel, grid=(hidden // chunk,), in_specs=whol...  35.7 us
    pallas_call x1, Pallas kernels, enter_layer(): pl.pallas_call(enter_kernel, grid=(rows // block,), in_specs=[part, part,...  19 us

profile of v8, /device:TPU:0, one launch (start us, length us, event | category | flops | bytes accessed | tf_op | source)
XLA Modules:
  0.0 880.5 jit_solution(3631266773716858551)
XLA Ops:
  1.4 1.3 multiply_reduce_fusion.1
  2.7 1.4 maximum_bitcast_fusion
  7.2 1.9 constant_dynamic-slice_fusion
  9.0 105.4 %gather_early.1 = (bf16[2,2,2,2,2,64,1024]{6,5,4,3,2,1,0:T(8,128)(2,1)}, bf16[2,2,2,2,2,32,3072]{6,5,4,3,2,1,0:T(8,128)(2,1)}, bf16[2,2,32,1024]{3,2,1,0:T(8,128...) custom-call(bf16[256,1024]{1,0:T(8,128)(2,1)} %refs_0_.1, ...), custom_call_target="tpu_custom_call" | custom-call | tf_op jit(solution)/shard_map/gather_early/pallas_call | solution.py:1455
  115.2 0.9 slice.31
  118.8 1.1 reduce_sum.47
  120.5 1.0 copy.28
  121.5 19.0 %enter_layer.1 = (f32[1024,1024]{1,0:T(8,128)}, bf16[3,1024,1024]{2,1,0:T(8,128)(2,1)}) custom-call(bf16[1024,1024]{1,0:T(8,128)(2,1)} %bitcast.57, bf16[1024,1024]{1,0:T(8,128)(2,1)} %bitcast.59, bf16[2048,1024]{1,0:T(8,128)(2,1)} %bitcast.53, bf16[1024,3072]{1,0:T(8,128)(2,1)} %bitcast.51, f32[2,6,1024]{2,1,0:T(8,128)} %reshape.183.mod_ref, ...), custom_call_target="tpu_custom_call" | custom-call | flops 10737418240 | bytes 41943040 | tf_op jit(solution)/shard_map/enter_layer/pallas_call | solution.py:860
  140.6 223.1 %attend_forward.1 = (bf16[2,3,4096,128]{3,2,1,0:T(8,128)(2,1)}, bf16[2,4096,128]{2,1,0:T(8,128)(2,1)}, f32[2,8,4096]{2,1,0:T(8,128)}, bf16[1024,1024]{1,0:T(8,12...) custom-call(s32[2]{0:T(128)} %len_ref.3, ...), custom_call_target="tpu_custom_call" | custom-call | flops 34359738368 | bytes 8388608 | tf_op jit(solution)/shard_map/attend_forward/pallas_call | solution.py:327
  363.7 35.7 %ffn_forward.1 = (f32[1024,1024]{1,0:T(8,128)}, bf16[1024,4096]{1,0:T(8,128)(2,1)}, bf16[1024,4096]{1,0:T(8,128)(2,1)}, bf16[1024,1024]{1,0:T(8,128)(2,1)}, bf16...) custom-call(bf16[1024,1024]{1,0:T(8,128)(2,1)} %get-tuple-element.66.att_ref, bf16[1024,1024]{1,0:T(8,128)(2,1)} %bitcast.72, ...), custom_call_target="tpu_custom_call" | custom-call | flops 19327352832 | bytes 62914560 | tf_op jit(solution)/shard_map/ffn_forward/pallas_call | solution.py:751
  399.4 1.3 stack.19
  400.7 58.5 %ffn_backward.1 = (bf16[1024,4096]{1,0:T(8,128)(2,1)}, bf16[4096,1024]{1,0:T(8,128)(2,1)}, f32[1024,1024]{1,0:T(8,128)}, bf16[1024,1024]{1,0:T(8,128)(2,1)}, bf1...) custom-call(bf16[1024,1024]{1,0:T(8,128)(2,1)} %get-tuple-element.66.att_ref, bf16[1024,1024]{1,0:T(8,128)(2,1)} %bitcast.73, ...), custom_call_target="tpu_custom_call" | custom-call | flops 38654705664 | bytes 94371840 | tf_op jit(solution)/shard_map/ffn_backward/pallas_call | solution.py:794
  460.9 228.9 %attend_backward.1 = (bf16[1024,3072]{1,0:T(8,128)(2,1)}, bf16[3,2,2,2,128,1024]{5,4,3,2,1,0:T(8,128)(2,1)}, bf16[3,2,2,2,32,4096]{5,4,3,2,1,0:T(8,128)(2,1)}, bf16[3,2,2,2,32,1024]{5,4,3,2,1,0:T(8,128)(2,1)}) custom-call(s32[2]{0:T(128)} %len_ref.3, bf16[1024,1024]{1,0:T(8,128)(2,1)} %get-tuple-element.77.dout, ...), custom_call_target="tpu_custom_call" | custom-call | flops 85899345920 | bytes 8388608 | tf_op jit(solution)/shard_map/attend_backward/pallas_call | solution.py:573
  689.8 73.8 %leave_layer.1 = (bf16[1024,1024]{1,0:T(8,128)(2,1)}, bf16[1024,1024]{1,0:T(8,128)(2,1)}, f32[2,8,1024]{2,1,0:T(8,128)}, bf16[1024,3072]{1,0:T(8,128)(2,1)}, bf1...) custom-call(bf16[1024,3072]{1,0:T(8,128)(2,1)} %get-tuple-element.84, ...), custom_call_target="tpu_custom_call" | custom-call | flops 21474836480 | bytes 62914560 | tf_op jit(solution)/shard_map/leave_layer/pallas_call | solution.py:1066
  765.1 97.8 %reduce_grads.1 = (bf16[2,2,32,3072]{3,2,1,0:T(8,128)(2,1)}, bf16[2,2,64,1024]{3,2,1,0:T(8,128)(2,1)}, bf16[2,2,128,1024]{3,2,1,0:T(8,128)(2,1)}, bf16[2,2,32,40...) custom-call(bf16[2,2,2,2,2,32,3072]{6,5,4,3,2,1,0:T(8,128)(2,1)} %bitcast.44, ...), custom_call_target="tpu_custom_call" | custom-call | tf_op jit(solution)/shard_map/reduce_grads/pallas_call | solution.py:1284
  862.9 1.1 reshape.196
  864.8 2.2 bitcast_convert_fusion.3
  867.9 1.3 bitcast_convert_fusion.2
  869.2 1.6 bitcast_convert_fusion.1
  870.8 1.6 bitcast_convert_fusion
  872.5 3.9 fusion.8
  876.4 1.3 copy.32
  877.7 1.0 copy-done.2
  878.7 1.3 copy.33
  (41 shorter events, 11.4 us)
Async XLA Ops:
  0.6 5.6 copy-start
  9.0 109.6 %copy-start.9 = (s32[2]{0:T(128)S(1)}, s32[2]{0:T(128)}, u32[]{:S(2)}) copy-start(s32[2]{0:T(128)} %len_ref.3) | copy-start | bytes 28
  689.8 74.6 %copy-start.8 = (f32[2,1,1024]{2,1,0:T(1,128)S(1)}, f32[2,1,1024]{2,1,0:T(1,128)}, u32[]{:S(2)}) copy-start(f32[2,1,1024]{2,1,0:T(1,128)} %stack.19) | copy-start | bytes 24580
  862.9 4.1 copy-start.7
  862.9 4.9 copy-start.6
  864.8 4.4 copy-start.5
  869.2 1.6 copy-start.4
  872.5 3.9 copy-start.3
  876.4 2.3 copy-start.2
  876.4 3.7 copy-start.1

commit v9 on v8

--- a/solution.py
+++ b/solution.py
@@ -68,6 +68,11 @@
     for device in devices:
         pl.semaphore_signal(barrier, inc=1, device_id=device, device_id_type=MESH_IDS)
     pl.semaphore_wait(barrier, len(devices))
+
+
+def far_first(at, count):
+    near = lax.axis_index("seq") // 4
+    return (at + (count // 2) * (1 - near)) % count
 
 
 def remote(source, target, send, recv, device):
@@ -242,7 +247,8 @@
 
         lax.fori_loop(0, frames // bk, build, 0)
 
-        def block(i, carry):
+        def block(i_at, carry):
+            i = far_first(i_at, frames // bq)
             here = pl.ds(pl.multiple_of(i * bq, bq), bq)
             lane = lanes_of(bq)
             queries = qkv[utt, 0, here, :].astype(F32)
@@ -472,7 +478,8 @@
 
         lax.fori_loop(0, count, build, 0)
 
-        def keys_block(i, carry):
+        def keys_block(step_at, carry):
+            i = far_first(step_at, count)
             here = pl.ds(pl.multiple_of(i * block, block), block)
             lane = lanes_of(block)
             pos = i * block + lax.broadcasted_iota(jnp.int32, (block, 128), 0)
@@ -486,7 +493,8 @@
             va = jnp.where(lane < 64, vals, ones_a).astype(BF)
             vb = jnp.where(lane >= 64, vals, ones_b).astype(BF)
 
-            def body(j, inner):
+            def body(j_at, inner):
+                j = far_first(j_at, count)
                 rows = pl.ds(pl.multiple_of(j * block, block), block)
                 result = []
                 for head, (qh, dh, kh, vh, dq) in enumerate(
@@ -500,7 +508,7 @@
                     dq[rows, :] += nn(grad, kh)
                     result += [dk, dv]
 
-                @pl.when(i == count - 1)
+                @pl.when(step_at == count - 1)
                 def _():
                     low = jnp.where(lanes_of(block) < 64, dqa[rows, :], dqb[rows, :]) * 0.125
                     low = turn_back(low, cos_ref[rows, :], sin_ref[rows, :])
@@ -824,64 +832,6 @@
         ),
         name="ffn_backward",
     )(att, outw, res, branch, mods, cot, weight, gb, act, slope, up, down)
-
-
-def enter_kernel(
-    in_ref, skip_ref, skip_w, qkv_w, mod_ref, cos_ref, sin_ref, res_ref, proj_ref
-):
-    width = in_ref.shape[1]
-    mod = mod_ref[0]
-    residual = nn(in_ref[...], skip_w[:width, :]) + nn(skip_ref[...], skip_w[width:, :])
-    res_ref[...] = residual
-    hat, _ = layer_norm(residual)
-    normed = (hat * (1.0 + mod[1:2]) + mod[0:1]).astype(BF)
-    lane = lanes_of(in_ref.shape[0])
-    cos, sin = cos_ref[...], sin_ref[...]
-    for part in range(3):
-        projected = nn(normed, qkv_w[:, part * width : (part + 1) * width])
-        for group in range(width // 128):
-            cols = slice(group * 128, group * 128 + 128)
-            piece = projected[:, cols]
-            if part < 2:
-                turned = jnp.where(
-                    (lane & 63) < 32, pltpu.roll(piece, 96, 1), pltpu.roll(piece, 32, 1)
-                )
-                piece = piece * cos + turned * sin
-            if part == 0:
-                piece = piece * (0.125 * LOG2E)
-            proj_ref[part, :, cols] = piece.astype(BF)
-
-
-def enter_layer(first, second, skip_w, qkv_w, mods, cos, sin, block=256):
-    rows, width = first.shape
-    steps = rows // mods.shape[0] // block
-    part = pl.BlockSpec((block, width), lambda i: (i, 0))
-    table = pl.BlockSpec((block, 128), lambda i: (i % steps, 0))
-    return pl.pallas_call(
-        enter_kernel,
-        grid=(rows // block,),
-        in_specs=[
-            part,
-            part,
-            whole_spec(skip_w.shape),
-            whole_spec(qkv_w.shape),
-            pl.BlockSpec((1,) + mods.shape[1:], lambda i: (i // steps, 0, 0)),
-            table,
-            table,
-        ],
-        out_specs=[part, pl.BlockSpec((3, block, width), lambda i: (0, i, 0))],
-        out_shape=[
-            jax.ShapeDtypeStruct((rows, width), F32),
-            jax.ShapeDtypeStruct((3, rows, width), BF),
-        ],
-        compiler_params=pltpu.CompilerParams(vmem_limit_bytes=VMEM_LIMIT),
-        cost_estimate=pl.CostEstimate(
-            flops=2 * rows * (skip_w.size + qkv_w.size),
-            bytes_accessed=40 * 2**20,
-            transcendentals=0,
-        ),
-        name="enter_layer",
-    )(first, second, skip_w, qkv_w, mods, cos, sin)
 
 
 FOLD_DIMS = (2, 1)
@@ -1382,12 +1332,17 @@
     return lax.all_gather(shard, BATCH, axis=0, tiled=True).astype(jnp.float32)
 
 
-def gather_kernel(*refs, count, ahead):
+def gather_kernel(*refs, count, ahead, block):
     weights, laters = refs[:count], refs[count : count + ahead]
-    seq_small, batch_small = refs[count + ahead : count + ahead + 2]
-    outs = refs[count + ahead + 2 :]
+    refs = refs[count + ahead :]
+    seq_small, batch_small, first, second, cos_ref, sin_ref = refs[:6]
+    outs = refs[6:]
     fulls, helds = outs[:count], outs[count : count + ahead]
-    seq_out, batch_out, send, recv, asend, arecv, small_send, small_recv, local = outs[count + ahead :]
+    batch_out, mod_out, res_out, proj_out = outs[count + ahead : count + ahead + 4]
+    (
+        seq_out, mods, skip_w, qkv_w, res, proj,
+        send, recv, asend, arecv, small_send, small_recv, local, lift, put,
+    ) = outs[count + ahead + 4 :]
     me, x, core = lax.axis_index("seq"), lax.axis_index("x"), lax.axis_index("core")
     bits = (me // 4, (me // 2) % 2, me % 2, x, core)
 
@@ -1434,35 +1389,97 @@
     chain.stage()
     chain.stage()
     later.stage()
+    for copy in small:
+        copy.wait()
+    own_seq.wait()
+    own_batch.wait()
+    total = seq_out[0]
+    for index in range(1, 8):
+        total = total + seq_out[index]
+    mod_out[...] = total
+    utts = mods.shape[0]
+    for utt in range(utts):
+        mods[utt, 0:6, :] = total[utt * 6 : utt * 6 + 6]
     chain.stage()
     later.stage()
     chain.stage()
     chain.stage()
     chain.finish()
+    for index, (full, flat) in enumerate(zip(fulls, (skip_w, qkv_w))):
+        span = full.shape[5]
+
+        def carry_in(p, carry):
+            bits = (p // 16, (p // 8) % 2, (p // 4) % 2, (p // 2) % 2, p % 2)
+            rows = pl.ds(pl.multiple_of(p * span, span), span)
+            pltpu.make_async_copy(full.at[bits], flat.at[rows, :], lift.at[index]).start()
+            return carry
+
+        lax.fori_loop(0, 32, carry_in, 0)
+    for index, flat in enumerate((skip_w, qkv_w)):
+        pltpu.make_async_copy(flat, flat, lift.at[index]).wait()
+    rows, width = first.shape
+    steps = rows // utts // block
+
+    def enter(i, carry):
+        here = pl.ds(pl.multiple_of(i * block, block), block)
+        table = pl.ds(pl.multiple_of((i % steps) * block, block), block)
+        mod = mods[i // steps]
+        residual = nn(first[here, :], skip_w[:width, :]) + nn(second[here, :], skip_w[width:, :])
+        res[here, :] = residual
+        hat, _ = layer_norm(residual)
+        normed = (hat * (1.0 + mod[1:2]) + mod[0:1]).astype(BF)
+        lane = lanes_of(block)
+        cos, sin = cos_ref[table, :], sin_ref[table, :]
+        for part in range(3):
+            projected = nn(normed, qkv_w[:, part * width : (part + 1) * width])
+            for group in range(width // 128):
+                cols = slice(group * 128, group * 128 + 128)
+                piece = projected[:, cols]
+                if part < 2:
+                    turned = jnp.where(
+                        (lane & 63) < 32, pltpu.roll(piece, 96, 1), pltpu.roll(piece, 32, 1)
+                    )
+                    piece = piece * cos + turned * sin
+                if part == 0:
+                    piece = piece * (0.125 * LOG2E)
+                proj[part, here, cols] = piece.astype(BF)
+        pltpu.make_async_copy(res.at[here, :], res_out.at[here, :], put.at[0]).start()
+        pltpu.make_async_copy(proj.at[:, here, :], proj_out.at[:, here, :], put.at[1]).start()
+        return carry
+
+    lax.fori_loop(0, rows // block, enter, 0)
     later.finish()
-    for copy in small:
-        copy.wait()
-    own_seq.wait()
-    own_batch.wait()
-
-
-def gather_early(weights, laters, seq_small, batch_small):
+    pltpu.make_async_copy(res, res_out, put.at[0]).wait()
+    pltpu.make_async_copy(proj, proj_out, put.at[1]).wait()
+
+
+def gather_early(weights, laters, seq_small, batch_small, first, second, cos, sin, block=256):
     anywhere = pl.BlockSpec(memory_space=pl.ANY)
+    vmem = pl.BlockSpec(memory_space=pltpu.VMEM)
     jobs, ahead = 3 * len(weights), len(laters)
-    total = len(weights) + ahead + 2
+    rows, width = first.shape
     dma = pltpu.SemaphoreType.DMA
     quarter = lambda lead, w: jax.ShapeDtypeStruct((2,) * lead + (w.shape[0] // 4, w.shape[1]), BF)
     outs = pl.pallas_call(
-        functools.partial(gather_kernel, count=len(weights), ahead=ahead),
-        in_specs=[anywhere] * total,
-        out_specs=[anywhere] * total,
+        functools.partial(gather_kernel, count=len(weights), ahead=ahead, block=block),
+        in_specs=[anywhere] * (len(weights) + ahead + 2) + [vmem] * 4,
+        out_specs=[anywhere] * (len(weights) + ahead + 1) + [vmem] + [anywhere] * 2,
         out_shape=[quarter(5, w) for w in weights]
         + [quarter(2, w) for w in laters]
         + [
-            jax.ShapeDtypeStruct((8,) + seq_small.shape, F32),
             jax.ShapeDtypeStruct((4,) + batch_small.shape, F32),
+            jax.ShapeDtypeStruct(seq_small.shape, F32),
+            jax.ShapeDtypeStruct((rows, width), F32),
+            jax.ShapeDtypeStruct((3, rows, width), BF),
         ],
         scratch_shapes=[
+            pltpu.VMEM((8,) + seq_small.shape, F32),
+            pltpu.VMEM((seq_small.shape[0] // 6, 8, width), F32),
+        ]
+        + [pltpu.VMEM((8 * w.shape[0], w.shape[1]), BF) for w in weights]
+        + [
+            pltpu.VMEM((rows, width), F32),
+            pltpu.VMEM((3, rows, width), BF),
             dma((5 * jobs,)),
             dma((5 * jobs,)),
             dma((5 * ahead,)),
@@ -1470,12 +1487,16 @@
             dma((10,)),
             dma((10,)),
             dma((2 + jobs + ahead,)),
+            dma((2,)),
+            dma((2,)),
         ],
-        compiler_params=pltpu.CompilerParams(collective_id=0, has_side_effects=True),
+        compiler_params=pltpu.CompilerParams(
+            vmem_limit_bytes=VMEM_LIMIT, collective_id=0, has_side_effects=True
+        ),
         name="gather_early",
-    )(*weights, *laters, seq_small, batch_small)
+    )(*weights, *laters, seq_small, batch_small, first, second, cos, sin)
     fulls = [full.reshape(8 * w.shape[0], w.shape[1]) for full, w in zip(outs, weights)]
-    return fulls, outs[len(weights) : len(weights) + ahead], outs[-2], outs[-1]
+    return fulls, outs[len(weights) : len(weights) + ahead], *outs[-4:]
 
 
 def paired_tables(count):
@@ -1542,13 +1563,20 @@
             ],
             axis=0,
         )
-        (skip_full, qkv_full), late_held, mod_every, small_every = gather_early(
+        cos_all, sin_all = paired_tables(frame_count)
+        first_rows = layer_input.reshape(row_count, model_width)
+        second_rows = skip_input.reshape(row_count, model_width)
+        gathered = gather_early(
             (skip_weight, qkv_weight),
             (out_weight, up_weight, down_weight),
             mod_part.reshape(-1, model_width),
             small,
-        )
-        modulation = jnp.sum(mod_every, axis=0)
+            first_rows,
+            second_rows,
+            lax.dynamic_slice_in_dim(cos_all, seq_here * frame_span, frame_span, 0),
+            lax.dynamic_slice_in_dim(sin_all, seq_here * frame_span, frame_span, 0),
+        )
+        (skip_full, qkv_full), late_held, small_every, modulation, residual_rows, proj = gathered
         totals = jnp.sum(small_every[:, utt_count, :2], axis=0)
         silu_every = small_every[:, :utt_count].reshape(-1, model_width)
     else:
@@ -1564,15 +1592,7 @@
     loss_weight = (valid_mask - dropped) * (every_count / (2.0 * kept_total)) + dropped * (
         every_count / (2.0 * drop_total)
     )
-    first_rows = layer_input.reshape(row_count, model_width)
-    second_rows = skip_input.reshape(row_count, model_width)
     if by_heads:
-        cos_all, sin_all = paired_tables(frame_count)
-        cos_here = lax.dynamic_slice_in_dim(cos_all, seq_here * frame_span, frame_span, 0)
-        sin_here = lax.dynamic_slice_in_dim(sin_all, seq_here * frame_span, frame_span, 0)
-        residual_rows, proj = enter_layer(
-            first_rows, second_rows, skip_full, qkv_full, modulation, cos_here, sin_here
-        )
         (qkv_all, out_all, lse_all, attended_low), (out_full, up_full, down_full) = attend_forward(
             lengths, proj, *late_held, frame_span
         )

time: 890 us -> 868 us (0.975)
  Pallas kernels: 842 us -> 820 us
    pallas_call x1, Pallas kernels: 73.8 us -> 50.5 us  [leave_layer(): pl.pallas_call(leave_kernel, grid=(steps,), in_specs=[whole_spec(a.shape)...]
    pallas_call x1, Pallas kernels: 105 us -> 127 us  [gather_early(): pl.pallas_call(functools.partial(gather_kernel, count=len(weights), ahead...]
    pallas_call x1 -> x0, Pallas kernels: 19 us -> none  [enter_layer(): pl.pallas_call(enter_kernel, grid=(rows // block,), in_specs=[part, part,...]
where the time goes in v9:
time: 868 us; the launch traced here: 858 us
  Pallas kernels  820 us (94%)
  local copies, waits for them, and re-layouts  17.2 us (2%)
  other arithmetic  14.1 us (2%)
    pallas_call x1, Pallas kernels, attend_backward(): pl.pallas_call(functools.partial(attend_backward_kernel, span=span, block...  224 us
    pallas_call x1, Pallas kernels, attend_forward(): pl.pallas_call(functools.partial(attend_forward_kernel, span=span, bq=bq,...  224 us
    pallas_call x1, Pallas kernels, gather_early(): pl.pallas_call(functools.partial(gather_kernel, count=len(weights), ahead...  127 us
    pallas_call x1, Pallas kernels, reduce_grads(): pl.pallas_call(functools.partial(reduce_kernel, halves=len(halves), folds...  100 us
    pallas_call x1, Pallas kernels, ffn_backward(): pl.pallas_call(ffn_backward_kernel, grid=(hidden // chunk,), in_specs=who...  58.5 us
    pallas_call x1, Pallas kernels, leave_layer(): pl.pallas_call(leave_kernel, grid=(steps,), in_specs=[whole_spec(a.shape)...  50.5 us
    pallas_call x1, Pallas kernels, ffn_forward(): pl.pallas_call(ffn_forward_kernel, grid=(hidden // chunk,), in_specs=whol...  35.8 us

profile of v9, /device:TPU:0, one launch (start us, length us, event | category | flops | bytes accessed | tf_op | source)
XLA Modules:
  0.0 858.0 jit_solution(9736579419635027557)
XLA Ops:
  1.4 1.3 multiply_reduce_fusion.1
  2.7 1.4 maximum_bitcast_fusion
  7.2 1.9 constant_dynamic-slice_fusion
  9.0 126.7 %gather_early.1 = (bf16[2,2,2,2,2,64,1024]{6,5,4,3,2,1,0:T(8,128)(2,1)}, bf16[2,2,2,2,2,32,3072]{6,5,4,3,2,1,0:T(8,128)(2,1)}, bf16[2,2,32,1024]{3,2,1,0:T(8,128...) custom-call(bf16[256,1024]{1,0:T(8,128)(2,1)} %refs_0_.1, ...), custom_call_target="tpu_custom_call" | custom-call | tf_op jit(solution)/shard_map/gather_early/pallas_call | solution.py:1463
  136.5 0.9 slice.31
  140.1 1.5 reshape.182.mod_ref
  141.6 1.0 copy.28
  142.6 223.6 %attend_forward.1 = (bf16[2,3,4096,128]{3,2,1,0:T(8,128)(2,1)}, bf16[2,4096,128]{2,1,0:T(8,128)(2,1)}, f32[2,8,4096]{2,1,0:T(8,128)}, bf16[1024,1024]{1,0:T(8,12...) custom-call(s32[2]{0:T(128)} %len_ref.3, ...), custom_call_target="tpu_custom_call" | custom-call | flops 34359738368 | bytes 8388608 | tf_op jit(solution)/shard_map/attend_forward/pallas_call | solution.py:333
  366.2 35.8 %ffn_forward.1 = (f32[1024,1024]{1,0:T(8,128)}, bf16[1024,4096]{1,0:T(8,128)(2,1)}, bf16[1024,4096]{1,0:T(8,128)(2,1)}, bf16[1024,1024]{1,0:T(8,128)(2,1)}, bf16...) custom-call(bf16[1024,1024]{1,0:T(8,128)(2,1)} %get-tuple-element.63.att_ref, bf16[1024,1024]{1,0:T(8,128)(2,1)} %bitcast.70, ...), custom_call_target="tpu_custom_call" | custom-call | flops 19327352832 | bytes 62914560 | tf_op jit(solution)/shard_map/ffn_forward/pallas_call | solution.py:759
  402.0 1.3 stack.19
  403.3 58.5 %ffn_backward.1 = (bf16[1024,4096]{1,0:T(8,128)(2,1)}, bf16[4096,1024]{1,0:T(8,128)(2,1)}, f32[1024,1024]{1,0:T(8,128)}, bf16[1024,1024]{1,0:T(8,128)(2,1)}, bf1...) custom-call(bf16[1024,1024]{1,0:T(8,128)(2,1)} %get-tuple-element.63.att_ref, bf16[1024,1024]{1,0:T(8,128)(2,1)} %bitcast.71, ...), custom_call_target="tpu_custom_call" | custom-call | flops 38654705664 | bytes 94371840 | tf_op jit(solution)/shard_map/ffn_backward/pallas_call | solution.py:802
  463.4 224.5 %attend_backward.1 = (bf16[1024,3072]{1,0:T(8,128)(2,1)}, bf16[3,2,2,2,128,1024]{5,4,3,2,1,0:T(8,128)(2,1)}, bf16[3,2,2,2,32,4096]{5,4,3,2,1,0:T(8,128)(2,1)}, bf16[3,2,2,2,32,1024]{5,4,3,2,1,0:T(8,128)(2,1)}) custom-call(s32[2]{0:T(128)} %len_ref.3, bf16[1024,1024]{1,0:T(8,128)(2,1)} %get-tuple-element.75.dout, ...), custom_call_target="tpu_custom_call" | custom-call | flops 85899345920 | bytes 8388608 | tf_op jit(solution)/shard_map/attend_backward/pallas_call | solution.py:581
  687.9 50.5 %leave_layer.1 = (bf16[1024,1024]{1,0:T(8,128)(2,1)}, bf16[1024,1024]{1,0:T(8,128)(2,1)}, f32[2,8,1024]{2,1,0:T(8,128)}, bf16[1024,3072]{1,0:T(8,128)(2,1)}, bf1...) custom-call(bf16[1024,3072]{1,0:T(8,128)(2,1)} %get-tuple-element.82, ...), custom_call_target="tpu_custom_call" | custom-call | flops 21474836480 | bytes 62914560 | tf_op jit(solution)/shard_map/leave_layer/pallas_call | solution.py:1016
  740.0 100.4 %reduce_grads.1 = (bf16[2,2,32,3072]{3,2,1,0:T(8,128)(2,1)}, bf16[2,2,64,1024]{3,2,1,0:T(8,128)(2,1)}, bf16[2,2,128,1024]{3,2,1,0:T(8,128)(2,1)}, bf16[2,2,32,40...) custom-call(bf16[2,2,2,2,2,32,3072]{6,5,4,3,2,1,0:T(8,128)(2,1)} %bitcast.44, ...), custom_call_target="tpu_custom_call" | custom-call | tf_op jit(solution)/shard_map/reduce_grads/pallas_call | solution.py:1234
  840.4 1.1 reshape.196
  842.2 2.2 bitcast_convert_fusion.3
  844.5 0.9 bitcast_convert_fusion.4
  845.3 1.3 bitcast_convert_fusion.2
  846.7 1.6 bitcast_convert_fusion.1
  848.3 1.6 bitcast_convert_fusion
  849.9 3.9 fusion.8
  853.9 1.3 copy.32
  855.2 1.0 copy-done.2
  856.2 1.3 copy.33
  (39 shorter events, 9.9 us)
Async XLA Ops:
  0.6 5.6 copy-start
  9.0 131.0 %copy-start.9 = (s32[2]{0:T(128)S(1)}, s32[2]{0:T(128)}, u32[]{:S(2)}) copy-start(s32[2]{0:T(128)} %len_ref.3) | copy-start | bytes 28
  687.9 51.4 %copy-start.8 = (f32[2,1,1024]{2,1,0:T(1,128)S(1)}, f32[2,1,1024]{2,1,0:T(1,128)}, u32[]{:S(2)}) copy-start(f32[2,1,1024]{2,1,0:T(1,128)} %stack.19) | copy-start | bytes 24580
  840.4 4.1 copy-start.7
  840.4 4.9 copy-start.6
  842.2 4.4 copy-start.5
  846.7 1.6 copy-start.4
  849.9 3.9 copy-start.3
  853.9 2.3 copy-start.2
  853.9 3.7 copy-start.1

commit v10 on v9

--- a/solution.py
+++ b/solution.py
@@ -144,17 +144,12 @@
 
 
 def early_jobs(weights, fulls):
-    orders = ((0, 1, 2, 3, 4), (0, 2, 3, 1, 4), (0, 3, 1, 2, 4))
+    orders = ((0, 1, 2, 3, 4), (0, 1, 3, 2, 4)) * 2
     return [
         (full, cols, quarter_of(weight, cols), (), order)
         for weight, full in zip(weights, fulls)
-        for cols, order in zip(split_columns(weight.shape[1], (1, 1, 1)), orders)
+        for cols, order in zip(split_columns(weight.shape[1], (1,) * 4), orders)
     ]
-
-
-def ahead_jobs(weights, helds):
-    every = [(weight, held, pl.ds(0, weight.shape[1])) for weight, held in zip(weights, helds)]
-    return [(held, cols, quarter_of(weight, cols), (), (0, 1)) for weight, held, cols in every]
 
 
 def late_jobs(helds, fulls):
@@ -280,10 +275,10 @@
                     send_out(utt, i * (bq // span) + part)
             return carry
 
-        half = frames // bq // 2
-        lax.fori_loop(0, half, block, 0)
+        most = frames // bq - 1
+        lax.fori_loop(0, most, block, 0)
         between()
-        lax.fori_loop(half, 2 * half, block, 0)
+        lax.fori_loop(most, most + 1, block, 0)
         keep = pltpu.make_async_copy(outs.at[utt], o_all.at[utt], slocal.at[2 + utt])
         keep.start()
         return [save, keep]
@@ -1383,12 +1378,20 @@
 
     jobs = early_jobs(weights, fulls)
     chain = WeightGather(jobs, send, recv, local.at[pl.ds(2, len(jobs))])
-    later = WeightGather(
-        ahead_jobs(laters, helds), asend, arecv, local.at[pl.ds(2 + len(jobs), ahead)]
-    )
     chain.stage()
     chain.stage()
-    later.stage()
+    late = []
+    for index, (weight, held) in enumerate(zip(laters, helds)):
+        source = quarter_of(weight, pl.ds(0, weight.shape[1]))
+        spot = held.at[me // 4, (me // 2) % 2]
+        own = pltpu.make_async_copy(source, spot, local.at[2 + len(jobs) + index])
+        own.start()
+        late.append(own)
+        for flip in (2, 3, 1):
+            at = 3 * index + flip - 1
+            copy = remote(source, spot, asend.at[at], arecv.at[at], seq_flip(2 * flip))
+            copy.start()
+            late.append(copy)
     for copy in small:
         copy.wait()
     own_seq.wait()
@@ -1401,7 +1404,6 @@
     for utt in range(utts):
         mods[utt, 0:6, :] = total[utt * 6 : utt * 6 + 6]
     chain.stage()
-    later.stage()
     chain.stage()
     chain.stage()
     chain.finish()
@@ -1448,7 +1450,8 @@
         return carry
 
     lax.fori_loop(0, rows // block, enter, 0)
-    later.finish()
+    for copy in late:
+        copy.wait()
     pltpu.make_async_copy(res, res_out, put.at[0]).wait()
     pltpu.make_async_copy(proj, proj_out, put.at[1]).wait()
 
@@ -1456,7 +1459,7 @@
 def gather_early(weights, laters, seq_small, batch_small, first, second, cos, sin, block=256):
     anywhere = pl.BlockSpec(memory_space=pl.ANY)
     vmem = pl.BlockSpec(memory_space=pltpu.VMEM)
-    jobs, ahead = 3 * len(weights), len(laters)
+    jobs, ahead = 4 * len(weights), len(laters)
     rows, width = first.shape
     dma = pltpu.SemaphoreType.DMA
     quarter = lambda lead, w: jax.ShapeDtypeStruct((2,) * lead + (w.shape[0] // 4, w.shape[1]), BF)

time: 868 us -> 836 us (0.963)
  Pallas kernels: 820 us -> 789 us
    pallas_call x1, Pallas kernels: 127 us -> 107 us  [gather_early(): pl.pallas_call(functools.partial(gather_kernel, count=len(weights), ahead...]
    pallas_call x1, Pallas kernels: 224 us -> 212 us  [attend_forward(): pl.pallas_call(functools.partial(attend_forward_kernel, span=span, bq=bq,...]
where the time goes in v10:
time: 836 us; the launch traced here: 827 us
  Pallas kernels  789 us (94%)
  local copies, waits for them, and re-layouts  17.2 us (2%)
  other arithmetic  14.1 us (2%)
    pallas_call x1, Pallas kernels, attend_backward(): pl.pallas_call(functools.partial(attend_backward_kernel, span=span, block...  225 us
    pallas_call x1, Pallas kernels, attend_forward(): pl.pallas_call(functools.partial(attend_forward_kernel, span=span, bq=bq,...  212 us
    pallas_call x1, Pallas kernels, gather_early(): pl.pallas_call(functools.partial(gather_kernel, count=len(weights), ahead...  107 us
    pallas_call x1, Pallas kernels, reduce_grads(): pl.pallas_call(functools.partial(reduce_kernel, halves=len(halves), folds...  99.7 us
    pallas_call x1, Pallas kernels, ffn_backward(): pl.pallas_call(ffn_backward_kernel, grid=(hidden // chunk,), in_specs=who...  58.5 us
    pallas_call x1, Pallas kernels, leave_layer(): pl.pallas_call(leave_kernel, grid=(steps,), in_specs=[whole_spec(a.shape)...  50.5 us
    pallas_call x1, Pallas kernels, ffn_forward(): pl.pallas_call(ffn_forward_kernel, grid=(hidden // chunk,), in_specs=whol...  35.8 us

profile of v10, /device:TPU:0, one launch (start us, length us, event | category | flops | bytes accessed | tf_op | source)
XLA Modules:
  0.0 826.8 jit_solution(13450144227356557802)
XLA Ops:
  1.4 1.3 multiply_reduce_fusion.1
  2.7 1.4 maximum_bitcast_fusion
  7.2 1.9 constant_dynamic-slice_fusion
  9.0 106.8 %gather_early.1 = (bf16[2,2,2,2,2,64,1024]{6,5,4,3,2,1,0:T(8,128)(2,1)}, bf16[2,2,2,2,2,32,3072]{6,5,4,3,2,1,0:T(8,128)(2,1)}, bf16[2,2,32,1024]{3,2,1,0:T(8,128...) custom-call(bf16[256,1024]{1,0:T(8,128)(2,1)} %refs_0_.1, ...), custom_call_target="tpu_custom_call" | custom-call | tf_op jit(solution)/shard_map/gather_early/pallas_call | solution.py:1466
  116.5 0.9 slice.31
  120.2 1.5 reshape.182.mod_ref
  121.6 1.0 copy.28
  122.7 212.2 %attend_forward.1 = (bf16[2,3,4096,128]{3,2,1,0:T(8,128)(2,1)}, bf16[2,4096,128]{2,1,0:T(8,128)(2,1)}, f32[2,8,4096]{2,1,0:T(8,128)}, bf16[1024,1024]{1,0:T(8,12...) custom-call(s32[2]{0:T(128)} %len_ref.3, ...), custom_call_target="tpu_custom_call" | custom-call | flops 34359738368 | bytes 8388608 | tf_op jit(solution)/shard_map/attend_forward/pallas_call | solution.py:328
  334.9 35.8 %ffn_forward.1 = (f32[1024,1024]{1,0:T(8,128)}, bf16[1024,4096]{1,0:T(8,128)(2,1)}, bf16[1024,4096]{1,0:T(8,128)(2,1)}, bf16[1024,1024]{1,0:T(8,128)(2,1)}, bf16...) custom-call(bf16[1024,1024]{1,0:T(8,128)(2,1)} %get-tuple-element.63.att_ref, bf16[1024,1024]{1,0:T(8,128)(2,1)} %bitcast.70, ...), custom_call_target="tpu_custom_call" | custom-call | flops 19327352832 | bytes 62914560 | tf_op jit(solution)/shard_map/ffn_forward/pallas_call | solution.py:754
  370.7 1.3 stack.19
  372.0 58.5 %ffn_backward.1 = (bf16[1024,4096]{1,0:T(8,128)(2,1)}, bf16[4096,1024]{1,0:T(8,128)(2,1)}, f32[1024,1024]{1,0:T(8,128)}, bf16[1024,1024]{1,0:T(8,128)(2,1)}, bf1...) custom-call(bf16[1024,1024]{1,0:T(8,128)(2,1)} %get-tuple-element.63.att_ref, bf16[1024,1024]{1,0:T(8,128)(2,1)} %bitcast.71, ...), custom_call_target="tpu_custom_call" | custom-call | flops 38654705664 | bytes 94371840 | tf_op jit(solution)/shard_map/ffn_backward/pallas_call | solution.py:797
  432.1 225.2 %attend_backward.1 = (bf16[1024,3072]{1,0:T(8,128)(2,1)}, bf16[3,2,2,2,128,1024]{5,4,3,2,1,0:T(8,128)(2,1)}, bf16[3,2,2,2,32,4096]{5,4,3,2,1,0:T(8,128)(2,1)}, bf16[3,2,2,2,32,1024]{5,4,3,2,1,0:T(8,128)(2,1)}) custom-call(s32[2]{0:T(128)} %len_ref.3, bf16[1024,1024]{1,0:T(8,128)(2,1)} %get-tuple-element.75.dout, ...), custom_call_target="tpu_custom_call" | custom-call | flops 85899345920 | bytes 8388608 | tf_op jit(solution)/shard_map/attend_backward/pallas_call | solution.py:576
  657.4 50.5 %leave_layer.1 = (bf16[1024,1024]{1,0:T(8,128)(2,1)}, bf16[1024,1024]{1,0:T(8,128)(2,1)}, f32[2,8,1024]{2,1,0:T(8,128)}, bf16[1024,3072]{1,0:T(8,128)(2,1)}, bf1...) custom-call(bf16[1024,3072]{1,0:T(8,128)(2,1)} %get-tuple-element.82, ...), custom_call_target="tpu_custom_call" | custom-call | flops 21474836480 | bytes 62914560 | tf_op jit(solution)/shard_map/leave_layer/pallas_call | solution.py:1011
  709.4 99.7 %reduce_grads.1 = (bf16[2,2,32,3072]{3,2,1,0:T(8,128)(2,1)}, bf16[2,2,64,1024]{3,2,1,0:T(8,128)(2,1)}, bf16[2,2,128,1024]{3,2,1,0:T(8,128)(2,1)}, bf16[2,2,32,40...) custom-call(bf16[2,2,2,2,2,32,3072]{6,5,4,3,2,1,0:T(8,128)(2,1)} %bitcast.44, ...), custom_call_target="tpu_custom_call" | custom-call | tf_op jit(solution)/shard_map/reduce_grads/pallas_call | solution.py:1229
  809.2 1.1 reshape.196
  811.0 2.2 bitcast_convert_fusion.3
  813.3 0.9 bitcast_convert_fusion.4
  814.1 1.3 bitcast_convert_fusion.2
  815.5 1.6 bitcast_convert_fusion.1
  817.1 1.6 bitcast_convert_fusion
  818.7 3.9 fusion.8
  822.6 1.3 copy.32
  824.0 1.0 copy-done.2
  825.0 1.3 copy.33
  (39 shorter events, 9.9 us)
Async XLA Ops:
  0.6 5.6 copy-start
  9.0 111.0 %copy-start.9 = (s32[2]{0:T(128)S(1)}, s32[2]{0:T(128)}, u32[]{:S(2)}) copy-start(s32[2]{0:T(128)} %len_ref.3) | copy-start | bytes 28
  657.4 51.4 %copy-start.8 = (f32[2,1,1024]{2,1,0:T(1,128)S(1)}, f32[2,1,1024]{2,1,0:T(1,128)}, u32[]{:S(2)}) copy-start(f32[2,1,1024]{2,1,0:T(1,128)} %stack.19) | copy-start | bytes 24580
  809.2 4.1 copy-start.7
  809.2 4.9 copy-start.6
  811.0 4.4 copy-start.5
  815.5 1.6 copy-start.4
  818.7 3.9 copy-start.3
  822.6 2.3 copy-start.2
  822.6 3.7 copy-start.1

commit v11 on v10

--- a/solution.py
+++ b/solution.py
@@ -156,7 +156,7 @@
     return [
         (full, cols, held.at[:, :, :, cols], (0, 1), order)
         for held, full in zip(helds, fulls)
-        for cols, order in zip(split_columns(held.shape[3], (3, 1)), ((2, 3, 4), (3, 2, 4)))
+        for cols, order in zip(split_columns(held.shape[3], (2, 1)), ((2, 3, 4), (3, 2, 4)))
     ]
 
 

time: 836 us -> 836 us (level)
  no operation moved by 1% of the time
where the time goes in v11:
time: 836 us; the launch traced here: 827 us
  Pallas kernels  789 us (94%)
  local copies, waits for them, and re-layouts  17.2 us (2%)
  other arithmetic  14.1 us (2%)
    pallas_call x1, Pallas kernels, attend_backward(): pl.pallas_call(functools.partial(attend_backward_kernel, span=span, block...  225 us
    pallas_call x1, Pallas kernels, attend_forward(): pl.pallas_call(functools.partial(attend_forward_kernel, span=span, bq=bq,...  212 us
    pallas_call x1, Pallas kernels, gather_early(): pl.pallas_call(functools.partial(gather_kernel, count=len(weights), ahead...  107 us
    pallas_call x1, Pallas kernels, reduce_grads(): pl.pallas_call(functools.partial(reduce_kernel, halves=len(halves), folds...  99.7 us
    pallas_call x1, Pallas kernels, ffn_backward(): pl.pallas_call(ffn_backward_kernel, grid=(hidden // chunk,), in_specs=who...  58.5 us
    pallas_call x1, Pallas kernels, leave_layer(): pl.pallas_call(leave_kernel, grid=(steps,), in_specs=[whole_spec(a.shape)...  50.5 us
    pallas_call x1, Pallas kernels, ffn_forward(): pl.pallas_call(ffn_forward_kernel, grid=(hidden // chunk,), in_specs=whol...  35.8 us

profile of v11, /device:TPU:0, one launch (start us, length us, event | category | flops | bytes accessed | tf_op | source)
XLA Modules:
  0.0 826.8 jit_solution(8619951833005551435)
XLA Ops:
  1.4 1.3 multiply_reduce_fusion.1
  2.7 1.4 maximum_bitcast_fusion
  7.2 1.9 constant_dynamic-slice_fusion
  9.0 106.8 %gather_early.1 = (bf16[2,2,2,2,2,64,1024]{6,5,4,3,2,1,0:T(8,128)(2,1)}, bf16[2,2,2,2,2,32,3072]{6,5,4,3,2,1,0:T(8,128)(2,1)}, bf16[2,2,32,1024]{3,2,1,0:T(8,128...) custom-call(bf16[256,1024]{1,0:T(8,128)(2,1)} %refs_0_.1, ...), custom_call_target="tpu_custom_call" | custom-call | tf_op jit(solution)/shard_map/gather_early/pallas_call | solution.py:1466
  116.5 0.9 slice.31
  120.2 1.5 reshape.182.mod_ref
  121.6 1.0 copy.28
  122.7 212.3 %attend_forward.1 = (bf16[2,3,4096,128]{3,2,1,0:T(8,128)(2,1)}, bf16[2,4096,128]{2,1,0:T(8,128)(2,1)}, f32[2,8,4096]{2,1,0:T(8,128)}, bf16[1024,1024]{1,0:T(8,12...) custom-call(s32[2]{0:T(128)} %len_ref.3, ...), custom_call_target="tpu_custom_call" | custom-call | flops 34359738368 | bytes 8388608 | tf_op jit(solution)/shard_map/attend_forward/pallas_call | solution.py:328
  335.0 35.8 %ffn_forward.1 = (f32[1024,1024]{1,0:T(8,128)}, bf16[1024,4096]{1,0:T(8,128)(2,1)}, bf16[1024,4096]{1,0:T(8,128)(2,1)}, bf16[1024,1024]{1,0:T(8,128)(2,1)}, bf16...) custom-call(bf16[1024,1024]{1,0:T(8,128)(2,1)} %get-tuple-element.63.att_ref, bf16[1024,1024]{1,0:T(8,128)(2,1)} %bitcast.70, ...), custom_call_target="tpu_custom_call" | custom-call | flops 19327352832 | bytes 62914560 | tf_op jit(solution)/shard_map/ffn_forward/pallas_call | solution.py:754
  370.7 1.3 stack.19
  372.0 58.5 %ffn_backward.1 = (bf16[1024,4096]{1,0:T(8,128)(2,1)}, bf16[4096,1024]{1,0:T(8,128)(2,1)}, f32[1024,1024]{1,0:T(8,128)}, bf16[1024,1024]{1,0:T(8,128)(2,1)}, bf1...) custom-call(bf16[1024,1024]{1,0:T(8,128)(2,1)} %get-tuple-element.63.att_ref, bf16[1024,1024]{1,0:T(8,128)(2,1)} %bitcast.71, ...), custom_call_target="tpu_custom_call" | custom-call | flops 38654705664 | bytes 94371840 | tf_op jit(solution)/shard_map/ffn_backward/pallas_call | solution.py:797
  432.2 225.2 %attend_backward.1 = (bf16[1024,3072]{1,0:T(8,128)(2,1)}, bf16[3,2,2,2,128,1024]{5,4,3,2,1,0:T(8,128)(2,1)}, bf16[3,2,2,2,32,4096]{5,4,3,2,1,0:T(8,128)(2,1)}, bf16[3,2,2,2,32,1024]{5,4,3,2,1,0:T(8,128)(2,1)}) custom-call(s32[2]{0:T(128)} %len_ref.3, bf16[1024,1024]{1,0:T(8,128)(2,1)} %get-tuple-element.75.dout, ...), custom_call_target="tpu_custom_call" | custom-call | flops 85899345920 | bytes 8388608 | tf_op jit(solution)/shard_map/attend_backward/pallas_call | solution.py:576
  657.5 50.5 %leave_layer.1 = (bf16[1024,1024]{1,0:T(8,128)(2,1)}, bf16[1024,1024]{1,0:T(8,128)(2,1)}, f32[2,8,1024]{2,1,0:T(8,128)}, bf16[1024,3072]{1,0:T(8,128)(2,1)}, bf1...) custom-call(bf16[1024,3072]{1,0:T(8,128)(2,1)} %get-tuple-element.82, ...), custom_call_target="tpu_custom_call" | custom-call | flops 21474836480 | bytes 62914560 | tf_op jit(solution)/shard_map/leave_layer/pallas_call | solution.py:1011
  709.5 99.7 %reduce_grads.1 = (bf16[2,2,32,3072]{3,2,1,0:T(8,128)(2,1)}, bf16[2,2,64,1024]{3,2,1,0:T(8,128)(2,1)}, bf16[2,2,128,1024]{3,2,1,0:T(8,128)(2,1)}, bf16[2,2,32,40...) custom-call(bf16[2,2,2,2,2,32,3072]{6,5,4,3,2,1,0:T(8,128)(2,1)} %bitcast.44, ...), custom_call_target="tpu_custom_call" | custom-call | tf_op jit(solution)/shard_map/reduce_grads/pallas_call | solution.py:1229
  809.3 1.1 reshape.196
  811.1 2.2 bitcast_convert_fusion.3
  813.3 0.9 bitcast_convert_fusion.4
  814.2 1.3 bitcast_convert_fusion.2
  815.5 1.6 bitcast_convert_fusion.1
  817.2 1.6 bitcast_convert_fusion
  818.8 3.9 fusion.8
  822.7 1.3 copy.32
  824.0 1.0 copy-done.2
  825.1 1.3 copy.33
  (39 shorter events, 9.9 us)
Async XLA Ops:
  0.6 5.6 copy-start
  9.0 111.0 %copy-start.9 = (s32[2]{0:T(128)S(1)}, s32[2]{0:T(128)}, u32[]{:S(2)}) copy-start(s32[2]{0:T(128)} %len_ref.3) | copy-start | bytes 28
  657.5 51.4 %copy-start.8 = (f32[2,1,1024]{2,1,0:T(1,128)S(1)}, f32[2,1,1024]{2,1,0:T(1,128)}, u32[]{:S(2)}) copy-start(f32[2,1,1024]{2,1,0:T(1,128)} %stack.19) | copy-start | bytes 24580
  809.2 4.1 copy-start.7
  809.2 4.9 copy-start.6
  811.1 4.4 copy-start.5
  815.5 1.6 copy-start.4
  818.8 3.9 copy-start.3
  822.7 2.3 copy-start.2
  822.7 3.7 copy-start.1
